TPU v7x, 512 devices: a whole 4x8x8 slice. The times are simulated.
512 devices in a mesh: frame: 16 (over y_lo, x, core), row: 8 (over z), head: 4 (over y_hi).
Axes of the slice: x: 4, y: 8 (y_hi: 4, y_lo: 2; y = y_hi * 2 + y_lo), z: 8, core: 2. Of those that a mesh axis runs over, the one named last changes fastest.
Arguments:
- queries: bfloat16 [96, 32, 8, 1536], P('frame', 'row', None, 'head'), may hold values from -6 to 6
- key_tokens: bfloat16 [96, 32, 8, 1536], P('frame', 'row', None, 'head'), may hold values from -6 to 6
- value_tokens: bfloat16 [96, 32, 8, 1536], P('frame', 'row', None, 'head'), may hold values from -6 to 6
- grad_out: bfloat16 [96, 32, 8, 1536], P('frame', 'row', None, 'head'), may hold values from -6 to 6
- tile_pairs: int32 [16, 8, 1, 27], P('frame', 'row'), may hold values from 0 to 1, as said below
Outputs:
- attended: bfloat16 [96, 32, 8, 1536], P('frame', 'row', 'head')
- query_grad: bfloat16 [96, 32, 8, 1536], P('frame', 'row', 'head')
- key_grad: bfloat16 [96, 32, 8, 1536], P('frame', 'row', 'head')
- value_grad: bfloat16 [96, 32, 8, 1536], P('frame', 'row', 'head')
Inputs may be any that keep to these rules, and one draw needn't show every extreme that they name: tile_pairs[t, 13], the pair of a tile with itself, is 1 for every tile t.
All inputs are finite; a program needn't handle non-finite values.
Results may differ from a plain program's by a relative error of at most 0.012.
The roundings to bfloat16 on the way count: a program that leaves them out, or rounds other values in their place, can miss the bound.
Values may be sent and summed in bfloat16 or wider, within the bound.
No kernel may reach another device: no remote copies, remote signals or barrier semaphores. Data moves between devices by JAX's collectives and lax.ppermute only.
A program may use at most 64 MiB of HBM per device.

v0:
```python
import jax
import jax.numpy as jnp
from jax import lax
from jax.sharding import PartitionSpec as P

HEAD_DIM = 128
TILE_F = 6
TILE_R = 4
TILE_C = 8


def shifted(value, axis, steps):
    count = lax.axis_size(axis)
    first, last = (max(0, -steps), min(count, count - steps))
    return lax.ppermute(value, axis, [(source, source + steps) for source in range(first, last)])


def extended(cells, sides, width):
    for axis, dim in sides:
        count = lax.axis_size(axis)
        ends = count - 1
        head = lax.slice_in_dim(cells, 0, width, axis=dim)
        tail = lax.slice_in_dim(cells, cells.shape[dim] - width, cells.shape[dim], axis=dim)
        cells = jnp.concatenate(
            [
                lax.ppermute(tail, axis, [(i, (i + 1) % count) for i in range(ends)]),
                cells,
                lax.ppermute(head, axis, [((i + 1) % count, i) for i in range(ends)]),
            ],
            axis=dim,
        )
    return cells


def offset_table(inner_count, outer_count, tile_len, direction_sign, offset_add):
    near_tiles = jnp.arange(inner_count, dtype=jnp.int32) // tile_len
    far_tiles = jnp.arange(outer_count, dtype=jnp.int32) // tile_len
    offsets = direction_sign * (far_tiles[None, :] - near_tiles[:, None]) + offset_add
    return (offsets[:, :, None] == jnp.arange(3, dtype=jnp.int32)[None, None, :]).astype(
        jnp.float32
    )


def tile_tokens(pattern, span_f, span_r, span_c):
    grown_grid = jnp.repeat(
        jnp.repeat(jnp.repeat(pattern, span_f, axis=0), span_r, axis=1), span_c, axis=2
    )
    return grown_grid.reshape(grown_grid.shape[:3] + (3, 3, 3)).astype(jnp.float32)


def inside_mask(first_cell, cell_count, upper_bound):
    positions = first_cell + jnp.arange(cell_count, dtype=jnp.int32)
    return ((positions >= 0) & (positions < upper_bound)).astype(jnp.float32)


def heads_first(source, row_count, heads_dev):
    return source.reshape(row_count, heads_dev, HEAD_DIM).transpose(1, 0, 2)


def heads_last(source, target_shape):
    return source.transpose(1, 0, 2).reshape(target_shape)


def fold_rows(grown_grid, rim_width):
    inner_size = grown_grid.shape[1] - 2 * rim_width
    middle = grown_grid[:, rim_width : rim_width + inner_size]
    for direction in (-1, 1):
        if direction == -1:
            border = grown_grid[:, :rim_width]
        else:
            border = grown_grid[:, rim_width + inner_size :]
        arrived = shifted(border.astype(jnp.bfloat16), "row", direction).astype(border.dtype)
        if direction == -1:
            middle = middle.at[:, inner_size - rim_width :].add(arrived)
        else:
            middle = middle.at[:, :rim_width].add(arrived)
    return middle


def fold_frames(grown_grid, rim_width):
    inner_size = grown_grid.shape[0] - 2 * rim_width
    middle = grown_grid[rim_width : rim_width + inner_size]
    for direction in (-1, 1):
        if direction == -1:
            border = grown_grid[:rim_width]
        else:
            border = grown_grid[rim_width + inner_size :]
        arrived = shifted(border.astype(jnp.bfloat16), "frame", direction).astype(border.dtype)
        if direction == -1:
            middle = middle.at[inner_size - rim_width :].add(arrived)
        else:
            middle = middle.at[:rim_width].add(arrived)
    return middle


def body(queries, key_tokens, value_tokens, grad_out, tile_pairs):
    frames_dev, rows_dev, columns, feat_width = queries.shape
    heads_dev = feat_width // HEAD_DIM
    scaling = HEAD_DIM ** (-0.5)
    tokens = frames_dev * rows_dev * columns
    ext_f = frames_dev + 2 * TILE_F
    ext_r = rows_dev + 2 * TILE_R
    near_tokens = ext_f * ext_r * columns
    local_shape = (frames_dev, rows_dev, columns, feat_width)
    frame_first = lax.axis_index("frame") * frames_dev - TILE_F
    row_first = lax.axis_index("row") * rows_dev - TILE_R
    frame_limit = lax.axis_size("frame") * frames_dev
    row_limit = lax.axis_size("row") * rows_dev
    packed_kv = jnp.concatenate([key_tokens, value_tokens], axis=3)
    framed_kv = extended(packed_kv, (("frame", 0),), TILE_F)
    near_kv = extended(framed_kv, (("row", 1),), TILE_R)
    key_near = heads_first(near_kv[..., :feat_width], near_tokens, heads_dev)
    value_near = heads_first(near_kv[..., feat_width:], near_tokens, heads_dev)
    table_f = (
        offset_table(frames_dev, ext_f, TILE_F, 1, 0)
        * inside_mask(frame_first, ext_f, frame_limit)[None, :, None]
    )
    table_r = (
        offset_table(rows_dev, ext_r, TILE_R, 1, 0)
        * inside_mask(row_first, ext_r, row_limit)[None, :, None]
    )
    column_table = offset_table(columns, columns, TILE_C, 1, 1)
    pattern_tok = tile_tokens(tile_pairs, TILE_F, TILE_R, TILE_C)
    allowed = (
        jnp.einsum(
            "frcxyz,fex,rgy,chz->frcegh", pattern_tok, table_f, table_r, column_table
        ).reshape(tokens, near_tokens)
        > 0.5
    )

    def attend_head(head_items):
        query_one, key_one, value_one, grad_one = head_items
        scores = (
            jnp.einsum("qd,kd->qk", query_one, key_one, preferred_element_type=jnp.float32)
            * scaling
        )
        scores = jnp.where(allowed, scores, -jnp.inf)
        row_max = jnp.max(scores, axis=1)
        weights = jnp.exp(scores - row_max[:, None])
        row_sum = jnp.sum(weights, axis=1)
        weights = weights / row_sum[:, None]
        rounded = weights.astype(jnp.bfloat16)
        attended = jnp.dot(rounded, value_one, preferred_element_type=jnp.float32).astype(
            jnp.bfloat16
        )
        spread = jnp.sum(grad_one.astype(jnp.float32) * attended.astype(jnp.float32), axis=1)
        pushes = jnp.einsum("qd,kd->qk", grad_one, value_one, preferred_element_type=jnp.float32)
        slopes = (weights * (pushes - spread[:, None])).astype(jnp.bfloat16)
        query_grad = (
            scaling * jnp.dot(slopes, key_one, preferred_element_type=jnp.float32)
        ).astype(jnp.bfloat16)
        summary = jnp.stack([row_max, row_sum - 1.0, spread])
        key_term = scaling * jnp.einsum(
            "qk,qd->kd", slopes, query_one, preferred_element_type=jnp.float32
        )
        value_term = jnp.einsum("qk,qd->kd", rounded, grad_one, preferred_element_type=jnp.float32)
        return (attended, query_grad, summary, jnp.concatenate([key_term, value_term], axis=1))

    query_heads = heads_first(queries, tokens, heads_dev)
    grad_heads = heads_first(grad_out, tokens, heads_dev)
    head_inputs = (query_heads, key_near, value_near, grad_heads)
    attended, query_grad, summary, near_terms = lax.map(attend_head, head_inputs)
    grown_grid = heads_last(near_terms, (ext_f, ext_r, columns, 2 * feat_width))
    folded = fold_frames(fold_rows(grown_grid, TILE_R), TILE_F)
    split_terms = folded.reshape(frames_dev, rows_dev, columns, heads_dev, 2, HEAD_DIM)
    key_grad = split_terms[:, :, :, :, 0, :].reshape(local_shape).astype(jnp.bfloat16)
    value_grad = split_terms[:, :, :, :, 1, :].reshape(local_shape).astype(jnp.bfloat16)
    attended_grid = heads_last(attended, local_shape)
    query_grid = heads_last(query_grad, local_shape)
    attended_out, query_out, key_out, value_out = (
        lax.all_to_all(attended_grid, "head", split_axis=2, concat_axis=3, tiled=True),
        lax.all_to_all(query_grid, "head", split_axis=2, concat_axis=3, tiled=True),
        lax.all_to_all(key_grad, "head", split_axis=2, concat_axis=3, tiled=True),
        lax.all_to_all(value_grad, "head", split_axis=2, concat_axis=3, tiled=True),
    )
    return (attended_out, query_out, key_out, value_out)


def solution(mesh):
    placed = (
        P("frame", "row", None, "head"),
        P("frame", "row", None, "head"),
        P("frame", "row", None, "head"),
        P("frame", "row", None, "head"),
        P("frame", "row", None, None),
    )
    return jax.shard_map(
        body,
        mesh=mesh,
        in_specs=placed,
        out_specs=(
            P("frame", "row", "head", None),
            P("frame", "row", "head", None),
            P("frame", "row", "head", None),
            P("frame", "row", "head", None),
        ),
        check_vma=False,
    )
```

profile of v0, /device:TPU:200, one launch (start us, length us, event | category | flops | bytes accessed | tf_op | source)
XLA Modules:
  0.0 211.5 jit_solution(4459335140950308785)
XLA Ops:
  2.5 4.0 %collective-permute-start.1 = (bf16[6,4,8,768]{3,2,1,0:T(8,128)(2,1)S(1)}, bf16[6,4,8,768]{3,2,1,0:T(8,128)(2,1)S(1)}, u32[]{:S(2)}, u32[]{:S(2)}) collective-permute-start(bf16[6,4,8,768]{3,2,1,0:T(8,128)(2,1)S(1)} %constant_dynamic-update-slice_fusion), channel_id=1, source_target_pairs={{32,0},{64,32},{96,64},{128,96},{160,128},{192,160},{224,192},{256... | collective-permute-start | bytes 884744 | tf_op jit(solution)/shard_map/ppermute | solution.py:28
  6.5 1.9 collective-permute-start
  12.0 1.9 convolution_bitcast_fusion
  14.0 2.7 %collective-permute-done = bf16[6,4,8,768]{3,2,1,0:T(8,128)(2,1)S(1)} collective-permute-done((bf16[6,4,8,768]{3,2,1,0:T(8,128)(2,1)S(1)}, bf16[6,4,8,768]{3,2,1,0:T(8,128)(2,1)S(1)}, u32[]{:S(2)}, u32[]{:S(2)}) %collective-permute-start) | collective-permute-done | bytes 294944 | tf_op jit(solution)/shard_map/ppermute | solution.py:26
  16.7 1.1 pad_maximum_fusion.1
  17.8 1.9 collective-permute-start.3
  19.7 5.5 %collective-permute-start.2 = (bf16[18,4,8,768]{3,2,1,0:T(8,128)(2,1)}, bf16[18,4,8,768]{3,2,1,0:T(8,128)(2,1)}, u32[]{:S(2)}, u32[]{:S(2)}) collective-permute-start(bf16[18,4,8,768]{3,2,1,0:T(8,128)(2,1)} %pad_maximum_fusion.1), channel_id=1, source_target_pairs={{0,4},{4,8},{8,12},{12,16},{16,20},{20,24},{24,28},{1,5},{5,9},{9,... | collective-permute-start | bytes 2654216 | tf_op jit(solution)/shard_map/ppermute | solution.py:26
  25.2 3.2 %compare_bitcast_fusion = pred[6,4,8,18,12,8]{3,4,1,5,2,0:T(8,128)(4,1)S(1)} fusion(bf16[8,8,6,4,3,12]{5,1,4,2,0,3:T(8,128)(2,1)S(1)} %copy-done.1, bf16[18]{0:T(256)(128)(2,1)S(1)} %and_convert_fusion, s32[6,18]{1,0:T(8,128)S(1)} %broadcast_subtract_fusion), kind=kOutput, calls=%fused_computation.43 | convolution fusion | flops 2323080 | bytes 442836 | tf_op jit(solution)/shard_map/frcxyz,fex,rgy,chz->frcegh/dot_general | solution.py:125
  28.5 25.8 %copy.43 = pred[6,4,8,18,12,8]{2,1,0,5,4,3:T(4,128)(4,1)} copy(pred[6,4,8,18,12,8]{3,4,1,5,2,0:T(8,128)(4,1)S(1)} %compare_bitcast_fusion) | data formatting | bytes 663552 | tf_op jit(solution)/shard_map/gt | solution.py:125
  54.3 15.2 %gt.15 = pred[192,1728]{0,1:T(32,128)(4,1)S(1)} reshape(pred[6,4,8,18,12,8]{2,1,0,5,4,3:T(4,128)(4,1)} %copy.43) | data formatting | bytes 663552 | tf_op jit(solution)/shard_map/gt | solution.py:125
  70.1 1.7 pad_maximum_fusion
  71.7 1.4 fusion.68
  73.5 1.3 copy.47
  74.8 3.6 %reshape.370 = bf16[1728,3,128]{2,1,0:T(4,128)(2,1)S(1)} reshape(bf16[18,12,8,384]{3,2,1,0:T(8,128)(2,1)} %get-tuple-element.190) | data formatting | bytes 2654208 | tf_op jit(solution)/shard_map/reshape | solution.py:57
  78.6 22.6 %while.22 = (s32[]{:T(128)}, bf16[3,192,128]{2,1,0:T(8,128)(2,1)}, bf16[3,192,128]{2,1,0:T(8,128)(2,1)}, f32[3,1728,256]{2,1,0:T(8,128)}, bf16[3,192,128]{2,1,0:...) while((s32[]{:T(128)}, bf16[3,192,128]{2,1,0:T(8,128)(2,1)}, ...), condition=%wide.region_4.5_spmd, body=%wide.region_0.4_spmd.sunk | while | flops 515751360 | bytes 22575284 | solution.py:162
  78.6 1.4 fusion.94
  80.4 1.1 bitcast_dynamic-update-slice_fusion.2
  82.5 1.0 fusion.97
  83.5 1.3 convolution_multiply_fusion.4
  84.8 1.4 fusion.99
  86.2 1.4 fusion.94
  87.9 1.1 bitcast_dynamic-update-slice_fusion.2
  90.1 1.0 fusion.97
  91.1 1.3 convolution_multiply_fusion.4
  92.3 1.4 fusion.99
  93.7 1.4 fusion.94
  95.4 1.1 bitcast_dynamic-update-slice_fusion.2
  97.6 1.0 fusion.97
  98.6 1.3 convolution_multiply_fusion.4
  99.9 1.3 fusion.99
  101.2 13.0 %copy.57 = f32[1728,3,256]{2,1,0:T(4,128)} copy(f32[1728,3,256]{2,0,1:T(8,128)} %bitcast.123) | data formatting | bytes 10616832 | tf_op jit(solution)/shard_map/transpose | solution.py:61
  114.2 9.6 %reshape.375 = f32[18,12,8,768]{3,2,1,0:T(8,128)} reshape(f32[1728,3,256]{2,1,0:T(4,128)} %copy.57) | data formatting | bytes 10616832 | tf_op jit(solution)/shard_map/reshape | solution.py:61
  123.8 2.8 %convert.12 = bf16[18,12,8,768]{3,2,1,0:T(8,128)(2,1)S(1)} convert(f32[18,12,8,768]{3,2,1,0:T(8,128)} %reshape.375) | non-fusion elementwise | flops 1327104 | bytes 7962624 | tf_op jit(solution)/shard_map/convert.5
  126.8 1.9 collective-permute-start.4
  128.7 5.3 %collective-permute-start.5 = (bf16[18,4,8,768]{3,2,1,0:T(8,128)(2,1)S(1)}, bf16[18,4,8,768]{3,2,1,0:T(8,128)(2,1)S(1)}, u32[]{:S(2)}, u32[]{:S(2)}) collective-permute-start(bf16[18,4,8,768]{3,2,1,0:T(8,128)(2,1)S(1)} %get-tuple-element.188), channel_id=1, source_target_pairs={{0,4},{4,8},{8,12},{12,16},{16,20},{20,24},{24,28},{1,5},{5,9},{9,... | collective-permute-start | bytes 2654216 | tf_op jit(solution)/shard_map/ppermute | solution.py:15
  134.0 14.0 %collective-permute-done.4 = bf16[18,4,8,768]{3,2,1,0:T(8,128)(2,1)S(1)} collective-permute-done((bf16[18,4,8,768]{3,2,1,0:T(8,128)(2,1)S(1)}, bf16[18,4,8,768]{3,2,1,0:T(8,128)(2,1)S(1)}, u32[]{:S(2)}, u32[]{:S(2)}) %collective-permute-start.4) | collective-permute-done | bytes 884768 | tf_op jit(solution)/shard_map/ppermute | solution.py:15
  147.9 1.3 collective-permute-done.5
  149.3 1.9 fusion.64
  151.3 5.2 %collective-permute-start.6 = (bf16[6,4,8,768]{3,2,1,0:T(8,128)(2,1)S(1)}, bf16[6,4,8,768]{3,2,1,0:T(8,128)(2,1)S(1)}, u32[]{:S(2)}, u32[]{:S(2)}) collective-permute-start(bf16[6,4,8,768]{3,2,1,0:T(8,128)(2,1)S(1)} %get-tuple-element.191), channel_id=1, source_target_pairs={{32,0},{64,32},{96,64},{128,96},{160,128},{192,160},{224,192},{256... | collective-permute-start | bytes 884744 | tf_op jit(solution)/shard_map/ppermute | solution.py:15
  156.5 1.9 collective-permute-start.7
  159.4 7.1 %all-to-all-start = ((bf16[6,4,8,384]{3,1,0,2:T(4,128)(2,1)}), bf16[6,4,8,384]{3,1,0,2:T(4,128)(2,1)S(1)}, u32[]{:S(2)}, u32[]{:S(2)}) async-start(bf16[6,4,8,384]{3,1,0,2:T(4,128)(2,1)} %copy.50), calls=%async_computation | async-start | bytes 294912 | tf_op jit(solution)/shard_map/all_to_all | solution.py:171
  167.6 7.4 %all-to-all-done = bf16[6,4,8,384]{3,1,0,2:T(4,128)(2,1)S(1)} async-done(((bf16[6,4,8,384]{3,1,0,2:T(4,128)(2,1)}), bf16[6,4,8,384]{3,1,0,2:T(4,128)(2,1)S(1)}, u32[]{:S(2)}, u32[]{:S(2)}) %all-to-all-start) | async-done | bytes 147488 | tf_op jit(solution)/shard_map/all_to_all | solution.py:171
  175.0 3.3 %all-to-all-start.1 = ((bf16[6,4,8,384]{3,1,0,2:T(4,128)(2,1)}), bf16[6,4,8,384]{3,1,0,2:T(4,128)(2,1)S(1)}, u32[]{:S(2)}, u32[]{:S(2)}) async-start(bf16[6,4,8,384]{3,1,0,2:T(4,128)(2,1)} %copy.54), calls=%async_computation.1 | async-start | bytes 294912 | tf_op jit(solution)/shard_map/all_to_all | solution.py:172
  179.1 8.1 %all-to-all-done.1 = bf16[6,4,8,384]{3,1,0,2:T(4,128)(2,1)S(1)} async-done(((bf16[6,4,8,384]{3,1,0,2:T(4,128)(2,1)}), bf16[6,4,8,384]{3,1,0,2:T(4,128)(2,1)S(1)}, u32[]{:S(2)}, u32[]{:S(2)}) %all-to-all-start.1) | async-done | bytes 147488 | tf_op jit(solution)/shard_map/all_to_all | solution.py:172
  187.2 3.3 %all-to-all-start.3 = ((bf16[6,4,8,384]{3,1,0,2:T(4,128)(2,1)}), bf16[6,4,8,384]{3,1,0,2:T(4,128)(2,1)S(1)}, u32[]{:S(2)}, u32[]{:S(2)}) async-start(bf16[6,4,8,384]{3,1,0,2:T(4,128)(2,1)} %copy.61), calls=%async_computation.3 | async-start | bytes 294912 | tf_op jit(solution)/shard_map/all_to_all | solution.py:174
  191.2 7.7 %all-to-all-done.3 = bf16[6,4,8,384]{3,1,0,2:T(4,128)(2,1)S(1)} async-done(((bf16[6,4,8,384]{3,1,0,2:T(4,128)(2,1)}), bf16[6,4,8,384]{3,1,0,2:T(4,128)(2,1)S(1)}, u32[]{:S(2)}, u32[]{:S(2)}) %all-to-all-start.3) | async-done | bytes 147488 | tf_op jit(solution)/shard_map/all_to_all | solution.py:174
  198.9 3.3 %all-to-all-start.2 = ((bf16[6,4,8,384]{3,1,0,2:T(4,128)(2,1)}), bf16[6,4,8,384]{3,1,0,2:T(4,128)(2,1)S(1)}, u32[]{:S(2)}, u32[]{:S(2)}) async-start(bf16[6,4,8,384]{3,1,0,2:T(4,128)(2,1)} %copy.58), calls=%async_computation.2 | async-start | bytes 294912 | tf_op jit(solution)/shard_map/all_to_all | solution.py:173
  204.6 6.1 %all-to-all-done.2 = bf16[6,4,8,384]{3,1,0,2:T(4,128)(2,1)S(1)} async-done(((bf16[6,4,8,384]{3,1,0,2:T(4,128)(2,1)}), bf16[6,4,8,384]{3,1,0,2:T(4,128)(2,1)S(1)}, u32[]{:S(2)}, u32[]{:S(2)}) %all-to-all-start.2) | async-done | bytes 147488 | tf_op jit(solution)/shard_map/all_to_all | solution.py:173
  (90 shorter events, 17.8 us)
Async XLA Ops:
  0.6 10.7 %copy-start.7 = (bf16[6,4,8,384]{3,2,1,0:T(8,128)(2,1)S(1)}, bf16[6,4,8,384]{3,2,1,0:T(8,128)(2,1)}, u32[]{:S(2)}) copy-start(bf16[6,4,8,384]{3,2,1,0:T(8,128)(2,1)} %param.26) | copy-start | bytes 442372
  2.5 11.4 %collective-permute-start.1 = (bf16[6,4,8,768]{3,2,1,0:T(8,128)(2,1)S(1)}, bf16[6,4,8,768]{3,2,1,0:T(8,128)(2,1)S(1)}, u32[]{:S(2)}, u32[]{:S(2)}) collective-permute-start(bf16[6,4,8,768]{3,2,1,0:T(8,128)(2,1)S(1)} %constant_dynamic-update-slice_fusion), channel_id=1, source_target_pairs={{32,0},{64,32},{96,64},{128,96},{160,128},{192,160},{224,192},{256... | collective-permute-start | bytes 884744 | tf_op jit(solution)/shard_map/ppermute | solution.py:28
  6.5 10.2 %collective-permute-start = (bf16[6,4,8,768]{3,2,1,0:T(8,128)(2,1)S(1)}, bf16[6,4,8,768]{3,2,1,0:T(8,128)(2,1)S(1)}, u32[]{:S(2)}, u32[]{:S(2)}) collective-permute-start(bf16[6,4,8,768]{3,2,1,0:T(8,128)(2,1)S(1)} %constant_dynamic-update-slice_fusion), channel_id=1, source_target_pairs={{0,32},{32,64},{64,96},{96,128},{128,160},{160,192},{192,224},{224... | collective-permute-start | bytes 884744 | tf_op jit(solution)/shard_map/ppermute | solution.py:26
  14.0 11.3 %copy-start.1 = (bf16[8,8,6,4,3,12]{5,1,4,2,0,3:T(8,128)(2,1)S(1)}, bf16[8,8,6,4,3,12]{5,1,4,2,0,3:T(8,128)(2,1)}, u32[]{:S(2)}) copy-start(bf16[8,8,6,4,3,12]{5,1,4,2,0,3:T(8,128)(2,1)} %convolution_bitcast_fusion) | copy-start | bytes 331780
  14.0 11.2 %copy-start.2 = (bf16[6,4,8,768]{3,2,1,0:T(8,128)(2,1)}, bf16[6,4,8,768]{3,2,1,0:T(8,128)(2,1)S(1)}, u32[]{:S(2)}) copy-start(bf16[6,4,8,768]{3,2,1,0:T(8,128)(2,1)S(1)} %collective-permute-done.1) | copy-start | bytes 884740
  16.7 8.5 %copy-start.4 = (bf16[6,4,8,768]{3,2,1,0:T(8,128)(2,1)}, bf16[6,4,8,768]{3,2,1,0:T(8,128)(2,1)S(1)}, u32[]{:S(2)}) copy-start(bf16[6,4,8,768]{3,2,1,0:T(8,128)(2,1)S(1)} %collective-permute-done) | copy-start | bytes 884740
  17.8 52.2 %collective-permute-start.3 = (bf16[18,4,8,768]{3,2,1,0:T(8,128)(2,1)}, bf16[18,4,8,768]{3,2,1,0:T(8,128)(2,1)}, u32[]{:S(2)}, u32[]{:S(2)}) collective-permute-start(bf16[18,4,8,768]{3,2,1,0:T(8,128)(2,1)} %pad_maximum_fusion.1), channel_id=1, source_target_pairs={{4,0},{8,4},{12,8},{16,12},{20,16},{24,20},{28,24},{5,1},{9,5},{13... | collective-permute-start | bytes 2654216 | tf_op jit(solution)/shard_map/ppermute | solution.py:28
  19.7 50.3 %collective-permute-start.2 = (bf16[18,4,8,768]{3,2,1,0:T(8,128)(2,1)}, bf16[18,4,8,768]{3,2,1,0:T(8,128)(2,1)}, u32[]{:S(2)}, u32[]{:S(2)}) collective-permute-start(bf16[18,4,8,768]{3,2,1,0:T(8,128)(2,1)} %pad_maximum_fusion.1), channel_id=1, source_target_pairs={{0,4},{4,8},{8,12},{12,16},{16,20},{20,24},{24,28},{1,5},{5,9},{9,... | collective-permute-start | bytes 2654216 | tf_op jit(solution)/shard_map/ppermute | solution.py:26
  54.3 15.8 %copy-start.3 = (bf16[6,4,8,768]{3,2,1,0:T(8,128)(2,1)S(1)}, bf16[6,4,8,768]{3,2,1,0:T(8,128)(2,1)}, u32[]{:S(2)}) copy-start(bf16[6,4,8,768]{3,2,1,0:T(8,128)(2,1)} %copy-done.2) | copy-start | bytes 884740
  54.3 15.8 %copy-start.5 = (bf16[6,4,8,768]{3,2,1,0:T(8,128)(2,1)S(1)}, bf16[6,4,8,768]{3,2,1,0:T(8,128)(2,1)}, u32[]{:S(2)}) copy-start(bf16[6,4,8,768]{3,2,1,0:T(8,128)(2,1)} %copy-done.4) | copy-start | bytes 884740
  78.6 1.7 copy-start
  80.3 1.1 copy-start.6
  86.2 1.7 copy-start
  87.9 1.1 copy-start.6
  93.7 1.7 copy-start
  95.4 1.1 copy-start.6
  126.8 21.2 %collective-permute-start.4 = (bf16[18,4,8,768]{3,2,1,0:T(8,128)(2,1)S(1)}, bf16[18,4,8,768]{3,2,1,0:T(8,128)(2,1)S(1)}, u32[]{:S(2)}, u32[]{:S(2)}) collective-permute-start(bf16[18,4,8,768]{3,2,1,0:T(8,128)(2,1)S(1)} %get-tuple-element.187), channel_id=1, source_target_pairs={{4,0},{8,4},{12,8},{16,12},{20,16},{24,20},{28,24},{5,1},{9,5},{13... | collective-permute-start | bytes 2654216 | tf_op jit(solution)/shard_map/ppermute | solution.py:15
  128.7 29.7 %copy-start.9 = (bf16[3,192,128]{2,1,0:T(8,128)(2,1)S(1)}, bf16[3,192,128]{2,1,0:T(8,128)(2,1)}, u32[]{:S(2)}) copy-start(bf16[3,192,128]{2,1,0:T(8,128)(2,1)} %get-tuple-element.133) | copy-start | bytes 442372
  128.7 20.6 %collective-permute-start.5 = (bf16[18,4,8,768]{3,2,1,0:T(8,128)(2,1)S(1)}, bf16[18,4,8,768]{3,2,1,0:T(8,128)(2,1)S(1)}, u32[]{:S(2)}, u32[]{:S(2)}) collective-permute-start(bf16[18,4,8,768]{3,2,1,0:T(8,128)(2,1)S(1)} %get-tuple-element.188), channel_id=1, source_target_pairs={{0,4},{4,8},{8,12},{12,16},{16,20},{20,24},{24,28},{1,5},{5,9},{9,... | collective-permute-start | bytes 2654216 | tf_op jit(solution)/shard_map/ppermute | solution.py:15
  151.2 15.3 %copy-start.8 = (bf16[3,192,128]{2,1,0:T(8,128)(2,1)S(1)}, bf16[3,192,128]{2,1,0:T(8,128)(2,1)}, u32[]{:S(2)}) copy-start(bf16[3,192,128]{2,1,0:T(8,128)(2,1)} %get-tuple-element.134) | copy-start | bytes 442372
  151.3 16.2 %collective-permute-start.6 = (bf16[6,4,8,768]{3,2,1,0:T(8,128)(2,1)S(1)}, bf16[6,4,8,768]{3,2,1,0:T(8,128)(2,1)S(1)}, u32[]{:S(2)}, u32[]{:S(2)}) collective-permute-start(bf16[6,4,8,768]{3,2,1,0:T(8,128)(2,1)S(1)} %get-tuple-element.191), channel_id=1, source_target_pairs={{32,0},{64,32},{96,64},{128,96},{160,128},{192,160},{224,192},{256... | collective-permute-start | bytes 884744 | tf_op jit(solution)/shard_map/ppermute | solution.py:15
  156.5 11.0 %collective-permute-start.7 = (bf16[6,4,8,768]{3,2,1,0:T(8,128)(2,1)S(1)}, bf16[6,4,8,768]{3,2,1,0:T(8,128)(2,1)S(1)}, u32[]{:S(2)}, u32[]{:S(2)}) collective-permute-start(bf16[6,4,8,768]{3,2,1,0:T(8,128)(2,1)S(1)} %get-tuple-element.192), channel_id=1, source_target_pairs={{0,32},{32,64},{64,96},{96,128},{128,160},{160,192},{192,224},{224... | collective-permute-start | bytes 884744 | tf_op jit(solution)/shard_map/ppermute | solution.py:15
  159.4 15.6 %all-to-all-start = ((bf16[6,4,8,384]{3,1,0,2:T(4,128)(2,1)}), bf16[6,4,8,384]{3,1,0,2:T(4,128)(2,1)S(1)}, u32[]{:S(2)}, u32[]{:S(2)}) async-start(bf16[6,4,8,384]{3,1,0,2:T(4,128)(2,1)} %copy.50), calls=%async_computation | async-start | bytes 294912 | tf_op jit(solution)/shard_map/all_to_all | solution.py:171
  175.0 12.2 %all-to-all-start.1 = ((bf16[6,4,8,384]{3,1,0,2:T(4,128)(2,1)}), bf16[6,4,8,384]{3,1,0,2:T(4,128)(2,1)S(1)}, u32[]{:S(2)}, u32[]{:S(2)}) async-start(bf16[6,4,8,384]{3,1,0,2:T(4,128)(2,1)} %copy.54), calls=%async_computation.1 | async-start | bytes 294912 | tf_op jit(solution)/shard_map/all_to_all | solution.py:172
  187.2 11.8 %all-to-all-start.3 = ((bf16[6,4,8,384]{3,1,0,2:T(4,128)(2,1)}), bf16[6,4,8,384]{3,1,0,2:T(4,128)(2,1)S(1)}, u32[]{:S(2)}, u32[]{:S(2)}) async-start(bf16[6,4,8,384]{3,1,0,2:T(4,128)(2,1)} %copy.61), calls=%async_computation.3 | async-start | bytes 294912 | tf_op jit(solution)/shard_map/all_to_all | solution.py:174
  198.9 11.8 %all-to-all-start.2 = ((bf16[6,4,8,384]{3,1,0,2:T(4,128)(2,1)}), bf16[6,4,8,384]{3,1,0,2:T(4,128)(2,1)S(1)}, u32[]{:S(2)}, u32[]{:S(2)}) async-start(bf16[6,4,8,384]{3,1,0,2:T(4,128)(2,1)} %copy.58), calls=%async_computation.2 | async-start | bytes 294912 | tf_op jit(solution)/shard_map/all_to_all | solution.py:173
where the time goes:
time: 213 us; the launch traced here: 211 us
  local copies, waits for them, and re-layouts  82.1 us (39%)
  waiting for transfers between devices  47.3 us (22%)
  starting transfers between devices  44.7 us (21%)
  matrix products  22.1 us (10%)
  other arithmetic  14 us (7%)
    gt x2, local copies, waits for them, and re-layouts, body(): jnp.einsum('frcxyz,fex,rgy,chz->frcegh', pattern_tok, table_f, table_r, c...  41 us
    ppermute x4, waiting for transfers between devices, shifted(): lax.ppermute(value, axis, [(source, source + steps) for source in range(f...  15.3 us
    ppermute x4, starting transfers between devices, shifted(): lax.ppermute(value, axis, [(source, source + steps) for source in range(f...  14.3 us
    transpose x3, local copies, waits for them, and re-layouts, heads_last(): return source.transpose(1, 0, 2).reshape(target_shape)  13.2 us
    reshape x5, local copies, waits for them, and re-layouts, heads_last(): return source.transpose(1, 0, 2).reshape(target_shape)  11.3 us
    all_to_all x1, waiting for transfers between devices, body(): lax.all_to_all(query_grid, 'head', split_axis=2, concat_axis=3, tiled=True)  8.07 us
    all_to_all x1, waiting for transfers between devices, body(): lax.all_to_all(value_grad, 'head', split_axis=2, concat_axis=3, tiled=True)  7.71 us
    ppermute x2, starting transfers between devices, extended(): lax.ppermute(tail, axis, [(i, (i + 1) % count) for i in range(ends)])  7.41 us
  transfers between devices with their start and end apart: 12, of which 7 were waited for; matrix products, arithmetic and copies ran while one was open for 25% of the time, Pallas kernels for 0%

commit v1 on v0

v1 whole, which is shorter than its diff:
```python
import jax
import jax.numpy as jnp
from jax import lax
from jax.experimental import pallas as pl
from jax.experimental.pallas import tpu as pltpu
from jax.sharding import PartitionSpec as P

HEAD_DIM = 128
TILE = 192
SLOTS = 9
WIDE = SLOTS * TILE
SCALE = HEAD_DIM**-0.5
SCALE2 = SCALE * 1.4426950408889634
FAR = 1e30
VMEM_LIMIT = 48 * 1024 * 1024

VMEM = pl.BlockSpec(memory_space=pltpu.VMEM)
SMEM = pl.BlockSpec(memory_space=pltpu.SMEM)


def call(kernel, outs, in_specs, out_specs, scratch=()):
    return pl.pallas_call(
        kernel,
        out_shape=outs,
        in_specs=in_specs,
        out_specs=out_specs,
        scratch_shapes=list(scratch),
        compiler_params=pltpu.CompilerParams(vmem_limit_bytes=VMEM_LIMIT),
    )


def pair_swap(value, axis, parity):
    count = lax.axis_size(axis)
    pairs = []
    for low in range(parity, count - 1, 2):
        pairs += [(low, low + 1), (low + 1, low)]
    return lax.ppermute(value, axis, pairs)


def slot_steps(axis):
    near = 1 - 2 * (lax.axis_index(axis) % 2)
    return (0, near, -near)


def slot_offsets():
    return [(a, b) for a in slot_steps("frame") for b in slot_steps("row")]


def regroup_kernel(a_ref, b_ref, out_ref):
    out_ref[0 : 2 * TILE, :] = a_ref[...]
    out_ref[2 * TILE : 4 * TILE, :] = b_ref[...]


def gather_near(tiles, first_ref, second_ref):
    for slot, (ref, start) in enumerate(tiles):
        rows = slice(slot * TILE, (slot + 1) * TILE)
        first_ref[rows, :] = ref[start : start + TILE, :]
        second_ref[rows, :] = ref[start + TILE : start + 2 * TILE, :]


def store_sends(send_ref, firsts, seconds):
    heads = send_ref.shape[0]
    group, span = 8 // heads, TILE // heads
    row = lax.broadcasted_iota(jnp.int32, (TILE, TILE), 0)
    col = lax.broadcasted_iota(jnp.int32, (TILE, TILE), 1)
    block = jnp.zeros_like(row)
    for d in range(1, heads):
        block += (row >= d * span).astype(jnp.int32)
    inner = row - block * span
    shift = group.bit_length() - 1
    source = (inner >> shift) * 8 + block * group + (inner & (group - 1))
    order = (col == source).astype(jnp.bfloat16)
    joined = jnp.concatenate(firsts + seconds, axis=1)
    moved = jnp.dot(order, joined, preferred_element_type=jnp.float32).astype(jnp.bfloat16)
    feats = send_ref.shape[3]
    for k in range(heads):
        rows = slice(k * span, (k + 1) * span)
        send_ref[k, 0] = moved[rows, :feats]
        send_ref[k, 1] = moved[rows, feats:]


def assemble(got_ref, out_refs):
    heads, _, _, feats = got_ref.shape
    for k in range(heads):
        place = slice(k * feats, (k + 1) * feats)
        for i, out_ref in enumerate(out_refs):
            out_ref[:, :, place] = got_ref[k, i].reshape(out_ref.shape[:2] + (feats,))


def assemble_kernel(got_ref, *out_refs):
    assemble(got_ref, out_refs)


def query_kernel(
    pairs_s, pairs_v, own_qg, kv, kv_a, kv_b, kv_fb, kv_fa, corner_fb, corner_fa, *refs
):
    send_ref, stat_ref, key_ref, value_ref = refs
    frame, row = lax.axis_index("frame"), lax.axis_index("row")
    frames, rows = lax.axis_size("frame"), lax.axis_size("row")
    tiles = [(kv, 0), (kv_a, 0), (kv_b, 0)]
    tiles += [(kv_fa, 0), (corner_fa, 0), (corner_fa, 2 * TILE)]
    tiles += [(kv_fb, 0), (corner_fb, 0), (corner_fb, 2 * TILE)]
    gather_near(tiles, key_ref, value_ref)
    lane = lax.broadcasted_iota(jnp.int32, (1, WIDE), 1)
    bias = jnp.zeros((1, WIDE), jnp.float32)
    for slot, (a, b) in enumerate(slot_offsets()):
        bit = pairs_s[0, 0, 0, 9 * (a + 1) + 3 * (b + 1) + 1]
        inside = (frame + a >= 0) & (frame + a < frames) & (row + b >= 0) & (row + b < rows)
        level = jnp.where((bit == 1) & inside, 0.0, -FAR).astype(jnp.float32)
        here = (lane >= slot * TILE) & (lane < (slot + 1) * TILE)
        bias = jnp.where(here, level, bias)
    stat_lane = lax.broadcasted_iota(jnp.int32, (TILE, 128), 1)
    stats = jnp.zeros((TILE, 128), jnp.float32)
    count = own_qg.shape[1] // HEAD_DIM
    attended_parts, grad_parts = [], []
    for h in range(count):
        feat = slice(h * HEAD_DIM, (h + 1) * HEAD_DIM)
        query, grad = own_qg[0:TILE, feat], own_qg[TILE : 2 * TILE, feat]
        key, value = key_ref[:, feat], value_ref[:, feat]
        scores = lax.dot_general(
            query, key, (((1,), (1,)), ((), ())), preferred_element_type=jnp.float32
        )
        scores = scores * SCALE2 + bias
        top = jnp.max(scores, axis=1, keepdims=True)
        weights = jnp.exp2(scores - top)
        total = jnp.sum(weights, axis=1, keepdims=True)
        weights = weights * (1.0 / total)
        rounded = weights.astype(jnp.bfloat16)
        attended = jnp.dot(rounded, value, preferred_element_type=jnp.float32).astype(jnp.bfloat16)
        spread = jnp.sum(
            grad.astype(jnp.float32) * attended.astype(jnp.float32), axis=1, keepdims=True
        )
        pushes = lax.dot_general(
            grad, value, (((1,), (1,)), ((), ())), preferred_element_type=jnp.float32
        )
        slopes = (weights * (pushes - spread)).astype(jnp.bfloat16)
        query_grad = SCALE * jnp.dot(slopes, key, preferred_element_type=jnp.float32)
        attended_parts.append(attended)
        grad_parts.append(query_grad.astype(jnp.bfloat16))
        stats = jnp.where(stat_lane == h, top + jnp.log2(total), stats)
        stats = jnp.where(stat_lane == count + h, spread, stats)
    stat_ref[...] = stats.T[0:8, :]
    stat_ref[7:8, 0:27] = pairs_v[0, 0].astype(jnp.float32)
    store_sends(send_ref, attended_parts, grad_parts)


def key_kernel(kv, kv_fa, kv_fb, qg, qg_a, qg_b, st, st_a, st_b, *refs):
    own_ref, term_a_ref, term_b_ref, query_ref, grad_ref, stat_ref = refs
    count = kv.shape[1] // HEAD_DIM
    frame, frames = lax.axis_index("frame"), lax.axis_size("frame")
    gather_near([(qg, 0), (qg_a, 0), (qg_b, 0)], query_ref, grad_ref)
    lane = lax.broadcasted_iota(jnp.int32, (1, TILE), 1)
    level = lax.broadcasted_iota(jnp.int32, (8, TILE), 0)
    frame_steps = slot_steps("frame")
    for slot, (ref, b) in enumerate(zip((st, st_a, st_b), slot_steps("row"))):
        block = ref[...]
        for i, a in enumerate(frame_steps):
            index = 9 * (a + 1) + 3 * (1 - b) + 1
            bit = jnp.sum(jnp.where(lane == index, block[7:8, :], 0.0), axis=1, keepdims=True)
            inside = (frame + a >= 0) & (frame + a < frames)
            bit = bit * jnp.where(inside, 1.0, 0.0).astype(jnp.float32)
            closed = (level < count) & (bit < 0.5)
            stat_ref[i, :, slot * TILE : (slot + 1) * TILE] = jnp.where(closed, FAR, block)
    for h in range(count):
        feat = slice(h * HEAD_DIM, (h + 1) * HEAD_DIM)
        query, grad = query_ref[:, feat], grad_ref[:, feat]
        for i, (kv_ref, out_ref) in enumerate(
            ((kv, own_ref), (kv_fa, term_a_ref), (kv_fb, term_b_ref))
        ):
            key, value = kv_ref[0:TILE, feat], kv_ref[TILE : 2 * TILE, feat]
            scores = lax.dot_general(
                key, query, (((1,), (1,)), ((), ())), preferred_element_type=jnp.float32
            )
            weights = jnp.exp2(scores * SCALE2 - stat_ref[i, h : h + 1, :])
            rounded = weights.astype(jnp.bfloat16)
            value_grad = jnp.dot(rounded, grad, preferred_element_type=jnp.float32)
            pushes = lax.dot_general(
                value, grad, (((1,), (1,)), ((), ())), preferred_element_type=jnp.float32
            )
            spread = stat_ref[i, count + h : count + h + 1, :]
            slopes = (weights * (pushes - spread)).astype(jnp.bfloat16)
            key_grad = SCALE * jnp.dot(slopes, query, preferred_element_type=jnp.float32)
            out_ref[0:TILE, feat] = key_grad.astype(out_ref.dtype)
            out_ref[TILE : 2 * TILE, feat] = value_grad.astype(out_ref.dtype)


def fold_kernel(own_ref, got_a, got_b, send_ref):
    total = own_ref[...] + got_a[...].astype(jnp.float32) + got_b[...].astype(jnp.float32)
    total = total.astype(jnp.bfloat16)
    store_sends(send_ref, [total[0:TILE]], [total[TILE : 2 * TILE]])


def after(value, *others):
    return lax.optimization_barrier((value,) + others)[0]


def stacked(first, second):
    rows = first.shape[0]
    low = jnp.pad(first, ((0, rows), (0, 0)), constant_values=-jnp.inf)
    return jnp.maximum(low, jnp.pad(second, ((rows, 0), (0, 0)), constant_values=-jnp.inf))


def body(queries, key_tokens, value_tokens, grad_out, tile_pairs):
    frames_dev, rows_dev, columns, feats = queries.shape
    heads = lax.axis_size("head")
    bf16, f32 = jnp.bfloat16, jnp.float32
    flat = [x.reshape(TILE, feats) for x in (key_tokens, value_tokens, queries, grad_out)]

    kv = stacked(flat[0], flat[1])
    qg = stacked(flat[2], flat[3])
    kv_a, kv_b = pair_swap(kv, "row", 0), pair_swap(kv, "row", 1)
    kv_fb, kv_fa = pair_swap(kv, "frame", 1), pair_swap(kv, "frame", 0)
    rows = call(regroup_kernel, jax.ShapeDtypeStruct((4 * TILE, feats), bf16), [VMEM] * 2, VMEM)(
        kv_a, kv_b
    )
    rows = after(rows, kv_fb, kv_fa)
    corner_fb, corner_fa = pair_swap(rows, "frame", 1), pair_swap(rows, "frame", 0)
    qg_late = after(qg, kv_fb, kv_fa)
    qg_a, qg_b = pair_swap(qg_late, "row", 0), pair_swap(qg_late, "row", 1)

    send_shape = jax.ShapeDtypeStruct((heads, 2, TILE // heads, feats), bf16)
    near = pltpu.VMEM((WIDE, feats), bf16)
    sent_q, stat = call(
        query_kernel,
        (send_shape, jax.ShapeDtypeStruct((8, TILE), f32)),
        [SMEM] + [VMEM] * 9,
        (VMEM, VMEM),
        [near, near],
    )(tile_pairs, tile_pairs, qg, kv, kv_a, kv_b, kv_fb, kv_fa, corner_fb, corner_fa)
    st_a, st_b = pair_swap(stat, "row", 0), pair_swap(stat, "row", 1)

    row_near = pltpu.VMEM((3 * TILE, feats), bf16)
    term = jax.ShapeDtypeStruct((2 * TILE, feats), bf16)
    own, term_a, term_b = call(
        key_kernel,
        (jax.ShapeDtypeStruct((2 * TILE, feats), f32), term, term),
        [VMEM] * 9,
        (VMEM,) * 3,
        [row_near, row_near, pltpu.VMEM((3, 8, 3 * TILE), f32)],
    )(kv, kv_fa, kv_fb, qg, qg_a, qg_b, stat, st_a, st_b)
    got_b, got_a = pair_swap(term_b, "frame", 1), pair_swap(term_a, "frame", 0)
    sent_k = call(fold_kernel, send_shape, [VMEM] * 3, VMEM)(own, got_b, got_a)

    out = jax.ShapeDtypeStruct((frames_dev * rows_dev, columns // heads, heads * feats), bf16)
    outs = []
    for sent in (after(sent_q, own), sent_k):
        got = lax.all_to_all(sent, "head", split_axis=0, concat_axis=0, tiled=True)
        outs += call(assemble_kernel, (out, out), [VMEM], (VMEM, VMEM))(got)
    return tuple(x.reshape((frames_dev, rows_dev) + out.shape[1:]) for x in outs)


def solution(mesh):
    inputs = P("frame", "row", None, "head")
    outputs = P("frame", "row", "head", None)
    return jax.shard_map(
        body,
        mesh=mesh,
        in_specs=(inputs,) * 4 + (P("frame", "row", None, None),),
        out_specs=(outputs,) * 4,
        check_vma=False,
    )
```

time: 213 us -> 88.8 us (0.42)
  the two profiles are of different devices: /device:TPU:200 before, /device:TPU:72 now
where the time goes in v1:
time: 88.8 us; the launch traced here: 88.2 us
  starting transfers between devices  52.9 us (60%)
  waiting for transfers between devices  21.5 us (24%)
  Pallas kernels  11.9 us (13%)
  other arithmetic  1.05 us (1%)
    ppermute x12, starting transfers between devices, pair_swap(): return lax.ppermute(value, axis, pairs)  41 us
    ppermute x12, waiting for transfers between devices, pair_swap(): return lax.ppermute(value, axis, pairs)  13.1 us
    all_to_all x2, starting transfers between devices, body(): got = lax.all_to_all(sent, 'head', split_axis=0, concat_axis=0, tiled=True)  11.9 us
    all_to_all x2, waiting for transfers between devices, body(): got = lax.all_to_all(sent, 'head', split_axis=0, concat_axis=0, tiled=True)  8.47 us
    pallas_call x1, Pallas kernels, body(): call(query_kernel, (send_shape, jax.ShapeDtypeStruct((8, TILE), f32)), [S...  5.3 us
    pallas_call x1, Pallas kernels, body(): call(key_kernel, (jax.ShapeDtypeStruct((2 * TILE, feats), f32), term, ter...  3.95 us
  transfers between devices with their start and end apart: 14, of which 5 were waited for; matrix products, arithmetic and copies ran while one was open for 0% of the time, Pallas kernels for 8%

profile of v1, /device:TPU:72, one launch (start us, length us, event | category | flops | bytes accessed | tf_op | source)
XLA Modules:
  0.0 88.2 jit_solution(255123232472139804)
XLA Ops:
  0.6 1.0 %pad_maximum_fusion.kv = bf16[384,384]{1,0:T(8,128)(2,1)S(1)} fusion(bf16[192,384]{1,0:T(8,128)(2,1)} %bitcast.8, bf16[192,384]{1,0:T(8,128)(2,1)} %bitcast.9), kind=kLoop, calls=%fused_computation | loop fusion | flops 589824 | bytes 589824 | tf_op jit(solution)/shard_map/max | solution.py:200
  1.6 0.0 copy-start.1
  1.7 0.0 copy-start.2
  1.7 2.1 %collective-permute-start = (bf16[384,384]{1,0:T(8,128)(2,1)S(1)}, bf16[384,384]{1,0:T(8,128)(2,1)S(1)}, u32[]{:S(2)}, u32[]{:S(2)}) collective-permute-start(bf16[384,384]{1,0:T(8,128)(2,1)S(1)} %pad_maximum_fusion.kv), channel_id=1, source_target_pairs={{0,4},{4,0},{8,12},{12,8},{16,20},{20,16},{24,28},{28,24},{1,5},{5... | collective-permute-start | bytes 884744 | tf_op jit(solution)/shard_map/ppermute | solution.py:37
  3.7 6.6 %collective-permute-start.1 = (bf16[384,384]{1,0:T(8,128)(2,1)S(1)}, bf16[384,384]{1,0:T(8,128)(2,1)S(1)}, u32[]{:S(2)}, u32[]{:S(2)}) collective-permute-start(bf16[384,384]{1,0:T(8,128)(2,1)S(1)} %pad_maximum_fusion.kv), channel_id=1, source_target_pairs={{4,8},{8,4},{12,16},{16,12},{20,24},{24,20},{5,9},{9,5},{13,17},{1... | collective-permute-start | bytes 884744 | tf_op jit(solution)/shard_map/ppermute | solution.py:37
  10.4 3.4 %collective-permute-start.2 = (bf16[384,384]{1,0:T(8,128)(2,1)S(1)}, bf16[384,384]{1,0:T(8,128)(2,1)S(1)}, u32[]{:S(2)}, u32[]{:S(2)}) collective-permute-start(bf16[384,384]{1,0:T(8,128)(2,1)S(1)} %pad_maximum_fusion.kv), channel_id=1, source_target_pairs={{32,64},{64,32},{96,128},{128,96},{160,192},{192,160},{224,256},{2... | collective-permute-start | bytes 884744 | tf_op jit(solution)/shard_map/ppermute | solution.py:37
  13.8 2.0 %collective-permute-start.3 = (bf16[384,384]{1,0:T(8,128)(2,1)S(1)}, bf16[384,384]{1,0:T(8,128)(2,1)S(1)}, u32[]{:S(2)}, u32[]{:S(2)}) collective-permute-start(bf16[384,384]{1,0:T(8,128)(2,1)S(1)} %pad_maximum_fusion.kv), channel_id=1, source_target_pairs={{0,32},{32,0},{64,96},{96,64},{128,160},{160,128},{192,224},{224,1... | collective-permute-start | bytes 884744 | tf_op jit(solution)/shard_map/ppermute | solution.py:37
  15.8 0.0 collective-permute-done.a_ref.kv_a
  15.8 1.3 %collective-permute-done.1.b_ref.kv_b = bf16[384,384]{1,0:T(8,128)(2,1)S(1)} collective-permute-done((bf16[384,384]{1,0:T(8,128)(2,1)S(1)}, bf16[384,384]{1,0:T(8,128)(2,1)S(1)}, u32[]{:S(2)}, u32[]{:S(2)}) %collective-permute-start.1) | collective-permute-done | bytes 294944 | tf_op jit(solution)/shard_map/ppermute | solution.py:37
  17.1 0.1 shard_map.84
  17.1 3.4 %collective-permute-done.2.kv_fb = bf16[384,384]{1,0:T(8,128)(2,1)S(1)} collective-permute-done((bf16[384,384]{1,0:T(8,128)(2,1)S(1)}, bf16[384,384]{1,0:T(8,128)(2,1)S(1)}, u32[]{:S(2)}, u32[]{:S(2)}) %collective-permute-start.2) | collective-permute-done | bytes 294944 | tf_op jit(solution)/shard_map/ppermute | solution.py:37
  20.5 0.0 collective-permute-done.3.kv_fa
  20.5 3.4 %collective-permute-start.4 = (bf16[768,384]{1,0:T(8,128)(2,1)S(1)}, bf16[768,384]{1,0:T(8,128)(2,1)S(1)}, u32[]{:S(2)}, u32[]{:S(2)}) collective-permute-start(bf16[768,384]{1,0:T(8,128)(2,1)S(1)} %shard_map.84), channel_id=1, source_target_pairs={{32,64},{64,32},{96,128},{128,96},{160,192},{192,160},{224,256},{2... | collective-permute-start | bytes 1769480 | tf_op jit(solution)/shard_map/ppermute | solution.py:37
  24.0 1.9 %collective-permute-start.5 = (bf16[768,384]{1,0:T(8,128)(2,1)S(1)}, bf16[768,384]{1,0:T(8,128)(2,1)S(1)}, u32[]{:S(2)}, u32[]{:S(2)}) collective-permute-start(bf16[768,384]{1,0:T(8,128)(2,1)S(1)} %shard_map.84), channel_id=1, source_target_pairs={{0,32},{32,0},{64,96},{96,64},{128,160},{160,128},{192,224},{224,1... | collective-permute-start | bytes 1769480 | tf_op jit(solution)/shard_map/ppermute | solution.py:37
  25.9 0.0 copy-done.1
  25.9 0.0 copy-done.2
  25.9 0.0 copy-start
  26.0 1.9 %collective-permute-start.6 = (bf16[384,384]{1,0:T(8,128)(2,1)S(1)}, bf16[384,384]{1,0:T(8,128)(2,1)S(1)}, u32[]{:S(2)}, u32[]{:S(2)}) collective-permute-start(bf16[384,384]{1,0:T(8,128)(2,1)S(1)} %pad_maximum_fusion.1.own_qg.qg), channel_id=1, source_target_pairs={{0,4},{4,0},{8,12},{12,8},{16,20},{20,16},{24,28},{28,24},{1,5},{5... | collective-permute-start | bytes 884744 | tf_op jit(solution)/shard_map/ppermute | solution.py:37
  27.9 7.0 %collective-permute-start.7 = (bf16[384,384]{1,0:T(8,128)(2,1)S(1)}, bf16[384,384]{1,0:T(8,128)(2,1)S(1)}, u32[]{:S(2)}, u32[]{:S(2)}) collective-permute-start(bf16[384,384]{1,0:T(8,128)(2,1)S(1)} %pad_maximum_fusion.1.own_qg.qg), channel_id=1, source_target_pairs={{4,8},{8,4},{12,16},{16,12},{20,24},{24,20},{5,9},{9,5},{13,17},{1... | collective-permute-start | bytes 884744 | tf_op jit(solution)/shard_map/ppermute | solution.py:37
  34.9 0.0 collective-permute-done.4.corner_fb
  34.9 0.0 collective-permute-done.5.corner_fa
  34.9 0.0 copy-done
  34.9 5.3 %shard_map.85 = (bf16[4,2,48,384]{3,2,1,0:T(8,128)(2,1)}, f32[8,192]{1,0:T(8,128)S(1)}) custom-call(s32[1,1,1,27]{3,2,1,0:T(1,128)S(1)} %copy-done, s32[1,1,1,27]{3,2,1,0:T(1,128)S(1)} %copy-done, bf16[384,384]{1,0:T(8,128)(2,1)S(1)} %pad_maximum_fusion.1.own_qg.qg, bf16[384,384]{1,0:T(8,128)(2,1)S(1)} %pad_maximum_fusion.kv, ...), custom_call_target="tpu_custom_call" | custom-call | tf_op jit(solution)/shard_map/pallas_call | solution.py:223
  40.2 1.9 %collective-permute-start.8 = (f32[8,192]{1,0:T(8,128)S(1)}, f32[8,192]{1,0:T(8,128)S(1)}, u32[]{:S(2)}, u32[]{:S(2)}) collective-permute-start(f32[8,192]{1,0:T(8,128)S(1)} %get-tuple-element.19.st), channel_id=1, source_target_pairs={{0,4},{4,0},{8,12},{12,8},{16,20},{20,16},{24,28},{28,24},{1,5},{5... | collective-permute-start | bytes 18440 | tf_op jit(solution)/shard_map/ppermute | solution.py:37
  42.1 5.9 %collective-permute-start.9 = (f32[8,192]{1,0:T(8,128)S(1)}, f32[8,192]{1,0:T(8,128)S(1)}, u32[]{:S(2)}, u32[]{:S(2)}) collective-permute-start(f32[8,192]{1,0:T(8,128)S(1)} %get-tuple-element.19.st), channel_id=1, source_target_pairs={{4,8},{8,4},{12,16},{16,12},{20,24},{24,20},{5,9},{9,5},{13,17},{1... | collective-permute-start | bytes 18440 | tf_op jit(solution)/shard_map/ppermute | solution.py:37
  48.0 0.0 collective-permute-done.6.qg_a
  48.0 0.0 collective-permute-done.7.qg_b
  48.0 0.0 collective-permute-done.8.st_a
  48.0 1.6 %collective-permute-done.9.st_b = f32[8,192]{1,0:T(8,128)S(1)} collective-permute-done((f32[8,192]{1,0:T(8,128)S(1)}, f32[8,192]{1,0:T(8,128)S(1)}, u32[]{:S(2)}, u32[]{:S(2)}) %collective-permute-start.9) | collective-permute-done | bytes 6176 | tf_op jit(solution)/shard_map/ppermute | solution.py:37
  49.6 4.0 %shard_map.86 = (f32[384,384]{1,0:T(8,128)S(1)}, bf16[384,384]{1,0:T(8,128)(2,1)S(1)}, bf16[384,384]{1,0:T(8,128)(2,1)S(1)}) custom-call(bf16[384,384]{1,0:T(8,128)(2,1)S(1)} %pad_maximum_fusion.kv, bf16[384,384]{1,0:T(8,128)(2,1)S(1)} %collective-permute-done.3.kv_fa, bf16[384,384]{1,0:T(8,128)(2,1)S(1)} %collective-permute-done.2.kv_fb, ...), custom_call_target="tpu_custom_call" | custom-call | tf_op jit(solution)/shard_map/pallas_call | solution.py:234
  53.6 6.2 %all-to-all-start = ((bf16[4,2,48,384]{3,2,1,0:T(8,128)(2,1)}), bf16[4,2,48,384]{3,2,1,0:T(8,128)(2,1)S(1)}, u32[]{:S(2)}, u32[]{:S(2)}) async-start(bf16[4,2,48,384]{3,2,1,0:T(8,128)(2,1)} %get-tuple-element.21), calls=%async_computation | async-start | bytes 589824 | tf_op jit(solution)/shard_map/all_to_all | solution.py:247
  59.8 3.0 %collective-permute-start.10 = (bf16[384,384]{1,0:T(8,128)(2,1)S(1)}, bf16[384,384]{1,0:T(8,128)(2,1)S(1)}, u32[]{:S(2)}, u32[]{:S(2)}) collective-permute-start(bf16[384,384]{1,0:T(8,128)(2,1)S(1)} %get-tuple-element.24), channel_id=1, source_target_pairs={{32,64},{64,32},{96,128},{128,96},{160,192},{192,160},{224,256},{2... | collective-permute-start | bytes 884744 | tf_op jit(solution)/shard_map/ppermute | solution.py:37
  62.8 1.9 %collective-permute-start.11 = (bf16[384,384]{1,0:T(8,128)(2,1)S(1)}, bf16[384,384]{1,0:T(8,128)(2,1)S(1)}, u32[]{:S(2)}, u32[]{:S(2)}) collective-permute-start(bf16[384,384]{1,0:T(8,128)(2,1)S(1)} %get-tuple-element.25), channel_id=1, source_target_pairs={{0,32},{32,0},{64,96},{96,64},{128,160},{160,128},{192,224},{224,1... | collective-permute-start | bytes 884744 | tf_op jit(solution)/shard_map/ppermute | solution.py:37
  64.7 6.8 %collective-permute-done.10.got_a = bf16[384,384]{1,0:T(8,128)(2,1)S(1)} collective-permute-done((bf16[384,384]{1,0:T(8,128)(2,1)S(1)}, bf16[384,384]{1,0:T(8,128)(2,1)S(1)}, u32[]{:S(2)}, u32[]{:S(2)}) %collective-permute-start.10) | collective-permute-done | bytes 294944 | tf_op jit(solution)/shard_map/ppermute | solution.py:37
  71.5 0.0 collective-permute-done.11.got_b
  71.5 1.0 %shard_map.88 = bf16[4,2,48,384]{3,2,1,0:T(8,128)(2,1)} custom-call(f32[384,384]{1,0:T(8,128)S(1)} %get-tuple-element.20.own_ref, bf16[384,384]{1,0:T(8,128)(2,1)S(1)} %collective-permute-done.10.got_a, bf16[384,384]{1,0:T(8,128)(2,1)S(1)} %collective-permute-done.11.got_b), custom_call_target="tpu_custom_call" | custom-call | tf_op jit(solution)/shard_map/pallas_call | solution.py:242
  72.6 0.0 all-to-all-done.got_ref
  72.6 5.6 %all-to-all-start.1 = ((bf16[4,2,48,384]{3,2,1,0:T(8,128)(2,1)}), bf16[4,2,48,384]{3,2,1,0:T(8,128)(2,1)S(1)}, u32[]{:S(2)}, u32[]{:S(2)}) async-start(bf16[4,2,48,384]{3,2,1,0:T(8,128)(2,1)} %shard_map.88), calls=%async_computation.1 | async-start | bytes 589824 | tf_op jit(solution)/shard_map/all_to_all | solution.py:247
  78.2 0.8 shard_map.87
  79.0 8.5 %all-to-all-done.1.got_ref = bf16[4,2,48,384]{3,2,1,0:T(8,128)(2,1)S(1)} async-done(((bf16[4,2,48,384]{3,2,1,0:T(8,128)(2,1)}), bf16[4,2,48,384]{3,2,1,0:T(8,128)(2,1)S(1)}, u32[]{:S(2)}, u32[]{:S(2)}) %all-to-all-start.1) | async-done | bytes 294944 | tf_op jit(solution)/shard_map/all_to_all | solution.py:247
  87.4 0.8 shard_map.89
  (1 shorter events, 0.0 us)
Async XLA Ops:
  1.6 24.2 %copy-start.1 = (bf16[6,4,8,384]{3,2,1,0:T(8,128)(2,1)S(1)}, bf16[6,4,8,384]{3,2,1,0:T(8,128)(2,1)}, u32[]{:S(2)}) copy-start(bf16[6,4,8,384]{3,2,1,0:T(8,128)(2,1)} %param.8) | copy-start | bytes 442372
  1.7 24.2 %copy-start.2 = (bf16[6,4,8,384]{3,2,1,0:T(8,128)(2,1)S(1)}, bf16[6,4,8,384]{3,2,1,0:T(8,128)(2,1)}, u32[]{:S(2)}) copy-start(bf16[6,4,8,384]{3,2,1,0:T(8,128)(2,1)} %param.5) | copy-start | bytes 442372
  1.7 14.2 %collective-permute-start = (bf16[384,384]{1,0:T(8,128)(2,1)S(1)}, bf16[384,384]{1,0:T(8,128)(2,1)S(1)}, u32[]{:S(2)}, u32[]{:S(2)}) collective-permute-start(bf16[384,384]{1,0:T(8,128)(2,1)S(1)} %pad_maximum_fusion.kv), channel_id=1, source_target_pairs={{0,4},{4,0},{8,12},{12,8},{16,20},{20,16},{24,28},{28,24},{1,5},{5... | collective-permute-start | bytes 884744 | tf_op jit(solution)/shard_map/ppermute | solution.py:37
  3.7 13.4 %collective-permute-start.1 = (bf16[384,384]{1,0:T(8,128)(2,1)S(1)}, bf16[384,384]{1,0:T(8,128)(2,1)S(1)}, u32[]{:S(2)}, u32[]{:S(2)}) collective-permute-start(bf16[384,384]{1,0:T(8,128)(2,1)S(1)} %pad_maximum_fusion.kv), channel_id=1, source_target_pairs={{4,8},{8,4},{12,16},{16,12},{20,24},{24,20},{5,9},{9,5},{13,17},{1... | collective-permute-start | bytes 884744 | tf_op jit(solution)/shard_map/ppermute | solution.py:37
  10.4 10.2 %collective-permute-start.2 = (bf16[384,384]{1,0:T(8,128)(2,1)S(1)}, bf16[384,384]{1,0:T(8,128)(2,1)S(1)}, u32[]{:S(2)}, u32[]{:S(2)}) collective-permute-start(bf16[384,384]{1,0:T(8,128)(2,1)S(1)} %pad_maximum_fusion.kv), channel_id=1, source_target_pairs={{32,64},{64,32},{96,128},{128,96},{160,192},{192,160},{224,256},{2... | collective-permute-start | bytes 884744 | tf_op jit(solution)/shard_map/ppermute | solution.py:37
  13.8 6.7 %collective-permute-start.3 = (bf16[384,384]{1,0:T(8,128)(2,1)S(1)}, bf16[384,384]{1,0:T(8,128)(2,1)S(1)}, u32[]{:S(2)}, u32[]{:S(2)}) collective-permute-start(bf16[384,384]{1,0:T(8,128)(2,1)S(1)} %pad_maximum_fusion.kv), channel_id=1, source_target_pairs={{0,32},{32,0},{64,96},{96,64},{128,160},{160,128},{192,224},{224,1... | collective-permute-start | bytes 884744 | tf_op jit(solution)/shard_map/ppermute | solution.py:37
  20.5 14.3 %collective-permute-start.4 = (bf16[768,384]{1,0:T(8,128)(2,1)S(1)}, bf16[768,384]{1,0:T(8,128)(2,1)S(1)}, u32[]{:S(2)}, u32[]{:S(2)}) collective-permute-start(bf16[768,384]{1,0:T(8,128)(2,1)S(1)} %shard_map.84), channel_id=1, source_target_pairs={{32,64},{64,32},{96,128},{128,96},{160,192},{192,160},{224,256},{2... | collective-permute-start | bytes 1769480 | tf_op jit(solution)/shard_map/ppermute | solution.py:37
  24.0 10.9 %collective-permute-start.5 = (bf16[768,384]{1,0:T(8,128)(2,1)S(1)}, bf16[768,384]{1,0:T(8,128)(2,1)S(1)}, u32[]{:S(2)}, u32[]{:S(2)}) collective-permute-start(bf16[768,384]{1,0:T(8,128)(2,1)S(1)} %shard_map.84), channel_id=1, source_target_pairs={{0,32},{32,0},{64,96},{96,64},{128,160},{160,128},{192,224},{224,1... | collective-permute-start | bytes 1769480 | tf_op jit(solution)/shard_map/ppermute | solution.py:37
  25.9 9.0 %copy-start = (s32[1,1,1,27]{3,2,1,0:T(1,128)S(1)}, s32[1,1,1,27]{3,2,1,0:T(1,128)}, u32[]{:S(2)}) copy-start(s32[1,1,1,27]{3,2,1,0:T(1,128)} %pairs_v.1) | copy-start | bytes 328
  26.0 22.1 %collective-permute-start.6 = (bf16[384,384]{1,0:T(8,128)(2,1)S(1)}, bf16[384,384]{1,0:T(8,128)(2,1)S(1)}, u32[]{:S(2)}, u32[]{:S(2)}) collective-permute-start(bf16[384,384]{1,0:T(8,128)(2,1)S(1)} %pad_maximum_fusion.1.own_qg.qg), channel_id=1, source_target_pairs={{0,4},{4,0},{8,12},{12,8},{16,20},{20,16},{24,28},{28,24},{1,5},{5... | collective-permute-start | bytes 884744 | tf_op jit(solution)/shard_map/ppermute | solution.py:37
  27.9 20.1 %collective-permute-start.7 = (bf16[384,384]{1,0:T(8,128)(2,1)S(1)}, bf16[384,384]{1,0:T(8,128)(2,1)S(1)}, u32[]{:S(2)}, u32[]{:S(2)}) collective-permute-start(bf16[384,384]{1,0:T(8,128)(2,1)S(1)} %pad_maximum_fusion.1.own_qg.qg), channel_id=1, source_target_pairs={{4,8},{8,4},{12,16},{16,12},{20,24},{24,20},{5,9},{9,5},{13,17},{1... | collective-permute-start | bytes 884744 | tf_op jit(solution)/shard_map/ppermute | solution.py:37
  40.2 7.9 %collective-permute-start.8 = (f32[8,192]{1,0:T(8,128)S(1)}, f32[8,192]{1,0:T(8,128)S(1)}, u32[]{:S(2)}, u32[]{:S(2)}) collective-permute-start(f32[8,192]{1,0:T(8,128)S(1)} %get-tuple-element.19.st), channel_id=1, source_target_pairs={{0,4},{4,0},{8,12},{12,8},{16,20},{20,16},{24,28},{28,24},{1,5},{5... | collective-permute-start | bytes 18440 | tf_op jit(solution)/shard_map/ppermute | solution.py:37
  42.1 7.5 %collective-permute-start.9 = (f32[8,192]{1,0:T(8,128)S(1)}, f32[8,192]{1,0:T(8,128)S(1)}, u32[]{:S(2)}, u32[]{:S(2)}) collective-permute-start(f32[8,192]{1,0:T(8,128)S(1)} %get-tuple-element.19.st), channel_id=1, source_target_pairs={{4,8},{8,4},{12,16},{16,12},{20,24},{24,20},{5,9},{9,5},{13,17},{1... | collective-permute-start | bytes 18440 | tf_op jit(solution)/shard_map/ppermute | solution.py:37
  53.6 19.0 %all-to-all-start = ((bf16[4,2,48,384]{3,2,1,0:T(8,128)(2,1)}), bf16[4,2,48,384]{3,2,1,0:T(8,128)(2,1)S(1)}, u32[]{:S(2)}, u32[]{:S(2)}) async-start(bf16[4,2,48,384]{3,2,1,0:T(8,128)(2,1)} %get-tuple-element.21), calls=%async_computation | async-start | bytes 589824 | tf_op jit(solution)/shard_map/all_to_all | solution.py:247
  59.8 11.7 %collective-permute-start.10 = (bf16[384,384]{1,0:T(8,128)(2,1)S(1)}, bf16[384,384]{1,0:T(8,128)(2,1)S(1)}, u32[]{:S(2)}, u32[]{:S(2)}) collective-permute-start(bf16[384,384]{1,0:T(8,128)(2,1)S(1)} %get-tuple-element.24), channel_id=1, source_target_pairs={{32,64},{64,32},{96,128},{128,96},{160,192},{192,160},{224,256},{2... | collective-permute-start | bytes 884744 | tf_op jit(solution)/shard_map/ppermute | solution.py:37
  62.8 8.7 %collective-permute-start.11 = (bf16[384,384]{1,0:T(8,128)(2,1)S(1)}, bf16[384,384]{1,0:T(8,128)(2,1)S(1)}, u32[]{:S(2)}, u32[]{:S(2)}) collective-permute-start(bf16[384,384]{1,0:T(8,128)(2,1)S(1)} %get-tuple-element.25), channel_id=1, source_target_pairs={{0,32},{32,0},{64,96},{96,64},{128,160},{160,128},{192,224},{224,1... | collective-permute-start | bytes 884744 | tf_op jit(solution)/shard_map/ppermute | solution.py:37
  72.6 14.9 %all-to-all-start.1 = ((bf16[4,2,48,384]{3,2,1,0:T(8,128)(2,1)}), bf16[4,2,48,384]{3,2,1,0:T(8,128)(2,1)S(1)}, u32[]{:S(2)}, u32[]{:S(2)}) async-start(bf16[4,2,48,384]{3,2,1,0:T(8,128)(2,1)} %shard_map.88), calls=%async_computation.1 | async-start | bytes 589824 | tf_op jit(solution)/shard_map/all_to_all | solution.py:247

commit v2 on v1

--- a/solution.py
+++ b/solution.py
@@ -46,9 +46,9 @@
     return [(a, b) for a in slot_steps("frame") for b in slot_steps("row")]
 
 
-def regroup_kernel(a_ref, b_ref, out_ref):
-    out_ref[0 : 2 * TILE, :] = a_ref[...]
-    out_ref[2 * TILE : 4 * TILE, :] = b_ref[...]
+def regroup_kernel(own_ref, a_ref, b_ref, out_ref):
+    for i, ref in enumerate((own_ref, a_ref, b_ref)):
+        out_ref[2 * TILE * i : 2 * TILE * (i + 1), :] = ref[...]
 
 
 def gather_near(tiles, first_ref, second_ref):
@@ -92,14 +92,11 @@
 
 
 def query_kernel(
-    pairs_s, pairs_v, own_qg, kv, kv_a, kv_b, kv_fb, kv_fa, corner_fb, corner_fa, *refs
+    pairs_s, pairs_v, own_qg, kv, kv_fb, kv_fa, send_ref, stat_ref, key_ref, value_ref
 ):
-    send_ref, stat_ref, key_ref, value_ref = refs
     frame, row = lax.axis_index("frame"), lax.axis_index("row")
     frames, rows = lax.axis_size("frame"), lax.axis_size("row")
-    tiles = [(kv, 0), (kv_a, 0), (kv_b, 0)]
-    tiles += [(kv_fa, 0), (corner_fa, 0), (corner_fa, 2 * TILE)]
-    tiles += [(kv_fb, 0), (corner_fb, 0), (corner_fb, 2 * TILE)]
+    tiles = [(ref, 2 * TILE * i) for ref in (kv, kv_fa, kv_fb) for i in range(3)]
     gather_near(tiles, key_ref, value_ref)
     lane = lax.broadcasted_iota(jnp.int32, (1, WIDE), 1)
     bias = jnp.zeros((1, WIDE), jnp.float32)
@@ -144,14 +141,16 @@
     store_sends(send_ref, attended_parts, grad_parts)
 
 
-def key_kernel(kv, kv_fa, kv_fb, qg, qg_a, qg_b, st, st_a, st_b, *refs):
-    own_ref, term_a_ref, term_b_ref, query_ref, grad_ref, stat_ref = refs
-    count = kv.shape[1] // HEAD_DIM
+def key_kernel(sides, *refs):
+    kvs, refs = refs[: len(sides)], refs[len(sides) :]
+    (qg, qg_a, qg_b, st, st_a, st_b), refs = refs[:6], refs[6:]
+    outs, (query_ref, grad_ref, stat_ref) = refs[: len(sides)], refs[len(sides) :]
+    count = qg.shape[1] // HEAD_DIM
     frame, frames = lax.axis_index("frame"), lax.axis_size("frame")
     gather_near([(qg, 0), (qg_a, 0), (qg_b, 0)], query_ref, grad_ref)
     lane = lax.broadcasted_iota(jnp.int32, (1, TILE), 1)
     level = lax.broadcasted_iota(jnp.int32, (8, TILE), 0)
-    frame_steps = slot_steps("frame")
+    frame_steps = [slot_steps("frame")[side] for side in sides]
     for slot, (ref, b) in enumerate(zip((st, st_a, st_b), slot_steps("row"))):
         block = ref[...]
         for i, a in enumerate(frame_steps):
@@ -164,9 +163,7 @@
     for h in range(count):
         feat = slice(h * HEAD_DIM, (h + 1) * HEAD_DIM)
         query, grad = query_ref[:, feat], grad_ref[:, feat]
-        for i, (kv_ref, out_ref) in enumerate(
-            ((kv, own_ref), (kv_fa, term_a_ref), (kv_fb, term_b_ref))
-        ):
+        for i, (kv_ref, out_ref) in enumerate(zip(kvs, outs)):
             key, value = kv_ref[0:TILE, feat], kv_ref[TILE : 2 * TILE, feat]
             scores = lax.dot_general(
                 key, query, (((1,), (1,)), ((), ())), preferred_element_type=jnp.float32
@@ -206,16 +203,13 @@
     bf16, f32 = jnp.bfloat16, jnp.float32
     flat = [x.reshape(TILE, feats) for x in (key_tokens, value_tokens, queries, grad_out)]
 
-    kv = stacked(flat[0], flat[1])
+    own_kv = stacked(flat[0], flat[1])
+    kv_a, kv_b = pair_swap(own_kv, "row", 0), pair_swap(own_kv, "row", 1)
+    triple = jax.ShapeDtypeStruct((6 * TILE, feats), bf16)
+    kv = call(regroup_kernel, triple, [VMEM] * 3, VMEM)(own_kv, kv_a, kv_b)
+    kv_fb, kv_fa = pair_swap(kv, "frame", 1), pair_swap(kv, "frame", 0)
     qg = stacked(flat[2], flat[3])
-    kv_a, kv_b = pair_swap(kv, "row", 0), pair_swap(kv, "row", 1)
-    kv_fb, kv_fa = pair_swap(kv, "frame", 1), pair_swap(kv, "frame", 0)
-    rows = call(regroup_kernel, jax.ShapeDtypeStruct((4 * TILE, feats), bf16), [VMEM] * 2, VMEM)(
-        kv_a, kv_b
-    )
-    rows = after(rows, kv_fb, kv_fa)
-    corner_fb, corner_fa = pair_swap(rows, "frame", 1), pair_swap(rows, "frame", 0)
-    qg_late = after(qg, kv_fb, kv_fa)
+    qg_late = after(qg, kv)
     qg_a, qg_b = pair_swap(qg_late, "row", 0), pair_swap(qg_late, "row", 1)
 
     send_shape = jax.ShapeDtypeStruct((heads, 2, TILE // heads, feats), bf16)
@@ -223,27 +217,31 @@
     sent_q, stat = call(
         query_kernel,
         (send_shape, jax.ShapeDtypeStruct((8, TILE), f32)),
-        [SMEM] + [VMEM] * 9,
+        [SMEM] + [VMEM] * 5,
         (VMEM, VMEM),
         [near, near],
-    )(tile_pairs, tile_pairs, qg, kv, kv_a, kv_b, kv_fb, kv_fa, corner_fb, corner_fa)
+    )(tile_pairs, tile_pairs, qg, kv, kv_fb, kv_fa)
     st_a, st_b = pair_swap(stat, "row", 0), pair_swap(stat, "row", 1)
 
-    row_near = pltpu.VMEM((3 * TILE, feats), bf16)
-    term = jax.ShapeDtypeStruct((2 * TILE, feats), bf16)
-    own, term_a, term_b = call(
-        key_kernel,
-        (jax.ShapeDtypeStruct((2 * TILE, feats), f32), term, term),
-        [VMEM] * 9,
-        (VMEM,) * 3,
-        [row_near, row_near, pltpu.VMEM((3, 8, 3 * TILE), f32)],
-    )(kv, kv_fa, kv_fb, qg, qg_a, qg_b, stat, st_a, st_b)
-    got_b, got_a = pair_swap(term_b, "frame", 1), pair_swap(term_a, "frame", 0)
+    def terms(sides, kinds, *kvs):
+        row_near = pltpu.VMEM((3 * TILE, feats), bf16)
+        return call(
+            lambda *refs: key_kernel(sides, *refs),
+            [jax.ShapeDtypeStruct((2 * TILE, feats), kind) for kind in kinds],
+            [VMEM] * (len(sides) + 6),
+            [VMEM] * len(sides),
+            [row_near, row_near, pltpu.VMEM((len(sides), 8, 3 * TILE), f32)],
+        )(*kvs, qg, qg_a, qg_b, stat, st_a, st_b)
+
+    (term_b,) = terms((2,), (bf16,), kv_fb)
+    got_b = pair_swap(term_b, "frame", 1)
+    term_a, own = terms((1, 0), (bf16, f32), kv_fa, after(own_kv, term_b))
+    got_a = pair_swap(term_a, "frame", 0)
     sent_k = call(fold_kernel, send_shape, [VMEM] * 3, VMEM)(own, got_b, got_a)
 
     out = jax.ShapeDtypeStruct((frames_dev * rows_dev, columns // heads, heads * feats), bf16)
     outs = []
-    for sent in (after(sent_q, own), sent_k):
+    for sent in (after(sent_q, st_a, st_b), sent_k):
         got = lax.all_to_all(sent, "head", split_axis=0, concat_axis=0, tiled=True)
         outs += call(assemble_kernel, (out, out), [VMEM], (VMEM, VMEM))(got)
     return tuple(x.reshape((frames_dev, rows_dev) + out.shape[1:]) for x in outs)

time: 88.8 us -> 91.1 us (1.026)
  waiting for transfers between devices: 21.5 us -> 25.9 us
  starting transfers between devices: 52.9 us -> 50.6 us
    ppermute x12 -> x10, waiting for transfers between devices: 13.1 us -> 17.1 us  [pair_swap(): return lax.ppermute(value, axis, pairs)]
    ppermute x12 -> x10, starting transfers between devices: 41 us -> 37.2 us  [pair_swap(): return lax.ppermute(value, axis, pairs)]
    all_to_all x2, starting transfers between devices: 11.9 us -> 13.4 us  [body(): got = lax.all_to_all(sent, 'head', split_axis=0, concat_axis=0, tiled=True)]
    pallas_call x2 -> x3, Pallas kernels: 4.01 us -> 4.35 us  [the longest x2 4.27 us: terms(): call(lambda *refs: key_kernel(sides, *refs), [jax.ShapeDtypeStruct((2 * T...]
  transfers between devices with their start and end apart: 14 -> 12, of which waited for: 5 -> 6; matrix products, arithmetic and copies ran while one was open for 0% -> 0% of each run, Pallas kernels for 8% -> 13%
where the time goes in v2:
time: 91.1 us; the launch traced here: 90.6 us
  starting transfers between devices  50.6 us (56%)
  waiting for transfers between devices  25.9 us (28%)
  Pallas kernels  12.2 us (13%)
  other arithmetic  1.05 us (1%)
    ppermute x10, starting transfers between devices, pair_swap(): return lax.ppermute(value, axis, pairs)  37.2 us
    ppermute x10, waiting for transfers between devices, pair_swap(): return lax.ppermute(value, axis, pairs)  17.1 us
    all_to_all x2, starting transfers between devices, body(): got = lax.all_to_all(sent, 'head', split_axis=0, concat_axis=0, tiled=True)  13.4 us
    all_to_all x2, waiting for transfers between devices, body(): got = lax.all_to_all(sent, 'head', split_axis=0, concat_axis=0, tiled=True)  8.8 us
    pallas_call x1, Pallas kernels, body(): call(query_kernel, (send_shape, jax.ShapeDtypeStruct((8, TILE), f32)), [S...  5.26 us
    pallas_call x2, Pallas kernels, terms(): call(lambda *refs: key_kernel(sides, *refs), [jax.ShapeDtypeStruct((2 * T...  4.27 us
  transfers between devices with their start and end apart: 12, of which 6 were waited for; matrix products, arithmetic and copies ran while one was open for 0% of the time, Pallas kernels for 13%

profile of v2, /device:TPU:72, one launch (start us, length us, event | category | flops | bytes accessed | tf_op | source)
XLA Modules:
  0.0 90.6 jit_solution(4491884943535741071)
XLA Ops:
  0.6 1.0 %pad_maximum_fusion.own_ref.refs_1_ = bf16[384,384]{1,0:T(8,128)(2,1)S(1)} fusion(bf16[192,384]{1,0:T(8,128)(2,1)} %bitcast.8, bf16[192,384]{1,0:T(8,128)(2,1)} %bitcast.9), kind=kLoop, calls=%fused_computation | loop fusion | flops 589824 | bytes 589824 | tf_op jit(solution)/shard_map/max | solution.py:197
  1.6 0.0 copy-start.1
  1.7 0.0 copy-start.2
  1.7 2.1 %collective-permute-start = (bf16[384,384]{1,0:T(8,128)(2,1)S(1)}, bf16[384,384]{1,0:T(8,128)(2,1)S(1)}, u32[]{:S(2)}, u32[]{:S(2)}) collective-permute-start(bf16[384,384]{1,0:T(8,128)(2,1)S(1)} %pad_maximum_fusion.own_ref.refs_1_), channel_id=1, source_target_pairs={{0,4},{4,0},{8,12},{12,8},{16,20},{20,16},{24,28},{28,24},{1,5},{5... | collective-permute-start | bytes 884744 | tf_op jit(solution)/shard_map/ppermute | solution.py:37
  3.7 6.6 %collective-permute-start.1 = (bf16[384,384]{1,0:T(8,128)(2,1)S(1)}, bf16[384,384]{1,0:T(8,128)(2,1)S(1)}, u32[]{:S(2)}, u32[]{:S(2)}) collective-permute-start(bf16[384,384]{1,0:T(8,128)(2,1)S(1)} %pad_maximum_fusion.own_ref.refs_1_), channel_id=1, source_target_pairs={{4,8},{8,4},{12,16},{16,12},{20,24},{24,20},{5,9},{9,5},{13,17},{1... | collective-permute-start | bytes 884744 | tf_op jit(solution)/shard_map/ppermute | solution.py:37
  10.4 2.1 %collective-permute-done.a_ref = bf16[384,384]{1,0:T(8,128)(2,1)S(1)} collective-permute-done((bf16[384,384]{1,0:T(8,128)(2,1)S(1)}, bf16[384,384]{1,0:T(8,128)(2,1)S(1)}, u32[]{:S(2)}, u32[]{:S(2)}) %collective-permute-start) | collective-permute-done | bytes 294944 | tf_op jit(solution)/shard_map/ppermute | solution.py:37
  12.4 4.6 %collective-permute-done.1.b_ref = bf16[384,384]{1,0:T(8,128)(2,1)S(1)} collective-permute-done((bf16[384,384]{1,0:T(8,128)(2,1)S(1)}, bf16[384,384]{1,0:T(8,128)(2,1)S(1)}, u32[]{:S(2)}, u32[]{:S(2)}) %collective-permute-start.1) | collective-permute-done | bytes 294944 | tf_op jit(solution)/shard_map/ppermute | solution.py:37
  17.1 0.1 shard_map.84.kv
  17.2 3.1 %collective-permute-start.2 = (bf16[1152,384]{1,0:T(8,128)(2,1)S(1)}, bf16[1152,384]{1,0:T(8,128)(2,1)S(1)}, u32[]{:S(2)}, u32[]{:S(2)}) collective-permute-start(bf16[1152,384]{1,0:T(8,128)(2,1)S(1)} %shard_map.84.kv), channel_id=1, source_target_pairs={{32,64},{64,32},{96,128},{128,96},{160,192},{192,160},{224,256},{2... | collective-permute-start | bytes 2654216 | tf_op jit(solution)/shard_map/ppermute | solution.py:37
  20.3 2.3 %collective-permute-start.3 = (bf16[1152,384]{1,0:T(8,128)(2,1)S(1)}, bf16[1152,384]{1,0:T(8,128)(2,1)S(1)}, u32[]{:S(2)}, u32[]{:S(2)}) collective-permute-start(bf16[1152,384]{1,0:T(8,128)(2,1)S(1)} %shard_map.84.kv), channel_id=1, source_target_pairs={{0,32},{32,0},{64,96},{96,64},{128,160},{160,128},{192,224},{224,1... | collective-permute-start | bytes 2654216 | tf_op jit(solution)/shard_map/ppermute | solution.py:37
  22.6 0.0 copy-done.1
  22.6 0.0 copy-done.2
  22.6 0.0 copy-start
  22.7 1.9 %collective-permute-start.6 = (bf16[384,384]{1,0:T(8,128)(2,1)S(1)}, bf16[384,384]{1,0:T(8,128)(2,1)S(1)}, u32[]{:S(2)}, u32[]{:S(2)}) collective-permute-start(bf16[384,384]{1,0:T(8,128)(2,1)S(1)} %pad_maximum_fusion.1.own_qg.refs_1_.refs_2_), channel_id=1, source_target_pairs={{0,4},{4,0},{8,12},{12,8},{16,20},{20,16},{24,28},{28,24},{1,5},{5... | collective-permute-start | bytes 884744 | tf_op jit(solution)/shard_map/ppermute | solution.py:37
  24.6 7.0 %collective-permute-start.7 = (bf16[384,384]{1,0:T(8,128)(2,1)S(1)}, bf16[384,384]{1,0:T(8,128)(2,1)S(1)}, u32[]{:S(2)}, u32[]{:S(2)}) collective-permute-start(bf16[384,384]{1,0:T(8,128)(2,1)S(1)} %pad_maximum_fusion.1.own_qg.refs_1_.refs_2_), channel_id=1, source_target_pairs={{4,8},{8,4},{12,16},{16,12},{20,24},{24,20},{5,9},{9,5},{13,17},{1... | collective-permute-start | bytes 884744 | tf_op jit(solution)/shard_map/ppermute | solution.py:37
  31.6 2.1 %collective-permute-done.2.kv_fb.refs_0_ = bf16[1152,384]{1,0:T(8,128)(2,1)S(1)} collective-permute-done((bf16[1152,384]{1,0:T(8,128)(2,1)S(1)}, bf16[1152,384]{1,0:T(8,128)(2,1)S(1)}, u32[]{:S(2)}, u32[]{:S(2)}) %collective-permute-start.2) | collective-permute-done | bytes 884768 | tf_op jit(solution)/shard_map/ppermute | solution.py:37
  33.6 0.0 collective-permute-done.3.kv_fa.refs_0_
  33.6 0.0 copy-done
  33.6 5.3 %shard_map.85 = (bf16[4,2,48,384]{3,2,1,0:T(8,128)(2,1)}, f32[8,192]{1,0:T(8,128)S(1)}) custom-call(s32[1,1,1,27]{3,2,1,0:T(1,128)S(1)} %copy-done, s32[1,1,1,27]{3,2,1,0:T(1,128)S(1)} %copy-done, bf16[384,384]{1,0:T(8,128)(2,1)S(1)} %pad_maximum_fusion.1.own_qg.refs_1_.refs_2_, bf16[1152,384]{1,0:T(8,128)(2,1)S(1)} %shard_map.84.kv, ...), custom_call_target="tpu_custom_call" | custom-call | tf_op jit(solution)/shard_map/pallas_call | solution.py:217
  38.9 1.9 %collective-permute-start.4 = (f32[8,192]{1,0:T(8,128)S(1)}, f32[8,192]{1,0:T(8,128)S(1)}, u32[]{:S(2)}, u32[]{:S(2)}) collective-permute-start(f32[8,192]{1,0:T(8,128)S(1)} %get-tuple-element.16.refs_4_.refs_5_), channel_id=1, source_target_pairs={{0,4},{4,0},{8,12},{12,8},{16,20},{20,16},{24,28},{28,24},{1,5},{5... | collective-permute-start | bytes 18440 | tf_op jit(solution)/shard_map/ppermute | solution.py:37
  40.8 7.0 %collective-permute-start.5 = (f32[8,192]{1,0:T(8,128)S(1)}, f32[8,192]{1,0:T(8,128)S(1)}, u32[]{:S(2)}, u32[]{:S(2)}) collective-permute-start(f32[8,192]{1,0:T(8,128)S(1)} %get-tuple-element.16.refs_4_.refs_5_), channel_id=1, source_target_pairs={{4,8},{8,4},{12,16},{16,12},{20,24},{24,20},{5,9},{9,5},{13,17},{1... | collective-permute-start | bytes 18440 | tf_op jit(solution)/shard_map/ppermute | solution.py:37
  47.8 0.0 collective-permute-done.4.refs_5_.refs_6_
  47.8 1.6 %collective-permute-done.5.refs_6_.refs_7_ = f32[8,192]{1,0:T(8,128)S(1)} collective-permute-done((f32[8,192]{1,0:T(8,128)S(1)}, f32[8,192]{1,0:T(8,128)S(1)}, u32[]{:S(2)}, u32[]{:S(2)}) %collective-permute-start.5) | collective-permute-done | bytes 6176 | tf_op jit(solution)/shard_map/ppermute | solution.py:37
  49.4 6.2 %all-to-all-start = ((bf16[4,2,48,384]{3,2,1,0:T(8,128)(2,1)}), bf16[4,2,48,384]{3,2,1,0:T(8,128)(2,1)S(1)}, u32[]{:S(2)}, u32[]{:S(2)}) async-start(bf16[4,2,48,384]{3,2,1,0:T(8,128)(2,1)} %get-tuple-element.17), calls=%async_computation | async-start | bytes 589824 | tf_op jit(solution)/shard_map/all_to_all | solution.py:245
  55.6 0.0 collective-permute-done.6.refs_2_.refs_3_
  55.6 0.0 collective-permute-done.7.refs_3_.refs_4_
  55.6 1.5 %shard_map.87 = bf16[384,384]{1,0:T(8,128)(2,1)S(1)} custom-call(bf16[1152,384]{1,0:T(8,128)(2,1)S(1)} %collective-permute-done.2.kv_fb.refs_0_, bf16[384,384]{1,0:T(8,128)(2,1)S(1)} %pad_maximum_fusion.1.own_qg.refs_1_.refs_2_, bf16[384,384]{1,0:T(8,128)(2,1)S(1)} %collective-permute-done.6.refs_2_.refs_3_, ...), custom_call_target="tpu_custom_call" | custom-call | tf_op jit(solution)/shard_map/pallas_call | solution.py:228
  57.1 2.8 %shard_map.88 = (bf16[384,384]{1,0:T(8,128)(2,1)S(1)}, f32[384,384]{1,0:T(8,128)S(1)}) custom-call(bf16[1152,384]{1,0:T(8,128)(2,1)S(1)} %collective-permute-done.3.kv_fa.refs_0_, bf16[384,384]{1,0:T(8,128)(2,1)S(1)} %pad_maximum_fusion.own_ref.refs_1_, bf16[384,384]{1,0:T(8,128)(2,1)S(1)} %pad_maximum_fusion.1.own_qg.refs_1_.refs_2_, ...), custom_call_target="tpu_custom_call" | custom-call | tf_op jit(solution)/shard_map/pallas_call | solution.py:228
  59.9 1.9 %collective-permute-start.9 = (bf16[384,384]{1,0:T(8,128)(2,1)S(1)}, bf16[384,384]{1,0:T(8,128)(2,1)S(1)}, u32[]{:S(2)}, u32[]{:S(2)}) collective-permute-start(bf16[384,384]{1,0:T(8,128)(2,1)S(1)} %get-tuple-element.23), channel_id=1, source_target_pairs={{0,32},{32,0},{64,96},{96,64},{128,160},{160,128},{192,224},{224,1... | collective-permute-start | bytes 884744 | tf_op jit(solution)/shard_map/ppermute | solution.py:37
  61.8 3.4 %collective-permute-start.8 = (bf16[384,384]{1,0:T(8,128)(2,1)S(1)}, bf16[384,384]{1,0:T(8,128)(2,1)S(1)}, u32[]{:S(2)}, u32[]{:S(2)}) collective-permute-start(bf16[384,384]{1,0:T(8,128)(2,1)S(1)} %shard_map.87), channel_id=1, source_target_pairs={{32,64},{64,32},{96,128},{128,96},{160,192},{192,160},{224,256},{2... | collective-permute-start | bytes 884744 | tf_op jit(solution)/shard_map/ppermute | solution.py:37
  65.3 0.0 collective-permute-done.9.got_b
  65.3 6.7 %collective-permute-done.8.got_a = bf16[384,384]{1,0:T(8,128)(2,1)S(1)} collective-permute-done((bf16[384,384]{1,0:T(8,128)(2,1)S(1)}, bf16[384,384]{1,0:T(8,128)(2,1)S(1)}, u32[]{:S(2)}, u32[]{:S(2)}) %collective-permute-start.8) | collective-permute-done | bytes 294944 | tf_op jit(solution)/shard_map/ppermute | solution.py:37
  72.0 1.0 %shard_map.89 = bf16[4,2,48,384]{3,2,1,0:T(8,128)(2,1)} custom-call(f32[384,384]{1,0:T(8,128)S(1)} %get-tuple-element.22.own_ref, bf16[384,384]{1,0:T(8,128)(2,1)S(1)} %collective-permute-done.8.got_a, bf16[384,384]{1,0:T(8,128)(2,1)S(1)} %collective-permute-done.9.got_b), custom_call_target="tpu_custom_call" | custom-call | tf_op jit(solution)/shard_map/pallas_call | solution.py:240
  73.0 0.0 all-to-all-done.got_ref
  73.0 7.2 %all-to-all-start.1 = ((bf16[4,2,48,384]{3,2,1,0:T(8,128)(2,1)}), bf16[4,2,48,384]{3,2,1,0:T(8,128)(2,1)S(1)}, u32[]{:S(2)}, u32[]{:S(2)}) async-start(bf16[4,2,48,384]{3,2,1,0:T(8,128)(2,1)} %shard_map.89), calls=%async_computation.1 | async-start | bytes 589824 | tf_op jit(solution)/shard_map/all_to_all | solution.py:245
  80.2 0.8 shard_map.86
  81.0 8.8 %all-to-all-done.1.got_ref = bf16[4,2,48,384]{3,2,1,0:T(8,128)(2,1)S(1)} async-done(((bf16[4,2,48,384]{3,2,1,0:T(8,128)(2,1)}), bf16[4,2,48,384]{3,2,1,0:T(8,128)(2,1)S(1)}, u32[]{:S(2)}, u32[]{:S(2)}) %all-to-all-start.1) | async-done | bytes 294944 | tf_op jit(solution)/shard_map/all_to_all | solution.py:245
  89.8 0.8 shard_map.90
  (1 shorter events, 0.0 us)
Async XLA Ops:
  1.6 21.0 %copy-start.1 = (bf16[6,4,8,384]{3,2,1,0:T(8,128)(2,1)S(1)}, bf16[6,4,8,384]{3,2,1,0:T(8,128)(2,1)}, u32[]{:S(2)}) copy-start(bf16[6,4,8,384]{3,2,1,0:T(8,128)(2,1)} %param.8) | copy-start | bytes 442372
  1.7 21.0 %copy-start.2 = (bf16[6,4,8,384]{3,2,1,0:T(8,128)(2,1)S(1)}, bf16[6,4,8,384]{3,2,1,0:T(8,128)(2,1)}, u32[]{:S(2)}) copy-start(bf16[6,4,8,384]{3,2,1,0:T(8,128)(2,1)} %param.5) | copy-start | bytes 442372
  1.7 10.8 %collective-permute-start = (bf16[384,384]{1,0:T(8,128)(2,1)S(1)}, bf16[384,384]{1,0:T(8,128)(2,1)S(1)}, u32[]{:S(2)}, u32[]{:S(2)}) collective-permute-start(bf16[384,384]{1,0:T(8,128)(2,1)S(1)} %pad_maximum_fusion.own_ref.refs_1_), channel_id=1, source_target_pairs={{0,4},{4,0},{8,12},{12,8},{16,20},{20,16},{24,28},{28,24},{1,5},{5... | collective-permute-start | bytes 884744 | tf_op jit(solution)/shard_map/ppermute | solution.py:37
  3.7 13.4 %collective-permute-start.1 = (bf16[384,384]{1,0:T(8,128)(2,1)S(1)}, bf16[384,384]{1,0:T(8,128)(2,1)S(1)}, u32[]{:S(2)}, u32[]{:S(2)}) collective-permute-start(bf16[384,384]{1,0:T(8,128)(2,1)S(1)} %pad_maximum_fusion.own_ref.refs_1_), channel_id=1, source_target_pairs={{4,8},{8,4},{12,16},{16,12},{20,24},{24,20},{5,9},{9,5},{13,17},{1... | collective-permute-start | bytes 884744 | tf_op jit(solution)/shard_map/ppermute | solution.py:37
  17.2 16.5 %collective-permute-start.2 = (bf16[1152,384]{1,0:T(8,128)(2,1)S(1)}, bf16[1152,384]{1,0:T(8,128)(2,1)S(1)}, u32[]{:S(2)}, u32[]{:S(2)}) collective-permute-start(bf16[1152,384]{1,0:T(8,128)(2,1)S(1)} %shard_map.84.kv), channel_id=1, source_target_pairs={{32,64},{64,32},{96,128},{128,96},{160,192},{192,160},{224,256},{2... | collective-permute-start | bytes 2654216 | tf_op jit(solution)/shard_map/ppermute | solution.py:37
  20.3 13.3 %collective-permute-start.3 = (bf16[1152,384]{1,0:T(8,128)(2,1)S(1)}, bf16[1152,384]{1,0:T(8,128)(2,1)S(1)}, u32[]{:S(2)}, u32[]{:S(2)}) collective-permute-start(bf16[1152,384]{1,0:T(8,128)(2,1)S(1)} %shard_map.84.kv), channel_id=1, source_target_pairs={{0,32},{32,0},{64,96},{96,64},{128,160},{160,128},{192,224},{224,1... | collective-permute-start | bytes 2654216 | tf_op jit(solution)/shard_map/ppermute | solution.py:37
  22.6 11.0 %copy-start = (s32[1,1,1,27]{3,2,1,0:T(1,128)S(1)}, s32[1,1,1,27]{3,2,1,0:T(1,128)}, u32[]{:S(2)}) copy-start(s32[1,1,1,27]{3,2,1,0:T(1,128)} %pairs_v.1) | copy-start | bytes 328
  22.7 32.9 %collective-permute-start.6 = (bf16[384,384]{1,0:T(8,128)(2,1)S(1)}, bf16[384,384]{1,0:T(8,128)(2,1)S(1)}, u32[]{:S(2)}, u32[]{:S(2)}) collective-permute-start(bf16[384,384]{1,0:T(8,128)(2,1)S(1)} %pad_maximum_fusion.1.own_qg.refs_1_.refs_2_), channel_id=1, source_target_pairs={{0,4},{4,0},{8,12},{12,8},{16,20},{20,16},{24,28},{28,24},{1,5},{5... | collective-permute-start | bytes 884744 | tf_op jit(solution)/shard_map/ppermute | solution.py:37
  24.6 31.0 %collective-permute-start.7 = (bf16[384,384]{1,0:T(8,128)(2,1)S(1)}, bf16[384,384]{1,0:T(8,128)(2,1)S(1)}, u32[]{:S(2)}, u32[]{:S(2)}) collective-permute-start(bf16[384,384]{1,0:T(8,128)(2,1)S(1)} %pad_maximum_fusion.1.own_qg.refs_1_.refs_2_), channel_id=1, source_target_pairs={{4,8},{8,4},{12,16},{16,12},{20,24},{24,20},{5,9},{9,5},{13,17},{1... | collective-permute-start | bytes 884744 | tf_op jit(solution)/shard_map/ppermute | solution.py:37
  38.9 8.9 %collective-permute-start.4 = (f32[8,192]{1,0:T(8,128)S(1)}, f32[8,192]{1,0:T(8,128)S(1)}, u32[]{:S(2)}, u32[]{:S(2)}) collective-permute-start(f32[8,192]{1,0:T(8,128)S(1)} %get-tuple-element.16.refs_4_.refs_5_), channel_id=1, source_target_pairs={{0,4},{4,0},{8,12},{12,8},{16,20},{20,16},{24,28},{28,24},{1,5},{5... | collective-permute-start | bytes 18440 | tf_op jit(solution)/shard_map/ppermute | solution.py:37
  40.8 8.6 %collective-permute-start.5 = (f32[8,192]{1,0:T(8,128)S(1)}, f32[8,192]{1,0:T(8,128)S(1)}, u32[]{:S(2)}, u32[]{:S(2)}) collective-permute-start(f32[8,192]{1,0:T(8,128)S(1)} %get-tuple-element.16.refs_4_.refs_5_), channel_id=1, source_target_pairs={{4,8},{8,4},{12,16},{16,12},{20,24},{24,20},{5,9},{9,5},{13,17},{1... | collective-permute-start | bytes 18440 | tf_op jit(solution)/shard_map/ppermute | solution.py:37
  49.4 23.6 %all-to-all-start = ((bf16[4,2,48,384]{3,2,1,0:T(8,128)(2,1)}), bf16[4,2,48,384]{3,2,1,0:T(8,128)(2,1)S(1)}, u32[]{:S(2)}, u32[]{:S(2)}) async-start(bf16[4,2,48,384]{3,2,1,0:T(8,128)(2,1)} %get-tuple-element.17), calls=%async_computation | async-start | bytes 589824 | tf_op jit(solution)/shard_map/all_to_all | solution.py:245
  59.9 5.4 %collective-permute-start.9 = (bf16[384,384]{1,0:T(8,128)(2,1)S(1)}, bf16[384,384]{1,0:T(8,128)(2,1)S(1)}, u32[]{:S(2)}, u32[]{:S(2)}) collective-permute-start(bf16[384,384]{1,0:T(8,128)(2,1)S(1)} %get-tuple-element.23), channel_id=1, source_target_pairs={{0,32},{32,0},{64,96},{96,64},{128,160},{160,128},{192,224},{224,1... | collective-permute-start | bytes 884744 | tf_op jit(solution)/shard_map/ppermute | solution.py:37
  61.8 10.2 %collective-permute-start.8 = (bf16[384,384]{1,0:T(8,128)(2,1)S(1)}, bf16[384,384]{1,0:T(8,128)(2,1)S(1)}, u32[]{:S(2)}, u32[]{:S(2)}) collective-permute-start(bf16[384,384]{1,0:T(8,128)(2,1)S(1)} %shard_map.87), channel_id=1, source_target_pairs={{32,64},{64,32},{96,128},{128,96},{160,192},{192,160},{224,256},{2... | collective-permute-start | bytes 884744 | tf_op jit(solution)/shard_map/ppermute | solution.py:37
  73.0 16.8 %all-to-all-start.1 = ((bf16[4,2,48,384]{3,2,1,0:T(8,128)(2,1)}), bf16[4,2,48,384]{3,2,1,0:T(8,128)(2,1)S(1)}, u32[]{:S(2)}, u32[]{:S(2)}) async-start(bf16[4,2,48,384]{3,2,1,0:T(8,128)(2,1)} %shard_map.89), calls=%async_computation.1 | async-start | bytes 589824 | tf_op jit(solution)/shard_map/all_to_all | solution.py:245

commit v3 on v1

--- a/solution.py
+++ b/solution.py
@@ -58,9 +58,9 @@
         second_ref[rows, :] = ref[start + TILE : start + 2 * TILE, :]
 
 
-def store_sends(send_ref, firsts, seconds):
-    heads = send_ref.shape[0]
+def column_blocks(firsts, seconds, heads):
     group, span = 8 // heads, TILE // heads
+    me = lax.axis_index("head")
     row = lax.broadcasted_iota(jnp.int32, (TILE, TILE), 0)
     col = lax.broadcasted_iota(jnp.int32, (TILE, TILE), 1)
     block = jnp.zeros_like(row)
@@ -68,33 +68,42 @@
         block += (row >= d * span).astype(jnp.int32)
     inner = row - block * span
     shift = group.bit_length() - 1
-    source = (inner >> shift) * 8 + block * group + (inner & (group - 1))
+    source = (inner >> shift) * 8 + (block ^ me) * group + (inner & (group - 1))
     order = (col == source).astype(jnp.bfloat16)
     joined = jnp.concatenate(firsts + seconds, axis=1)
     moved = jnp.dot(order, joined, preferred_element_type=jnp.float32).astype(jnp.bfloat16)
-    feats = send_ref.shape[3]
-    for k in range(heads):
-        rows = slice(k * span, (k + 1) * span)
-        send_ref[k, 0] = moved[rows, :feats]
-        send_ref[k, 1] = moved[rows, feats:]
-
-
-def assemble(got_ref, out_refs):
-    heads, _, _, feats = got_ref.shape
-    for k in range(heads):
-        place = slice(k * feats, (k + 1) * feats)
-        for i, out_ref in enumerate(out_refs):
-            out_ref[:, :, place] = got_ref[k, i].reshape(out_ref.shape[:2] + (feats,))
-
-
-def assemble_kernel(got_ref, *out_refs):
-    assemble(got_ref, out_refs)
+    feats = joined.shape[1] // 2
+    return [
+        [moved[k * span : (k + 1) * span, i * feats : (i + 1) * feats] for i in range(2)]
+        for k in range(heads)
+    ]
+
+
+def near_heads(heads):
+    return [k for k in range(heads) if k != heads // 2]
+
+
+def assemble_kernel(heads, far_q, far_k, *refs):
+    near_refs, out_refs = refs[: heads - 1], refs[heads - 1 :]
+    feats = far_q.shape[2]
+    me = lax.axis_index("head")
+
+    def put(k, i, rows):
+        place = pl.ds(pl.multiple_of((me ^ k) * feats, HEAD_DIM), feats)
+        out_refs[i][:, :, place] = rows.reshape(out_refs[i].shape[:2] + (feats,))
+
+    for i in range(2):
+        put(heads // 2, i, far_q[i])
+        put(heads // 2, 2 + i, far_k[i])
+    for k, ref in zip(near_heads(heads), near_refs):
+        for i in range(4):
+            put(k, i, ref[i])
 
 
 def query_kernel(
-    pairs_s, pairs_v, own_qg, kv, kv_a, kv_b, kv_fb, kv_fa, corner_fb, corner_fa, *refs
+    heads, pairs_s, pairs_v, own_qg, kv, kv_a, kv_b, kv_fb, kv_fa, corner_fb, corner_fa, *refs
 ):
-    send_ref, stat_ref, key_ref, value_ref = refs
+    far_ref, near_ref, stat_ref, key_ref, value_ref = refs
     frame, row = lax.axis_index("frame"), lax.axis_index("row")
     frames, rows = lax.axis_size("frame"), lax.axis_size("row")
     tiles = [(kv, 0), (kv_a, 0), (kv_b, 0)]
@@ -141,7 +150,11 @@
         stats = jnp.where(stat_lane == count + h, spread, stats)
     stat_ref[...] = stats.T[0:8, :]
     stat_ref[7:8, 0:27] = pairs_v[0, 0].astype(jnp.float32)
-    store_sends(send_ref, attended_parts, grad_parts)
+    blocks = column_blocks(attended_parts, grad_parts, heads)
+    for i in range(2):
+        far_ref[i] = blocks[heads // 2][i]
+        for at, k in enumerate(near_heads(heads)):
+            near_ref[at, i] = blocks[k][i]
 
 
 def key_kernel(kv, kv_fa, kv_fb, qg, qg_a, qg_b, st, st_a, st_b, *refs):
@@ -184,14 +197,24 @@
             out_ref[TILE : 2 * TILE, feat] = value_grad.astype(out_ref.dtype)
 
 
-def fold_kernel(own_ref, got_a, got_b, send_ref):
+def fold_kernel(heads, own_ref, got_a, got_b, near_q, far_ref, *near_refs):
     total = own_ref[...] + got_a[...].astype(jnp.float32) + got_b[...].astype(jnp.float32)
     total = total.astype(jnp.bfloat16)
-    store_sends(send_ref, [total[0:TILE]], [total[TILE : 2 * TILE]])
+    blocks = column_blocks([total[0:TILE]], [total[TILE : 2 * TILE]], heads)
+    for i in range(2):
+        far_ref[i] = blocks[heads // 2][i]
+        for at, (k, ref) in enumerate(zip(near_heads(heads), near_refs)):
+            ref[i] = near_q[at, i]
+            ref[2 + i] = blocks[k][i]
 
 
 def after(value, *others):
     return lax.optimization_barrier((value,) + others)[0]
+
+
+def head_swap(value, k):
+    count = lax.axis_size("head")
+    return lax.ppermute(value, "head", [(i, i ^ k) for i in range(count)]) if k else value
 
 
 def stacked(first, second):
@@ -218,16 +241,19 @@
     qg_late = after(qg, kv_fb, kv_fa)
     qg_a, qg_b = pair_swap(qg_late, "row", 0), pair_swap(qg_late, "row", 1)
 
-    send_shape = jax.ShapeDtypeStruct((heads, 2, TILE // heads, feats), bf16)
+    span = TILE // heads
+    pair, four = (jax.ShapeDtypeStruct((n, span, feats), bf16) for n in (2, 4))
+    near_shape = jax.ShapeDtypeStruct((heads - 1, 2, span, feats), bf16)
     near = pltpu.VMEM((WIDE, feats), bf16)
-    sent_q, stat = call(
-        query_kernel,
-        (send_shape, jax.ShapeDtypeStruct((8, TILE), f32)),
+    far_q, near_q, stat = call(
+        lambda *refs: query_kernel(heads, *refs),
+        (pair, near_shape, jax.ShapeDtypeStruct((8, TILE), f32)),
         [SMEM] + [VMEM] * 9,
-        (VMEM, VMEM),
+        (VMEM,) * 3,
         [near, near],
     )(tile_pairs, tile_pairs, qg, kv, kv_a, kv_b, kv_fb, kv_fa, corner_fb, corner_fa)
     st_a, st_b = pair_swap(stat, "row", 0), pair_swap(stat, "row", 1)
+    got_far_q = head_swap(far_q, heads // 2)
 
     row_near = pltpu.VMEM((3 * TILE, feats), bf16)
     term = jax.ShapeDtypeStruct((2 * TILE, feats), bf16)
@@ -237,15 +263,24 @@
         [VMEM] * 9,
         (VMEM,) * 3,
         [row_near, row_near, pltpu.VMEM((3, 8, 3 * TILE), f32)],
-    )(kv, kv_fa, kv_fb, qg, qg_a, qg_b, stat, st_a, st_b)
+    )(after(kv, got_far_q), kv_fa, kv_fb, qg, qg_a, qg_b, stat, st_a, st_b)
     got_b, got_a = pair_swap(term_b, "frame", 1), pair_swap(term_a, "frame", 0)
-    sent_k = call(fold_kernel, send_shape, [VMEM] * 3, VMEM)(own, got_b, got_a)
+    far_k, *near_k = call(
+        lambda *refs: fold_kernel(heads, *refs),
+        [pair] + [four] * (heads - 1),
+        [VMEM] * 4,
+        [VMEM] * heads,
+    )(own, got_b, got_a, near_q)
+    got_far_k = head_swap(far_k, heads // 2)
+    got_near = [head_swap(sent, k) for k, sent in zip(near_heads(heads), near_k)]
 
     out = jax.ShapeDtypeStruct((frames_dev * rows_dev, columns // heads, heads * feats), bf16)
-    outs = []
-    for sent in (after(sent_q, own), sent_k):
-        got = lax.all_to_all(sent, "head", split_axis=0, concat_axis=0, tiled=True)
-        outs += call(assemble_kernel, (out, out), [VMEM], (VMEM, VMEM))(got)
+    outs = call(
+        lambda *refs: assemble_kernel(heads, *refs),
+        [out] * 4,
+        [VMEM] * (heads + 1),
+        [VMEM] * 4,
+    )(got_far_q, got_far_k, *got_near)
     return tuple(x.reshape((frames_dev, rows_dev) + out.shape[1:]) for x in outs)
 
 

time: 88.8 us -> 88.6 us (level)
  starting transfers between devices: 52.9 us -> 56 us
  Pallas kernels: 11.9 us -> 9.89 us
  waiting for transfers between devices: 21.5 us -> 19.9 us
    ppermute x0 -> x4, starting transfers between devices: none -> 20 us  [head_swap(): lax.ppermute(value, 'head', [(i, i ^ k) for i in range(count)])]
    all_to_all x2 -> x0, starting transfers between devices: 11.9 us -> none  [body(): got = lax.all_to_all(sent, 'head', split_axis=0, concat_axis=0, tiled=True)]
    all_to_all x2 -> x0, waiting for transfers between devices: 8.47 us -> none  [body(): got = lax.all_to_all(sent, 'head', split_axis=0, concat_axis=0, tiled=True)]
    ppermute x0 -> x4, waiting for transfers between devices: none -> 5.35 us  [head_swap(): lax.ppermute(value, 'head', [(i, i ^ k) for i in range(count)])]
    ppermute x12, starting transfers between devices: 41 us -> 36 us  [pair_swap(): return lax.ppermute(value, axis, pairs)]
    pallas_call x4 -> x3, Pallas kernels: 7.89 us -> 5.86 us  [the longest x1 4.57 us: body(): call(lambda *refs: query_kernel(heads, *refs), (pair, near_shape, jax.Sha...]
    ppermute x12, waiting for transfers between devices: 13.1 us -> 14.5 us  [pair_swap(): return lax.ppermute(value, axis, pairs)]
  transfers between devices with their start and end apart: 14 -> 16, of which waited for: 5 -> 6; matrix products, arithmetic and copies ran while one was open for 0% -> 0% of each run, Pallas kernels for 8% -> 5%
where the time goes in v3:
time: 88.6 us; the launch traced here: 87.7 us
  starting transfers between devices  56 us (63%)
  waiting for transfers between devices  19.9 us (22%)
  Pallas kernels  9.89 us (11%)
  other arithmetic  1.05 us (1%)
  between operations  0.89 us (1%)
    ppermute x12, starting transfers between devices, pair_swap(): return lax.ppermute(value, axis, pairs)  36 us
    ppermute x4, starting transfers between devices, head_swap(): lax.ppermute(value, 'head', [(i, i ^ k) for i in range(count)])  20 us
    ppermute x12, waiting for transfers between devices, pair_swap(): return lax.ppermute(value, axis, pairs)  14.5 us
    ppermute x4, waiting for transfers between devices, head_swap(): lax.ppermute(value, 'head', [(i, i ^ k) for i in range(count)])  5.35 us
    pallas_call x1, Pallas kernels, body(): call(lambda *refs: query_kernel(heads, *refs), (pair, near_shape, jax.Sha...  4.57 us
    pallas_call x1, Pallas kernels, body(): call(key_kernel, (jax.ShapeDtypeStruct((2 * TILE, feats), f32), term, ter...  3.97 us
  transfers between devices with their start and end apart: 16, of which 6 were waited for; matrix products, arithmetic and copies ran while one was open for 0% of the time, Pallas kernels for 5%

profile of v3, /device:TPU:72, one launch (start us, length us, event | category | flops | bytes accessed | tf_op | source)
XLA Modules:
  0.0 87.7 jit_solution(3703587673041732710)
XLA Ops:
  0.6 1.0 %pad_maximum_fusion.refs_3_.kv = bf16[384,384]{1,0:T(8,128)(2,1)S(1)} fusion(bf16[192,384]{1,0:T(8,128)(2,1)} %bitcast.8, bf16[192,384]{1,0:T(8,128)(2,1)} %bitcast.9), kind=kLoop, calls=%fused_computation | loop fusion | flops 589824 | bytes 589824 | tf_op jit(solution)/shard_map/max | solution.py:223
  1.6 0.0 copy-start.1
  1.7 0.0 copy-start.2
  1.7 2.1 %collective-permute-start = (bf16[384,384]{1,0:T(8,128)(2,1)S(1)}, bf16[384,384]{1,0:T(8,128)(2,1)S(1)}, u32[]{:S(2)}, u32[]{:S(2)}) collective-permute-start(bf16[384,384]{1,0:T(8,128)(2,1)S(1)} %pad_maximum_fusion.refs_3_.kv), channel_id=1, source_target_pairs={{0,4},{4,0},{8,12},{12,8},{16,20},{20,16},{24,28},{28,24},{1,5},{5... | collective-permute-start | bytes 884744 | tf_op jit(solution)/shard_map/ppermute | solution.py:37
  3.7 6.6 %collective-permute-start.1 = (bf16[384,384]{1,0:T(8,128)(2,1)S(1)}, bf16[384,384]{1,0:T(8,128)(2,1)S(1)}, u32[]{:S(2)}, u32[]{:S(2)}) collective-permute-start(bf16[384,384]{1,0:T(8,128)(2,1)S(1)} %pad_maximum_fusion.refs_3_.kv), channel_id=1, source_target_pairs={{4,8},{8,4},{12,16},{16,12},{20,24},{24,20},{5,9},{9,5},{13,17},{1... | collective-permute-start | bytes 884744 | tf_op jit(solution)/shard_map/ppermute | solution.py:37
  10.4 3.4 %collective-permute-start.2 = (bf16[384,384]{1,0:T(8,128)(2,1)S(1)}, bf16[384,384]{1,0:T(8,128)(2,1)S(1)}, u32[]{:S(2)}, u32[]{:S(2)}) collective-permute-start(bf16[384,384]{1,0:T(8,128)(2,1)S(1)} %pad_maximum_fusion.refs_3_.kv), channel_id=1, source_target_pairs={{32,64},{64,32},{96,128},{128,96},{160,192},{192,160},{224,256},{2... | collective-permute-start | bytes 884744 | tf_op jit(solution)/shard_map/ppermute | solution.py:37
  13.8 2.0 %collective-permute-start.3 = (bf16[384,384]{1,0:T(8,128)(2,1)S(1)}, bf16[384,384]{1,0:T(8,128)(2,1)S(1)}, u32[]{:S(2)}, u32[]{:S(2)}) collective-permute-start(bf16[384,384]{1,0:T(8,128)(2,1)S(1)} %pad_maximum_fusion.refs_3_.kv), channel_id=1, source_target_pairs={{0,32},{32,0},{64,96},{96,64},{128,160},{160,128},{192,224},{224,1... | collective-permute-start | bytes 884744 | tf_op jit(solution)/shard_map/ppermute | solution.py:37
  15.8 0.0 collective-permute-done.a_ref.refs_4_
  15.8 1.3 %collective-permute-done.1.b_ref.refs_5_ = bf16[384,384]{1,0:T(8,128)(2,1)S(1)} collective-permute-done((bf16[384,384]{1,0:T(8,128)(2,1)S(1)}, bf16[384,384]{1,0:T(8,128)(2,1)S(1)}, u32[]{:S(2)}, u32[]{:S(2)}) %collective-permute-start.1) | collective-permute-done | bytes 294944 | tf_op jit(solution)/shard_map/ppermute | solution.py:37
  17.1 0.1 shard_map.84
  17.1 3.4 %collective-permute-done.2.refs_6_.kv_fb = bf16[384,384]{1,0:T(8,128)(2,1)S(1)} collective-permute-done((bf16[384,384]{1,0:T(8,128)(2,1)S(1)}, bf16[384,384]{1,0:T(8,128)(2,1)S(1)}, u32[]{:S(2)}, u32[]{:S(2)}) %collective-permute-start.2) | collective-permute-done | bytes 294944 | tf_op jit(solution)/shard_map/ppermute | solution.py:37
  20.5 0.0 collective-permute-done.3.refs_7_.kv_fa
  20.5 3.4 %collective-permute-start.4 = (bf16[768,384]{1,0:T(8,128)(2,1)S(1)}, bf16[768,384]{1,0:T(8,128)(2,1)S(1)}, u32[]{:S(2)}, u32[]{:S(2)}) collective-permute-start(bf16[768,384]{1,0:T(8,128)(2,1)S(1)} %shard_map.84), channel_id=1, source_target_pairs={{32,64},{64,32},{96,128},{128,96},{160,192},{192,160},{224,256},{2... | collective-permute-start | bytes 1769480 | tf_op jit(solution)/shard_map/ppermute | solution.py:37
  24.0 1.9 %collective-permute-start.5 = (bf16[768,384]{1,0:T(8,128)(2,1)S(1)}, bf16[768,384]{1,0:T(8,128)(2,1)S(1)}, u32[]{:S(2)}, u32[]{:S(2)}) collective-permute-start(bf16[768,384]{1,0:T(8,128)(2,1)S(1)} %shard_map.84), channel_id=1, source_target_pairs={{0,32},{32,0},{64,96},{96,64},{128,160},{160,128},{192,224},{224,1... | collective-permute-start | bytes 1769480 | tf_op jit(solution)/shard_map/ppermute | solution.py:37
  25.9 0.0 copy-done.1
  25.9 0.0 copy-done.2
  25.9 0.0 copy-start
  26.0 1.9 %collective-permute-start.7 = (bf16[384,384]{1,0:T(8,128)(2,1)S(1)}, bf16[384,384]{1,0:T(8,128)(2,1)S(1)}, u32[]{:S(2)}, u32[]{:S(2)}) collective-permute-start(bf16[384,384]{1,0:T(8,128)(2,1)S(1)} %pad_maximum_fusion.1.refs_2_.qg), channel_id=1, source_target_pairs={{0,4},{4,0},{8,12},{12,8},{16,20},{20,16},{24,28},{28,24},{1,5},{5... | collective-permute-start | bytes 884744 | tf_op jit(solution)/shard_map/ppermute | solution.py:37
  27.9 7.0 %collective-permute-start.8 = (bf16[384,384]{1,0:T(8,128)(2,1)S(1)}, bf16[384,384]{1,0:T(8,128)(2,1)S(1)}, u32[]{:S(2)}, u32[]{:S(2)}) collective-permute-start(bf16[384,384]{1,0:T(8,128)(2,1)S(1)} %pad_maximum_fusion.1.refs_2_.qg), channel_id=1, source_target_pairs={{4,8},{8,4},{12,16},{16,12},{20,24},{24,20},{5,9},{9,5},{13,17},{1... | collective-permute-start | bytes 884744 | tf_op jit(solution)/shard_map/ppermute | solution.py:37
  34.9 0.0 collective-permute-done.4.refs_8_
  34.9 0.0 collective-permute-done.5.refs_9_
  34.9 0.0 copy-done
  34.9 4.6 %shard_map.85 = (bf16[2,48,384]{2,1,0:T(8,128)(2,1)S(1)}, bf16[3,2,48,384]{3,2,1,0:T(8,128)(2,1)S(1)}, f32[8,192]{1,0:T(8,128)S(1)}) custom-call(s32[1,1,1,27]{3,2,1,0:T(1,128)S(1)} %copy-done, s32[1,1,1,27]{3,2,1,0:T(1,128)S(1)} %copy-done, bf16[384,384]{1,0:T(8,128)(2,1)S(1)} %pad_maximum_fusion.1.refs_2_.qg, ...), custom_call_target="tpu_custom_call" | custom-call | tf_op jit(solution)/shard_map/pallas_call | solution.py:248
  39.5 7.7 %collective-permute-start.6 = (bf16[2,48,384]{2,1,0:T(8,128)(2,1)S(1)}, bf16[2,48,384]{2,1,0:T(8,128)(2,1)S(1)}, u32[]{:S(2)}, u32[]{:S(2)}) collective-permute-start(bf16[2,48,384]{2,1,0:T(8,128)(2,1)S(1)} %get-tuple-element.22), channel_id=1, source_target_pairs={{0,2},{1,3},{2,0},{3,1},{4,6},{5,7},{6,4},{7,5},{8,10},{9,11},{10,... | collective-permute-start | bytes 221192 | tf_op jit(solution)/shard_map/ppermute | solution.py:217
  47.2 1.9 %collective-permute-start.10 = (f32[8,192]{1,0:T(8,128)S(1)}, f32[8,192]{1,0:T(8,128)S(1)}, u32[]{:S(2)}, u32[]{:S(2)}) collective-permute-start(f32[8,192]{1,0:T(8,128)S(1)} %get-tuple-element.25.st), channel_id=1, source_target_pairs={{4,8},{8,4},{12,16},{16,12},{20,24},{24,20},{5,9},{9,5},{13,17},{1... | collective-permute-start | bytes 18440 | tf_op jit(solution)/shard_map/ppermute | solution.py:37
  49.1 1.9 %collective-permute-start.9 = (f32[8,192]{1,0:T(8,128)S(1)}, f32[8,192]{1,0:T(8,128)S(1)}, u32[]{:S(2)}, u32[]{:S(2)}) collective-permute-start(f32[8,192]{1,0:T(8,128)S(1)} %get-tuple-element.25.st), channel_id=1, source_target_pairs={{0,4},{4,0},{8,12},{12,8},{16,20},{20,16},{24,28},{28,24},{1,5},{5... | collective-permute-start | bytes 18440 | tf_op jit(solution)/shard_map/ppermute | solution.py:37
  51.1 0.0 collective-permute-done.6.refs_0_
  51.1 0.0 collective-permute-done.7.qg_a
  51.1 0.0 collective-permute-done.8.qg_b
  51.1 1.7 %collective-permute-done.10.st_b = f32[8,192]{1,0:T(8,128)S(1)} collective-permute-done((f32[8,192]{1,0:T(8,128)S(1)}, f32[8,192]{1,0:T(8,128)S(1)}, u32[]{:S(2)}, u32[]{:S(2)}) %collective-permute-start.10) | collective-permute-done | bytes 6176 | tf_op jit(solution)/shard_map/ppermute | solution.py:37
  52.8 1.9 %collective-permute-done.9.st_a = f32[8,192]{1,0:T(8,128)S(1)} collective-permute-done((f32[8,192]{1,0:T(8,128)S(1)}, f32[8,192]{1,0:T(8,128)S(1)}, u32[]{:S(2)}, u32[]{:S(2)}) %collective-permute-start.9) | collective-permute-done | bytes 6176 | tf_op jit(solution)/shard_map/ppermute | solution.py:37
  54.7 4.0 %shard_map.86 = (f32[384,384]{1,0:T(8,128)S(1)}, bf16[384,384]{1,0:T(8,128)(2,1)S(1)}, bf16[384,384]{1,0:T(8,128)(2,1)S(1)}) custom-call(bf16[384,384]{1,0:T(8,128)(2,1)S(1)} %pad_maximum_fusion.refs_3_.kv, bf16[384,384]{1,0:T(8,128)(2,1)S(1)} %collective-permute-done.3.refs_7_.kv_fa, bf16[384,384]{1,0:T(8,128)(2,1)S(1)} %collective-permute-done.2.refs_6_.kv_fb, ...), custom_call_target="tpu_custom_call" | custom-call | tf_op jit(solution)/shard_map/pallas_call | solution.py:260
  58.7 1.9 %collective-permute-start.11 = (bf16[384,384]{1,0:T(8,128)(2,1)S(1)}, bf16[384,384]{1,0:T(8,128)(2,1)S(1)}, u32[]{:S(2)}, u32[]{:S(2)}) collective-permute-start(bf16[384,384]{1,0:T(8,128)(2,1)S(1)} %get-tuple-element.27), channel_id=1, source_target_pairs={{32,64},{64,32},{96,128},{128,96},{160,192},{192,160},{224,256},{2... | collective-permute-start | bytes 884744 | tf_op jit(solution)/shard_map/ppermute | solution.py:37
  60.6 1.9 %collective-permute-start.12 = (bf16[384,384]{1,0:T(8,128)(2,1)S(1)}, bf16[384,384]{1,0:T(8,128)(2,1)S(1)}, u32[]{:S(2)}, u32[]{:S(2)}) collective-permute-start(bf16[384,384]{1,0:T(8,128)(2,1)S(1)} %get-tuple-element.28), channel_id=1, source_target_pairs={{0,32},{32,0},{64,96},{96,64},{128,160},{160,128},{192,224},{224,1... | collective-permute-start | bytes 884744 | tf_op jit(solution)/shard_map/ppermute | solution.py:37
  62.5 6.3 %collective-permute-done.11.refs_1_ = bf16[384,384]{1,0:T(8,128)(2,1)S(1)} collective-permute-done((bf16[384,384]{1,0:T(8,128)(2,1)S(1)}, bf16[384,384]{1,0:T(8,128)(2,1)S(1)}, u32[]{:S(2)}, u32[]{:S(2)}) %collective-permute-start.11) | collective-permute-done | bytes 294944 | tf_op jit(solution)/shard_map/ppermute | solution.py:37
  68.8 0.0 collective-permute-done.12.refs_2_
  68.8 0.3 shard_map.87
  69.1 4.3 %collective-permute-start.14 = (bf16[4,48,384]{2,1,0:T(8,128)(2,1)S(1)}, bf16[4,48,384]{2,1,0:T(8,128)(2,1)S(1)}, u32[]{:S(2)}, u32[]{:S(2)}) collective-permute-start(bf16[4,48,384]{2,1,0:T(8,128)(2,1)S(1)} %get-tuple-element.32), channel_id=1, source_target_pairs={{0,1},{1,0},{2,3},{3,2},{4,5},{5,4},{6,7},{7,6},{8,9},{9,8},{10,11... | collective-permute-start | bytes 442376 | tf_op jit(solution)/shard_map/ppermute | solution.py:217
  73.4 2.4 %collective-permute-start.15 = (bf16[4,48,384]{2,1,0:T(8,128)(2,1)S(1)}, bf16[4,48,384]{2,1,0:T(8,128)(2,1)S(1)}, u32[]{:S(2)}, u32[]{:S(2)}) collective-permute-start(bf16[4,48,384]{2,1,0:T(8,128)(2,1)S(1)} %get-tuple-element.33), channel_id=1, source_target_pairs={{0,3},{1,2},{2,1},{3,0},{4,7},{5,6},{6,5},{7,4},{8,11},{9,10},{10,... | collective-permute-start | bytes 442376 | tf_op jit(solution)/shard_map/ppermute | solution.py:217
  75.8 5.6 %collective-permute-start.13 = (bf16[2,48,384]{2,1,0:T(8,128)(2,1)S(1)}, bf16[2,48,384]{2,1,0:T(8,128)(2,1)S(1)}, u32[]{:S(2)}, u32[]{:S(2)}) collective-permute-start(bf16[2,48,384]{2,1,0:T(8,128)(2,1)S(1)} %get-tuple-element.30), channel_id=1, source_target_pairs={{0,2},{1,3},{2,0},{3,1},{4,6},{5,7},{6,4},{7,5},{8,10},{9,11},{10,... | collective-permute-start | bytes 221192 | tf_op jit(solution)/shard_map/ppermute | solution.py:217
  81.4 5.3 %collective-permute-done.13.refs_1_ = bf16[2,48,384]{2,1,0:T(8,128)(2,1)S(1)} collective-permute-done((bf16[2,48,384]{2,1,0:T(8,128)(2,1)S(1)}, bf16[2,48,384]{2,1,0:T(8,128)(2,1)S(1)}, u32[]{:S(2)}, u32[]{:S(2)}) %collective-permute-start.13) | collective-permute-done | bytes 73760 | tf_op jit(solution)/shard_map/ppermute | solution.py:217
  86.7 0.0 collective-permute-done.14.refs_3_
  86.7 0.0 collective-permute-done.15.refs_4_
  86.7 1.0 %shard_map.88 = (bf16[24,2,1536]{2,1,0:T(2,128)(2,1)}, bf16[24,2,1536]{2,1,0:T(2,128)(2,1)}, bf16[24,2,1536]{2,1,0:T(2,128)(2,1)}, bf16[24,2,1536]{2,1,0:T(2,128)(2,1)}) custom-call(bf16[2,48,384]{2,1,0:T(8,128)(2,1)S(1)} %collective-permute-done.6.refs_0_, bf16[2,48,384]{2,1,0:T(8,128)(2,1)S(1)} %collective-permute-done.13.refs_1_, ...), custom_call_target="tpu_custom_call" | custom-call | tf_op jit(solution)/shard_map/pallas_call | solution.py:278
  (1 shorter events, 0.0 us)
Async XLA Ops:
  1.6 24.2 %copy-start.1 = (bf16[6,4,8,384]{3,2,1,0:T(8,128)(2,1)S(1)}, bf16[6,4,8,384]{3,2,1,0:T(8,128)(2,1)}, u32[]{:S(2)}) copy-start(bf16[6,4,8,384]{3,2,1,0:T(8,128)(2,1)} %param.8) | copy-start | bytes 442372
  1.7 24.2 %copy-start.2 = (bf16[6,4,8,384]{3,2,1,0:T(8,128)(2,1)S(1)}, bf16[6,4,8,384]{3,2,1,0:T(8,128)(2,1)}, u32[]{:S(2)}) copy-start(bf16[6,4,8,384]{3,2,1,0:T(8,128)(2,1)} %param.5) | copy-start | bytes 442372
  1.7 14.2 %collective-permute-start = (bf16[384,384]{1,0:T(8,128)(2,1)S(1)}, bf16[384,384]{1,0:T(8,128)(2,1)S(1)}, u32[]{:S(2)}, u32[]{:S(2)}) collective-permute-start(bf16[384,384]{1,0:T(8,128)(2,1)S(1)} %pad_maximum_fusion.refs_3_.kv), channel_id=1, source_target_pairs={{0,4},{4,0},{8,12},{12,8},{16,20},{20,16},{24,28},{28,24},{1,5},{5... | collective-permute-start | bytes 884744 | tf_op jit(solution)/shard_map/ppermute | solution.py:37
  3.7 13.4 %collective-permute-start.1 = (bf16[384,384]{1,0:T(8,128)(2,1)S(1)}, bf16[384,384]{1,0:T(8,128)(2,1)S(1)}, u32[]{:S(2)}, u32[]{:S(2)}) collective-permute-start(bf16[384,384]{1,0:T(8,128)(2,1)S(1)} %pad_maximum_fusion.refs_3_.kv), channel_id=1, source_target_pairs={{4,8},{8,4},{12,16},{16,12},{20,24},{24,20},{5,9},{9,5},{13,17},{1... | collective-permute-start | bytes 884744 | tf_op jit(solution)/shard_map/ppermute | solution.py:37
  10.4 10.2 %collective-permute-start.2 = (bf16[384,384]{1,0:T(8,128)(2,1)S(1)}, bf16[384,384]{1,0:T(8,128)(2,1)S(1)}, u32[]{:S(2)}, u32[]{:S(2)}) collective-permute-start(bf16[384,384]{1,0:T(8,128)(2,1)S(1)} %pad_maximum_fusion.refs_3_.kv), channel_id=1, source_target_pairs={{32,64},{64,32},{96,128},{128,96},{160,192},{192,160},{224,256},{2... | collective-permute-start | bytes 884744 | tf_op jit(solution)/shard_map/ppermute | solution.py:37
  13.8 6.7 %collective-permute-start.3 = (bf16[384,384]{1,0:T(8,128)(2,1)S(1)}, bf16[384,384]{1,0:T(8,128)(2,1)S(1)}, u32[]{:S(2)}, u32[]{:S(2)}) collective-permute-start(bf16[384,384]{1,0:T(8,128)(2,1)S(1)} %pad_maximum_fusion.refs_3_.kv), channel_id=1, source_target_pairs={{0,32},{32,0},{64,96},{96,64},{128,160},{160,128},{192,224},{224,1... | collective-permute-start | bytes 884744 | tf_op jit(solution)/shard_map/ppermute | solution.py:37
  20.5 14.3 %collective-permute-start.4 = (bf16[768,384]{1,0:T(8,128)(2,1)S(1)}, bf16[768,384]{1,0:T(8,128)(2,1)S(1)}, u32[]{:S(2)}, u32[]{:S(2)}) collective-permute-start(bf16[768,384]{1,0:T(8,128)(2,1)S(1)} %shard_map.84), channel_id=1, source_target_pairs={{32,64},{64,32},{96,128},{128,96},{160,192},{192,160},{224,256},{2... | collective-permute-start | bytes 1769480 | tf_op jit(solution)/shard_map/ppermute | solution.py:37
  24.0 10.9 %collective-permute-start.5 = (bf16[768,384]{1,0:T(8,128)(2,1)S(1)}, bf16[768,384]{1,0:T(8,128)(2,1)S(1)}, u32[]{:S(2)}, u32[]{:S(2)}) collective-permute-start(bf16[768,384]{1,0:T(8,128)(2,1)S(1)} %shard_map.84), channel_id=1, source_target_pairs={{0,32},{32,0},{64,96},{96,64},{128,160},{160,128},{192,224},{224,1... | collective-permute-start | bytes 1769480 | tf_op jit(solution)/shard_map/ppermute | solution.py:37
  25.9 9.0 %copy-start = (s32[1,1,1,27]{3,2,1,0:T(1,128)S(1)}, s32[1,1,1,27]{3,2,1,0:T(1,128)}, u32[]{:S(2)}) copy-start(s32[1,1,1,27]{3,2,1,0:T(1,128)} %refs_1_.1) | copy-start | bytes 328
  26.0 25.1 %collective-permute-start.7 = (bf16[384,384]{1,0:T(8,128)(2,1)S(1)}, bf16[384,384]{1,0:T(8,128)(2,1)S(1)}, u32[]{:S(2)}, u32[]{:S(2)}) collective-permute-start(bf16[384,384]{1,0:T(8,128)(2,1)S(1)} %pad_maximum_fusion.1.refs_2_.qg), channel_id=1, source_target_pairs={{0,4},{4,0},{8,12},{12,8},{16,20},{20,16},{24,28},{28,24},{1,5},{5... | collective-permute-start | bytes 884744 | tf_op jit(solution)/shard_map/ppermute | solution.py:37
  27.9 23.2 %collective-permute-start.8 = (bf16[384,384]{1,0:T(8,128)(2,1)S(1)}, bf16[384,384]{1,0:T(8,128)(2,1)S(1)}, u32[]{:S(2)}, u32[]{:S(2)}) collective-permute-start(bf16[384,384]{1,0:T(8,128)(2,1)S(1)} %pad_maximum_fusion.1.refs_2_.qg), channel_id=1, source_target_pairs={{4,8},{8,4},{12,16},{16,12},{20,24},{24,20},{5,9},{9,5},{13,17},{1... | collective-permute-start | bytes 884744 | tf_op jit(solution)/shard_map/ppermute | solution.py:37
  39.5 11.6 %collective-permute-start.6 = (bf16[2,48,384]{2,1,0:T(8,128)(2,1)S(1)}, bf16[2,48,384]{2,1,0:T(8,128)(2,1)S(1)}, u32[]{:S(2)}, u32[]{:S(2)}) collective-permute-start(bf16[2,48,384]{2,1,0:T(8,128)(2,1)S(1)} %get-tuple-element.22), channel_id=1, source_target_pairs={{0,2},{1,3},{2,0},{3,1},{4,6},{5,7},{6,4},{7,5},{8,10},{9,11},{10,... | collective-permute-start | bytes 221192 | tf_op jit(solution)/shard_map/ppermute | solution.py:217
  47.2 5.5 %collective-permute-start.10 = (f32[8,192]{1,0:T(8,128)S(1)}, f32[8,192]{1,0:T(8,128)S(1)}, u32[]{:S(2)}, u32[]{:S(2)}) collective-permute-start(f32[8,192]{1,0:T(8,128)S(1)} %get-tuple-element.25.st), channel_id=1, source_target_pairs={{4,8},{8,4},{12,16},{16,12},{20,24},{24,20},{5,9},{9,5},{13,17},{1... | collective-permute-start | bytes 18440 | tf_op jit(solution)/shard_map/ppermute | solution.py:37
  49.1 5.5 %collective-permute-start.9 = (f32[8,192]{1,0:T(8,128)S(1)}, f32[8,192]{1,0:T(8,128)S(1)}, u32[]{:S(2)}, u32[]{:S(2)}) collective-permute-start(f32[8,192]{1,0:T(8,128)S(1)} %get-tuple-element.25.st), channel_id=1, source_target_pairs={{0,4},{4,0},{8,12},{12,8},{16,20},{20,16},{24,28},{28,24},{1,5},{5... | collective-permute-start | bytes 18440 | tf_op jit(solution)/shard_map/ppermute | solution.py:37
  58.7 10.2 %collective-permute-start.11 = (bf16[384,384]{1,0:T(8,128)(2,1)S(1)}, bf16[384,384]{1,0:T(8,128)(2,1)S(1)}, u32[]{:S(2)}, u32[]{:S(2)}) collective-permute-start(bf16[384,384]{1,0:T(8,128)(2,1)S(1)} %get-tuple-element.27), channel_id=1, source_target_pairs={{32,64},{64,32},{96,128},{128,96},{160,192},{192,160},{224,256},{2... | collective-permute-start | bytes 884744 | tf_op jit(solution)/shard_map/ppermute | solution.py:37
  60.6 8.2 %collective-permute-start.12 = (bf16[384,384]{1,0:T(8,128)(2,1)S(1)}, bf16[384,384]{1,0:T(8,128)(2,1)S(1)}, u32[]{:S(2)}, u32[]{:S(2)}) collective-permute-start(bf16[384,384]{1,0:T(8,128)(2,1)S(1)} %get-tuple-element.28), channel_id=1, source_target_pairs={{0,32},{32,0},{64,96},{96,64},{128,160},{160,128},{192,224},{224,1... | collective-permute-start | bytes 884744 | tf_op jit(solution)/shard_map/ppermute | solution.py:37
  69.1 17.6 %collective-permute-start.14 = (bf16[4,48,384]{2,1,0:T(8,128)(2,1)S(1)}, bf16[4,48,384]{2,1,0:T(8,128)(2,1)S(1)}, u32[]{:S(2)}, u32[]{:S(2)}) collective-permute-start(bf16[4,48,384]{2,1,0:T(8,128)(2,1)S(1)} %get-tuple-element.32), channel_id=1, source_target_pairs={{0,1},{1,0},{2,3},{3,2},{4,5},{5,4},{6,7},{7,6},{8,9},{9,8},{10,11... | collective-permute-start | bytes 442376 | tf_op jit(solution)/shard_map/ppermute | solution.py:217
  73.4 13.3 %collective-permute-start.15 = (bf16[4,48,384]{2,1,0:T(8,128)(2,1)S(1)}, bf16[4,48,384]{2,1,0:T(8,128)(2,1)S(1)}, u32[]{:S(2)}, u32[]{:S(2)}) collective-permute-start(bf16[4,48,384]{2,1,0:T(8,128)(2,1)S(1)} %get-tuple-element.33), channel_id=1, source_target_pairs={{0,3},{1,2},{2,1},{3,0},{4,7},{5,6},{6,5},{7,4},{8,11},{9,10},{10,... | collective-permute-start | bytes 442376 | tf_op jit(solution)/shard_map/ppermute | solution.py:217
  75.8 10.9 %collective-permute-start.13 = (bf16[2,48,384]{2,1,0:T(8,128)(2,1)S(1)}, bf16[2,48,384]{2,1,0:T(8,128)(2,1)S(1)}, u32[]{:S(2)}, u32[]{:S(2)}) collective-permute-start(bf16[2,48,384]{2,1,0:T(8,128)(2,1)S(1)} %get-tuple-element.30), channel_id=1, source_target_pairs={{0,2},{1,3},{2,0},{3,1},{4,6},{5,7},{6,4},{7,5},{8,10},{9,11},{10,... | collective-permute-start | bytes 221192 | tf_op jit(solution)/shard_map/ppermute | solution.py:217

commit v4 on v3

--- a/solution.py
+++ b/solution.py
@@ -101,9 +101,9 @@
 
 
 def query_kernel(
-    heads, pairs_s, pairs_v, own_qg, kv, kv_a, kv_b, kv_fb, kv_fa, corner_fb, corner_fa, *refs
+    pairs_s, pairs_v, own_qg, kv, kv_a, kv_b, kv_fb, kv_fa, corner_fb, corner_fa, *refs
 ):
-    far_ref, near_ref, stat_ref, key_ref, value_ref = refs
+    attended_ref, stat_ref, column_ref, bias_ref, key_ref, value_ref = refs
     frame, row = lax.axis_index("frame"), lax.axis_index("row")
     frames, rows = lax.axis_size("frame"), lax.axis_size("row")
     tiles = [(kv, 0), (kv_a, 0), (kv_b, 0)]
@@ -121,50 +121,68 @@
     stat_lane = lax.broadcasted_iota(jnp.int32, (TILE, 128), 1)
     stats = jnp.zeros((TILE, 128), jnp.float32)
     count = own_qg.shape[1] // HEAD_DIM
-    attended_parts, grad_parts = [], []
     for h in range(count):
         feat = slice(h * HEAD_DIM, (h + 1) * HEAD_DIM)
         query, grad = own_qg[0:TILE, feat], own_qg[TILE : 2 * TILE, feat]
-        key, value = key_ref[:, feat], value_ref[:, feat]
         scores = lax.dot_general(
-            query, key, (((1,), (1,)), ((), ())), preferred_element_type=jnp.float32
+            query, key_ref[:, feat], (((1,), (1,)), ((), ())), preferred_element_type=jnp.float32
         )
         scores = scores * SCALE2 + bias
         top = jnp.max(scores, axis=1, keepdims=True)
         weights = jnp.exp2(scores - top)
         total = jnp.sum(weights, axis=1, keepdims=True)
-        weights = weights * (1.0 / total)
-        rounded = weights.astype(jnp.bfloat16)
-        attended = jnp.dot(rounded, value, preferred_element_type=jnp.float32).astype(jnp.bfloat16)
+        rounded = (weights * (1.0 / total)).astype(jnp.bfloat16)
+        attended = jnp.dot(rounded, value_ref[:, feat], preferred_element_type=jnp.float32)
+        attended = attended.astype(jnp.bfloat16)
         spread = jnp.sum(
             grad.astype(jnp.float32) * attended.astype(jnp.float32), axis=1, keepdims=True
         )
+        attended_ref[:, feat] = attended
+        stats = jnp.where(stat_lane == h, top + jnp.log2(total), stats)
+        stats = jnp.where(stat_lane == count + h, spread, stats)
+    bias_ref[...] = bias
+    column_ref[...] = stats
+    stat_ref[...] = stats.T[0:8, :]
+    stat_ref[7:8, 0:27] = pairs_v[0, 0].astype(jnp.float32)
+
+
+def query_grad_kernel(heads, own_qg, key_ref, value_ref, attended_ref, column_ref, bias_ref, *refs):
+    far_ref, near_ref = refs
+    bias = bias_ref[...]
+    count = own_qg.shape[1] // HEAD_DIM
+    grad_parts = []
+    for h in range(count):
+        feat = slice(h * HEAD_DIM, (h + 1) * HEAD_DIM)
+        query, grad = own_qg[0:TILE, feat], own_qg[TILE : 2 * TILE, feat]
+        key = key_ref[:, feat]
+        scores = lax.dot_general(
+            query, key, (((1,), (1,)), ((), ())), preferred_element_type=jnp.float32
+        )
+        weights = jnp.exp2(scores * SCALE2 + bias - column_ref[:, h : h + 1])
         pushes = lax.dot_general(
-            grad, value, (((1,), (1,)), ((), ())), preferred_element_type=jnp.float32
+            grad, value_ref[:, feat], (((1,), (1,)), ((), ())), preferred_element_type=jnp.float32
         )
+        spread = column_ref[:, count + h : count + h + 1]
         slopes = (weights * (pushes - spread)).astype(jnp.bfloat16)
         query_grad = SCALE * jnp.dot(slopes, key, preferred_element_type=jnp.float32)
-        attended_parts.append(attended)
         grad_parts.append(query_grad.astype(jnp.bfloat16))
-        stats = jnp.where(stat_lane == h, top + jnp.log2(total), stats)
-        stats = jnp.where(stat_lane == count + h, spread, stats)
-    stat_ref[...] = stats.T[0:8, :]
-    stat_ref[7:8, 0:27] = pairs_v[0, 0].astype(jnp.float32)
-    blocks = column_blocks(attended_parts, grad_parts, heads)
+    blocks = column_blocks([attended_ref[...]], grad_parts, heads)
     for i in range(2):
         far_ref[i] = blocks[heads // 2][i]
         for at, k in enumerate(near_heads(heads)):
             near_ref[at, i] = blocks[k][i]
 
 
-def key_kernel(kv, kv_fa, kv_fb, qg, qg_a, qg_b, st, st_a, st_b, *refs):
-    own_ref, term_a_ref, term_b_ref, query_ref, grad_ref, stat_ref = refs
-    count = kv.shape[1] // HEAD_DIM
+def key_kernel(sides, *refs):
+    kvs, refs = refs[: len(sides)], refs[len(sides) :]
+    (qg, qg_a, qg_b, st, st_a, st_b), refs = refs[:6], refs[6:]
+    outs, (query_ref, grad_ref, stat_ref) = refs[: len(sides)], refs[len(sides) :]
+    count = qg.shape[1] // HEAD_DIM
     frame, frames = lax.axis_index("frame"), lax.axis_size("frame")
     gather_near([(qg, 0), (qg_a, 0), (qg_b, 0)], query_ref, grad_ref)
     lane = lax.broadcasted_iota(jnp.int32, (1, TILE), 1)
     level = lax.broadcasted_iota(jnp.int32, (8, TILE), 0)
-    frame_steps = slot_steps("frame")
+    frame_steps = [slot_steps("frame")[side] for side in sides]
     for slot, (ref, b) in enumerate(zip((st, st_a, st_b), slot_steps("row"))):
         block = ref[...]
         for i, a in enumerate(frame_steps):
@@ -177,9 +195,7 @@
     for h in range(count):
         feat = slice(h * HEAD_DIM, (h + 1) * HEAD_DIM)
         query, grad = query_ref[:, feat], grad_ref[:, feat]
-        for i, (kv_ref, out_ref) in enumerate(
-            ((kv, own_ref), (kv_fa, term_a_ref), (kv_fb, term_b_ref))
-        ):
+        for i, (kv_ref, out_ref) in enumerate(zip(kvs, outs)):
             key, value = kv_ref[0:TILE, feat], kv_ref[TILE : 2 * TILE, feat]
             scores = lax.dot_general(
                 key, query, (((1,), (1,)), ((), ())), preferred_element_type=jnp.float32
@@ -244,34 +260,50 @@
     span = TILE // heads
     pair, four = (jax.ShapeDtypeStruct((n, span, feats), bf16) for n in (2, 4))
     near_shape = jax.ShapeDtypeStruct((heads - 1, 2, span, feats), bf16)
-    near = pltpu.VMEM((WIDE, feats), bf16)
-    far_q, near_q, stat = call(
-        lambda *refs: query_kernel(heads, *refs),
-        (pair, near_shape, jax.ShapeDtypeStruct((8, TILE), f32)),
+    wide = jax.ShapeDtypeStruct((WIDE, feats), bf16)
+    attended, stat, column, bias, key_near, value_near = call(
+        query_kernel,
+        (
+            jax.ShapeDtypeStruct((TILE, feats), bf16),
+            jax.ShapeDtypeStruct((8, TILE), f32),
+            jax.ShapeDtypeStruct((TILE, 128), f32),
+            jax.ShapeDtypeStruct((1, WIDE), f32),
+            wide,
+            wide,
+        ),
         [SMEM] + [VMEM] * 9,
-        (VMEM,) * 3,
-        [near, near],
+        (VMEM,) * 6,
     )(tile_pairs, tile_pairs, qg, kv, kv_a, kv_b, kv_fb, kv_fa, corner_fb, corner_fa)
     st_a, st_b = pair_swap(stat, "row", 0), pair_swap(stat, "row", 1)
+
+    def terms(sides, kinds, *kvs):
+        row_near = pltpu.VMEM((3 * TILE, feats), bf16)
+        return call(
+            lambda *refs: key_kernel(sides, *refs),
+            [jax.ShapeDtypeStruct((2 * TILE, feats), kind) for kind in kinds],
+            [VMEM] * (len(sides) + 6),
+            [VMEM] * len(sides),
+            [row_near, row_near, pltpu.VMEM((len(sides), 8, 3 * TILE), f32)],
+        )(*kvs, qg, qg_a, qg_b, stat, st_a, st_b)
+
+    term_b, term_a = terms((2, 1), (bf16, bf16), kv_fb, kv_fa)
+    got_b, got_a = pair_swap(term_b, "frame", 1), pair_swap(term_a, "frame", 0)
+    (own,) = terms((0,), (f32,), after(kv, got_a))
+    far_q, near_q = call(
+        lambda *refs: query_grad_kernel(heads, *refs),
+        (pair, near_shape),
+        [VMEM] * 6,
+        (VMEM, VMEM),
+    )(after(qg, got_a), key_near, value_near, attended, column, bias)
     got_far_q = head_swap(far_q, heads // 2)
 
-    row_near = pltpu.VMEM((3 * TILE, feats), bf16)
-    term = jax.ShapeDtypeStruct((2 * TILE, feats), bf16)
-    own, term_a, term_b = call(
-        key_kernel,
-        (jax.ShapeDtypeStruct((2 * TILE, feats), f32), term, term),
-        [VMEM] * 9,
-        (VMEM,) * 3,
-        [row_near, row_near, pltpu.VMEM((3, 8, 3 * TILE), f32)],
-    )(after(kv, got_far_q), kv_fa, kv_fb, qg, qg_a, qg_b, stat, st_a, st_b)
-    got_b, got_a = pair_swap(term_b, "frame", 1), pair_swap(term_a, "frame", 0)
     far_k, *near_k = call(
         lambda *refs: fold_kernel(heads, *refs),
         [pair] + [four] * (heads - 1),
         [VMEM] * 4,
         [VMEM] * heads,
     )(own, got_b, got_a, near_q)
-    got_far_k = head_swap(far_k, heads // 2)
+    got_far_k = head_swap(after(far_k, got_far_q), heads // 2)
     got_near = [head_swap(sent, k) for k, sent in zip(near_heads(heads), near_k)]
 
     out = jax.ShapeDtypeStruct((frames_dev * rows_dev, columns // heads, heads * feats), bf16)

time: 88.6 us -> 85 us (0.959)
  the two profiles are of different devices: /device:TPU:72 before, /device:TPU:120 now
where the time goes in v4:
time: 85 us; the launch traced here: 84.4 us
  starting transfers between devices  59.4 us (70%)
  waiting for transfers between devices  11.6 us (14%)
  Pallas kernels  11.3 us (13%)
  other arithmetic  1.09 us (1%)
  between operations  0.93 us (1%)
    ppermute x12, starting transfers between devices, pair_swap(): return lax.ppermute(value, axis, pairs)  42.4 us
    ppermute x4, starting transfers between devices, head_swap(): lax.ppermute(value, 'head', [(i, i ^ k) for i in range(count)])  16.9 us
    ppermute x4, waiting for transfers between devices, head_swap(): lax.ppermute(value, 'head', [(i, i ^ k) for i in range(count)])  6.22 us
    ppermute x12, waiting for transfers between devices, pair_swap(): return lax.ppermute(value, axis, pairs)  5.42 us
    pallas_call x2, Pallas kernels, terms(): call(lambda *refs: key_kernel(sides, *refs), [jax.ShapeDtypeStruct((2 * T...  4.27 us
    pallas_call x1, Pallas kernels, body(): call(query_kernel, (jax.ShapeDtypeStruct((TILE, feats), bf16), jax.ShapeD...  3.44 us
    pallas_call x1, Pallas kernels, body(): call(lambda *refs: query_grad_kernel(heads, *refs), (pair, near_shape), [...  2.28 us
  transfers between devices with their start and end apart: 16, of which 5 were waited for; matrix products, arithmetic and copies ran while one was open for 0% of the time, Pallas kernels for 9%

profile of v4, /device:TPU:120, one launch (start us, length us, event | category | flops | bytes accessed | tf_op | source)
XLA Modules:
  0.0 84.4 jit_solution(10851753528626239544)
XLA Ops:
  0.6 0.0 copy-start.2
  0.6 0.0 copy-start.1
  0.7 0.0 copy-start
  0.7 1.1 %pad_maximum_fusion.kv.refs_0_ = bf16[384,384]{1,0:T(8,128)(2,1)S(1)} fusion(bf16[192,384]{1,0:T(8,128)(2,1)} %bitcast.8, bf16[192,384]{1,0:T(8,128)(2,1)} %bitcast.9), kind=kLoop, calls=%fused_computation | loop fusion | flops 589824 | bytes 589824 | tf_op jit(solution)/shard_map/max | solution.py:239
  1.7 1.9 %collective-permute-start.4 = (bf16[384,384]{1,0:T(8,128)(2,1)S(1)}, bf16[384,384]{1,0:T(8,128)(2,1)S(1)}, u32[]{:S(2)}, u32[]{:S(2)}) collective-permute-start(bf16[384,384]{1,0:T(8,128)(2,1)S(1)} %pad_maximum_fusion.kv.refs_0_), channel_id=1, source_target_pairs={{0,4},{4,0},{8,12},{12,8},{16,20},{20,16},{24,28},{28,24},{1,5},{5... | collective-permute-start | bytes 884744 | tf_op jit(solution)/shard_map/ppermute | solution.py:37
  3.6 6.6 %collective-permute-start.5 = (bf16[384,384]{1,0:T(8,128)(2,1)S(1)}, bf16[384,384]{1,0:T(8,128)(2,1)S(1)}, u32[]{:S(2)}, u32[]{:S(2)}) collective-permute-start(bf16[384,384]{1,0:T(8,128)(2,1)S(1)} %pad_maximum_fusion.kv.refs_0_), channel_id=1, source_target_pairs={{4,8},{8,4},{12,16},{16,12},{20,24},{24,20},{5,9},{9,5},{13,17},{1... | collective-permute-start | bytes 884744 | tf_op jit(solution)/shard_map/ppermute | solution.py:37
  10.3 4.3 %collective-permute-start = (bf16[384,384]{1,0:T(8,128)(2,1)S(1)}, bf16[384,384]{1,0:T(8,128)(2,1)S(1)}, u32[]{:S(2)}, u32[]{:S(2)}) collective-permute-start(bf16[384,384]{1,0:T(8,128)(2,1)S(1)} %pad_maximum_fusion.kv.refs_0_), channel_id=1, source_target_pairs={{32,64},{64,32},{96,128},{128,96},{160,192},{192,160},{224,256},{2... | collective-permute-start | bytes 884744 | tf_op jit(solution)/shard_map/ppermute | solution.py:37
  14.6 1.9 %collective-permute-start.1 = (bf16[384,384]{1,0:T(8,128)(2,1)S(1)}, bf16[384,384]{1,0:T(8,128)(2,1)S(1)}, u32[]{:S(2)}, u32[]{:S(2)}) collective-permute-start(bf16[384,384]{1,0:T(8,128)(2,1)S(1)} %pad_maximum_fusion.kv.refs_0_), channel_id=1, source_target_pairs={{0,32},{32,0},{64,96},{96,64},{128,160},{160,128},{192,224},{224,1... | collective-permute-start | bytes 884744 | tf_op jit(solution)/shard_map/ppermute | solution.py:37
  16.6 0.0 collective-permute-done.4.a_ref.kv_a
  16.6 0.4 collective-permute-done.5.b_ref.kv_b
  17.0 0.1 shard_map.84
  17.1 3.4 %collective-permute-done.kv_fb.refs_0_ = bf16[384,384]{1,0:T(8,128)(2,1)S(1)} collective-permute-done((bf16[384,384]{1,0:T(8,128)(2,1)S(1)}, bf16[384,384]{1,0:T(8,128)(2,1)S(1)}, u32[]{:S(2)}, u32[]{:S(2)}) %collective-permute-start) | collective-permute-done | bytes 294944 | tf_op jit(solution)/shard_map/ppermute | solution.py:37
  20.4 0.0 collective-permute-done.1.kv_fa.refs_1_
  20.5 4.3 %collective-permute-start.6 = (bf16[768,384]{1,0:T(8,128)(2,1)S(1)}, bf16[768,384]{1,0:T(8,128)(2,1)S(1)}, u32[]{:S(2)}, u32[]{:S(2)}) collective-permute-start(bf16[768,384]{1,0:T(8,128)(2,1)S(1)} %shard_map.84), channel_id=1, source_target_pairs={{32,64},{64,32},{96,128},{128,96},{160,192},{192,160},{224,256},{2... | collective-permute-start | bytes 1769480 | tf_op jit(solution)/shard_map/ppermute | solution.py:37
  24.8 1.9 %collective-permute-start.7 = (bf16[768,384]{1,0:T(8,128)(2,1)S(1)}, bf16[768,384]{1,0:T(8,128)(2,1)S(1)}, u32[]{:S(2)}, u32[]{:S(2)}) collective-permute-start(bf16[768,384]{1,0:T(8,128)(2,1)S(1)} %shard_map.84), channel_id=1, source_target_pairs={{0,32},{32,0},{64,96},{96,64},{128,160},{160,128},{192,224},{224,1... | collective-permute-start | bytes 1769480 | tf_op jit(solution)/shard_map/ppermute | solution.py:37
  26.7 0.0 copy-done.2
  26.7 0.0 copy-done.1
  26.8 1.9 %collective-permute-start.2 = (bf16[384,384]{1,0:T(8,128)(2,1)S(1)}, bf16[384,384]{1,0:T(8,128)(2,1)S(1)}, u32[]{:S(2)}, u32[]{:S(2)}) collective-permute-start(bf16[384,384]{1,0:T(8,128)(2,1)S(1)} %pad_maximum_fusion.1.own_qg.refs_2_.refs_0_.refs_1_), channel_id=1, source_target_pairs={{0,4},{4,0},{8,12},{12,8},{16,20},{20,16},{24,28},{28,24},{1,5},{5... | collective-permute-start | bytes 884744 | tf_op jit(solution)/shard_map/ppermute | solution.py:37
  28.7 7.0 %collective-permute-start.3 = (bf16[384,384]{1,0:T(8,128)(2,1)S(1)}, bf16[384,384]{1,0:T(8,128)(2,1)S(1)}, u32[]{:S(2)}, u32[]{:S(2)}) collective-permute-start(bf16[384,384]{1,0:T(8,128)(2,1)S(1)} %pad_maximum_fusion.1.own_qg.refs_2_.refs_0_.refs_1_), channel_id=1, source_target_pairs={{4,8},{8,4},{12,16},{16,12},{20,24},{24,20},{5,9},{9,5},{13,17},{1... | collective-permute-start | bytes 884744 | tf_op jit(solution)/shard_map/ppermute | solution.py:37
  35.7 0.0 collective-permute-done.6.corner_fb
  35.7 0.0 collective-permute-done.7.corner_fa
  35.7 0.0 copy-done
  35.7 3.4 %shard_map.85 = (bf16[192,384]{1,0:T(8,128)(2,1)S(1)}, f32[8,192]{1,0:T(8,128)S(1)}, f32[192,128]{1,0:T(8,128)S(1)}, f32[1,1728]{1,0:T(1,128)S(1)}, bf16[1728,38...) custom-call(s32[1,1,1,27]{3,2,1,0:T(1,128)S(1)} %copy-done, s32[1,1,1,27]{3,2,1,0:T(1,128)S(1)} %copy-done, ...), custom_call_target="tpu_custom_call" | custom-call | tf_op jit(solution)/shard_map/pallas_call | solution.py:264
  39.1 1.9 %collective-permute-start.8 = (f32[8,192]{1,0:T(8,128)S(1)}, f32[8,192]{1,0:T(8,128)S(1)}, u32[]{:S(2)}, u32[]{:S(2)}) collective-permute-start(f32[8,192]{1,0:T(8,128)S(1)} %get-tuple-element.29.refs_5_.refs_4_), channel_id=1, source_target_pairs={{0,4},{4,0},{8,12},{12,8},{16,20},{20,16},{24,28},{28,24},{1,5},{5... | collective-permute-start | bytes 18440 | tf_op jit(solution)/shard_map/ppermute | solution.py:37
  41.1 5.0 %collective-permute-start.9 = (f32[8,192]{1,0:T(8,128)S(1)}, f32[8,192]{1,0:T(8,128)S(1)}, u32[]{:S(2)}, u32[]{:S(2)}) collective-permute-start(f32[8,192]{1,0:T(8,128)S(1)} %get-tuple-element.29.refs_5_.refs_4_), channel_id=1, source_target_pairs={{4,8},{8,4},{12,16},{16,12},{20,24},{24,20},{5,9},{9,5},{13,17},{1... | collective-permute-start | bytes 18440 | tf_op jit(solution)/shard_map/ppermute | solution.py:37
  46.1 0.0 collective-permute-done.2.refs_3_.refs_2_
  46.1 0.0 collective-permute-done.3.refs_4_.refs_3_
  46.1 0.0 collective-permute-done.8.refs_6_.refs_5_
  46.1 1.6 %collective-permute-done.9.refs_7_.refs_6_ = f32[8,192]{1,0:T(8,128)S(1)} collective-permute-done((f32[8,192]{1,0:T(8,128)S(1)}, f32[8,192]{1,0:T(8,128)S(1)}, u32[]{:S(2)}, u32[]{:S(2)}) %collective-permute-start.9) | collective-permute-done | bytes 6176 | tf_op jit(solution)/shard_map/ppermute | solution.py:37
  47.7 2.7 %shard_map.86 = (bf16[384,384]{1,0:T(8,128)(2,1)S(1)}, bf16[384,384]{1,0:T(8,128)(2,1)S(1)}) custom-call(bf16[384,384]{1,0:T(8,128)(2,1)S(1)} %collective-permute-done.kv_fb.refs_0_, bf16[384,384]{1,0:T(8,128)(2,1)S(1)} %collective-permute-done.1.kv_fa.refs_1_, bf16[384,384]{1,0:T(8,128)(2,1)S(1)} %pad_maximum_fusion.1.own_qg.refs_2_.refs_0_.refs_1_, ...), custom_call_target="tpu_custom_call" | custom-call | tf_op jit(solution)/shard_map/pallas_call | solution.py:281
  50.4 1.9 %collective-permute-start.10 = (bf16[384,384]{1,0:T(8,128)(2,1)S(1)}, bf16[384,384]{1,0:T(8,128)(2,1)S(1)}, u32[]{:S(2)}, u32[]{:S(2)}) collective-permute-start(bf16[384,384]{1,0:T(8,128)(2,1)S(1)} %get-tuple-element.30), channel_id=1, source_target_pairs={{0,32},{32,0},{64,96},{96,64},{128,160},{160,128},{192,224},{224,1... | collective-permute-start | bytes 884744 | tf_op jit(solution)/shard_map/ppermute | solution.py:37
  52.4 3.7 %collective-permute-start.12 = (bf16[384,384]{1,0:T(8,128)(2,1)S(1)}, bf16[384,384]{1,0:T(8,128)(2,1)S(1)}, u32[]{:S(2)}, u32[]{:S(2)}) collective-permute-start(bf16[384,384]{1,0:T(8,128)(2,1)S(1)} %get-tuple-element.39), channel_id=1, source_target_pairs={{32,64},{64,32},{96,128},{128,96},{160,192},{192,160},{224,256},{2... | collective-permute-start | bytes 884744 | tf_op jit(solution)/shard_map/ppermute | solution.py:37
  56.0 0.0 collective-permute-done.10.refs_2_
  56.0 2.3 %shard_map.87 = (bf16[2,48,384]{2,1,0:T(8,128)(2,1)S(1)}, bf16[3,2,48,384]{3,2,1,0:T(8,128)(2,1)S(1)}) custom-call(bf16[384,384]{1,0:T(8,128)(2,1)S(1)} %pad_maximum_fusion.1.own_qg.refs_2_.refs_0_.refs_1_, bf16[1728,384]{1,0:T(8,128)(2,1)S(1)} %get-tuple-element.32.refs_1_, bf16[1728,384]{1,0:T(8,128)(2,1)S(1)} %get-tuple-element.33.refs_2_, ...), custom_call_target="tpu_custom_call" | custom-call | tf_op jit(solution)/shard_map/pallas_call | solution.py:292
  58.3 4.7 %collective-permute-start.11 = (bf16[2,48,384]{2,1,0:T(8,128)(2,1)S(1)}, bf16[2,48,384]{2,1,0:T(8,128)(2,1)S(1)}, u32[]{:S(2)}, u32[]{:S(2)}) collective-permute-start(bf16[2,48,384]{2,1,0:T(8,128)(2,1)S(1)} %get-tuple-element.37), channel_id=1, source_target_pairs={{0,2},{1,3},{2,0},{3,1},{4,6},{5,7},{6,4},{7,5},{8,10},{9,11},{10,... | collective-permute-start | bytes 221192 | tf_op jit(solution)/shard_map/ppermute | solution.py:233
  63.1 1.5 %shard_map.88.refs_0_ = f32[384,384]{1,0:T(8,128)S(1)} custom-call(bf16[384,384]{1,0:T(8,128)(2,1)S(1)} %pad_maximum_fusion.kv.refs_0_, bf16[384,384]{1,0:T(8,128)(2,1)S(1)} %pad_maximum_fusion.1.own_qg.refs_2_.refs_0_.refs_1_, bf16[384,384]{1,0:T(8,128)(2,1)S(1)} %collective-permute-done.2.refs_3_.refs_2_, ...), custom_call_target="tpu_custom_call" | custom-call | tf_op jit(solution)/shard_map/pallas_call | solution.py:281
  64.6 0.0 collective-permute-done.12.refs_1_
  64.6 0.3 shard_map.89
  64.9 2.3 %collective-permute-start.14 = (bf16[4,48,384]{2,1,0:T(8,128)(2,1)S(1)}, bf16[4,48,384]{2,1,0:T(8,128)(2,1)S(1)}, u32[]{:S(2)}, u32[]{:S(2)}) collective-permute-start(bf16[4,48,384]{2,1,0:T(8,128)(2,1)S(1)} %get-tuple-element.44), channel_id=1, source_target_pairs={{0,1},{1,0},{2,3},{3,2},{4,5},{5,4},{6,7},{7,6},{8,9},{9,8},{10,11... | collective-permute-start | bytes 442376 | tf_op jit(solution)/shard_map/ppermute | solution.py:233
  67.2 5.3 %collective-permute-start.15 = (bf16[4,48,384]{2,1,0:T(8,128)(2,1)S(1)}, bf16[4,48,384]{2,1,0:T(8,128)(2,1)S(1)}, u32[]{:S(2)}, u32[]{:S(2)}) collective-permute-start(bf16[4,48,384]{2,1,0:T(8,128)(2,1)S(1)} %get-tuple-element.45), channel_id=1, source_target_pairs={{0,3},{1,2},{2,1},{3,0},{4,7},{5,6},{6,5},{7,4},{8,11},{9,10},{10,... | collective-permute-start | bytes 442376 | tf_op jit(solution)/shard_map/ppermute | solution.py:233
  72.4 0.0 collective-permute-done.11.refs_0_
  72.5 4.7 %collective-permute-start.13 = (bf16[2,48,384]{2,1,0:T(8,128)(2,1)S(1)}, bf16[2,48,384]{2,1,0:T(8,128)(2,1)S(1)}, u32[]{:S(2)}, u32[]{:S(2)}) collective-permute-start(bf16[2,48,384]{2,1,0:T(8,128)(2,1)S(1)} %get-tuple-element.42), channel_id=1, source_target_pairs={{0,2},{1,3},{2,0},{3,1},{4,6},{5,7},{6,4},{7,5},{8,10},{9,11},{10,... | collective-permute-start | bytes 221192 | tf_op jit(solution)/shard_map/ppermute | solution.py:233
  77.2 0.0 collective-permute-done.14.refs_3_
  77.2 2.3 %collective-permute-done.15.refs_4_ = bf16[4,48,384]{2,1,0:T(8,128)(2,1)S(1)} collective-permute-done((bf16[4,48,384]{2,1,0:T(8,128)(2,1)S(1)}, bf16[4,48,384]{2,1,0:T(8,128)(2,1)S(1)}, u32[]{:S(2)}, u32[]{:S(2)}) %collective-permute-start.15) | collective-permute-done | bytes 147488 | tf_op jit(solution)/shard_map/ppermute | solution.py:233
  79.5 3.9 %collective-permute-done.13.refs_1_ = bf16[2,48,384]{2,1,0:T(8,128)(2,1)S(1)} collective-permute-done((bf16[2,48,384]{2,1,0:T(8,128)(2,1)S(1)}, bf16[2,48,384]{2,1,0:T(8,128)(2,1)S(1)}, u32[]{:S(2)}, u32[]{:S(2)}) %collective-permute-start.13) | collective-permute-done | bytes 73760 | tf_op jit(solution)/shard_map/ppermute | solution.py:233
  83.4 1.0 %shard_map.90 = (bf16[24,2,1536]{2,1,0:T(2,128)(2,1)}, bf16[24,2,1536]{2,1,0:T(2,128)(2,1)}, bf16[24,2,1536]{2,1,0:T(2,128)(2,1)}, bf16[24,2,1536]{2,1,0:T(2,128)(2,1)}) custom-call(bf16[2,48,384]{2,1,0:T(8,128)(2,1)S(1)} %collective-permute-done.11.refs_0_, bf16[2,48,384]{2,1,0:T(8,128)(2,1)S(1)} %collective-permute-done.13.refs_1_, ...), custom_call_target="tpu_custom_call" | custom-call | tf_op jit(solution)/shard_map/pallas_call | solution.py:310
  (1 shorter events, 0.0 us)
Async XLA Ops:
  0.6 26.1 %copy-start.2 = (bf16[6,4,8,384]{3,2,1,0:T(8,128)(2,1)S(1)}, bf16[6,4,8,384]{3,2,1,0:T(8,128)(2,1)}, u32[]{:S(2)}) copy-start(bf16[6,4,8,384]{3,2,1,0:T(8,128)(2,1)} %param.5) | copy-start | bytes 442372
  0.6 26.1 %copy-start.1 = (bf16[6,4,8,384]{3,2,1,0:T(8,128)(2,1)S(1)}, bf16[6,4,8,384]{3,2,1,0:T(8,128)(2,1)}, u32[]{:S(2)}) copy-start(bf16[6,4,8,384]{3,2,1,0:T(8,128)(2,1)} %param.8) | copy-start | bytes 442372
  0.7 35.0 %copy-start = (s32[1,1,1,27]{3,2,1,0:T(1,128)S(1)}, s32[1,1,1,27]{3,2,1,0:T(1,128)}, u32[]{:S(2)}) copy-start(s32[1,1,1,27]{3,2,1,0:T(1,128)} %pairs_v.1) | copy-start | bytes 328
  1.7 14.8 %collective-permute-start.4 = (bf16[384,384]{1,0:T(8,128)(2,1)S(1)}, bf16[384,384]{1,0:T(8,128)(2,1)S(1)}, u32[]{:S(2)}, u32[]{:S(2)}) collective-permute-start(bf16[384,384]{1,0:T(8,128)(2,1)S(1)} %pad_maximum_fusion.kv.refs_0_), channel_id=1, source_target_pairs={{0,4},{4,0},{8,12},{12,8},{16,20},{20,16},{24,28},{28,24},{1,5},{5... | collective-permute-start | bytes 884744 | tf_op jit(solution)/shard_map/ppermute | solution.py:37
  3.6 13.4 %collective-permute-start.5 = (bf16[384,384]{1,0:T(8,128)(2,1)S(1)}, bf16[384,384]{1,0:T(8,128)(2,1)S(1)}, u32[]{:S(2)}, u32[]{:S(2)}) collective-permute-start(bf16[384,384]{1,0:T(8,128)(2,1)S(1)} %pad_maximum_fusion.kv.refs_0_), channel_id=1, source_target_pairs={{4,8},{8,4},{12,16},{16,12},{20,24},{24,20},{5,9},{9,5},{13,17},{1... | collective-permute-start | bytes 884744 | tf_op jit(solution)/shard_map/ppermute | solution.py:37
  10.3 10.2 %collective-permute-start = (bf16[384,384]{1,0:T(8,128)(2,1)S(1)}, bf16[384,384]{1,0:T(8,128)(2,1)S(1)}, u32[]{:S(2)}, u32[]{:S(2)}) collective-permute-start(bf16[384,384]{1,0:T(8,128)(2,1)S(1)} %pad_maximum_fusion.kv.refs_0_), channel_id=1, source_target_pairs={{32,64},{64,32},{96,128},{128,96},{160,192},{192,160},{224,256},{2... | collective-permute-start | bytes 884744 | tf_op jit(solution)/shard_map/ppermute | solution.py:37
  14.6 5.8 %collective-permute-start.1 = (bf16[384,384]{1,0:T(8,128)(2,1)S(1)}, bf16[384,384]{1,0:T(8,128)(2,1)S(1)}, u32[]{:S(2)}, u32[]{:S(2)}) collective-permute-start(bf16[384,384]{1,0:T(8,128)(2,1)S(1)} %pad_maximum_fusion.kv.refs_0_), channel_id=1, source_target_pairs={{0,32},{32,0},{64,96},{96,64},{128,160},{160,128},{192,224},{224,1... | collective-permute-start | bytes 884744 | tf_op jit(solution)/shard_map/ppermute | solution.py:37
  20.5 15.2 %collective-permute-start.6 = (bf16[768,384]{1,0:T(8,128)(2,1)S(1)}, bf16[768,384]{1,0:T(8,128)(2,1)S(1)}, u32[]{:S(2)}, u32[]{:S(2)}) collective-permute-start(bf16[768,384]{1,0:T(8,128)(2,1)S(1)} %shard_map.84), channel_id=1, source_target_pairs={{32,64},{64,32},{96,128},{128,96},{160,192},{192,160},{224,256},{2... | collective-permute-start | bytes 1769480 | tf_op jit(solution)/shard_map/ppermute | solution.py:37
  24.8 10.9 %collective-permute-start.7 = (bf16[768,384]{1,0:T(8,128)(2,1)S(1)}, bf16[768,384]{1,0:T(8,128)(2,1)S(1)}, u32[]{:S(2)}, u32[]{:S(2)}) collective-permute-start(bf16[768,384]{1,0:T(8,128)(2,1)S(1)} %shard_map.84), channel_id=1, source_target_pairs={{0,32},{32,0},{64,96},{96,64},{128,160},{160,128},{192,224},{224,1... | collective-permute-start | bytes 1769480 | tf_op jit(solution)/shard_map/ppermute | solution.py:37
  26.8 19.3 %collective-permute-start.2 = (bf16[384,384]{1,0:T(8,128)(2,1)S(1)}, bf16[384,384]{1,0:T(8,128)(2,1)S(1)}, u32[]{:S(2)}, u32[]{:S(2)}) collective-permute-start(bf16[384,384]{1,0:T(8,128)(2,1)S(1)} %pad_maximum_fusion.1.own_qg.refs_2_.refs_0_.refs_1_), channel_id=1, source_target_pairs={{0,4},{4,0},{8,12},{12,8},{16,20},{20,16},{24,28},{28,24},{1,5},{5... | collective-permute-start | bytes 884744 | tf_op jit(solution)/shard_map/ppermute | solution.py:37
  28.7 17.4 %collective-permute-start.3 = (bf16[384,384]{1,0:T(8,128)(2,1)S(1)}, bf16[384,384]{1,0:T(8,128)(2,1)S(1)}, u32[]{:S(2)}, u32[]{:S(2)}) collective-permute-start(bf16[384,384]{1,0:T(8,128)(2,1)S(1)} %pad_maximum_fusion.1.own_qg.refs_2_.refs_0_.refs_1_), channel_id=1, source_target_pairs={{4,8},{8,4},{12,16},{16,12},{20,24},{24,20},{5,9},{9,5},{13,17},{1... | collective-permute-start | bytes 884744 | tf_op jit(solution)/shard_map/ppermute | solution.py:37
  39.1 7.0 %collective-permute-start.8 = (f32[8,192]{1,0:T(8,128)S(1)}, f32[8,192]{1,0:T(8,128)S(1)}, u32[]{:S(2)}, u32[]{:S(2)}) collective-permute-start(f32[8,192]{1,0:T(8,128)S(1)} %get-tuple-element.29.refs_5_.refs_4_), channel_id=1, source_target_pairs={{0,4},{4,0},{8,12},{12,8},{16,20},{20,16},{24,28},{28,24},{1,5},{5... | collective-permute-start | bytes 18440 | tf_op jit(solution)/shard_map/ppermute | solution.py:37
  41.1 6.6 %collective-permute-start.9 = (f32[8,192]{1,0:T(8,128)S(1)}, f32[8,192]{1,0:T(8,128)S(1)}, u32[]{:S(2)}, u32[]{:S(2)}) collective-permute-start(f32[8,192]{1,0:T(8,128)S(1)} %get-tuple-element.29.refs_5_.refs_4_), channel_id=1, source_target_pairs={{4,8},{8,4},{12,16},{16,12},{20,24},{24,20},{5,9},{9,5},{13,17},{1... | collective-permute-start | bytes 18440 | tf_op jit(solution)/shard_map/ppermute | solution.py:37
  50.4 5.6 %collective-permute-start.10 = (bf16[384,384]{1,0:T(8,128)(2,1)S(1)}, bf16[384,384]{1,0:T(8,128)(2,1)S(1)}, u32[]{:S(2)}, u32[]{:S(2)}) collective-permute-start(bf16[384,384]{1,0:T(8,128)(2,1)S(1)} %get-tuple-element.30), channel_id=1, source_target_pairs={{0,32},{32,0},{64,96},{96,64},{128,160},{160,128},{192,224},{224,1... | collective-permute-start | bytes 884744 | tf_op jit(solution)/shard_map/ppermute | solution.py:37
  52.4 12.2 %collective-permute-start.12 = (bf16[384,384]{1,0:T(8,128)(2,1)S(1)}, bf16[384,384]{1,0:T(8,128)(2,1)S(1)}, u32[]{:S(2)}, u32[]{:S(2)}) collective-permute-start(bf16[384,384]{1,0:T(8,128)(2,1)S(1)} %get-tuple-element.39), channel_id=1, source_target_pairs={{32,64},{64,32},{96,128},{128,96},{160,192},{192,160},{224,256},{2... | collective-permute-start | bytes 884744 | tf_op jit(solution)/shard_map/ppermute | solution.py:37
  58.3 14.1 %collective-permute-start.11 = (bf16[2,48,384]{2,1,0:T(8,128)(2,1)S(1)}, bf16[2,48,384]{2,1,0:T(8,128)(2,1)S(1)}, u32[]{:S(2)}, u32[]{:S(2)}) collective-permute-start(bf16[2,48,384]{2,1,0:T(8,128)(2,1)S(1)} %get-tuple-element.37), channel_id=1, source_target_pairs={{0,2},{1,3},{2,0},{3,1},{4,6},{5,7},{6,4},{7,5},{8,10},{9,11},{10,... | collective-permute-start | bytes 221192 | tf_op jit(solution)/shard_map/ppermute | solution.py:233
  64.9 12.3 %collective-permute-start.14 = (bf16[4,48,384]{2,1,0:T(8,128)(2,1)S(1)}, bf16[4,48,384]{2,1,0:T(8,128)(2,1)S(1)}, u32[]{:S(2)}, u32[]{:S(2)}) collective-permute-start(bf16[4,48,384]{2,1,0:T(8,128)(2,1)S(1)} %get-tuple-element.44), channel_id=1, source_target_pairs={{0,1},{1,0},{2,3},{3,2},{4,5},{5,4},{6,7},{7,6},{8,9},{9,8},{10,11... | collective-permute-start | bytes 442376 | tf_op jit(solution)/shard_map/ppermute | solution.py:233
  67.2 12.3 %collective-permute-start.15 = (bf16[4,48,384]{2,1,0:T(8,128)(2,1)S(1)}, bf16[4,48,384]{2,1,0:T(8,128)(2,1)S(1)}, u32[]{:S(2)}, u32[]{:S(2)}) collective-permute-start(bf16[4,48,384]{2,1,0:T(8,128)(2,1)S(1)} %get-tuple-element.45), channel_id=1, source_target_pairs={{0,3},{1,2},{2,1},{3,0},{4,7},{5,6},{6,5},{7,4},{8,11},{9,10},{10,... | collective-permute-start | bytes 442376 | tf_op jit(solution)/shard_map/ppermute | solution.py:233
  72.5 10.9 %collective-permute-start.13 = (bf16[2,48,384]{2,1,0:T(8,128)(2,1)S(1)}, bf16[2,48,384]{2,1,0:T(8,128)(2,1)S(1)}, u32[]{:S(2)}, u32[]{:S(2)}) collective-permute-start(bf16[2,48,384]{2,1,0:T(8,128)(2,1)S(1)} %get-tuple-element.42), channel_id=1, source_target_pairs={{0,2},{1,3},{2,0},{3,1},{4,6},{5,7},{6,4},{7,5},{8,10},{9,11},{10,... | collective-permute-start | bytes 221192 | tf_op jit(solution)/shard_map/ppermute | solution.py:233

commit v5 on v4

--- a/solution.py
+++ b/solution.py
@@ -58,9 +58,9 @@
         second_ref[rows, :] = ref[start + TILE : start + 2 * TILE, :]
 
 
-def column_blocks(firsts, seconds, heads):
+def store_sends(send_ref, firsts, seconds):
+    heads = send_ref.shape[0]
     group, span = 8 // heads, TILE // heads
-    me = lax.axis_index("head")
     row = lax.broadcasted_iota(jnp.int32, (TILE, TILE), 0)
     col = lax.broadcasted_iota(jnp.int32, (TILE, TILE), 1)
     block = jnp.zeros_like(row)
@@ -68,36 +68,27 @@
         block += (row >= d * span).astype(jnp.int32)
     inner = row - block * span
     shift = group.bit_length() - 1
-    source = (inner >> shift) * 8 + (block ^ me) * group + (inner & (group - 1))
+    source = (inner >> shift) * 8 + block * group + (inner & (group - 1))
     order = (col == source).astype(jnp.bfloat16)
     joined = jnp.concatenate(firsts + seconds, axis=1)
     moved = jnp.dot(order, joined, preferred_element_type=jnp.float32).astype(jnp.bfloat16)
-    feats = joined.shape[1] // 2
-    return [
-        [moved[k * span : (k + 1) * span, i * feats : (i + 1) * feats] for i in range(2)]
-        for k in range(heads)
-    ]
-
-
-def near_heads(heads):
-    return [k for k in range(heads) if k != heads // 2]
-
-
-def assemble_kernel(heads, far_q, far_k, *refs):
-    near_refs, out_refs = refs[: heads - 1], refs[heads - 1 :]
-    feats = far_q.shape[2]
-    me = lax.axis_index("head")
-
-    def put(k, i, rows):
-        place = pl.ds(pl.multiple_of((me ^ k) * feats, HEAD_DIM), feats)
-        out_refs[i][:, :, place] = rows.reshape(out_refs[i].shape[:2] + (feats,))
-
-    for i in range(2):
-        put(heads // 2, i, far_q[i])
-        put(heads // 2, 2 + i, far_k[i])
-    for k, ref in zip(near_heads(heads), near_refs):
-        for i in range(4):
-            put(k, i, ref[i])
+    feats = send_ref.shape[3]
+    for k in range(heads):
+        rows = slice(k * span, (k + 1) * span)
+        send_ref[k, 0] = moved[rows, :feats]
+        send_ref[k, 1] = moved[rows, feats:]
+
+
+def assemble(got_ref, out_refs):
+    heads, _, _, feats = got_ref.shape
+    for k in range(heads):
+        place = slice(k * feats, (k + 1) * feats)
+        for i, out_ref in enumerate(out_refs):
+            out_ref[:, :, place] = got_ref[k, i].reshape(out_ref.shape[:2] + (feats,))
+
+
+def assemble_kernel(got_ref, *out_refs):
+    assemble(got_ref, out_refs)
 
 
 def query_kernel(
@@ -146,8 +137,7 @@
     stat_ref[7:8, 0:27] = pairs_v[0, 0].astype(jnp.float32)
 
 
-def query_grad_kernel(heads, own_qg, key_ref, value_ref, attended_ref, column_ref, bias_ref, *refs):
-    far_ref, near_ref = refs
+def query_grad_kernel(own_qg, key_ref, value_ref, attended_ref, column_ref, bias_ref, send_ref):
     bias = bias_ref[...]
     count = own_qg.shape[1] // HEAD_DIM
     grad_parts = []
@@ -166,11 +156,7 @@
         slopes = (weights * (pushes - spread)).astype(jnp.bfloat16)
         query_grad = SCALE * jnp.dot(slopes, key, preferred_element_type=jnp.float32)
         grad_parts.append(query_grad.astype(jnp.bfloat16))
-    blocks = column_blocks([attended_ref[...]], grad_parts, heads)
-    for i in range(2):
-        far_ref[i] = blocks[heads // 2][i]
-        for at, k in enumerate(near_heads(heads)):
-            near_ref[at, i] = blocks[k][i]
+    store_sends(send_ref, [attended_ref[...]], grad_parts)
 
 
 def key_kernel(sides, *refs):
@@ -195,42 +181,38 @@
     for h in range(count):
         feat = slice(h * HEAD_DIM, (h + 1) * HEAD_DIM)
         query, grad = query_ref[:, feat], grad_ref[:, feat]
-        for i, (kv_ref, out_ref) in enumerate(zip(kvs, outs)):
-            key, value = kv_ref[0:TILE, feat], kv_ref[TILE : 2 * TILE, feat]
-            scores = lax.dot_general(
-                key, query, (((1,), (1,)), ((), ())), preferred_element_type=jnp.float32
-            )
-            weights = jnp.exp2(scores * SCALE2 - stat_ref[i, h : h + 1, :])
-            rounded = weights.astype(jnp.bfloat16)
-            value_grad = jnp.dot(rounded, grad, preferred_element_type=jnp.float32)
-            pushes = lax.dot_general(
-                value, grad, (((1,), (1,)), ((), ())), preferred_element_type=jnp.float32
-            )
+        keys = jnp.concatenate([ref[0:TILE, feat] for ref in kvs], axis=0)
+        values = jnp.concatenate([ref[TILE : 2 * TILE, feat] for ref in kvs], axis=0)
+        scores = lax.dot_general(
+            keys, query, (((1,), (1,)), ((), ())), preferred_element_type=jnp.float32
+        )
+        pushes = lax.dot_general(
+            values, grad, (((1,), (1,)), ((), ())), preferred_element_type=jnp.float32
+        )
+        rounded, slopes = [], []
+        for i in range(len(sides)):
+            rows = slice(i * TILE, (i + 1) * TILE)
+            weights = jnp.exp2(scores[rows] * SCALE2 - stat_ref[i, h : h + 1, :])
             spread = stat_ref[i, count + h : count + h + 1, :]
-            slopes = (weights * (pushes - spread)).astype(jnp.bfloat16)
-            key_grad = SCALE * jnp.dot(slopes, query, preferred_element_type=jnp.float32)
-            out_ref[0:TILE, feat] = key_grad.astype(out_ref.dtype)
-            out_ref[TILE : 2 * TILE, feat] = value_grad.astype(out_ref.dtype)
-
-
-def fold_kernel(heads, own_ref, got_a, got_b, near_q, far_ref, *near_refs):
+            rounded.append(weights.astype(jnp.bfloat16))
+            slopes.append((weights * (pushes[rows] - spread)).astype(jnp.bfloat16))
+        rounded, slopes = jnp.concatenate(rounded, axis=0), jnp.concatenate(slopes, axis=0)
+        value_grad = jnp.dot(rounded, grad, preferred_element_type=jnp.float32)
+        key_grad = SCALE * jnp.dot(slopes, query, preferred_element_type=jnp.float32)
+        for i, ref in enumerate(outs):
+            rows = slice(i * TILE, (i + 1) * TILE)
+            ref[0:TILE, feat] = key_grad[rows].astype(ref.dtype)
+            ref[TILE : 2 * TILE, feat] = value_grad[rows].astype(ref.dtype)
+
+
+def fold_kernel(own_ref, got_a, got_b, send_ref):
     total = own_ref[...] + got_a[...].astype(jnp.float32) + got_b[...].astype(jnp.float32)
     total = total.astype(jnp.bfloat16)
-    blocks = column_blocks([total[0:TILE]], [total[TILE : 2 * TILE]], heads)
-    for i in range(2):
-        far_ref[i] = blocks[heads // 2][i]
-        for at, (k, ref) in enumerate(zip(near_heads(heads), near_refs)):
-            ref[i] = near_q[at, i]
-            ref[2 + i] = blocks[k][i]
+    store_sends(send_ref, [total[0:TILE]], [total[TILE : 2 * TILE]])
 
 
 def after(value, *others):
     return lax.optimization_barrier((value,) + others)[0]
-
-
-def head_swap(value, k):
-    count = lax.axis_size("head")
-    return lax.ppermute(value, "head", [(i, i ^ k) for i in range(count)]) if k else value
 
 
 def stacked(first, second):
@@ -257,9 +239,7 @@
     qg_late = after(qg, kv_fb, kv_fa)
     qg_a, qg_b = pair_swap(qg_late, "row", 0), pair_swap(qg_late, "row", 1)
 
-    span = TILE // heads
-    pair, four = (jax.ShapeDtypeStruct((n, span, feats), bf16) for n in (2, 4))
-    near_shape = jax.ShapeDtypeStruct((heads - 1, 2, span, feats), bf16)
+    send_shape = jax.ShapeDtypeStruct((heads, 2, TILE // heads, feats), bf16)
     wide = jax.ShapeDtypeStruct((WIDE, feats), bf16)
     attended, stat, column, bias, key_near, value_near = call(
         query_kernel,
@@ -289,30 +269,16 @@
     term_b, term_a = terms((2, 1), (bf16, bf16), kv_fb, kv_fa)
     got_b, got_a = pair_swap(term_b, "frame", 1), pair_swap(term_a, "frame", 0)
     (own,) = terms((0,), (f32,), after(kv, got_a))
-    far_q, near_q = call(
-        lambda *refs: query_grad_kernel(heads, *refs),
-        (pair, near_shape),
-        [VMEM] * 6,
-        (VMEM, VMEM),
-    )(after(qg, got_a), key_near, value_near, attended, column, bias)
-    got_far_q = head_swap(far_q, heads // 2)
-
-    far_k, *near_k = call(
-        lambda *refs: fold_kernel(heads, *refs),
-        [pair] + [four] * (heads - 1),
-        [VMEM] * 4,
-        [VMEM] * heads,
-    )(own, got_b, got_a, near_q)
-    got_far_k = head_swap(after(far_k, got_far_q), heads // 2)
-    got_near = [head_swap(sent, k) for k, sent in zip(near_heads(heads), near_k)]
+    sent_q = call(query_grad_kernel, send_shape, [VMEM] * 6, VMEM)(
+        after(qg, got_a), key_near, value_near, attended, column, bias
+    )
+    sent_k = call(fold_kernel, send_shape, [VMEM] * 3, VMEM)(after(own, sent_q), got_b, got_a)
 
     out = jax.ShapeDtypeStruct((frames_dev * rows_dev, columns // heads, heads * feats), bf16)
-    outs = call(
-        lambda *refs: assemble_kernel(heads, *refs),
-        [out] * 4,
-        [VMEM] * (heads + 1),
-        [VMEM] * 4,
-    )(got_far_q, got_far_k, *got_near)
+    outs = []
+    for sent in (sent_q, sent_k):
+        got = lax.all_to_all(sent, "head", split_axis=0, concat_axis=0, tiled=True)
+        outs += call(assemble_kernel, (out, out), [VMEM], (VMEM, VMEM))(got)
     return tuple(x.reshape((frames_dev, rows_dev) + out.shape[1:]) for x in outs)
 
 

time: 85 us -> 91.9 us (1.081)
  the two profiles are of different devices: /device:TPU:120 before, /device:TPU:72 now
where the time goes in v5:
time: 91.9 us; the launch traced here: 91.4 us
  starting transfers between devices  45.1 us (49%)
  waiting for transfers between devices  17.1 us (19%)
  blocking collectives  16 us (17%)
  Pallas kernels  11.3 us (12%)
  other arithmetic  1.09 us (1%)
    ppermute x12, starting transfers between devices, pair_swap(): return lax.ppermute(value, axis, pairs)  41.6 us
    all_to_all x1, blocking collectives, body(): got = lax.all_to_all(sent, 'head', split_axis=0, concat_axis=0, tiled=True)  16 us
    ppermute x12, waiting for transfers between devices, pair_swap(): return lax.ppermute(value, axis, pairs)  8.65 us
    all_to_all x1, waiting for transfers between devices, body(): got = lax.all_to_all(sent, 'head', split_axis=0, concat_axis=0, tiled=True)  8.43 us
    all_to_all x1, starting transfers between devices, body(): got = lax.all_to_all(sent, 'head', split_axis=0, concat_axis=0, tiled=True)  3.45 us
    pallas_call x1, Pallas kernels, body(): call(query_kernel, (jax.ShapeDtypeStruct((TILE, feats), bf16), jax.ShapeD...  3.44 us
    pallas_call x1, Pallas kernels, body(): call(query_grad_kernel, send_shape, [VMEM] * 6, VMEM)  3 us
    pallas_call x2, Pallas kernels, terms(): call(lambda *refs: key_kernel(sides, *refs), [jax.ShapeDtypeStruct((2 * T...  2.88 us
  transfers between devices with their start and end apart: 13, of which 5 were waited for; matrix products, arithmetic and copies ran while one was open for 0% of the time, Pallas kernels for 9%

profile of v5, /device:TPU:72, one launch (start us, length us, event | category | flops | bytes accessed | tf_op | source)
XLA Modules:
  0.0 91.4 jit_solution(7418453836337085735)
XLA Ops:
  0.6 0.0 copy-start.2
  0.6 0.0 copy-start.1
  0.7 0.0 copy-start
  0.7 1.1 %pad_maximum_fusion.kv.refs_0_ = bf16[384,384]{1,0:T(8,128)(2,1)S(1)} fusion(bf16[192,384]{1,0:T(8,128)(2,1)} %bitcast.8, bf16[192,384]{1,0:T(8,128)(2,1)} %bitcast.9), kind=kLoop, calls=%fused_computation | loop fusion | flops 589824 | bytes 589824 | tf_op jit(solution)/shard_map/max | solution.py:221
  1.7 1.9 %collective-permute-start.4 = (bf16[384,384]{1,0:T(8,128)(2,1)S(1)}, bf16[384,384]{1,0:T(8,128)(2,1)S(1)}, u32[]{:S(2)}, u32[]{:S(2)}) collective-permute-start(bf16[384,384]{1,0:T(8,128)(2,1)S(1)} %pad_maximum_fusion.kv.refs_0_), channel_id=1, source_target_pairs={{0,4},{4,0},{8,12},{12,8},{16,20},{20,16},{24,28},{28,24},{1,5},{5... | collective-permute-start | bytes 884744 | tf_op jit(solution)/shard_map/ppermute | solution.py:37
  3.6 6.6 %collective-permute-start.5 = (bf16[384,384]{1,0:T(8,128)(2,1)S(1)}, bf16[384,384]{1,0:T(8,128)(2,1)S(1)}, u32[]{:S(2)}, u32[]{:S(2)}) collective-permute-start(bf16[384,384]{1,0:T(8,128)(2,1)S(1)} %pad_maximum_fusion.kv.refs_0_), channel_id=1, source_target_pairs={{4,8},{8,4},{12,16},{16,12},{20,24},{24,20},{5,9},{9,5},{13,17},{1... | collective-permute-start | bytes 884744 | tf_op jit(solution)/shard_map/ppermute | solution.py:37
  10.3 3.4 %collective-permute-start = (bf16[384,384]{1,0:T(8,128)(2,1)S(1)}, bf16[384,384]{1,0:T(8,128)(2,1)S(1)}, u32[]{:S(2)}, u32[]{:S(2)}) collective-permute-start(bf16[384,384]{1,0:T(8,128)(2,1)S(1)} %pad_maximum_fusion.kv.refs_0_), channel_id=1, source_target_pairs={{32,64},{64,32},{96,128},{128,96},{160,192},{192,160},{224,256},{2... | collective-permute-start | bytes 884744 | tf_op jit(solution)/shard_map/ppermute | solution.py:37
  13.7 2.0 %collective-permute-start.1 = (bf16[384,384]{1,0:T(8,128)(2,1)S(1)}, bf16[384,384]{1,0:T(8,128)(2,1)S(1)}, u32[]{:S(2)}, u32[]{:S(2)}) collective-permute-start(bf16[384,384]{1,0:T(8,128)(2,1)S(1)} %pad_maximum_fusion.kv.refs_0_), channel_id=1, source_target_pairs={{0,32},{32,0},{64,96},{96,64},{128,160},{160,128},{192,224},{224,1... | collective-permute-start | bytes 884744 | tf_op jit(solution)/shard_map/ppermute | solution.py:37
  15.7 0.0 collective-permute-done.4.a_ref.kv_a
  15.7 1.3 %collective-permute-done.5.b_ref.kv_b = bf16[384,384]{1,0:T(8,128)(2,1)S(1)} collective-permute-done((bf16[384,384]{1,0:T(8,128)(2,1)S(1)}, bf16[384,384]{1,0:T(8,128)(2,1)S(1)}, u32[]{:S(2)}, u32[]{:S(2)}) %collective-permute-start.5) | collective-permute-done | bytes 294944 | tf_op jit(solution)/shard_map/ppermute | solution.py:37
  17.0 0.1 shard_map.84
  17.1 3.4 %collective-permute-done.kv_fb.refs_0_ = bf16[384,384]{1,0:T(8,128)(2,1)S(1)} collective-permute-done((bf16[384,384]{1,0:T(8,128)(2,1)S(1)}, bf16[384,384]{1,0:T(8,128)(2,1)S(1)}, u32[]{:S(2)}, u32[]{:S(2)}) %collective-permute-start) | collective-permute-done | bytes 294944 | tf_op jit(solution)/shard_map/ppermute | solution.py:37
  20.4 0.0 collective-permute-done.1.kv_fa.refs_1_
  20.5 3.4 %collective-permute-start.6 = (bf16[768,384]{1,0:T(8,128)(2,1)S(1)}, bf16[768,384]{1,0:T(8,128)(2,1)S(1)}, u32[]{:S(2)}, u32[]{:S(2)}) collective-permute-start(bf16[768,384]{1,0:T(8,128)(2,1)S(1)} %shard_map.84), channel_id=1, source_target_pairs={{32,64},{64,32},{96,128},{128,96},{160,192},{192,160},{224,256},{2... | collective-permute-start | bytes 1769480 | tf_op jit(solution)/shard_map/ppermute | solution.py:37
  23.9 1.9 %collective-permute-start.7 = (bf16[768,384]{1,0:T(8,128)(2,1)S(1)}, bf16[768,384]{1,0:T(8,128)(2,1)S(1)}, u32[]{:S(2)}, u32[]{:S(2)}) collective-permute-start(bf16[768,384]{1,0:T(8,128)(2,1)S(1)} %shard_map.84), channel_id=1, source_target_pairs={{0,32},{32,0},{64,96},{96,64},{128,160},{160,128},{192,224},{224,1... | collective-permute-start | bytes 1769480 | tf_op jit(solution)/shard_map/ppermute | solution.py:37
  25.8 0.0 copy-done.2
  25.8 0.0 copy-done.1
  25.9 1.9 %collective-permute-start.2 = (bf16[384,384]{1,0:T(8,128)(2,1)S(1)}, bf16[384,384]{1,0:T(8,128)(2,1)S(1)}, u32[]{:S(2)}, u32[]{:S(2)}) collective-permute-start(bf16[384,384]{1,0:T(8,128)(2,1)S(1)} %pad_maximum_fusion.1.own_qg.refs_2_.refs_1_), channel_id=1, source_target_pairs={{0,4},{4,0},{8,12},{12,8},{16,20},{20,16},{24,28},{28,24},{1,5},{5... | collective-permute-start | bytes 884744 | tf_op jit(solution)/shard_map/ppermute | solution.py:37
  27.8 7.0 %collective-permute-start.3 = (bf16[384,384]{1,0:T(8,128)(2,1)S(1)}, bf16[384,384]{1,0:T(8,128)(2,1)S(1)}, u32[]{:S(2)}, u32[]{:S(2)}) collective-permute-start(bf16[384,384]{1,0:T(8,128)(2,1)S(1)} %pad_maximum_fusion.1.own_qg.refs_2_.refs_1_), channel_id=1, source_target_pairs={{4,8},{8,4},{12,16},{16,12},{20,24},{24,20},{5,9},{9,5},{13,17},{1... | collective-permute-start | bytes 884744 | tf_op jit(solution)/shard_map/ppermute | solution.py:37
  34.8 0.0 collective-permute-done.6.corner_fb
  34.8 0.0 collective-permute-done.7.corner_fa
  34.8 0.0 copy-done
  34.8 3.4 %shard_map.85 = (bf16[192,384]{1,0:T(8,128)(2,1)S(1)}, f32[8,192]{1,0:T(8,128)S(1)}, f32[192,128]{1,0:T(8,128)S(1)}, f32[1,1728]{1,0:T(1,128)S(1)}, bf16[1728,38...) custom-call(s32[1,1,1,27]{3,2,1,0:T(1,128)S(1)} %copy-done, s32[1,1,1,27]{3,2,1,0:T(1,128)S(1)} %copy-done, ...), custom_call_target="tpu_custom_call" | custom-call | tf_op jit(solution)/shard_map/pallas_call | solution.py:244
  38.2 1.9 %collective-permute-start.8 = (f32[8,192]{1,0:T(8,128)S(1)}, f32[8,192]{1,0:T(8,128)S(1)}, u32[]{:S(2)}, u32[]{:S(2)}) collective-permute-start(f32[8,192]{1,0:T(8,128)S(1)} %get-tuple-element.23.refs_5_.refs_4_), channel_id=1, source_target_pairs={{0,4},{4,0},{8,12},{12,8},{16,20},{20,16},{24,28},{28,24},{1,5},{5... | collective-permute-start | bytes 18440 | tf_op jit(solution)/shard_map/ppermute | solution.py:37
  40.2 5.9 %collective-permute-start.9 = (f32[8,192]{1,0:T(8,128)S(1)}, f32[8,192]{1,0:T(8,128)S(1)}, u32[]{:S(2)}, u32[]{:S(2)}) collective-permute-start(f32[8,192]{1,0:T(8,128)S(1)} %get-tuple-element.23.refs_5_.refs_4_), channel_id=1, source_target_pairs={{4,8},{8,4},{12,16},{16,12},{20,24},{24,20},{5,9},{9,5},{13,17},{1... | collective-permute-start | bytes 18440 | tf_op jit(solution)/shard_map/ppermute | solution.py:37
  46.1 0.0 collective-permute-done.2.refs_3_.refs_2_
  46.1 0.0 collective-permute-done.3.refs_4_.refs_3_
  46.1 0.0 collective-permute-done.8.refs_6_.refs_5_
  46.1 1.6 %collective-permute-done.9.refs_7_.refs_6_ = f32[8,192]{1,0:T(8,128)S(1)} collective-permute-done((f32[8,192]{1,0:T(8,128)S(1)}, f32[8,192]{1,0:T(8,128)S(1)}, u32[]{:S(2)}, u32[]{:S(2)}) %collective-permute-start.9) | collective-permute-done | bytes 6176 | tf_op jit(solution)/shard_map/ppermute | solution.py:37
  47.7 1.8 %shard_map.86 = (bf16[384,384]{1,0:T(8,128)(2,1)S(1)}, bf16[384,384]{1,0:T(8,128)(2,1)S(1)}) custom-call(bf16[384,384]{1,0:T(8,128)(2,1)S(1)} %collective-permute-done.kv_fb.refs_0_, bf16[384,384]{1,0:T(8,128)(2,1)S(1)} %collective-permute-done.1.kv_fa.refs_1_, bf16[384,384]{1,0:T(8,128)(2,1)S(1)} %pad_maximum_fusion.1.own_qg.refs_2_.refs_1_, ...), custom_call_target="tpu_custom_call" | custom-call | tf_op jit(solution)/shard_map/pallas_call | solution.py:261
  49.5 1.9 %collective-permute-start.10 = (bf16[384,384]{1,0:T(8,128)(2,1)S(1)}, bf16[384,384]{1,0:T(8,128)(2,1)S(1)}, u32[]{:S(2)}, u32[]{:S(2)}) collective-permute-start(bf16[384,384]{1,0:T(8,128)(2,1)S(1)} %get-tuple-element.24), channel_id=1, source_target_pairs={{0,32},{32,0},{64,96},{96,64},{128,160},{160,128},{192,224},{224,1... | collective-permute-start | bytes 884744 | tf_op jit(solution)/shard_map/ppermute | solution.py:37
  51.4 3.7 %collective-permute-start.11 = (bf16[384,384]{1,0:T(8,128)(2,1)S(1)}, bf16[384,384]{1,0:T(8,128)(2,1)S(1)}, u32[]{:S(2)}, u32[]{:S(2)}) collective-permute-start(bf16[384,384]{1,0:T(8,128)(2,1)S(1)} %get-tuple-element.35), channel_id=1, source_target_pairs={{32,64},{64,32},{96,128},{128,96},{160,192},{192,160},{224,256},{2... | collective-permute-start | bytes 884744 | tf_op jit(solution)/shard_map/ppermute | solution.py:37
  55.1 0.0 collective-permute-done.10.got_b
  55.1 3.0 %shard_map.87 = bf16[4,2,48,384]{3,2,1,0:T(8,128)(2,1)} custom-call(bf16[384,384]{1,0:T(8,128)(2,1)S(1)} %pad_maximum_fusion.1.own_qg.refs_2_.refs_1_, bf16[1728,384]{1,0:T(8,128)(2,1)S(1)} %get-tuple-element.26.key_ref, bf16[1728,384]{1,0:T(8,128)(2,1)S(1)} %get-tuple-element.27.value_ref, bf16[192,384]{1,0:T(8,128)(2,1)S(1)} %get-tuple-element.28.attended_ref, ...), custom_call_target="tpu_custom_call" | custom-call | tf_op jit(solution)/shard_map/pallas_call | solution.py:272
  58.1 1.1 %shard_map.89.own_ref = f32[384,384]{1,0:T(8,128)S(1)} custom-call(bf16[384,384]{1,0:T(8,128)(2,1)S(1)} %pad_maximum_fusion.kv.refs_0_, bf16[384,384]{1,0:T(8,128)(2,1)S(1)} %pad_maximum_fusion.1.own_qg.refs_2_.refs_1_, bf16[384,384]{1,0:T(8,128)(2,1)S(1)} %collective-permute-done.2.refs_3_.refs_2_, ...), custom_call_target="tpu_custom_call" | custom-call | tf_op jit(solution)/shard_map/pallas_call | solution.py:261
  59.2 2.4 %collective-permute-done.11.got_a = bf16[384,384]{1,0:T(8,128)(2,1)S(1)} collective-permute-done((bf16[384,384]{1,0:T(8,128)(2,1)S(1)}, bf16[384,384]{1,0:T(8,128)(2,1)S(1)}, u32[]{:S(2)}, u32[]{:S(2)}) %collective-permute-start.11) | collective-permute-done | bytes 294944 | tf_op jit(solution)/shard_map/ppermute | solution.py:37
  61.6 0.3 shard_map.90
  61.9 16.0 %all_to_all.10.got_ref = bf16[4,2,48,384]{3,2,1,0:T(8,128)(2,1)S(1)} all-to-all(bf16[4,2,48,384]{3,2,1,0:T(8,128)(2,1)S(1)} %shard_map.90), channel_id=1, replica_groups=mesh['frame'=16,'row'=8,'head'=4] {'head'}, dimensions={0} | all-to-all | bytes 589824 | tf_op jit(solution)/shard_map/all_to_all | solution.py:280
  77.9 3.5 %all-to-all-start = ((bf16[4,2,48,384]{3,2,1,0:T(8,128)(2,1)}), bf16[4,2,48,384]{3,2,1,0:T(8,128)(2,1)S(1)}, u32[]{:S(2)}, u32[]{:S(2)}) async-start(bf16[4,2,48,384]{3,2,1,0:T(8,128)(2,1)} %shard_map.87), calls=%async_computation | async-start | bytes 589824 | tf_op jit(solution)/shard_map/all_to_all | solution.py:280
  81.4 0.8 shard_map.91
  82.2 8.4 %all-to-all-done.got_ref = bf16[4,2,48,384]{3,2,1,0:T(8,128)(2,1)S(1)} async-done(((bf16[4,2,48,384]{3,2,1,0:T(8,128)(2,1)}), bf16[4,2,48,384]{3,2,1,0:T(8,128)(2,1)S(1)}, u32[]{:S(2)}, u32[]{:S(2)}) %all-to-all-start) | async-done | bytes 294944 | tf_op jit(solution)/shard_map/all_to_all | solution.py:280
  90.6 0.8 shard_map.88
  (1 shorter events, 0.0 us)
Async XLA Ops:
  0.6 25.2 %copy-start.2 = (bf16[6,4,8,384]{3,2,1,0:T(8,128)(2,1)S(1)}, bf16[6,4,8,384]{3,2,1,0:T(8,128)(2,1)}, u32[]{:S(2)}) copy-start(bf16[6,4,8,384]{3,2,1,0:T(8,128)(2,1)} %param.5) | copy-start | bytes 442372
  0.6 25.2 %copy-start.1 = (bf16[6,4,8,384]{3,2,1,0:T(8,128)(2,1)S(1)}, bf16[6,4,8,384]{3,2,1,0:T(8,128)(2,1)}, u32[]{:S(2)}) copy-start(bf16[6,4,8,384]{3,2,1,0:T(8,128)(2,1)} %param.8) | copy-start | bytes 442372
  0.7 34.1 %copy-start = (s32[1,1,1,27]{3,2,1,0:T(1,128)S(1)}, s32[1,1,1,27]{3,2,1,0:T(1,128)}, u32[]{:S(2)}) copy-start(s32[1,1,1,27]{3,2,1,0:T(1,128)} %pairs_v.1) | copy-start | bytes 328
  1.7 14.0 %collective-permute-start.4 = (bf16[384,384]{1,0:T(8,128)(2,1)S(1)}, bf16[384,384]{1,0:T(8,128)(2,1)S(1)}, u32[]{:S(2)}, u32[]{:S(2)}) collective-permute-start(bf16[384,384]{1,0:T(8,128)(2,1)S(1)} %pad_maximum_fusion.kv.refs_0_), channel_id=1, source_target_pairs={{0,4},{4,0},{8,12},{12,8},{16,20},{20,16},{24,28},{28,24},{1,5},{5... | collective-permute-start | bytes 884744 | tf_op jit(solution)/shard_map/ppermute | solution.py:37
  3.6 13.4 %collective-permute-start.5 = (bf16[384,384]{1,0:T(8,128)(2,1)S(1)}, bf16[384,384]{1,0:T(8,128)(2,1)S(1)}, u32[]{:S(2)}, u32[]{:S(2)}) collective-permute-start(bf16[384,384]{1,0:T(8,128)(2,1)S(1)} %pad_maximum_fusion.kv.refs_0_), channel_id=1, source_target_pairs={{4,8},{8,4},{12,16},{16,12},{20,24},{24,20},{5,9},{9,5},{13,17},{1... | collective-permute-start | bytes 884744 | tf_op jit(solution)/shard_map/ppermute | solution.py:37
  10.3 10.2 %collective-permute-start = (bf16[384,384]{1,0:T(8,128)(2,1)S(1)}, bf16[384,384]{1,0:T(8,128)(2,1)S(1)}, u32[]{:S(2)}, u32[]{:S(2)}) collective-permute-start(bf16[384,384]{1,0:T(8,128)(2,1)S(1)} %pad_maximum_fusion.kv.refs_0_), channel_id=1, source_target_pairs={{32,64},{64,32},{96,128},{128,96},{160,192},{192,160},{224,256},{2... | collective-permute-start | bytes 884744 | tf_op jit(solution)/shard_map/ppermute | solution.py:37
  13.7 6.7 %collective-permute-start.1 = (bf16[384,384]{1,0:T(8,128)(2,1)S(1)}, bf16[384,384]{1,0:T(8,128)(2,1)S(1)}, u32[]{:S(2)}, u32[]{:S(2)}) collective-permute-start(bf16[384,384]{1,0:T(8,128)(2,1)S(1)} %pad_maximum_fusion.kv.refs_0_), channel_id=1, source_target_pairs={{0,32},{32,0},{64,96},{96,64},{128,160},{160,128},{192,224},{224,1... | collective-permute-start | bytes 884744 | tf_op jit(solution)/shard_map/ppermute | solution.py:37
  20.5 14.3 %collective-permute-start.6 = (bf16[768,384]{1,0:T(8,128)(2,1)S(1)}, bf16[768,384]{1,0:T(8,128)(2,1)S(1)}, u32[]{:S(2)}, u32[]{:S(2)}) collective-permute-start(bf16[768,384]{1,0:T(8,128)(2,1)S(1)} %shard_map.84), channel_id=1, source_target_pairs={{32,64},{64,32},{96,128},{128,96},{160,192},{192,160},{224,256},{2... | collective-permute-start | bytes 1769480 | tf_op jit(solution)/shard_map/ppermute | solution.py:37
  23.9 10.9 %collective-permute-start.7 = (bf16[768,384]{1,0:T(8,128)(2,1)S(1)}, bf16[768,384]{1,0:T(8,128)(2,1)S(1)}, u32[]{:S(2)}, u32[]{:S(2)}) collective-permute-start(bf16[768,384]{1,0:T(8,128)(2,1)S(1)} %shard_map.84), channel_id=1, source_target_pairs={{0,32},{32,0},{64,96},{96,64},{128,160},{160,128},{192,224},{224,1... | collective-permute-start | bytes 1769480 | tf_op jit(solution)/shard_map/ppermute | solution.py:37
  25.9 20.2 %collective-permute-start.2 = (bf16[384,384]{1,0:T(8,128)(2,1)S(1)}, bf16[384,384]{1,0:T(8,128)(2,1)S(1)}, u32[]{:S(2)}, u32[]{:S(2)}) collective-permute-start(bf16[384,384]{1,0:T(8,128)(2,1)S(1)} %pad_maximum_fusion.1.own_qg.refs_2_.refs_1_), channel_id=1, source_target_pairs={{0,4},{4,0},{8,12},{12,8},{16,20},{20,16},{24,28},{28,24},{1,5},{5... | collective-permute-start | bytes 884744 | tf_op jit(solution)/shard_map/ppermute | solution.py:37
  27.8 18.3 %collective-permute-start.3 = (bf16[384,384]{1,0:T(8,128)(2,1)S(1)}, bf16[384,384]{1,0:T(8,128)(2,1)S(1)}, u32[]{:S(2)}, u32[]{:S(2)}) collective-permute-start(bf16[384,384]{1,0:T(8,128)(2,1)S(1)} %pad_maximum_fusion.1.own_qg.refs_2_.refs_1_), channel_id=1, source_target_pairs={{4,8},{8,4},{12,16},{16,12},{20,24},{24,20},{5,9},{9,5},{13,17},{1... | collective-permute-start | bytes 884744 | tf_op jit(solution)/shard_map/ppermute | solution.py:37
  38.2 7.9 %collective-permute-start.8 = (f32[8,192]{1,0:T(8,128)S(1)}, f32[8,192]{1,0:T(8,128)S(1)}, u32[]{:S(2)}, u32[]{:S(2)}) collective-permute-start(f32[8,192]{1,0:T(8,128)S(1)} %get-tuple-element.23.refs_5_.refs_4_), channel_id=1, source_target_pairs={{0,4},{4,0},{8,12},{12,8},{16,20},{20,16},{24,28},{28,24},{1,5},{5... | collective-permute-start | bytes 18440 | tf_op jit(solution)/shard_map/ppermute | solution.py:37
  40.2 7.5 %collective-permute-start.9 = (f32[8,192]{1,0:T(8,128)S(1)}, f32[8,192]{1,0:T(8,128)S(1)}, u32[]{:S(2)}, u32[]{:S(2)}) collective-permute-start(f32[8,192]{1,0:T(8,128)S(1)} %get-tuple-element.23.refs_5_.refs_4_), channel_id=1, source_target_pairs={{4,8},{8,4},{12,16},{16,12},{20,24},{24,20},{5,9},{9,5},{13,17},{1... | collective-permute-start | bytes 18440 | tf_op jit(solution)/shard_map/ppermute | solution.py:37
  49.5 5.6 %collective-permute-start.10 = (bf16[384,384]{1,0:T(8,128)(2,1)S(1)}, bf16[384,384]{1,0:T(8,128)(2,1)S(1)}, u32[]{:S(2)}, u32[]{:S(2)}) collective-permute-start(bf16[384,384]{1,0:T(8,128)(2,1)S(1)} %get-tuple-element.24), channel_id=1, source_target_pairs={{0,32},{32,0},{64,96},{96,64},{128,160},{160,128},{192,224},{224,1... | collective-permute-start | bytes 884744 | tf_op jit(solution)/shard_map/ppermute | solution.py:37
  51.4 10.2 %collective-permute-start.11 = (bf16[384,384]{1,0:T(8,128)(2,1)S(1)}, bf16[384,384]{1,0:T(8,128)(2,1)S(1)}, u32[]{:S(2)}, u32[]{:S(2)}) collective-permute-start(bf16[384,384]{1,0:T(8,128)(2,1)S(1)} %get-tuple-element.35), channel_id=1, source_target_pairs={{32,64},{64,32},{96,128},{128,96},{160,192},{192,160},{224,256},{2... | collective-permute-start | bytes 884744 | tf_op jit(solution)/shard_map/ppermute | solution.py:37
  77.9 12.7 %all-to-all-start = ((bf16[4,2,48,384]{3,2,1,0:T(8,128)(2,1)}), bf16[4,2,48,384]{3,2,1,0:T(8,128)(2,1)S(1)}, u32[]{:S(2)}, u32[]{:S(2)}) async-start(bf16[4,2,48,384]{3,2,1,0:T(8,128)(2,1)} %shard_map.87), calls=%async_computation | async-start | bytes 589824 | tf_op jit(solution)/shard_map/all_to_all | solution.py:280

commit v6 on v4

--- a/solution.py
+++ b/solution.py
@@ -46,9 +46,9 @@
     return [(a, b) for a in slot_steps("frame") for b in slot_steps("row")]
 
 
-def regroup_kernel(a_ref, b_ref, out_ref):
-    out_ref[0 : 2 * TILE, :] = a_ref[...]
-    out_ref[2 * TILE : 4 * TILE, :] = b_ref[...]
+def regroup_kernel(own_ref, a_ref, b_ref, out_ref):
+    for i, ref in enumerate((own_ref, a_ref, b_ref)):
+        out_ref[2 * TILE * i : 2 * TILE * (i + 1), :] = ref[...]
 
 
 def gather_near(tiles, first_ref, second_ref):
@@ -100,15 +100,11 @@
             put(k, i, ref[i])
 
 
-def query_kernel(
-    pairs_s, pairs_v, own_qg, kv, kv_a, kv_b, kv_fb, kv_fa, corner_fb, corner_fa, *refs
-):
+def query_kernel(pairs_s, pairs_v, own_qg, kv, kv_fb, kv_fa, *refs):
     attended_ref, stat_ref, column_ref, bias_ref, key_ref, value_ref = refs
     frame, row = lax.axis_index("frame"), lax.axis_index("row")
     frames, rows = lax.axis_size("frame"), lax.axis_size("row")
-    tiles = [(kv, 0), (kv_a, 0), (kv_b, 0)]
-    tiles += [(kv_fa, 0), (corner_fa, 0), (corner_fa, 2 * TILE)]
-    tiles += [(kv_fb, 0), (corner_fb, 0), (corner_fb, 2 * TILE)]
+    tiles = [(ref, 2 * TILE * i) for ref in (kv, kv_fa, kv_fb) for i in range(3)]
     gather_near(tiles, key_ref, value_ref)
     lane = lax.broadcasted_iota(jnp.int32, (1, WIDE), 1)
     bias = jnp.zeros((1, WIDE), jnp.float32)
@@ -195,22 +191,28 @@
     for h in range(count):
         feat = slice(h * HEAD_DIM, (h + 1) * HEAD_DIM)
         query, grad = query_ref[:, feat], grad_ref[:, feat]
-        for i, (kv_ref, out_ref) in enumerate(zip(kvs, outs)):
-            key, value = kv_ref[0:TILE, feat], kv_ref[TILE : 2 * TILE, feat]
-            scores = lax.dot_general(
-                key, query, (((1,), (1,)), ((), ())), preferred_element_type=jnp.float32
-            )
-            weights = jnp.exp2(scores * SCALE2 - stat_ref[i, h : h + 1, :])
-            rounded = weights.astype(jnp.bfloat16)
-            value_grad = jnp.dot(rounded, grad, preferred_element_type=jnp.float32)
-            pushes = lax.dot_general(
-                value, grad, (((1,), (1,)), ((), ())), preferred_element_type=jnp.float32
-            )
+        keys = jnp.concatenate([ref[0:TILE, feat] for ref in kvs], axis=0)
+        values = jnp.concatenate([ref[TILE : 2 * TILE, feat] for ref in kvs], axis=0)
+        scores = lax.dot_general(
+            keys, query, (((1,), (1,)), ((), ())), preferred_element_type=jnp.float32
+        )
+        pushes = lax.dot_general(
+            values, grad, (((1,), (1,)), ((), ())), preferred_element_type=jnp.float32
+        )
+        rounded, slopes = [], []
+        for i in range(len(sides)):
+            rows = slice(i * TILE, (i + 1) * TILE)
+            weights = jnp.exp2(scores[rows] * SCALE2 - stat_ref[i, h : h + 1, :])
             spread = stat_ref[i, count + h : count + h + 1, :]
-            slopes = (weights * (pushes - spread)).astype(jnp.bfloat16)
-            key_grad = SCALE * jnp.dot(slopes, query, preferred_element_type=jnp.float32)
-            out_ref[0:TILE, feat] = key_grad.astype(out_ref.dtype)
-            out_ref[TILE : 2 * TILE, feat] = value_grad.astype(out_ref.dtype)
+            rounded.append(weights.astype(jnp.bfloat16))
+            slopes.append((weights * (pushes[rows] - spread)).astype(jnp.bfloat16))
+        rounded, slopes = jnp.concatenate(rounded, axis=0), jnp.concatenate(slopes, axis=0)
+        value_grad = jnp.dot(rounded, grad, preferred_element_type=jnp.float32)
+        key_grad = SCALE * jnp.dot(slopes, query, preferred_element_type=jnp.float32)
+        for i, ref in enumerate(outs):
+            rows = slice(i * TILE, (i + 1) * TILE)
+            ref[0:TILE, feat] = key_grad[rows].astype(ref.dtype)
+            ref[TILE : 2 * TILE, feat] = value_grad[rows].astype(ref.dtype)
 
 
 def fold_kernel(heads, own_ref, got_a, got_b, near_q, far_ref, *near_refs):
@@ -245,16 +247,13 @@
     bf16, f32 = jnp.bfloat16, jnp.float32
     flat = [x.reshape(TILE, feats) for x in (key_tokens, value_tokens, queries, grad_out)]
 
-    kv = stacked(flat[0], flat[1])
+    own_kv = stacked(flat[0], flat[1])
+    kv_a, kv_b = pair_swap(own_kv, "row", 0), pair_swap(own_kv, "row", 1)
+    triple = jax.ShapeDtypeStruct((6 * TILE, feats), bf16)
+    kv = call(regroup_kernel, triple, [VMEM] * 3, VMEM)(own_kv, kv_a, kv_b)
+    kv_fb, kv_fa = pair_swap(kv, "frame", 1), pair_swap(kv, "frame", 0)
     qg = stacked(flat[2], flat[3])
-    kv_a, kv_b = pair_swap(kv, "row", 0), pair_swap(kv, "row", 1)
-    kv_fb, kv_fa = pair_swap(kv, "frame", 1), pair_swap(kv, "frame", 0)
-    rows = call(regroup_kernel, jax.ShapeDtypeStruct((4 * TILE, feats), bf16), [VMEM] * 2, VMEM)(
-        kv_a, kv_b
-    )
-    rows = after(rows, kv_fb, kv_fa)
-    corner_fb, corner_fa = pair_swap(rows, "frame", 1), pair_swap(rows, "frame", 0)
-    qg_late = after(qg, kv_fb, kv_fa)
+    qg_late = after(qg, kv)
     qg_a, qg_b = pair_swap(qg_late, "row", 0), pair_swap(qg_late, "row", 1)
 
     span = TILE // heads
@@ -271,9 +270,9 @@
             wide,
             wide,
         ),
-        [SMEM] + [VMEM] * 9,
+        [SMEM] + [VMEM] * 5,
         (VMEM,) * 6,
-    )(tile_pairs, tile_pairs, qg, kv, kv_a, kv_b, kv_fb, kv_fa, corner_fb, corner_fa)
+    )(tile_pairs, tile_pairs, qg, kv, kv_fb, kv_fa)
     st_a, st_b = pair_swap(stat, "row", 0), pair_swap(stat, "row", 1)
 
     def terms(sides, kinds, *kvs):
@@ -288,7 +287,7 @@
 
     term_b, term_a = terms((2, 1), (bf16, bf16), kv_fb, kv_fa)
     got_b, got_a = pair_swap(term_b, "frame", 1), pair_swap(term_a, "frame", 0)
-    (own,) = terms((0,), (f32,), after(kv, got_a))
+    (own,) = terms((0,), (f32,), after(own_kv, got_a))
     far_q, near_q = call(
         lambda *refs: query_grad_kernel(heads, *refs),
         (pair, near_shape),

time: 85 us -> 84.2 us (level)
  the two profiles are of different devices: /device:TPU:120 before, /device:TPU:75 now
where the time goes in v6:
time: 84.2 us; the launch traced here: 83.7 us
  starting transfers between devices  55.5 us (66%)
  waiting for transfers between devices  16.3 us (19%)
  Pallas kernels  9.95 us (12%)
  other arithmetic  1.09 us (1%)
  between operations  0.89 us (1%)
    ppermute x10, starting transfers between devices, pair_swap(): return lax.ppermute(value, axis, pairs)  37.5 us
    ppermute x4, starting transfers between devices, head_swap(): lax.ppermute(value, 'head', [(i, i ^ k) for i in range(count)])  17.9 us
    ppermute x4, waiting for transfers between devices, head_swap(): lax.ppermute(value, 'head', [(i, i ^ k) for i in range(count)])  8.2 us
    ppermute x10, waiting for transfers between devices, pair_swap(): return lax.ppermute(value, axis, pairs)  8.1 us
    pallas_call x1, Pallas kernels, body(): call(query_kernel, (jax.ShapeDtypeStruct((TILE, feats), bf16), jax.ShapeD...  3.42 us
    pallas_call x2, Pallas kernels, terms(): call(lambda *refs: key_kernel(sides, *refs), [jax.ShapeDtypeStruct((2 * T...  2.88 us
    pallas_call x1, Pallas kernels, body(): call(lambda *refs: query_grad_kernel(heads, *refs), (pair, near_shape), [...  2.28 us
  transfers between devices with their start and end apart: 14, of which 5 were waited for; matrix products, arithmetic and copies ran while one was open for 0% of the time, Pallas kernels for 8%

profile of v6, /device:TPU:75, one launch (start us, length us, event | category | flops | bytes accessed | tf_op | source)
XLA Modules:
  0.0 83.7 jit_solution(9242493509534222821)
XLA Ops:
  0.6 0.0 copy-start.2
  0.6 0.0 copy-start.1
  0.7 1.1 %pad_maximum_fusion.own_ref.refs_0_ = bf16[384,384]{1,0:T(8,128)(2,1)S(1)} fusion(bf16[192,384]{1,0:T(8,128)(2,1)} %bitcast.8, bf16[192,384]{1,0:T(8,128)(2,1)} %bitcast.9), kind=kLoop, calls=%fused_computation | loop fusion | flops 589824 | bytes 589824 | tf_op jit(solution)/shard_map/max | solution.py:241
  1.7 0.0 copy-start
  1.7 1.9 %collective-permute-start = (bf16[384,384]{1,0:T(8,128)(2,1)S(1)}, bf16[384,384]{1,0:T(8,128)(2,1)S(1)}, u32[]{:S(2)}, u32[]{:S(2)}) collective-permute-start(bf16[384,384]{1,0:T(8,128)(2,1)S(1)} %pad_maximum_fusion.own_ref.refs_0_), channel_id=1, source_target_pairs={{0,4},{4,0},{8,12},{12,8},{16,20},{20,16},{24,28},{28,24},{1,5},{5... | collective-permute-start | bytes 884744 | tf_op jit(solution)/shard_map/ppermute | solution.py:37
  3.7 6.1 %collective-permute-start.1 = (bf16[384,384]{1,0:T(8,128)(2,1)S(1)}, bf16[384,384]{1,0:T(8,128)(2,1)S(1)}, u32[]{:S(2)}, u32[]{:S(2)}) collective-permute-start(bf16[384,384]{1,0:T(8,128)(2,1)S(1)} %pad_maximum_fusion.own_ref.refs_0_), channel_id=1, source_target_pairs={{4,8},{8,4},{12,16},{16,12},{20,24},{24,20},{5,9},{9,5},{13,17},{1... | collective-permute-start | bytes 884744 | tf_op jit(solution)/shard_map/ppermute | solution.py:37
  9.7 1.8 %collective-permute-done.a_ref = bf16[384,384]{1,0:T(8,128)(2,1)S(1)} collective-permute-done((bf16[384,384]{1,0:T(8,128)(2,1)S(1)}, bf16[384,384]{1,0:T(8,128)(2,1)S(1)}, u32[]{:S(2)}, u32[]{:S(2)}) %collective-permute-start) | collective-permute-done | bytes 294944 | tf_op jit(solution)/shard_map/ppermute | solution.py:37
  11.5 4.6 %collective-permute-done.1.b_ref = bf16[384,384]{1,0:T(8,128)(2,1)S(1)} collective-permute-done((bf16[384,384]{1,0:T(8,128)(2,1)S(1)}, bf16[384,384]{1,0:T(8,128)(2,1)S(1)}, u32[]{:S(2)}, u32[]{:S(2)}) %collective-permute-start.1) | collective-permute-done | bytes 294944 | tf_op jit(solution)/shard_map/ppermute | solution.py:37
  16.1 0.1 shard_map.84.kv
  16.2 4.6 %collective-permute-start.2 = (bf16[1152,384]{1,0:T(8,128)(2,1)S(1)}, bf16[1152,384]{1,0:T(8,128)(2,1)S(1)}, u32[]{:S(2)}, u32[]{:S(2)}) collective-permute-start(bf16[1152,384]{1,0:T(8,128)(2,1)S(1)} %shard_map.84.kv), channel_id=1, source_target_pairs={{32,64},{64,32},{96,128},{128,96},{160,192},{192,160},{224,256},{2... | collective-permute-start | bytes 2654216 | tf_op jit(solution)/shard_map/ppermute | solution.py:37
  20.8 1.9 %collective-permute-start.3 = (bf16[1152,384]{1,0:T(8,128)(2,1)S(1)}, bf16[1152,384]{1,0:T(8,128)(2,1)S(1)}, u32[]{:S(2)}, u32[]{:S(2)}) collective-permute-start(bf16[1152,384]{1,0:T(8,128)(2,1)S(1)} %shard_map.84.kv), channel_id=1, source_target_pairs={{0,32},{32,0},{64,96},{96,64},{128,160},{160,128},{192,224},{224,1... | collective-permute-start | bytes 2654216 | tf_op jit(solution)/shard_map/ppermute | solution.py:37
  22.7 0.0 copy-done.2
  22.7 0.0 copy-done.1
  22.8 1.9 %collective-permute-start.4 = (bf16[384,384]{1,0:T(8,128)(2,1)S(1)}, bf16[384,384]{1,0:T(8,128)(2,1)S(1)}, u32[]{:S(2)}, u32[]{:S(2)}) collective-permute-start(bf16[384,384]{1,0:T(8,128)(2,1)S(1)} %pad_maximum_fusion.1.own_qg.refs_2_.refs_0_.refs_1_), channel_id=1, source_target_pairs={{0,4},{4,0},{8,12},{12,8},{16,20},{20,16},{24,28},{28,24},{1,5},{5... | collective-permute-start | bytes 884744 | tf_op jit(solution)/shard_map/ppermute | solution.py:37
  24.7 6.4 %collective-permute-start.5 = (bf16[384,384]{1,0:T(8,128)(2,1)S(1)}, bf16[384,384]{1,0:T(8,128)(2,1)S(1)}, u32[]{:S(2)}, u32[]{:S(2)}) collective-permute-start(bf16[384,384]{1,0:T(8,128)(2,1)S(1)} %pad_maximum_fusion.1.own_qg.refs_2_.refs_0_.refs_1_), channel_id=1, source_target_pairs={{4,8},{8,4},{12,16},{16,12},{20,24},{24,20},{5,9},{9,5},{13,17},{1... | collective-permute-start | bytes 884744 | tf_op jit(solution)/shard_map/ppermute | solution.py:37
  31.1 0.7 collective-permute-done.2.kv_fb.refs_0_
  31.8 0.0 collective-permute-done.3.kv_fa.refs_1_
  31.8 0.0 copy-done
  31.8 3.4 %shard_map.85 = (bf16[192,384]{1,0:T(8,128)(2,1)S(1)}, f32[8,192]{1,0:T(8,128)S(1)}, f32[192,128]{1,0:T(8,128)S(1)}, f32[1,1728]{1,0:T(1,128)S(1)}, bf16[1728,38...) custom-call(s32[1,1,1,27]{3,2,1,0:T(1,128)S(1)} %copy-done, s32[1,1,1,27]{3,2,1,0:T(1,128)S(1)} %copy-done, ...), custom_call_target="tpu_custom_call" | custom-call | tf_op jit(solution)/shard_map/pallas_call | solution.py:263
  35.2 1.9 %collective-permute-start.6 = (f32[8,192]{1,0:T(8,128)S(1)}, f32[8,192]{1,0:T(8,128)S(1)}, u32[]{:S(2)}, u32[]{:S(2)}) collective-permute-start(f32[8,192]{1,0:T(8,128)S(1)} %get-tuple-element.27.refs_5_.refs_4_), channel_id=1, source_target_pairs={{0,4},{4,0},{8,12},{12,8},{16,20},{20,16},{24,28},{28,24},{1,5},{5... | collective-permute-start | bytes 18440 | tf_op jit(solution)/shard_map/ppermute | solution.py:37
  37.1 6.4 %collective-permute-start.7 = (f32[8,192]{1,0:T(8,128)S(1)}, f32[8,192]{1,0:T(8,128)S(1)}, u32[]{:S(2)}, u32[]{:S(2)}) collective-permute-start(f32[8,192]{1,0:T(8,128)S(1)} %get-tuple-element.27.refs_5_.refs_4_), channel_id=1, source_target_pairs={{4,8},{8,4},{12,16},{16,12},{20,24},{24,20},{5,9},{9,5},{13,17},{1... | collective-permute-start | bytes 18440 | tf_op jit(solution)/shard_map/ppermute | solution.py:37
  43.5 0.0 collective-permute-done.4.refs_3_.refs_2_
  43.6 0.0 collective-permute-done.5.refs_4_.refs_3_
  43.6 0.0 collective-permute-done.6.refs_6_.refs_5_
  43.6 1.0 %collective-permute-done.7.refs_7_.refs_6_ = f32[8,192]{1,0:T(8,128)S(1)} collective-permute-done((f32[8,192]{1,0:T(8,128)S(1)}, f32[8,192]{1,0:T(8,128)S(1)}, u32[]{:S(2)}, u32[]{:S(2)}) %collective-permute-start.7) | collective-permute-done | bytes 6176 | tf_op jit(solution)/shard_map/ppermute | solution.py:37
  44.6 1.8 %shard_map.86 = (bf16[384,384]{1,0:T(8,128)(2,1)S(1)}, bf16[384,384]{1,0:T(8,128)(2,1)S(1)}) custom-call(bf16[1152,384]{1,0:T(8,128)(2,1)S(1)} %collective-permute-done.2.kv_fb.refs_0_, bf16[1152,384]{1,0:T(8,128)(2,1)S(1)} %collective-permute-done.3.kv_fa.refs_1_, bf16[384,384]{1,0:T(8,128)(2,1)S(1)} %pad_maximum_fusion.1.own_qg.refs_2_.refs_0_.refs_1_, ...), custom_call_target="tpu_custom_call" | custom-call | tf_op jit(solution)/shard_map/pallas_call | solution.py:280
  46.4 3.4 %collective-permute-start.8 = (bf16[384,384]{1,0:T(8,128)(2,1)S(1)}, bf16[384,384]{1,0:T(8,128)(2,1)S(1)}, u32[]{:S(2)}, u32[]{:S(2)}) collective-permute-start(bf16[384,384]{1,0:T(8,128)(2,1)S(1)} %get-tuple-element.28), channel_id=1, source_target_pairs={{0,32},{32,0},{64,96},{96,64},{128,160},{160,128},{192,224},{224,1... | collective-permute-start | bytes 884744 | tf_op jit(solution)/shard_map/ppermute | solution.py:37
  49.8 3.0 %collective-permute-start.10 = (bf16[384,384]{1,0:T(8,128)(2,1)S(1)}, bf16[384,384]{1,0:T(8,128)(2,1)S(1)}, u32[]{:S(2)}, u32[]{:S(2)}) collective-permute-start(bf16[384,384]{1,0:T(8,128)(2,1)S(1)} %get-tuple-element.37), channel_id=1, source_target_pairs={{32,64},{64,32},{96,128},{128,96},{160,192},{192,160},{224,256},{2... | collective-permute-start | bytes 884744 | tf_op jit(solution)/shard_map/ppermute | solution.py:37
  52.8 0.0 collective-permute-done.8.refs_2_
  52.8 2.3 %shard_map.87 = (bf16[2,48,384]{2,1,0:T(8,128)(2,1)S(1)}, bf16[3,2,48,384]{3,2,1,0:T(8,128)(2,1)S(1)}) custom-call(bf16[384,384]{1,0:T(8,128)(2,1)S(1)} %pad_maximum_fusion.1.own_qg.refs_2_.refs_0_.refs_1_, bf16[1728,384]{1,0:T(8,128)(2,1)S(1)} %get-tuple-element.30.refs_1_, bf16[1728,384]{1,0:T(8,128)(2,1)S(1)} %get-tuple-element.31.refs_2_, ...), custom_call_target="tpu_custom_call" | custom-call | tf_op jit(solution)/shard_map/pallas_call | solution.py:291
  55.1 6.6 %collective-permute-start.9 = (bf16[2,48,384]{2,1,0:T(8,128)(2,1)S(1)}, bf16[2,48,384]{2,1,0:T(8,128)(2,1)S(1)}, u32[]{:S(2)}, u32[]{:S(2)}) collective-permute-start(bf16[2,48,384]{2,1,0:T(8,128)(2,1)S(1)} %get-tuple-element.35), channel_id=1, source_target_pairs={{0,2},{1,3},{2,0},{3,1},{4,6},{5,7},{6,4},{7,5},{8,10},{9,11},{10,... | collective-permute-start | bytes 221192 | tf_op jit(solution)/shard_map/ppermute | solution.py:235
  61.7 1.1 %shard_map.88.refs_0_ = f32[384,384]{1,0:T(8,128)S(1)} custom-call(bf16[384,384]{1,0:T(8,128)(2,1)S(1)} %pad_maximum_fusion.own_ref.refs_0_, bf16[384,384]{1,0:T(8,128)(2,1)S(1)} %pad_maximum_fusion.1.own_qg.refs_2_.refs_0_.refs_1_, bf16[384,384]{1,0:T(8,128)(2,1)S(1)} %collective-permute-done.4.refs_3_.refs_2_, ...), custom_call_target="tpu_custom_call" | custom-call | tf_op jit(solution)/shard_map/pallas_call | solution.py:280
  62.8 0.0 collective-permute-done.10.refs_1_
  62.8 0.3 shard_map.89
  63.1 2.4 %collective-permute-start.12 = (bf16[4,48,384]{2,1,0:T(8,128)(2,1)S(1)}, bf16[4,48,384]{2,1,0:T(8,128)(2,1)S(1)}, u32[]{:S(2)}, u32[]{:S(2)}) collective-permute-start(bf16[4,48,384]{2,1,0:T(8,128)(2,1)S(1)} %get-tuple-element.42), channel_id=1, source_target_pairs={{0,1},{1,0},{2,3},{3,2},{4,5},{5,4},{6,7},{7,6},{8,9},{9,8},{10,11... | collective-permute-start | bytes 442376 | tf_op jit(solution)/shard_map/ppermute | solution.py:235
  65.5 2.4 %collective-permute-start.13 = (bf16[4,48,384]{2,1,0:T(8,128)(2,1)S(1)}, bf16[4,48,384]{2,1,0:T(8,128)(2,1)S(1)}, u32[]{:S(2)}, u32[]{:S(2)}) collective-permute-start(bf16[4,48,384]{2,1,0:T(8,128)(2,1)S(1)} %get-tuple-element.43), channel_id=1, source_target_pairs={{0,3},{1,2},{2,1},{3,0},{4,7},{5,6},{6,5},{7,4},{8,11},{9,10},{10,... | collective-permute-start | bytes 442376 | tf_op jit(solution)/shard_map/ppermute | solution.py:235
  67.9 0.0 collective-permute-done.9.refs_0_
  67.9 6.6 %collective-permute-start.11 = (bf16[2,48,384]{2,1,0:T(8,128)(2,1)S(1)}, bf16[2,48,384]{2,1,0:T(8,128)(2,1)S(1)}, u32[]{:S(2)}, u32[]{:S(2)}) collective-permute-start(bf16[2,48,384]{2,1,0:T(8,128)(2,1)S(1)} %get-tuple-element.40), channel_id=1, source_target_pairs={{0,2},{1,3},{2,0},{3,1},{4,6},{5,7},{6,4},{7,5},{8,10},{9,11},{10,... | collective-permute-start | bytes 221192 | tf_op jit(solution)/shard_map/ppermute | solution.py:235
  74.5 0.0 collective-permute-done.12.refs_3_
  74.5 0.0 collective-permute-done.13.refs_4_
  74.5 8.2 %collective-permute-done.11.refs_1_ = bf16[2,48,384]{2,1,0:T(8,128)(2,1)S(1)} collective-permute-done((bf16[2,48,384]{2,1,0:T(8,128)(2,1)S(1)}, bf16[2,48,384]{2,1,0:T(8,128)(2,1)S(1)}, u32[]{:S(2)}, u32[]{:S(2)}) %collective-permute-start.11) | collective-permute-done | bytes 73760 | tf_op jit(solution)/shard_map/ppermute | solution.py:235
  82.7 1.0 %shard_map.90 = (bf16[24,2,1536]{2,1,0:T(2,128)(2,1)}, bf16[24,2,1536]{2,1,0:T(2,128)(2,1)}, bf16[24,2,1536]{2,1,0:T(2,128)(2,1)}, bf16[24,2,1536]{2,1,0:T(2,128)(2,1)}) custom-call(bf16[2,48,384]{2,1,0:T(8,128)(2,1)S(1)} %collective-permute-done.9.refs_0_, bf16[2,48,384]{2,1,0:T(8,128)(2,1)S(1)} %collective-permute-done.11.refs_1_, ...), custom_call_target="tpu_custom_call" | custom-call | tf_op jit(solution)/shard_map/pallas_call | solution.py:309
  (1 shorter events, 0.0 us)
Async XLA Ops:
  0.6 22.1 %copy-start.2 = (bf16[6,4,8,384]{3,2,1,0:T(8,128)(2,1)S(1)}, bf16[6,4,8,384]{3,2,1,0:T(8,128)(2,1)}, u32[]{:S(2)}) copy-start(bf16[6,4,8,384]{3,2,1,0:T(8,128)(2,1)} %param.5) | copy-start | bytes 442372
  0.6 22.1 %copy-start.1 = (bf16[6,4,8,384]{3,2,1,0:T(8,128)(2,1)S(1)}, bf16[6,4,8,384]{3,2,1,0:T(8,128)(2,1)}, u32[]{:S(2)}) copy-start(bf16[6,4,8,384]{3,2,1,0:T(8,128)(2,1)} %param.8) | copy-start | bytes 442372
  1.7 30.1 %copy-start = (s32[1,1,1,27]{3,2,1,0:T(1,128)S(1)}, s32[1,1,1,27]{3,2,1,0:T(1,128)}, u32[]{:S(2)}) copy-start(s32[1,1,1,27]{3,2,1,0:T(1,128)} %pairs_v.1) | copy-start | bytes 328
  1.7 9.8 %collective-permute-start = (bf16[384,384]{1,0:T(8,128)(2,1)S(1)}, bf16[384,384]{1,0:T(8,128)(2,1)S(1)}, u32[]{:S(2)}, u32[]{:S(2)}) collective-permute-start(bf16[384,384]{1,0:T(8,128)(2,1)S(1)} %pad_maximum_fusion.own_ref.refs_0_), channel_id=1, source_target_pairs={{0,4},{4,0},{8,12},{12,8},{16,20},{20,16},{24,28},{28,24},{1,5},{5... | collective-permute-start | bytes 884744 | tf_op jit(solution)/shard_map/ppermute | solution.py:37
  3.7 12.5 %collective-permute-start.1 = (bf16[384,384]{1,0:T(8,128)(2,1)S(1)}, bf16[384,384]{1,0:T(8,128)(2,1)S(1)}, u32[]{:S(2)}, u32[]{:S(2)}) collective-permute-start(bf16[384,384]{1,0:T(8,128)(2,1)S(1)} %pad_maximum_fusion.own_ref.refs_0_), channel_id=1, source_target_pairs={{4,8},{8,4},{12,16},{16,12},{20,24},{24,20},{5,9},{9,5},{13,17},{1... | collective-permute-start | bytes 884744 | tf_op jit(solution)/shard_map/ppermute | solution.py:37
  16.2 15.6 %collective-permute-start.2 = (bf16[1152,384]{1,0:T(8,128)(2,1)S(1)}, bf16[1152,384]{1,0:T(8,128)(2,1)S(1)}, u32[]{:S(2)}, u32[]{:S(2)}) collective-permute-start(bf16[1152,384]{1,0:T(8,128)(2,1)S(1)} %shard_map.84.kv), channel_id=1, source_target_pairs={{32,64},{64,32},{96,128},{128,96},{160,192},{192,160},{224,256},{2... | collective-permute-start | bytes 2654216 | tf_op jit(solution)/shard_map/ppermute | solution.py:37
  20.8 11.0 %collective-permute-start.3 = (bf16[1152,384]{1,0:T(8,128)(2,1)S(1)}, bf16[1152,384]{1,0:T(8,128)(2,1)S(1)}, u32[]{:S(2)}, u32[]{:S(2)}) collective-permute-start(bf16[1152,384]{1,0:T(8,128)(2,1)S(1)} %shard_map.84.kv), channel_id=1, source_target_pairs={{0,32},{32,0},{64,96},{96,64},{128,160},{160,128},{192,224},{224,1... | collective-permute-start | bytes 2654216 | tf_op jit(solution)/shard_map/ppermute | solution.py:37
  22.8 20.8 %collective-permute-start.4 = (bf16[384,384]{1,0:T(8,128)(2,1)S(1)}, bf16[384,384]{1,0:T(8,128)(2,1)S(1)}, u32[]{:S(2)}, u32[]{:S(2)}) collective-permute-start(bf16[384,384]{1,0:T(8,128)(2,1)S(1)} %pad_maximum_fusion.1.own_qg.refs_2_.refs_0_.refs_1_), channel_id=1, source_target_pairs={{0,4},{4,0},{8,12},{12,8},{16,20},{20,16},{24,28},{28,24},{1,5},{5... | collective-permute-start | bytes 884744 | tf_op jit(solution)/shard_map/ppermute | solution.py:37
  24.7 18.9 %collective-permute-start.5 = (bf16[384,384]{1,0:T(8,128)(2,1)S(1)}, bf16[384,384]{1,0:T(8,128)(2,1)S(1)}, u32[]{:S(2)}, u32[]{:S(2)}) collective-permute-start(bf16[384,384]{1,0:T(8,128)(2,1)S(1)} %pad_maximum_fusion.1.own_qg.refs_2_.refs_0_.refs_1_), channel_id=1, source_target_pairs={{4,8},{8,4},{12,16},{16,12},{20,24},{24,20},{5,9},{9,5},{13,17},{1... | collective-permute-start | bytes 884744 | tf_op jit(solution)/shard_map/ppermute | solution.py:37
  35.2 8.4 %collective-permute-start.6 = (f32[8,192]{1,0:T(8,128)S(1)}, f32[8,192]{1,0:T(8,128)S(1)}, u32[]{:S(2)}, u32[]{:S(2)}) collective-permute-start(f32[8,192]{1,0:T(8,128)S(1)} %get-tuple-element.27.refs_5_.refs_4_), channel_id=1, source_target_pairs={{0,4},{4,0},{8,12},{12,8},{16,20},{20,16},{24,28},{28,24},{1,5},{5... | collective-permute-start | bytes 18440 | tf_op jit(solution)/shard_map/ppermute | solution.py:37
  37.1 7.4 %collective-permute-start.7 = (f32[8,192]{1,0:T(8,128)S(1)}, f32[8,192]{1,0:T(8,128)S(1)}, u32[]{:S(2)}, u32[]{:S(2)}) collective-permute-start(f32[8,192]{1,0:T(8,128)S(1)} %get-tuple-element.27.refs_5_.refs_4_), channel_id=1, source_target_pairs={{4,8},{8,4},{12,16},{16,12},{20,24},{24,20},{5,9},{9,5},{13,17},{1... | collective-permute-start | bytes 18440 | tf_op jit(solution)/shard_map/ppermute | solution.py:37
  46.4 6.4 %collective-permute-start.8 = (bf16[384,384]{1,0:T(8,128)(2,1)S(1)}, bf16[384,384]{1,0:T(8,128)(2,1)S(1)}, u32[]{:S(2)}, u32[]{:S(2)}) collective-permute-start(bf16[384,384]{1,0:T(8,128)(2,1)S(1)} %get-tuple-element.28), channel_id=1, source_target_pairs={{0,32},{32,0},{64,96},{96,64},{128,160},{160,128},{192,224},{224,1... | collective-permute-start | bytes 884744 | tf_op jit(solution)/shard_map/ppermute | solution.py:37
  49.8 13.0 %collective-permute-start.10 = (bf16[384,384]{1,0:T(8,128)(2,1)S(1)}, bf16[384,384]{1,0:T(8,128)(2,1)S(1)}, u32[]{:S(2)}, u32[]{:S(2)}) collective-permute-start(bf16[384,384]{1,0:T(8,128)(2,1)S(1)} %get-tuple-element.37), channel_id=1, source_target_pairs={{32,64},{64,32},{96,128},{128,96},{160,192},{192,160},{224,256},{2... | collective-permute-start | bytes 884744 | tf_op jit(solution)/shard_map/ppermute | solution.py:37
  55.1 12.8 %collective-permute-start.9 = (bf16[2,48,384]{2,1,0:T(8,128)(2,1)S(1)}, bf16[2,48,384]{2,1,0:T(8,128)(2,1)S(1)}, u32[]{:S(2)}, u32[]{:S(2)}) collective-permute-start(bf16[2,48,384]{2,1,0:T(8,128)(2,1)S(1)} %get-tuple-element.35), channel_id=1, source_target_pairs={{0,2},{1,3},{2,0},{3,1},{4,6},{5,7},{6,4},{7,5},{8,10},{9,11},{10,... | collective-permute-start | bytes 221192 | tf_op jit(solution)/shard_map/ppermute | solution.py:235
  63.1 11.4 %collective-permute-start.12 = (bf16[4,48,384]{2,1,0:T(8,128)(2,1)S(1)}, bf16[4,48,384]{2,1,0:T(8,128)(2,1)S(1)}, u32[]{:S(2)}, u32[]{:S(2)}) collective-permute-start(bf16[4,48,384]{2,1,0:T(8,128)(2,1)S(1)} %get-tuple-element.42), channel_id=1, source_target_pairs={{0,1},{1,0},{2,3},{3,2},{4,5},{5,4},{6,7},{7,6},{8,9},{9,8},{10,11... | collective-permute-start | bytes 442376 | tf_op jit(solution)/shard_map/ppermute | solution.py:235
  65.5 9.0 %collective-permute-start.13 = (bf16[4,48,384]{2,1,0:T(8,128)(2,1)S(1)}, bf16[4,48,384]{2,1,0:T(8,128)(2,1)S(1)}, u32[]{:S(2)}, u32[]{:S(2)}) collective-permute-start(bf16[4,48,384]{2,1,0:T(8,128)(2,1)S(1)} %get-tuple-element.43), channel_id=1, source_target_pairs={{0,3},{1,2},{2,1},{3,0},{4,7},{5,6},{6,5},{7,4},{8,11},{9,10},{10,... | collective-permute-start | bytes 442376 | tf_op jit(solution)/shard_map/ppermute | solution.py:235
  67.9 14.8 %collective-permute-start.11 = (bf16[2,48,384]{2,1,0:T(8,128)(2,1)S(1)}, bf16[2,48,384]{2,1,0:T(8,128)(2,1)S(1)}, u32[]{:S(2)}, u32[]{:S(2)}) collective-permute-start(bf16[2,48,384]{2,1,0:T(8,128)(2,1)S(1)} %get-tuple-element.40), channel_id=1, source_target_pairs={{0,2},{1,3},{2,0},{3,1},{4,6},{5,7},{6,4},{7,5},{8,10},{9,11},{10,... | collective-permute-start | bytes 221192 | tf_op jit(solution)/shard_map/ppermute | solution.py:235

commit v7 on v6

--- a/solution.py
+++ b/solution.py
@@ -46,9 +46,11 @@
     return [(a, b) for a in slot_steps("frame") for b in slot_steps("row")]
 
 
-def regroup_kernel(own_ref, a_ref, b_ref, out_ref):
-    for i, ref in enumerate((own_ref, a_ref, b_ref)):
-        out_ref[2 * TILE * i : 2 * TILE * (i + 1), :] = ref[...]
+def regroup_kernel(a_ref, b_ref, rows_ref, far_ref):
+    for ref in (rows_ref, far_ref):
+        ref[0 : 2 * TILE, :] = a_ref[...]
+        ref[2 * TILE : 4 * TILE, :] = b_ref[...]
+    far_ref[4 * TILE :, :] = jnp.zeros((16, far_ref.shape[1]), far_ref.dtype)
 
 
 def gather_near(tiles, first_ref, second_ref):
@@ -100,11 +102,13 @@
             put(k, i, ref[i])
 
 
-def query_kernel(pairs_s, pairs_v, own_qg, kv, kv_fb, kv_fa, *refs):
+def query_kernel(pairs_s, pairs_v, own_qg, kv, kv_rows, corner_fa, corner_fb, kv_fb, kv_fa, *refs):
     attended_ref, stat_ref, column_ref, bias_ref, key_ref, value_ref = refs
     frame, row = lax.axis_index("frame"), lax.axis_index("row")
     frames, rows = lax.axis_size("frame"), lax.axis_size("row")
-    tiles = [(ref, 2 * TILE * i) for ref in (kv, kv_fa, kv_fb) for i in range(3)]
+    tiles = []
+    for own, corners in ((kv, kv_rows), (kv_fa, corner_fa), (kv_fb, corner_fb)):
+        tiles += [(own, 0), (corners, 0), (corners, 2 * TILE)]
     gather_near(tiles, key_ref, value_ref)
     lane = lax.broadcasted_iota(jnp.int32, (1, WIDE), 1)
     bias = jnp.zeros((1, WIDE), jnp.float32)
@@ -211,12 +215,15 @@
         key_grad = SCALE * jnp.dot(slopes, query, preferred_element_type=jnp.float32)
         for i, ref in enumerate(outs):
             rows = slice(i * TILE, (i + 1) * TILE)
+            if ref.shape[0] > 2 * TILE:
+                ref[2 * TILE :, feat] = jnp.zeros((16, HEAD_DIM), ref.dtype)
             ref[0:TILE, feat] = key_grad[rows].astype(ref.dtype)
             ref[TILE : 2 * TILE, feat] = value_grad[rows].astype(ref.dtype)
 
 
-def fold_kernel(heads, own_ref, got_a, got_b, near_q, far_ref, *near_refs):
-    total = own_ref[...] + got_a[...].astype(jnp.float32) + got_b[...].astype(jnp.float32)
+def fold_kernel(heads, own_ref, got_b, got_a, near_q, far_ref, *near_refs):
+    total = own_ref[...] + got_a[...].astype(jnp.float32)
+    total += got_b[0 : 2 * TILE, :].astype(jnp.float32)
     total = total.astype(jnp.bfloat16)
     blocks = column_blocks([total[0:TILE]], [total[TILE : 2 * TILE]], heads)
     for i in range(2):
@@ -249,11 +256,13 @@
 
     own_kv = stacked(flat[0], flat[1])
     kv_a, kv_b = pair_swap(own_kv, "row", 0), pair_swap(own_kv, "row", 1)
-    triple = jax.ShapeDtypeStruct((6 * TILE, feats), bf16)
-    kv = call(regroup_kernel, triple, [VMEM] * 3, VMEM)(own_kv, kv_a, kv_b)
-    kv_fb, kv_fa = pair_swap(kv, "frame", 1), pair_swap(kv, "frame", 0)
+    kv_fb, kv_fa = pair_swap(own_kv, "frame", 1), pair_swap(own_kv, "frame", 0)
+    two = [jax.ShapeDtypeStruct((4 * TILE + extra, feats), bf16) for extra in (0, 16)]
+    rows, far_rows = call(regroup_kernel, two, [VMEM] * 2, (VMEM, VMEM))(kv_a, kv_b)
+    corner_fb = pair_swap(far_rows, "frame", 1)
+    corner_fa = pair_swap(after(rows, kv_fb, kv_fa), "frame", 0)
     qg = stacked(flat[2], flat[3])
-    qg_late = after(qg, kv)
+    qg_late = after(qg, rows)
     qg_a, qg_b = pair_swap(qg_late, "row", 0), pair_swap(qg_late, "row", 1)
 
     span = TILE // heads
@@ -270,24 +279,24 @@
             wide,
             wide,
         ),
-        [SMEM] + [VMEM] * 5,
+        [SMEM] + [VMEM] * 8,
         (VMEM,) * 6,
-    )(tile_pairs, tile_pairs, qg, kv, kv_fb, kv_fa)
+    )(tile_pairs, tile_pairs, qg, own_kv, rows, corner_fa, corner_fb, kv_fb, kv_fa)
     st_a, st_b = pair_swap(stat, "row", 0), pair_swap(stat, "row", 1)
 
     def terms(sides, kinds, *kvs):
         row_near = pltpu.VMEM((3 * TILE, feats), bf16)
         return call(
             lambda *refs: key_kernel(sides, *refs),
-            [jax.ShapeDtypeStruct((2 * TILE, feats), kind) for kind in kinds],
+            [jax.ShapeDtypeStruct((2 * TILE + extra, feats), kind) for kind, extra in kinds],
             [VMEM] * (len(sides) + 6),
             [VMEM] * len(sides),
             [row_near, row_near, pltpu.VMEM((len(sides), 8, 3 * TILE), f32)],
         )(*kvs, qg, qg_a, qg_b, stat, st_a, st_b)
 
-    term_b, term_a = terms((2, 1), (bf16, bf16), kv_fb, kv_fa)
+    term_b, term_a = terms((2, 1), ((bf16, 16), (bf16, 0)), kv_fb, kv_fa)
     got_b, got_a = pair_swap(term_b, "frame", 1), pair_swap(term_a, "frame", 0)
-    (own,) = terms((0,), (f32,), after(own_kv, got_a))
+    (own,) = terms((0,), ((f32, 0),), after(own_kv, got_a))
     far_q, near_q = call(
         lambda *refs: query_grad_kernel(heads, *refs),
         (pair, near_shape),

time: 84.2 us -> 84 us (level)
  the two profiles are of different devices: /device:TPU:75 before, /device:TPU:72 now
where the time goes in v7:
time: 84 us; the launch traced here: 83.3 us
  starting transfers between devices  59.4 us (71%)
  waiting for transfers between devices  11.2 us (13%)
  Pallas kernels  9.81 us (12%)
  other arithmetic  2.03 us (2%)
  between operations  0.88 us (1%)
    ppermute x12, starting transfers between devices, pair_swap(): return lax.ppermute(value, axis, pairs)  40.3 us
    ppermute x4, starting transfers between devices, head_swap(): lax.ppermute(value, 'head', [(i, i ^ k) for i in range(count)])  19.1 us
    ppermute x4, waiting for transfers between devices, head_swap(): lax.ppermute(value, 'head', [(i, i ^ k) for i in range(count)])  6.93 us
    ppermute x12, waiting for transfers between devices, pair_swap(): return lax.ppermute(value, axis, pairs)  4.26 us
    pallas_call x1, Pallas kernels, body(): call(query_kernel, (jax.ShapeDtypeStruct((TILE, feats), bf16), jax.ShapeD...  3.4 us
    pallas_call x2, Pallas kernels, terms(): call(lambda *refs: key_kernel(sides, *refs), [jax.ShapeDtypeStruct((2 * T...  2.87 us
    pallas_call x1, Pallas kernels, body(): call(lambda *refs: query_grad_kernel(heads, *refs), (pair, near_shape), [...  2.14 us
    max x2, other arithmetic, stacked(): jnp.maximum(low, jnp.pad(second, ((rows, 0), (0, 0)), constant_values=-jn...  2.03 us
  transfers between devices with their start and end apart: 16, of which 5 were waited for; matrix products, arithmetic and copies ran while one was open for 1% of the time, Pallas kernels for 8%

profile of v7, /device:TPU:72, one launch (start us, length us, event | category | flops | bytes accessed | tf_op | source)
XLA Modules:
  0.0 83.3 jit_solution(4261800955261825035)
XLA Ops:
  0.6 0.0 copy-start
  0.6 1.0 %pad_maximum_fusion.kv.refs_0_ = bf16[384,384]{1,0:T(8,128)(2,1)S(1)} fusion(bf16[192,384]{1,0:T(8,128)(2,1)} %bitcast.8, bf16[192,384]{1,0:T(8,128)(2,1)} %bitcast.9), kind=kLoop, calls=%fused_computation | loop fusion | flops 589824 | bytes 589824 | tf_op jit(solution)/shard_map/max | solution.py:248
  1.7 1.9 %collective-permute-start.2 = (bf16[384,384]{1,0:T(8,128)(2,1)S(1)}, bf16[384,384]{1,0:T(8,128)(2,1)S(1)}, u32[]{:S(2)}, u32[]{:S(2)}) collective-permute-start(bf16[384,384]{1,0:T(8,128)(2,1)S(1)} %pad_maximum_fusion.kv.refs_0_), channel_id=1, source_target_pairs={{0,4},{4,0},{8,12},{12,8},{16,20},{20,16},{24,28},{28,24},{1,5},{5... | collective-permute-start | bytes 884744 | tf_op jit(solution)/shard_map/ppermute | solution.py:37
  3.6 6.6 %collective-permute-start.3 = (bf16[384,384]{1,0:T(8,128)(2,1)S(1)}, bf16[384,384]{1,0:T(8,128)(2,1)S(1)}, u32[]{:S(2)}, u32[]{:S(2)}) collective-permute-start(bf16[384,384]{1,0:T(8,128)(2,1)S(1)} %pad_maximum_fusion.kv.refs_0_), channel_id=1, source_target_pairs={{4,8},{8,4},{12,16},{16,12},{20,24},{24,20},{5,9},{9,5},{13,17},{1... | collective-permute-start | bytes 884744 | tf_op jit(solution)/shard_map/ppermute | solution.py:37
  10.2 3.4 %collective-permute-start = (bf16[384,384]{1,0:T(8,128)(2,1)S(1)}, bf16[384,384]{1,0:T(8,128)(2,1)S(1)}, u32[]{:S(2)}, u32[]{:S(2)}) collective-permute-start(bf16[384,384]{1,0:T(8,128)(2,1)S(1)} %pad_maximum_fusion.kv.refs_0_), channel_id=1, source_target_pairs={{32,64},{64,32},{96,128},{128,96},{160,192},{192,160},{224,256},{2... | collective-permute-start | bytes 884744 | tf_op jit(solution)/shard_map/ppermute | solution.py:37
  13.7 2.0 %collective-permute-start.1 = (bf16[384,384]{1,0:T(8,128)(2,1)S(1)}, bf16[384,384]{1,0:T(8,128)(2,1)S(1)}, u32[]{:S(2)}, u32[]{:S(2)}) collective-permute-start(bf16[384,384]{1,0:T(8,128)(2,1)S(1)} %pad_maximum_fusion.kv.refs_0_), channel_id=1, source_target_pairs={{0,32},{32,0},{64,96},{96,64},{128,160},{160,128},{192,224},{224,1... | collective-permute-start | bytes 884744 | tf_op jit(solution)/shard_map/ppermute | solution.py:37
  15.7 0.0 collective-permute-done.2.a_ref
  15.7 1.3 %collective-permute-done.3.b_ref = bf16[384,384]{1,0:T(8,128)(2,1)S(1)} collective-permute-done((bf16[384,384]{1,0:T(8,128)(2,1)S(1)}, bf16[384,384]{1,0:T(8,128)(2,1)S(1)}, u32[]{:S(2)}, u32[]{:S(2)}) %collective-permute-start.3) | collective-permute-done | bytes 294944 | tf_op jit(solution)/shard_map/ppermute | solution.py:37
  17.0 0.1 shard_map.84
  17.1 3.1 %collective-permute-start.7 = (bf16[784,384]{1,0:T(8,128)(2,1)S(1)}, bf16[784,384]{1,0:T(8,128)(2,1)S(1)}, u32[]{:S(2)}, u32[]{:S(2)}) collective-permute-start(bf16[784,384]{1,0:T(8,128)(2,1)S(1)} %get-tuple-element.32), channel_id=1, source_target_pairs={{32,64},{64,32},{96,128},{128,96},{160,192},{192,160},{224,256},{2... | collective-permute-start | bytes 1806344 | tf_op jit(solution)/shard_map/ppermute | solution.py:37
  20.2 0.2 collective-permute-done.kv_fb.refs_0_
  20.4 0.0 collective-permute-done.1.kv_fa.refs_1_
  20.4 2.1 %collective-permute-start.6 = (bf16[768,384]{1,0:T(8,128)(2,1)S(1)}, bf16[768,384]{1,0:T(8,128)(2,1)S(1)}, u32[]{:S(2)}, u32[]{:S(2)}) collective-permute-start(bf16[768,384]{1,0:T(8,128)(2,1)S(1)} %get-tuple-element.31.kv_rows), channel_id=1, source_target_pairs={{0,32},{32,0},{64,96},{96,64},{128,160},{160,128},{192,224},{224,1... | collective-permute-start | bytes 1769480 | tf_op jit(solution)/shard_map/ppermute | solution.py:37
  22.5 1.0 %pad_maximum_fusion.1.own_qg.refs_2_.refs_0_.refs_1_ = bf16[384,384]{1,0:T(8,128)(2,1)S(1)} fusion(bf16[192,384]{1,0:T(8,128)(2,1)} %bitcast.10, bf16[192,384]{1,0:T(8,128)(2,1)} %bitcast.11), kind=kLoop, calls=%fused_computation.1 | loop fusion | flops 589824 | bytes 589824 | tf_op jit(solution)/shard_map/max | solution.py:248
  23.5 1.9 %collective-permute-start.4 = (bf16[384,384]{1,0:T(8,128)(2,1)S(1)}, bf16[384,384]{1,0:T(8,128)(2,1)S(1)}, u32[]{:S(2)}, u32[]{:S(2)}) collective-permute-start(bf16[384,384]{1,0:T(8,128)(2,1)S(1)} %pad_maximum_fusion.1.own_qg.refs_2_.refs_0_.refs_1_), channel_id=1, source_target_pairs={{0,4},{4,0},{8,12},{12,8},{16,20},{20,16},{24,28},{28,24},{1,5},{5... | collective-permute-start | bytes 884744 | tf_op jit(solution)/shard_map/ppermute | solution.py:37
  25.5 7.0 %collective-permute-start.5 = (bf16[384,384]{1,0:T(8,128)(2,1)S(1)}, bf16[384,384]{1,0:T(8,128)(2,1)S(1)}, u32[]{:S(2)}, u32[]{:S(2)}) collective-permute-start(bf16[384,384]{1,0:T(8,128)(2,1)S(1)} %pad_maximum_fusion.1.own_qg.refs_2_.refs_0_.refs_1_), channel_id=1, source_target_pairs={{4,8},{8,4},{12,16},{16,12},{20,24},{24,20},{5,9},{9,5},{13,17},{1... | collective-permute-start | bytes 884744 | tf_op jit(solution)/shard_map/ppermute | solution.py:37
  32.4 0.0 collective-permute-done.6.corner_fa
  32.4 0.0 collective-permute-done.7.corner_fb
  32.4 0.0 copy-done
  32.5 3.4 %shard_map.85 = (bf16[192,384]{1,0:T(8,128)(2,1)S(1)}, f32[8,192]{1,0:T(8,128)S(1)}, f32[192,128]{1,0:T(8,128)S(1)}, f32[1,1728]{1,0:T(1,128)S(1)}, bf16[1728,38...) custom-call(s32[1,1,1,27]{3,2,1,0:T(1,128)S(1)} %copy-done, s32[1,1,1,27]{3,2,1,0:T(1,128)S(1)} %copy-done, ...), custom_call_target="tpu_custom_call" | custom-call | tf_op jit(solution)/shard_map/pallas_call | solution.py:272
  35.9 1.9 %collective-permute-start.8 = (f32[8,192]{1,0:T(8,128)S(1)}, f32[8,192]{1,0:T(8,128)S(1)}, u32[]{:S(2)}, u32[]{:S(2)}) collective-permute-start(f32[8,192]{1,0:T(8,128)S(1)} %get-tuple-element.33.refs_5_.refs_4_), channel_id=1, source_target_pairs={{0,4},{4,0},{8,12},{12,8},{16,20},{20,16},{24,28},{28,24},{1,5},{5... | collective-permute-start | bytes 18440 | tf_op jit(solution)/shard_map/ppermute | solution.py:37
  37.8 5.0 %collective-permute-start.9 = (f32[8,192]{1,0:T(8,128)S(1)}, f32[8,192]{1,0:T(8,128)S(1)}, u32[]{:S(2)}, u32[]{:S(2)}) collective-permute-start(f32[8,192]{1,0:T(8,128)S(1)} %get-tuple-element.33.refs_5_.refs_4_), channel_id=1, source_target_pairs={{4,8},{8,4},{12,16},{16,12},{20,24},{24,20},{5,9},{9,5},{13,17},{1... | collective-permute-start | bytes 18440 | tf_op jit(solution)/shard_map/ppermute | solution.py:37
  42.8 0.0 collective-permute-done.4.refs_3_.refs_2_
  42.8 0.0 collective-permute-done.5.refs_4_.refs_3_
  42.8 0.0 collective-permute-done.8.refs_6_.refs_5_
  42.8 1.6 %collective-permute-done.9.refs_7_.refs_6_ = f32[8,192]{1,0:T(8,128)S(1)} collective-permute-done((f32[8,192]{1,0:T(8,128)S(1)}, f32[8,192]{1,0:T(8,128)S(1)}, u32[]{:S(2)}, u32[]{:S(2)}) %collective-permute-start.9) | collective-permute-done | bytes 6176 | tf_op jit(solution)/shard_map/ppermute | solution.py:37
  44.4 1.8 %shard_map.86 = (bf16[400,384]{1,0:T(8,128)(2,1)S(1)}, bf16[384,384]{1,0:T(8,128)(2,1)S(1)}) custom-call(bf16[384,384]{1,0:T(8,128)(2,1)S(1)} %collective-permute-done.kv_fb.refs_0_, bf16[384,384]{1,0:T(8,128)(2,1)S(1)} %collective-permute-done.1.kv_fa.refs_1_, bf16[384,384]{1,0:T(8,128)(2,1)S(1)} %pad_maximum_fusion.1.own_qg.refs_2_.refs_0_.refs_1_, ...), custom_call_target="tpu_custom_call" | custom-call | tf_op jit(solution)/shard_map/pallas_call | solution.py:289
  46.2 2.6 %collective-permute-start.12 = (bf16[400,384]{1,0:T(8,128)(2,1)S(1)}, bf16[400,384]{1,0:T(8,128)(2,1)S(1)}, u32[]{:S(2)}, u32[]{:S(2)}) collective-permute-start(bf16[400,384]{1,0:T(8,128)(2,1)S(1)} %get-tuple-element.43), channel_id=1, source_target_pairs={{32,64},{64,32},{96,128},{128,96},{160,192},{192,160},{224,256},{2... | collective-permute-start | bytes 921608 | tf_op jit(solution)/shard_map/ppermute | solution.py:37
  48.8 2.7 %collective-permute-start.10 = (bf16[384,384]{1,0:T(8,128)(2,1)S(1)}, bf16[384,384]{1,0:T(8,128)(2,1)S(1)}, u32[]{:S(2)}, u32[]{:S(2)}) collective-permute-start(bf16[384,384]{1,0:T(8,128)(2,1)S(1)} %get-tuple-element.34), channel_id=1, source_target_pairs={{0,32},{32,0},{64,96},{96,64},{128,160},{160,128},{192,224},{224,1... | collective-permute-start | bytes 884744 | tf_op jit(solution)/shard_map/ppermute | solution.py:37
  51.5 1.2 %collective-permute-done.10.refs_2_ = bf16[384,384]{1,0:T(8,128)(2,1)S(1)} collective-permute-done((bf16[384,384]{1,0:T(8,128)(2,1)S(1)}, bf16[384,384]{1,0:T(8,128)(2,1)S(1)}, u32[]{:S(2)}, u32[]{:S(2)}) %collective-permute-start.10) | collective-permute-done | bytes 294944 | tf_op jit(solution)/shard_map/ppermute | solution.py:37
  52.7 2.1 %shard_map.87 = (bf16[2,48,384]{2,1,0:T(8,128)(2,1)S(1)}, bf16[3,2,48,384]{3,2,1,0:T(8,128)(2,1)S(1)}) custom-call(bf16[384,384]{1,0:T(8,128)(2,1)S(1)} %pad_maximum_fusion.1.own_qg.refs_2_.refs_0_.refs_1_, bf16[1728,384]{1,0:T(8,128)(2,1)S(1)} %get-tuple-element.36.refs_1_, bf16[1728,384]{1,0:T(8,128)(2,1)S(1)} %get-tuple-element.37.refs_2_, ...), custom_call_target="tpu_custom_call" | custom-call | tf_op jit(solution)/shard_map/pallas_call | solution.py:300
  54.8 6.8 %collective-permute-start.11 = (bf16[2,48,384]{2,1,0:T(8,128)(2,1)S(1)}, bf16[2,48,384]{2,1,0:T(8,128)(2,1)S(1)}, u32[]{:S(2)}, u32[]{:S(2)}) collective-permute-start(bf16[2,48,384]{2,1,0:T(8,128)(2,1)S(1)} %get-tuple-element.41), channel_id=1, source_target_pairs={{0,2},{1,3},{2,0},{3,1},{4,6},{5,7},{6,4},{7,5},{8,10},{9,11},{10,... | collective-permute-start | bytes 221192 | tf_op jit(solution)/shard_map/ppermute | solution.py:242
  61.7 1.1 %shard_map.88.refs_0_ = f32[384,384]{1,0:T(8,128)S(1)} custom-call(bf16[384,384]{1,0:T(8,128)(2,1)S(1)} %pad_maximum_fusion.kv.refs_0_, bf16[384,384]{1,0:T(8,128)(2,1)S(1)} %pad_maximum_fusion.1.own_qg.refs_2_.refs_0_.refs_1_, bf16[384,384]{1,0:T(8,128)(2,1)S(1)} %collective-permute-done.4.refs_3_.refs_2_, ...), custom_call_target="tpu_custom_call" | custom-call | tf_op jit(solution)/shard_map/pallas_call | solution.py:289
  62.8 0.0 collective-permute-done.12.refs_1_
  62.8 0.3 shard_map.89
  63.1 2.7 %collective-permute-start.14 = (bf16[4,48,384]{2,1,0:T(8,128)(2,1)S(1)}, bf16[4,48,384]{2,1,0:T(8,128)(2,1)S(1)}, u32[]{:S(2)}, u32[]{:S(2)}) collective-permute-start(bf16[4,48,384]{2,1,0:T(8,128)(2,1)S(1)} %get-tuple-element.48), channel_id=1, source_target_pairs={{0,1},{1,0},{2,3},{3,2},{4,5},{5,4},{6,7},{7,6},{8,9},{9,8},{10,11... | collective-permute-start | bytes 442376 | tf_op jit(solution)/shard_map/ppermute | solution.py:242
  65.8 2.7 %collective-permute-start.15 = (bf16[4,48,384]{2,1,0:T(8,128)(2,1)S(1)}, bf16[4,48,384]{2,1,0:T(8,128)(2,1)S(1)}, u32[]{:S(2)}, u32[]{:S(2)}) collective-permute-start(bf16[4,48,384]{2,1,0:T(8,128)(2,1)S(1)} %get-tuple-element.49), channel_id=1, source_target_pairs={{0,3},{1,2},{2,1},{3,0},{4,7},{5,6},{6,5},{7,4},{8,11},{9,10},{10,... | collective-permute-start | bytes 442376 | tf_op jit(solution)/shard_map/ppermute | solution.py:242
  68.5 0.0 collective-permute-done.11.refs_0_
  68.5 6.8 %collective-permute-start.13 = (bf16[2,48,384]{2,1,0:T(8,128)(2,1)S(1)}, bf16[2,48,384]{2,1,0:T(8,128)(2,1)S(1)}, u32[]{:S(2)}, u32[]{:S(2)}) collective-permute-start(bf16[2,48,384]{2,1,0:T(8,128)(2,1)S(1)} %get-tuple-element.46), channel_id=1, source_target_pairs={{0,2},{1,3},{2,0},{3,1},{4,6},{5,7},{6,4},{7,5},{8,10},{9,11},{10,... | collective-permute-start | bytes 221192 | tf_op jit(solution)/shard_map/ppermute | solution.py:242
  75.4 6.9 %collective-permute-done.13.refs_1_ = bf16[2,48,384]{2,1,0:T(8,128)(2,1)S(1)} collective-permute-done((bf16[2,48,384]{2,1,0:T(8,128)(2,1)S(1)}, bf16[2,48,384]{2,1,0:T(8,128)(2,1)S(1)}, u32[]{:S(2)}, u32[]{:S(2)}) %collective-permute-start.13) | collective-permute-done | bytes 73760 | tf_op jit(solution)/shard_map/ppermute | solution.py:242
  82.3 0.0 collective-permute-done.14.refs_3_
  82.3 0.0 collective-permute-done.15.refs_4_
  82.3 1.0 %shard_map.90 = (bf16[24,2,1536]{2,1,0:T(2,128)(2,1)}, bf16[24,2,1536]{2,1,0:T(2,128)(2,1)}, bf16[24,2,1536]{2,1,0:T(2,128)(2,1)}, bf16[24,2,1536]{2,1,0:T(2,128)(2,1)}) custom-call(bf16[2,48,384]{2,1,0:T(8,128)(2,1)S(1)} %collective-permute-done.11.refs_0_, bf16[2,48,384]{2,1,0:T(8,128)(2,1)S(1)} %collective-permute-done.13.refs_1_, ...), custom_call_target="tpu_custom_call" | custom-call | tf_op jit(solution)/shard_map/pallas_call | solution.py:318
Async XLA Ops:
  0.6 31.8 %copy-start = (s32[1,1,1,27]{3,2,1,0:T(1,128)S(1)}, s32[1,1,1,27]{3,2,1,0:T(1,128)}, u32[]{:S(2)}) copy-start(s32[1,1,1,27]{3,2,1,0:T(1,128)} %pairs_v.1) | copy-start | bytes 328
  1.7 14.0 %collective-permute-start.2 = (bf16[384,384]{1,0:T(8,128)(2,1)S(1)}, bf16[384,384]{1,0:T(8,128)(2,1)S(1)}, u32[]{:S(2)}, u32[]{:S(2)}) collective-permute-start(bf16[384,384]{1,0:T(8,128)(2,1)S(1)} %pad_maximum_fusion.kv.refs_0_), channel_id=1, source_target_pairs={{0,4},{4,0},{8,12},{12,8},{16,20},{20,16},{24,28},{28,24},{1,5},{5... | collective-permute-start | bytes 884744 | tf_op jit(solution)/shard_map/ppermute | solution.py:37
  3.6 13.4 %collective-permute-start.3 = (bf16[384,384]{1,0:T(8,128)(2,1)S(1)}, bf16[384,384]{1,0:T(8,128)(2,1)S(1)}, u32[]{:S(2)}, u32[]{:S(2)}) collective-permute-start(bf16[384,384]{1,0:T(8,128)(2,1)S(1)} %pad_maximum_fusion.kv.refs_0_), channel_id=1, source_target_pairs={{4,8},{8,4},{12,16},{16,12},{20,24},{24,20},{5,9},{9,5},{13,17},{1... | collective-permute-start | bytes 884744 | tf_op jit(solution)/shard_map/ppermute | solution.py:37
  10.2 10.2 %collective-permute-start = (bf16[384,384]{1,0:T(8,128)(2,1)S(1)}, bf16[384,384]{1,0:T(8,128)(2,1)S(1)}, u32[]{:S(2)}, u32[]{:S(2)}) collective-permute-start(bf16[384,384]{1,0:T(8,128)(2,1)S(1)} %pad_maximum_fusion.kv.refs_0_), channel_id=1, source_target_pairs={{32,64},{64,32},{96,128},{128,96},{160,192},{192,160},{224,256},{2... | collective-permute-start | bytes 884744 | tf_op jit(solution)/shard_map/ppermute | solution.py:37
  13.7 6.7 %collective-permute-start.1 = (bf16[384,384]{1,0:T(8,128)(2,1)S(1)}, bf16[384,384]{1,0:T(8,128)(2,1)S(1)}, u32[]{:S(2)}, u32[]{:S(2)}) collective-permute-start(bf16[384,384]{1,0:T(8,128)(2,1)S(1)} %pad_maximum_fusion.kv.refs_0_), channel_id=1, source_target_pairs={{0,32},{32,0},{64,96},{96,64},{128,160},{160,128},{192,224},{224,1... | collective-permute-start | bytes 884744 | tf_op jit(solution)/shard_map/ppermute | solution.py:37
  17.1 15.4 %collective-permute-start.7 = (bf16[784,384]{1,0:T(8,128)(2,1)S(1)}, bf16[784,384]{1,0:T(8,128)(2,1)S(1)}, u32[]{:S(2)}, u32[]{:S(2)}) collective-permute-start(bf16[784,384]{1,0:T(8,128)(2,1)S(1)} %get-tuple-element.32), channel_id=1, source_target_pairs={{32,64},{64,32},{96,128},{128,96},{160,192},{192,160},{224,256},{2... | collective-permute-start | bytes 1806344 | tf_op jit(solution)/shard_map/ppermute | solution.py:37
  20.4 12.0 %collective-permute-start.6 = (bf16[768,384]{1,0:T(8,128)(2,1)S(1)}, bf16[768,384]{1,0:T(8,128)(2,1)S(1)}, u32[]{:S(2)}, u32[]{:S(2)}) collective-permute-start(bf16[768,384]{1,0:T(8,128)(2,1)S(1)} %get-tuple-element.31.kv_rows), channel_id=1, source_target_pairs={{0,32},{32,0},{64,96},{96,64},{128,160},{160,128},{192,224},{224,1... | collective-permute-start | bytes 1769480 | tf_op jit(solution)/shard_map/ppermute | solution.py:37
  23.5 19.3 %collective-permute-start.4 = (bf16[384,384]{1,0:T(8,128)(2,1)S(1)}, bf16[384,384]{1,0:T(8,128)(2,1)S(1)}, u32[]{:S(2)}, u32[]{:S(2)}) collective-permute-start(bf16[384,384]{1,0:T(8,128)(2,1)S(1)} %pad_maximum_fusion.1.own_qg.refs_2_.refs_0_.refs_1_), channel_id=1, source_target_pairs={{0,4},{4,0},{8,12},{12,8},{16,20},{20,16},{24,28},{28,24},{1,5},{5... | collective-permute-start | bytes 884744 | tf_op jit(solution)/shard_map/ppermute | solution.py:37
  25.5 17.3 %collective-permute-start.5 = (bf16[384,384]{1,0:T(8,128)(2,1)S(1)}, bf16[384,384]{1,0:T(8,128)(2,1)S(1)}, u32[]{:S(2)}, u32[]{:S(2)}) collective-permute-start(bf16[384,384]{1,0:T(8,128)(2,1)S(1)} %pad_maximum_fusion.1.own_qg.refs_2_.refs_0_.refs_1_), channel_id=1, source_target_pairs={{4,8},{8,4},{12,16},{16,12},{20,24},{24,20},{5,9},{9,5},{13,17},{1... | collective-permute-start | bytes 884744 | tf_op jit(solution)/shard_map/ppermute | solution.py:37
  35.9 7.0 %collective-permute-start.8 = (f32[8,192]{1,0:T(8,128)S(1)}, f32[8,192]{1,0:T(8,128)S(1)}, u32[]{:S(2)}, u32[]{:S(2)}) collective-permute-start(f32[8,192]{1,0:T(8,128)S(1)} %get-tuple-element.33.refs_5_.refs_4_), channel_id=1, source_target_pairs={{0,4},{4,0},{8,12},{12,8},{16,20},{20,16},{24,28},{28,24},{1,5},{5... | collective-permute-start | bytes 18440 | tf_op jit(solution)/shard_map/ppermute | solution.py:37
  37.8 6.6 %collective-permute-start.9 = (f32[8,192]{1,0:T(8,128)S(1)}, f32[8,192]{1,0:T(8,128)S(1)}, u32[]{:S(2)}, u32[]{:S(2)}) collective-permute-start(f32[8,192]{1,0:T(8,128)S(1)} %get-tuple-element.33.refs_5_.refs_4_), channel_id=1, source_target_pairs={{4,8},{8,4},{12,16},{16,12},{20,24},{24,20},{5,9},{9,5},{13,17},{1... | collective-permute-start | bytes 18440 | tf_op jit(solution)/shard_map/ppermute | solution.py:37
  46.2 16.6 %collective-permute-start.12 = (bf16[400,384]{1,0:T(8,128)(2,1)S(1)}, bf16[400,384]{1,0:T(8,128)(2,1)S(1)}, u32[]{:S(2)}, u32[]{:S(2)}) collective-permute-start(bf16[400,384]{1,0:T(8,128)(2,1)S(1)} %get-tuple-element.43), channel_id=1, source_target_pairs={{32,64},{64,32},{96,128},{128,96},{160,192},{192,160},{224,256},{2... | collective-permute-start | bytes 921608 | tf_op jit(solution)/shard_map/ppermute | solution.py:37
  48.8 3.9 %collective-permute-start.10 = (bf16[384,384]{1,0:T(8,128)(2,1)S(1)}, bf16[384,384]{1,0:T(8,128)(2,1)S(1)}, u32[]{:S(2)}, u32[]{:S(2)}) collective-permute-start(bf16[384,384]{1,0:T(8,128)(2,1)S(1)} %get-tuple-element.34), channel_id=1, source_target_pairs={{0,32},{32,0},{64,96},{96,64},{128,160},{160,128},{192,224},{224,1... | collective-permute-start | bytes 884744 | tf_op jit(solution)/shard_map/ppermute | solution.py:37
  54.8 13.7 %collective-permute-start.11 = (bf16[2,48,384]{2,1,0:T(8,128)(2,1)S(1)}, bf16[2,48,384]{2,1,0:T(8,128)(2,1)S(1)}, u32[]{:S(2)}, u32[]{:S(2)}) collective-permute-start(bf16[2,48,384]{2,1,0:T(8,128)(2,1)S(1)} %get-tuple-element.41), channel_id=1, source_target_pairs={{0,2},{1,3},{2,0},{3,1},{4,6},{5,7},{6,4},{7,5},{8,10},{9,11},{10,... | collective-permute-start | bytes 221192 | tf_op jit(solution)/shard_map/ppermute | solution.py:242
  63.1 19.2 %collective-permute-start.14 = (bf16[4,48,384]{2,1,0:T(8,128)(2,1)S(1)}, bf16[4,48,384]{2,1,0:T(8,128)(2,1)S(1)}, u32[]{:S(2)}, u32[]{:S(2)}) collective-permute-start(bf16[4,48,384]{2,1,0:T(8,128)(2,1)S(1)} %get-tuple-element.48), channel_id=1, source_target_pairs={{0,1},{1,0},{2,3},{3,2},{4,5},{5,4},{6,7},{7,6},{8,9},{9,8},{10,11... | collective-permute-start | bytes 442376 | tf_op jit(solution)/shard_map/ppermute | solution.py:242
  65.8 16.5 %collective-permute-start.15 = (bf16[4,48,384]{2,1,0:T(8,128)(2,1)S(1)}, bf16[4,48,384]{2,1,0:T(8,128)(2,1)S(1)}, u32[]{:S(2)}, u32[]{:S(2)}) collective-permute-start(bf16[4,48,384]{2,1,0:T(8,128)(2,1)S(1)} %get-tuple-element.49), channel_id=1, source_target_pairs={{0,3},{1,2},{2,1},{3,0},{4,7},{5,6},{6,5},{7,4},{8,11},{9,10},{10,... | collective-permute-start | bytes 442376 | tf_op jit(solution)/shard_map/ppermute | solution.py:242
  68.5 13.8 %collective-permute-start.13 = (bf16[2,48,384]{2,1,0:T(8,128)(2,1)S(1)}, bf16[2,48,384]{2,1,0:T(8,128)(2,1)S(1)}, u32[]{:S(2)}, u32[]{:S(2)}) collective-permute-start(bf16[2,48,384]{2,1,0:T(8,128)(2,1)S(1)} %get-tuple-element.46), channel_id=1, source_target_pairs={{0,2},{1,3},{2,0},{3,1},{4,6},{5,7},{6,4},{7,5},{8,10},{9,11},{10,... | collective-permute-start | bytes 221192 | tf_op jit(solution)/shard_map/ppermute | solution.py:242

commit v8 on v7

--- a/solution.py
+++ b/solution.py
@@ -81,25 +81,19 @@
     ]
 
 
-def near_heads(heads):
-    return [k for k in range(heads) if k != heads // 2]
-
-
-def assemble_kernel(heads, far_q, far_k, *refs):
-    near_refs, out_refs = refs[: heads - 1], refs[heads - 1 :]
-    feats = far_q.shape[2]
+def far_first(heads):
+    return [heads // 2] + [k for k in range(heads) if k != heads // 2]
+
+
+def assemble_kernel(*refs):
+    heads = len(refs) - 4
+    got_refs, out_refs = refs[:heads], refs[heads:]
+    feats = got_refs[0].shape[2]
     me = lax.axis_index("head")
-
-    def put(k, i, rows):
+    for k, ref in zip(far_first(heads), got_refs):
         place = pl.ds(pl.multiple_of((me ^ k) * feats, HEAD_DIM), feats)
-        out_refs[i][:, :, place] = rows.reshape(out_refs[i].shape[:2] + (feats,))
-
-    for i in range(2):
-        put(heads // 2, i, far_q[i])
-        put(heads // 2, 2 + i, far_k[i])
-    for k, ref in zip(near_heads(heads), near_refs):
-        for i in range(4):
-            put(k, i, ref[i])
+        for i, out_ref in enumerate(out_refs):
+            out_ref[:, :, place] = ref[i].reshape(out_ref.shape[:2] + (feats,))
 
 
 def query_kernel(pairs_s, pairs_v, own_qg, kv, kv_rows, corner_fa, corner_fb, kv_fb, kv_fa, *refs):
@@ -146,8 +140,7 @@
     stat_ref[7:8, 0:27] = pairs_v[0, 0].astype(jnp.float32)
 
 
-def query_grad_kernel(heads, own_qg, key_ref, value_ref, attended_ref, column_ref, bias_ref, *refs):
-    far_ref, near_ref = refs
+def query_grad_kernel(own_qg, key_ref, value_ref, attended_ref, column_ref, bias_ref, send_ref):
     bias = bias_ref[...]
     count = own_qg.shape[1] // HEAD_DIM
     grad_parts = []
@@ -166,11 +159,10 @@
         slopes = (weights * (pushes - spread)).astype(jnp.bfloat16)
         query_grad = SCALE * jnp.dot(slopes, key, preferred_element_type=jnp.float32)
         grad_parts.append(query_grad.astype(jnp.bfloat16))
-    blocks = column_blocks([attended_ref[...]], grad_parts, heads)
-    for i in range(2):
-        far_ref[i] = blocks[heads // 2][i]
-        for at, k in enumerate(near_heads(heads)):
-            near_ref[at, i] = blocks[k][i]
+    blocks = column_blocks([attended_ref[...]], grad_parts, send_ref.shape[0])
+    for k, pair in enumerate(blocks):
+        for i in range(2):
+            send_ref[k, i] = pair[i]
 
 
 def key_kernel(sides, *refs):
@@ -221,15 +213,14 @@
             ref[TILE : 2 * TILE, feat] = value_grad[rows].astype(ref.dtype)
 
 
-def fold_kernel(heads, own_ref, got_b, got_a, near_q, far_ref, *near_refs):
+def fold_kernel(own_ref, got_b, got_a, query_blocks, *send_refs):
     total = own_ref[...] + got_a[...].astype(jnp.float32)
     total += got_b[0 : 2 * TILE, :].astype(jnp.float32)
     total = total.astype(jnp.bfloat16)
-    blocks = column_blocks([total[0:TILE]], [total[TILE : 2 * TILE]], heads)
-    for i in range(2):
-        far_ref[i] = blocks[heads // 2][i]
-        for at, (k, ref) in enumerate(zip(near_heads(heads), near_refs)):
-            ref[i] = near_q[at, i]
+    blocks = column_blocks([total[0:TILE]], [total[TILE : 2 * TILE]], len(send_refs))
+    for k, ref in enumerate(send_refs):
+        for i in range(2):
+            ref[i] = query_blocks[k, i]
             ref[2 + i] = blocks[k][i]
 
 
@@ -257,17 +248,15 @@
     own_kv = stacked(flat[0], flat[1])
     kv_a, kv_b = pair_swap(own_kv, "row", 0), pair_swap(own_kv, "row", 1)
     kv_fb, kv_fa = pair_swap(own_kv, "frame", 1), pair_swap(own_kv, "frame", 0)
+    qg = stacked(flat[2], flat[3])
     two = [jax.ShapeDtypeStruct((4 * TILE + extra, feats), bf16) for extra in (0, 16)]
-    rows, far_rows = call(regroup_kernel, two, [VMEM] * 2, (VMEM, VMEM))(kv_a, kv_b)
+    rows, far_rows = call(regroup_kernel, two, [VMEM] * 2, (VMEM, VMEM))(after(kv_a, qg), kv_b)
     corner_fb = pair_swap(far_rows, "frame", 1)
     corner_fa = pair_swap(after(rows, kv_fb, kv_fa), "frame", 0)
-    qg = stacked(flat[2], flat[3])
     qg_late = after(qg, rows)
     qg_a, qg_b = pair_swap(qg_late, "row", 0), pair_swap(qg_late, "row", 1)
 
     span = TILE // heads
-    pair, four = (jax.ShapeDtypeStruct((n, span, feats), bf16) for n in (2, 4))
-    near_shape = jax.ShapeDtypeStruct((heads - 1, 2, span, feats), bf16)
     wide = jax.ShapeDtypeStruct((WIDE, feats), bf16)
     attended, stat, column, bias, key_near, value_near = call(
         query_kernel,
@@ -297,30 +286,22 @@
     term_b, term_a = terms((2, 1), ((bf16, 16), (bf16, 0)), kv_fb, kv_fa)
     got_b, got_a = pair_swap(term_b, "frame", 1), pair_swap(term_a, "frame", 0)
     (own,) = terms((0,), ((f32, 0),), after(own_kv, got_a))
-    far_q, near_q = call(
-        lambda *refs: query_grad_kernel(heads, *refs),
-        (pair, near_shape),
+    sent_q = call(
+        query_grad_kernel,
+        jax.ShapeDtypeStruct((heads, 2, span, feats), bf16),
         [VMEM] * 6,
-        (VMEM, VMEM),
+        VMEM,
     )(after(qg, got_a), key_near, value_near, attended, column, bias)
-    got_far_q = head_swap(far_q, heads // 2)
-
-    far_k, *near_k = call(
-        lambda *refs: fold_kernel(heads, *refs),
-        [pair] + [four] * (heads - 1),
+    sent = call(
+        fold_kernel,
+        [jax.ShapeDtypeStruct((4, span, feats), bf16)] * heads,
         [VMEM] * 4,
         [VMEM] * heads,
-    )(own, got_b, got_a, near_q)
-    got_far_k = head_swap(after(far_k, got_far_q), heads // 2)
-    got_near = [head_swap(sent, k) for k, sent in zip(near_heads(heads), near_k)]
+    )(own, got_b, got_a, sent_q)
+    got = [head_swap(sent[k], k) for k in far_first(heads)]
 
     out = jax.ShapeDtypeStruct((frames_dev * rows_dev, columns // heads, heads * feats), bf16)
-    outs = call(
-        lambda *refs: assemble_kernel(heads, *refs),
-        [out] * 4,
-        [VMEM] * (heads + 1),
-        [VMEM] * 4,
-    )(got_far_q, got_far_k, *got_near)
+    outs = call(assemble_kernel, [out] * 4, [VMEM] * heads, [VMEM] * 4)(*got)
     return tuple(x.reshape((frames_dev, rows_dev) + out.shape[1:]) for x in outs)
 
 

time: 84 us -> 80.2 us (0.955)
  the two profiles are of different devices: /device:TPU:72 before, /device:TPU:88 now
where the time goes in v8:
time: 80.2 us; the launch traced here: 79.6 us
  starting transfers between devices  53.5 us (67%)
  waiting for transfers between devices  13.4 us (17%)
  Pallas kernels  9.84 us (12%)
  other arithmetic  2.03 us (3%)
  between operations  0.87 us (1%)
    ppermute x12, starting transfers between devices, pair_swap(): return lax.ppermute(value, axis, pairs)  41.3 us
    ppermute x3, starting transfers between devices, head_swap(): lax.ppermute(value, 'head', [(i, i ^ k) for i in range(count)])  12.2 us
    ppermute x3, waiting for transfers between devices, head_swap(): lax.ppermute(value, 'head', [(i, i ^ k) for i in range(count)])  9.61 us
    ppermute x12, waiting for transfers between devices, pair_swap(): return lax.ppermute(value, axis, pairs)  3.79 us
    pallas_call x1, Pallas kernels, body(): call(query_kernel, (jax.ShapeDtypeStruct((TILE, feats), bf16), jax.ShapeD...  3.4 us
    pallas_call x2, Pallas kernels, terms(): call(lambda *refs: key_kernel(sides, *refs), [jax.ShapeDtypeStruct((2 * T...  2.87 us
    pallas_call x1, Pallas kernels, body(): call(query_grad_kernel, jax.ShapeDtypeStruct((heads, 2, span, feats), bf1...  2.16 us
    max x2, other arithmetic, stacked(): jnp.maximum(low, jnp.pad(second, ((rows, 0), (0, 0)), constant_values=-jn...  2.03 us
  transfers between devices with their start and end apart: 15, of which 7 were waited for; matrix products, arithmetic and copies ran while one was open for 1% of the time, Pallas kernels for 8%

profile of v8, /device:TPU:88, one launch (start us, length us, event | category | flops | bytes accessed | tf_op | source)
XLA Modules:
  0.0 79.6 jit_solution(738470528322746297)
XLA Ops:
  0.6 0.0 copy-start
  0.6 1.0 %pad_maximum_fusion.1.kv.refs_0_ = bf16[384,384]{1,0:T(8,128)(2,1)S(1)} fusion(bf16[192,384]{1,0:T(8,128)(2,1)} %bitcast.8, bf16[192,384]{1,0:T(8,128)(2,1)} %bitcast.9), kind=kLoop, calls=%fused_computation.1 | loop fusion | flops 589824 | bytes 589824 | tf_op jit(solution)/shard_map/max | solution.py:239
  1.7 1.9 %collective-permute-start.2 = (bf16[384,384]{1,0:T(8,128)(2,1)S(1)}, bf16[384,384]{1,0:T(8,128)(2,1)S(1)}, u32[]{:S(2)}, u32[]{:S(2)}) collective-permute-start(bf16[384,384]{1,0:T(8,128)(2,1)S(1)} %pad_maximum_fusion.1.kv.refs_0_), channel_id=1, source_target_pairs={{0,4},{4,0},{8,12},{12,8},{16,20},{20,16},{24,28},{28,24},{1,5},{5... | collective-permute-start | bytes 884744 | tf_op jit(solution)/shard_map/ppermute | solution.py:37
  3.6 6.6 %collective-permute-start.3 = (bf16[384,384]{1,0:T(8,128)(2,1)S(1)}, bf16[384,384]{1,0:T(8,128)(2,1)S(1)}, u32[]{:S(2)}, u32[]{:S(2)}) collective-permute-start(bf16[384,384]{1,0:T(8,128)(2,1)S(1)} %pad_maximum_fusion.1.kv.refs_0_), channel_id=1, source_target_pairs={{4,8},{8,4},{12,16},{16,12},{20,24},{24,20},{5,9},{9,5},{13,17},{1... | collective-permute-start | bytes 884744 | tf_op jit(solution)/shard_map/ppermute | solution.py:37
  10.2 3.4 %collective-permute-start = (bf16[384,384]{1,0:T(8,128)(2,1)S(1)}, bf16[384,384]{1,0:T(8,128)(2,1)S(1)}, u32[]{:S(2)}, u32[]{:S(2)}) collective-permute-start(bf16[384,384]{1,0:T(8,128)(2,1)S(1)} %pad_maximum_fusion.1.kv.refs_0_), channel_id=1, source_target_pairs={{32,64},{64,32},{96,128},{128,96},{160,192},{192,160},{224,256},{2... | collective-permute-start | bytes 884744 | tf_op jit(solution)/shard_map/ppermute | solution.py:37
  13.7 2.0 %collective-permute-start.1 = (bf16[384,384]{1,0:T(8,128)(2,1)S(1)}, bf16[384,384]{1,0:T(8,128)(2,1)S(1)}, u32[]{:S(2)}, u32[]{:S(2)}) collective-permute-start(bf16[384,384]{1,0:T(8,128)(2,1)S(1)} %pad_maximum_fusion.1.kv.refs_0_), channel_id=1, source_target_pairs={{0,32},{32,0},{64,96},{96,64},{128,160},{160,128},{192,224},{224,1... | collective-permute-start | bytes 884744 | tf_op jit(solution)/shard_map/ppermute | solution.py:37
  15.7 1.0 %pad_maximum_fusion.own_qg.refs_2_.refs_1_ = bf16[384,384]{1,0:T(8,128)(2,1)S(1)} fusion(bf16[192,384]{1,0:T(8,128)(2,1)} %bitcast.10, bf16[192,384]{1,0:T(8,128)(2,1)} %bitcast.11), kind=kLoop, calls=%fused_computation | loop fusion | flops 589824 | bytes 589824 | tf_op jit(solution)/shard_map/max | solution.py:239
  16.7 0.0 collective-permute-done.2.a_ref
  16.7 0.2 collective-permute-done.3.b_ref
  17.0 0.1 shard_map.84
  17.1 3.9 %collective-permute-start.7 = (bf16[784,384]{1,0:T(8,128)(2,1)S(1)}, bf16[784,384]{1,0:T(8,128)(2,1)S(1)}, u32[]{:S(2)}, u32[]{:S(2)}) collective-permute-start(bf16[784,384]{1,0:T(8,128)(2,1)S(1)} %get-tuple-element.31), channel_id=1, source_target_pairs={{32,64},{64,32},{96,128},{128,96},{160,192},{192,160},{224,256},{2... | collective-permute-start | bytes 1806344 | tf_op jit(solution)/shard_map/ppermute | solution.py:37
  21.0 0.0 collective-permute-done.kv_fb.refs_0_
  21.0 0.0 collective-permute-done.1.kv_fa.refs_1_
  21.0 1.9 %collective-permute-start.6 = (bf16[768,384]{1,0:T(8,128)(2,1)S(1)}, bf16[768,384]{1,0:T(8,128)(2,1)S(1)}, u32[]{:S(2)}, u32[]{:S(2)}) collective-permute-start(bf16[768,384]{1,0:T(8,128)(2,1)S(1)} %get-tuple-element.30.kv_rows), channel_id=1, source_target_pairs={{0,32},{32,0},{64,96},{96,64},{128,160},{160,128},{192,224},{224,1... | collective-permute-start | bytes 1769480 | tf_op jit(solution)/shard_map/ppermute | solution.py:37
  23.0 1.9 %collective-permute-start.4 = (bf16[384,384]{1,0:T(8,128)(2,1)S(1)}, bf16[384,384]{1,0:T(8,128)(2,1)S(1)}, u32[]{:S(2)}, u32[]{:S(2)}) collective-permute-start(bf16[384,384]{1,0:T(8,128)(2,1)S(1)} %pad_maximum_fusion.own_qg.refs_2_.refs_1_), channel_id=1, source_target_pairs={{0,4},{4,0},{8,12},{12,8},{16,20},{20,16},{24,28},{28,24},{1,5},{5... | collective-permute-start | bytes 884744 | tf_op jit(solution)/shard_map/ppermute | solution.py:37
  24.9 7.0 %collective-permute-start.5 = (bf16[384,384]{1,0:T(8,128)(2,1)S(1)}, bf16[384,384]{1,0:T(8,128)(2,1)S(1)}, u32[]{:S(2)}, u32[]{:S(2)}) collective-permute-start(bf16[384,384]{1,0:T(8,128)(2,1)S(1)} %pad_maximum_fusion.own_qg.refs_2_.refs_1_), channel_id=1, source_target_pairs={{4,8},{8,4},{12,16},{16,12},{20,24},{24,20},{5,9},{9,5},{13,17},{1... | collective-permute-start | bytes 884744 | tf_op jit(solution)/shard_map/ppermute | solution.py:37
  31.8 0.0 collective-permute-done.6.corner_fa
  31.9 0.0 collective-permute-done.7.corner_fb
  31.9 0.0 copy-done
  31.9 3.4 %shard_map.85 = (bf16[192,384]{1,0:T(8,128)(2,1)S(1)}, f32[8,192]{1,0:T(8,128)S(1)}, f32[192,128]{1,0:T(8,128)S(1)}, f32[1,1728]{1,0:T(1,128)S(1)}, bf16[1728,38...) custom-call(s32[1,1,1,27]{3,2,1,0:T(1,128)S(1)} %copy-done, s32[1,1,1,27]{3,2,1,0:T(1,128)S(1)} %copy-done, ...), custom_call_target="tpu_custom_call" | custom-call | tf_op jit(solution)/shard_map/pallas_call | solution.py:261
  35.3 1.9 %collective-permute-start.8 = (f32[8,192]{1,0:T(8,128)S(1)}, f32[8,192]{1,0:T(8,128)S(1)}, u32[]{:S(2)}, u32[]{:S(2)}) collective-permute-start(f32[8,192]{1,0:T(8,128)S(1)} %get-tuple-element.32.refs_5_.refs_4_), channel_id=1, source_target_pairs={{0,4},{4,0},{8,12},{12,8},{16,20},{20,16},{24,28},{28,24},{1,5},{5... | collective-permute-start | bytes 18440 | tf_op jit(solution)/shard_map/ppermute | solution.py:37
  37.2 5.6 %collective-permute-start.9 = (f32[8,192]{1,0:T(8,128)S(1)}, f32[8,192]{1,0:T(8,128)S(1)}, u32[]{:S(2)}, u32[]{:S(2)}) collective-permute-start(f32[8,192]{1,0:T(8,128)S(1)} %get-tuple-element.32.refs_5_.refs_4_), channel_id=1, source_target_pairs={{4,8},{8,4},{12,16},{16,12},{20,24},{24,20},{5,9},{9,5},{13,17},{1... | collective-permute-start | bytes 18440 | tf_op jit(solution)/shard_map/ppermute | solution.py:37
  42.8 0.0 collective-permute-done.4.refs_3_.refs_2_
  42.8 0.0 collective-permute-done.5.refs_4_.refs_3_
  42.8 0.0 collective-permute-done.8.refs_6_.refs_5_
  42.8 1.6 %collective-permute-done.9.refs_7_.refs_6_ = f32[8,192]{1,0:T(8,128)S(1)} collective-permute-done((f32[8,192]{1,0:T(8,128)S(1)}, f32[8,192]{1,0:T(8,128)S(1)}, u32[]{:S(2)}, u32[]{:S(2)}) %collective-permute-start.9) | collective-permute-done | bytes 6176 | tf_op jit(solution)/shard_map/ppermute | solution.py:37
  44.4 1.8 %shard_map.86 = (bf16[400,384]{1,0:T(8,128)(2,1)S(1)}, bf16[384,384]{1,0:T(8,128)(2,1)S(1)}) custom-call(bf16[384,384]{1,0:T(8,128)(2,1)S(1)} %collective-permute-done.kv_fb.refs_0_, bf16[384,384]{1,0:T(8,128)(2,1)S(1)} %collective-permute-done.1.kv_fa.refs_1_, bf16[384,384]{1,0:T(8,128)(2,1)S(1)} %pad_maximum_fusion.own_qg.refs_2_.refs_1_, ...), custom_call_target="tpu_custom_call" | custom-call | tf_op jit(solution)/shard_map/pallas_call | solution.py:278
  46.2 3.2 %collective-permute-start.11 = (bf16[400,384]{1,0:T(8,128)(2,1)S(1)}, bf16[400,384]{1,0:T(8,128)(2,1)S(1)}, u32[]{:S(2)}, u32[]{:S(2)}) collective-permute-start(bf16[400,384]{1,0:T(8,128)(2,1)S(1)} %get-tuple-element.35), channel_id=1, source_target_pairs={{32,64},{64,32},{96,128},{128,96},{160,192},{192,160},{224,256},{2... | collective-permute-start | bytes 921608 | tf_op jit(solution)/shard_map/ppermute | solution.py:37
  49.4 1.9 %collective-permute-start.10 = (bf16[384,384]{1,0:T(8,128)(2,1)S(1)}, bf16[384,384]{1,0:T(8,128)(2,1)S(1)}, u32[]{:S(2)}, u32[]{:S(2)}) collective-permute-start(bf16[384,384]{1,0:T(8,128)(2,1)S(1)} %get-tuple-element.33), channel_id=1, source_target_pairs={{0,32},{32,0},{64,96},{96,64},{128,160},{160,128},{192,224},{224,1... | collective-permute-start | bytes 884744 | tf_op jit(solution)/shard_map/ppermute | solution.py:37
  51.3 1.5 %collective-permute-done.10.got_a = bf16[384,384]{1,0:T(8,128)(2,1)S(1)} collective-permute-done((bf16[384,384]{1,0:T(8,128)(2,1)S(1)}, bf16[384,384]{1,0:T(8,128)(2,1)S(1)}, u32[]{:S(2)}, u32[]{:S(2)}) %collective-permute-start.10) | collective-permute-done | bytes 294944 | tf_op jit(solution)/shard_map/ppermute | solution.py:37
  52.8 2.2 %shard_map.88.query_blocks = bf16[4,2,48,384]{3,2,1,0:T(8,128)(2,1)S(1)} custom-call(bf16[384,384]{1,0:T(8,128)(2,1)S(1)} %pad_maximum_fusion.own_qg.refs_2_.refs_1_, bf16[1728,384]{1,0:T(8,128)(2,1)S(1)} %get-tuple-element.37.key_ref, bf16[1728,384]{1,0:T(8,128)(2,1)S(1)} %get-tuple-element.38.value_ref, ...), custom_call_target="tpu_custom_call" | custom-call | tf_op jit(solution)/shard_map/pallas_call | solution.py:289
  55.0 1.1 %shard_map.87.own_ref = f32[384,384]{1,0:T(8,128)S(1)} custom-call(bf16[384,384]{1,0:T(8,128)(2,1)S(1)} %pad_maximum_fusion.1.kv.refs_0_, bf16[384,384]{1,0:T(8,128)(2,1)S(1)} %pad_maximum_fusion.own_qg.refs_2_.refs_1_, bf16[384,384]{1,0:T(8,128)(2,1)S(1)} %collective-permute-done.4.refs_3_.refs_2_, ...), custom_call_target="tpu_custom_call" | custom-call | tf_op jit(solution)/shard_map/pallas_call | solution.py:278
  56.1 0.4 collective-permute-done.11.got_b
  56.5 0.3 shard_map.89
  56.8 5.6 %collective-permute-start.12 = (bf16[4,48,384]{2,1,0:T(8,128)(2,1)S(1)}, bf16[4,48,384]{2,1,0:T(8,128)(2,1)S(1)}, u32[]{:S(2)}, u32[]{:S(2)}) collective-permute-start(bf16[4,48,384]{2,1,0:T(8,128)(2,1)S(1)} %get-tuple-element.42), channel_id=1, source_target_pairs={{0,2},{1,3},{2,0},{3,1},{4,6},{5,7},{6,4},{7,5},{8,10},{9,11},{10,... | collective-permute-start | bytes 442376 | tf_op jit(solution)/shard_map/ppermute | solution.py:233
  62.5 4.0 %collective-permute-start.13 = (bf16[4,48,384]{2,1,0:T(8,128)(2,1)S(1)}, bf16[4,48,384]{2,1,0:T(8,128)(2,1)S(1)}, u32[]{:S(2)}, u32[]{:S(2)}) collective-permute-start(bf16[4,48,384]{2,1,0:T(8,128)(2,1)S(1)} %get-tuple-element.44), channel_id=1, source_target_pairs={{0,1},{1,0},{2,3},{3,2},{4,5},{5,4},{6,7},{7,6},{8,9},{9,8},{10,11... | collective-permute-start | bytes 442376 | tf_op jit(solution)/shard_map/ppermute | solution.py:233
  66.5 2.5 %collective-permute-start.14 = (bf16[4,48,384]{2,1,0:T(8,128)(2,1)S(1)}, bf16[4,48,384]{2,1,0:T(8,128)(2,1)S(1)}, u32[]{:S(2)}, u32[]{:S(2)}) collective-permute-start(bf16[4,48,384]{2,1,0:T(8,128)(2,1)S(1)} %get-tuple-element.45), channel_id=1, source_target_pairs={{0,3},{1,2},{2,1},{3,0},{4,7},{5,6},{6,5},{7,4},{8,11},{9,10},{10,... | collective-permute-start | bytes 442376 | tf_op jit(solution)/shard_map/ppermute | solution.py:233
  69.0 3.1 %collective-permute-done.12.refs_0_ = bf16[4,48,384]{2,1,0:T(8,128)(2,1)S(1)} collective-permute-done((bf16[4,48,384]{2,1,0:T(8,128)(2,1)S(1)}, bf16[4,48,384]{2,1,0:T(8,128)(2,1)S(1)}, u32[]{:S(2)}, u32[]{:S(2)}) %collective-permute-start.12) | collective-permute-done | bytes 147488 | tf_op jit(solution)/shard_map/ppermute | solution.py:233
  72.1 4.6 %collective-permute-done.13.refs_2_ = bf16[4,48,384]{2,1,0:T(8,128)(2,1)S(1)} collective-permute-done((bf16[4,48,384]{2,1,0:T(8,128)(2,1)S(1)}, bf16[4,48,384]{2,1,0:T(8,128)(2,1)S(1)}, u32[]{:S(2)}, u32[]{:S(2)}) %collective-permute-start.13) | collective-permute-done | bytes 147488 | tf_op jit(solution)/shard_map/ppermute | solution.py:233
  76.8 1.9 %collective-permute-done.14.refs_3_ = bf16[4,48,384]{2,1,0:T(8,128)(2,1)S(1)} collective-permute-done((bf16[4,48,384]{2,1,0:T(8,128)(2,1)S(1)}, bf16[4,48,384]{2,1,0:T(8,128)(2,1)S(1)}, u32[]{:S(2)}, u32[]{:S(2)}) %collective-permute-start.14) | collective-permute-done | bytes 147488 | tf_op jit(solution)/shard_map/ppermute | solution.py:233
  78.7 1.0 %shard_map.90 = (bf16[24,2,1536]{2,1,0:T(2,128)(2,1)}, bf16[24,2,1536]{2,1,0:T(2,128)(2,1)}, bf16[24,2,1536]{2,1,0:T(2,128)(2,1)}, bf16[24,2,1536]{2,1,0:T(2,128)(2,1)}) custom-call(bf16[4,48,384]{2,1,0:T(8,128)(2,1)S(1)} %collective-permute-done.12.refs_0_, bf16[4,48,384]{2,1,0:T(8,128)(2,1)S(1)} %get-tuple-element.43.refs_1_, ...), custom_call_target="tpu_custom_call" | custom-call | tf_op jit(solution)/shard_map/pallas_call | solution.py:304
Async XLA Ops:
  0.6 31.2 %copy-start = (s32[1,1,1,27]{3,2,1,0:T(1,128)S(1)}, s32[1,1,1,27]{3,2,1,0:T(1,128)}, u32[]{:S(2)}) copy-start(s32[1,1,1,27]{3,2,1,0:T(1,128)} %pairs_v.1) | copy-start | bytes 328
  1.7 15.0 %collective-permute-start.2 = (bf16[384,384]{1,0:T(8,128)(2,1)S(1)}, bf16[384,384]{1,0:T(8,128)(2,1)S(1)}, u32[]{:S(2)}, u32[]{:S(2)}) collective-permute-start(bf16[384,384]{1,0:T(8,128)(2,1)S(1)} %pad_maximum_fusion.1.kv.refs_0_), channel_id=1, source_target_pairs={{0,4},{4,0},{8,12},{12,8},{16,20},{20,16},{24,28},{28,24},{1,5},{5... | collective-permute-start | bytes 884744 | tf_op jit(solution)/shard_map/ppermute | solution.py:37
  3.6 13.4 %collective-permute-start.3 = (bf16[384,384]{1,0:T(8,128)(2,1)S(1)}, bf16[384,384]{1,0:T(8,128)(2,1)S(1)}, u32[]{:S(2)}, u32[]{:S(2)}) collective-permute-start(bf16[384,384]{1,0:T(8,128)(2,1)S(1)} %pad_maximum_fusion.1.kv.refs_0_), channel_id=1, source_target_pairs={{4,8},{8,4},{12,16},{16,12},{20,24},{24,20},{5,9},{9,5},{13,17},{1... | collective-permute-start | bytes 884744 | tf_op jit(solution)/shard_map/ppermute | solution.py:37
  10.2 10.8 %collective-permute-start = (bf16[384,384]{1,0:T(8,128)(2,1)S(1)}, bf16[384,384]{1,0:T(8,128)(2,1)S(1)}, u32[]{:S(2)}, u32[]{:S(2)}) collective-permute-start(bf16[384,384]{1,0:T(8,128)(2,1)S(1)} %pad_maximum_fusion.1.kv.refs_0_), channel_id=1, source_target_pairs={{32,64},{64,32},{96,128},{128,96},{160,192},{192,160},{224,256},{2... | collective-permute-start | bytes 884744 | tf_op jit(solution)/shard_map/ppermute | solution.py:37
  13.7 7.3 %collective-permute-start.1 = (bf16[384,384]{1,0:T(8,128)(2,1)S(1)}, bf16[384,384]{1,0:T(8,128)(2,1)S(1)}, u32[]{:S(2)}, u32[]{:S(2)}) collective-permute-start(bf16[384,384]{1,0:T(8,128)(2,1)S(1)} %pad_maximum_fusion.1.kv.refs_0_), channel_id=1, source_target_pairs={{0,32},{32,0},{64,96},{96,64},{128,160},{160,128},{192,224},{224,1... | collective-permute-start | bytes 884744 | tf_op jit(solution)/shard_map/ppermute | solution.py:37
  17.1 14.8 %collective-permute-start.7 = (bf16[784,384]{1,0:T(8,128)(2,1)S(1)}, bf16[784,384]{1,0:T(8,128)(2,1)S(1)}, u32[]{:S(2)}, u32[]{:S(2)}) collective-permute-start(bf16[784,384]{1,0:T(8,128)(2,1)S(1)} %get-tuple-element.31), channel_id=1, source_target_pairs={{32,64},{64,32},{96,128},{128,96},{160,192},{192,160},{224,256},{2... | collective-permute-start | bytes 1806344 | tf_op jit(solution)/shard_map/ppermute | solution.py:37
  21.0 10.8 %collective-permute-start.6 = (bf16[768,384]{1,0:T(8,128)(2,1)S(1)}, bf16[768,384]{1,0:T(8,128)(2,1)S(1)}, u32[]{:S(2)}, u32[]{:S(2)}) collective-permute-start(bf16[768,384]{1,0:T(8,128)(2,1)S(1)} %get-tuple-element.30.kv_rows), channel_id=1, source_target_pairs={{0,32},{32,0},{64,96},{96,64},{128,160},{160,128},{192,224},{224,1... | collective-permute-start | bytes 1769480 | tf_op jit(solution)/shard_map/ppermute | solution.py:37
  23.0 19.8 %collective-permute-start.4 = (bf16[384,384]{1,0:T(8,128)(2,1)S(1)}, bf16[384,384]{1,0:T(8,128)(2,1)S(1)}, u32[]{:S(2)}, u32[]{:S(2)}) collective-permute-start(bf16[384,384]{1,0:T(8,128)(2,1)S(1)} %pad_maximum_fusion.own_qg.refs_2_.refs_1_), channel_id=1, source_target_pairs={{0,4},{4,0},{8,12},{12,8},{16,20},{20,16},{24,28},{28,24},{1,5},{5... | collective-permute-start | bytes 884744 | tf_op jit(solution)/shard_map/ppermute | solution.py:37
  24.9 17.9 %collective-permute-start.5 = (bf16[384,384]{1,0:T(8,128)(2,1)S(1)}, bf16[384,384]{1,0:T(8,128)(2,1)S(1)}, u32[]{:S(2)}, u32[]{:S(2)}) collective-permute-start(bf16[384,384]{1,0:T(8,128)(2,1)S(1)} %pad_maximum_fusion.own_qg.refs_2_.refs_1_), channel_id=1, source_target_pairs={{4,8},{8,4},{12,16},{16,12},{20,24},{24,20},{5,9},{9,5},{13,17},{1... | collective-permute-start | bytes 884744 | tf_op jit(solution)/shard_map/ppermute | solution.py:37
  35.3 7.5 %collective-permute-start.8 = (f32[8,192]{1,0:T(8,128)S(1)}, f32[8,192]{1,0:T(8,128)S(1)}, u32[]{:S(2)}, u32[]{:S(2)}) collective-permute-start(f32[8,192]{1,0:T(8,128)S(1)} %get-tuple-element.32.refs_5_.refs_4_), channel_id=1, source_target_pairs={{0,4},{4,0},{8,12},{12,8},{16,20},{20,16},{24,28},{28,24},{1,5},{5... | collective-permute-start | bytes 18440 | tf_op jit(solution)/shard_map/ppermute | solution.py:37
  37.2 7.2 %collective-permute-start.9 = (f32[8,192]{1,0:T(8,128)S(1)}, f32[8,192]{1,0:T(8,128)S(1)}, u32[]{:S(2)}, u32[]{:S(2)}) collective-permute-start(f32[8,192]{1,0:T(8,128)S(1)} %get-tuple-element.32.refs_5_.refs_4_), channel_id=1, source_target_pairs={{4,8},{8,4},{12,16},{16,12},{20,24},{24,20},{5,9},{9,5},{13,17},{1... | collective-permute-start | bytes 18440 | tf_op jit(solution)/shard_map/ppermute | solution.py:37
  46.2 10.3 %collective-permute-start.11 = (bf16[400,384]{1,0:T(8,128)(2,1)S(1)}, bf16[400,384]{1,0:T(8,128)(2,1)S(1)}, u32[]{:S(2)}, u32[]{:S(2)}) collective-permute-start(bf16[400,384]{1,0:T(8,128)(2,1)S(1)} %get-tuple-element.35), channel_id=1, source_target_pairs={{32,64},{64,32},{96,128},{128,96},{160,192},{192,160},{224,256},{2... | collective-permute-start | bytes 921608 | tf_op jit(solution)/shard_map/ppermute | solution.py:37
  49.4 3.5 %collective-permute-start.10 = (bf16[384,384]{1,0:T(8,128)(2,1)S(1)}, bf16[384,384]{1,0:T(8,128)(2,1)S(1)}, u32[]{:S(2)}, u32[]{:S(2)}) collective-permute-start(bf16[384,384]{1,0:T(8,128)(2,1)S(1)} %get-tuple-element.33), channel_id=1, source_target_pairs={{0,32},{32,0},{64,96},{96,64},{128,160},{160,128},{192,224},{224,1... | collective-permute-start | bytes 884744 | tf_op jit(solution)/shard_map/ppermute | solution.py:37
  56.8 15.3 %collective-permute-start.12 = (bf16[4,48,384]{2,1,0:T(8,128)(2,1)S(1)}, bf16[4,48,384]{2,1,0:T(8,128)(2,1)S(1)}, u32[]{:S(2)}, u32[]{:S(2)}) collective-permute-start(bf16[4,48,384]{2,1,0:T(8,128)(2,1)S(1)} %get-tuple-element.42), channel_id=1, source_target_pairs={{0,2},{1,3},{2,0},{3,1},{4,6},{5,7},{6,4},{7,5},{8,10},{9,11},{10,... | collective-permute-start | bytes 442376 | tf_op jit(solution)/shard_map/ppermute | solution.py:233
  62.5 14.3 %collective-permute-start.13 = (bf16[4,48,384]{2,1,0:T(8,128)(2,1)S(1)}, bf16[4,48,384]{2,1,0:T(8,128)(2,1)S(1)}, u32[]{:S(2)}, u32[]{:S(2)}) collective-permute-start(bf16[4,48,384]{2,1,0:T(8,128)(2,1)S(1)} %get-tuple-element.44), channel_id=1, source_target_pairs={{0,1},{1,0},{2,3},{3,2},{4,5},{5,4},{6,7},{7,6},{8,9},{9,8},{10,11... | collective-permute-start | bytes 442376 | tf_op jit(solution)/shard_map/ppermute | solution.py:233
  66.5 12.2 %collective-permute-start.14 = (bf16[4,48,384]{2,1,0:T(8,128)(2,1)S(1)}, bf16[4,48,384]{2,1,0:T(8,128)(2,1)S(1)}, u32[]{:S(2)}, u32[]{:S(2)}) collective-permute-start(bf16[4,48,384]{2,1,0:T(8,128)(2,1)S(1)} %get-tuple-element.45), channel_id=1, source_target_pairs={{0,3},{1,2},{2,1},{3,0},{4,7},{5,6},{6,5},{7,4},{8,11},{9,10},{10,... | collective-permute-start | bytes 442376 | tf_op jit(solution)/shard_map/ppermute | solution.py:233

commit v9 on v8

--- a/solution.py
+++ b/solution.py
@@ -82,7 +82,7 @@
 
 
 def far_first(heads):
-    return [heads // 2] + [k for k in range(heads) if k != heads // 2]
+    return [heads // 2] + [k for k in reversed(range(heads)) if k != heads // 2]
 
 
 def assemble_kernel(*refs):
@@ -167,7 +167,7 @@
 
 def key_kernel(sides, *refs):
     kvs, refs = refs[: len(sides)], refs[len(sides) :]
-    (qg, qg_a, qg_b, st, st_a, st_b), refs = refs[:6], refs[6:]
+    (qg, qg_b, qg_a, st, st_a, st_b), refs = refs[:6], refs[6:]
     outs, (query_ref, grad_ref, stat_ref) = refs[: len(sides)], refs[len(sides) :]
     count = qg.shape[1] // HEAD_DIM
     frame, frames = lax.axis_index("frame"), lax.axis_size("frame")
@@ -254,7 +254,7 @@
     corner_fb = pair_swap(far_rows, "frame", 1)
     corner_fa = pair_swap(after(rows, kv_fb, kv_fa), "frame", 0)
     qg_late = after(qg, rows)
-    qg_a, qg_b = pair_swap(qg_late, "row", 0), pair_swap(qg_late, "row", 1)
+    qg_b, qg_a = pair_swap(qg_late, "row", 1), pair_swap(qg_late, "row", 0)
 
     span = TILE // heads
     wide = jax.ShapeDtypeStruct((WIDE, feats), bf16)
@@ -281,7 +281,7 @@
             [VMEM] * (len(sides) + 6),
             [VMEM] * len(sides),
             [row_near, row_near, pltpu.VMEM((len(sides), 8, 3 * TILE), f32)],
-        )(*kvs, qg, qg_a, qg_b, stat, st_a, st_b)
+        )(*kvs, qg, qg_b, qg_a, stat, st_a, st_b)
 
     term_b, term_a = terms((2, 1), ((bf16, 16), (bf16, 0)), kv_fb, kv_fa)
     got_b, got_a = pair_swap(term_b, "frame", 1), pair_swap(term_a, "frame", 0)

time: 80.2 us -> 80.1 us (level)
  the two profiles are of different devices: /device:TPU:88 before, /device:TPU:65 now
where the time goes in v9:
time: 80.1 us; the launch traced here: 79.6 us
  starting transfers between devices  52.6 us (66%)
  waiting for transfers between devices  14.3 us (18%)
  Pallas kernels  9.84 us (12%)
  other arithmetic  2.03 us (3%)
  between operations  0.88 us (1%)
    ppermute x12, starting transfers between devices, pair_swap(): return lax.ppermute(value, axis, pairs)  40.8 us
    ppermute x3, starting transfers between devices, head_swap(): lax.ppermute(value, 'head', [(i, i ^ k) for i in range(count)])  11.8 us
    ppermute x3, waiting for transfers between devices, head_swap(): lax.ppermute(value, 'head', [(i, i ^ k) for i in range(count)])  11 us
    pallas_call x1, Pallas kernels, body(): call(query_kernel, (jax.ShapeDtypeStruct((TILE, feats), bf16), jax.ShapeD...  3.4 us
    ppermute x12, waiting for transfers between devices, pair_swap(): return lax.ppermute(value, axis, pairs)  3.29 us
    pallas_call x2, Pallas kernels, terms(): call(lambda *refs: key_kernel(sides, *refs), [jax.ShapeDtypeStruct((2 * T...  2.87 us
    pallas_call x1, Pallas kernels, body(): call(query_grad_kernel, jax.ShapeDtypeStruct((heads, 2, span, feats), bf1...  2.16 us
    max x2, other arithmetic, stacked(): jnp.maximum(low, jnp.pad(second, ((rows, 0), (0, 0)), constant_values=-jn...  2.03 us
  transfers between devices with their start and end apart: 15, of which 5 were waited for; matrix products, arithmetic and copies ran while one was open for 1% of the time, Pallas kernels for 8%

profile of v9, /device:TPU:65, one launch (start us, length us, event | category | flops | bytes accessed | tf_op | source)
XLA Modules:
  0.0 79.6 jit_solution(1400470304479207355)
XLA Ops:
  0.6 0.0 copy-start
  0.6 1.0 %pad_maximum_fusion.1.kv.refs_0_ = bf16[384,384]{1,0:T(8,128)(2,1)S(1)} fusion(bf16[192,384]{1,0:T(8,128)(2,1)} %bitcast.8, bf16[192,384]{1,0:T(8,128)(2,1)} %bitcast.9), kind=kLoop, calls=%fused_computation.1 | loop fusion | flops 589824 | bytes 589824 | tf_op jit(solution)/shard_map/max | solution.py:239
  1.7 1.9 %collective-permute-start.2 = (bf16[384,384]{1,0:T(8,128)(2,1)S(1)}, bf16[384,384]{1,0:T(8,128)(2,1)S(1)}, u32[]{:S(2)}, u32[]{:S(2)}) collective-permute-start(bf16[384,384]{1,0:T(8,128)(2,1)S(1)} %pad_maximum_fusion.1.kv.refs_0_), channel_id=1, source_target_pairs={{0,4},{4,0},{8,12},{12,8},{16,20},{20,16},{24,28},{28,24},{1,5},{5... | collective-permute-start | bytes 884744 | tf_op jit(solution)/shard_map/ppermute | solution.py:37
  3.6 6.1 %collective-permute-start.3 = (bf16[384,384]{1,0:T(8,128)(2,1)S(1)}, bf16[384,384]{1,0:T(8,128)(2,1)S(1)}, u32[]{:S(2)}, u32[]{:S(2)}) collective-permute-start(bf16[384,384]{1,0:T(8,128)(2,1)S(1)} %pad_maximum_fusion.1.kv.refs_0_), channel_id=1, source_target_pairs={{4,8},{8,4},{12,16},{16,12},{20,24},{24,20},{5,9},{9,5},{13,17},{1... | collective-permute-start | bytes 884744 | tf_op jit(solution)/shard_map/ppermute | solution.py:37
  9.7 4.2 %collective-permute-start = (bf16[384,384]{1,0:T(8,128)(2,1)S(1)}, bf16[384,384]{1,0:T(8,128)(2,1)S(1)}, u32[]{:S(2)}, u32[]{:S(2)}) collective-permute-start(bf16[384,384]{1,0:T(8,128)(2,1)S(1)} %pad_maximum_fusion.1.kv.refs_0_), channel_id=1, source_target_pairs={{32,64},{64,32},{96,128},{128,96},{160,192},{192,160},{224,256},{2... | collective-permute-start | bytes 884744 | tf_op jit(solution)/shard_map/ppermute | solution.py:37
  13.9 1.9 %collective-permute-start.1 = (bf16[384,384]{1,0:T(8,128)(2,1)S(1)}, bf16[384,384]{1,0:T(8,128)(2,1)S(1)}, u32[]{:S(2)}, u32[]{:S(2)}) collective-permute-start(bf16[384,384]{1,0:T(8,128)(2,1)S(1)} %pad_maximum_fusion.1.kv.refs_0_), channel_id=1, source_target_pairs={{0,32},{32,0},{64,96},{96,64},{128,160},{160,128},{192,224},{224,1... | collective-permute-start | bytes 884744 | tf_op jit(solution)/shard_map/ppermute | solution.py:37
  15.9 1.0 %pad_maximum_fusion.own_qg.refs_2_.refs_1_ = bf16[384,384]{1,0:T(8,128)(2,1)S(1)} fusion(bf16[192,384]{1,0:T(8,128)(2,1)} %bitcast.10, bf16[192,384]{1,0:T(8,128)(2,1)} %bitcast.11), kind=kLoop, calls=%fused_computation | loop fusion | flops 589824 | bytes 589824 | tf_op jit(solution)/shard_map/max | solution.py:239
  16.9 0.0 collective-permute-done.2.a_ref
  16.9 0.0 collective-permute-done.3.b_ref
  16.9 0.1 shard_map.84
  17.0 3.7 %collective-permute-start.7 = (bf16[784,384]{1,0:T(8,128)(2,1)S(1)}, bf16[784,384]{1,0:T(8,128)(2,1)S(1)}, u32[]{:S(2)}, u32[]{:S(2)}) collective-permute-start(bf16[784,384]{1,0:T(8,128)(2,1)S(1)} %get-tuple-element.31), channel_id=1, source_target_pairs={{32,64},{64,32},{96,128},{128,96},{160,192},{192,160},{224,256},{2... | collective-permute-start | bytes 1806344 | tf_op jit(solution)/shard_map/ppermute | solution.py:37
  20.7 0.0 collective-permute-done.kv_fb.refs_0_
  20.8 0.0 collective-permute-done.1.kv_fa.refs_1_
  20.8 1.9 %collective-permute-start.6 = (bf16[768,384]{1,0:T(8,128)(2,1)S(1)}, bf16[768,384]{1,0:T(8,128)(2,1)S(1)}, u32[]{:S(2)}, u32[]{:S(2)}) collective-permute-start(bf16[768,384]{1,0:T(8,128)(2,1)S(1)} %get-tuple-element.30.kv_rows), channel_id=1, source_target_pairs={{0,32},{32,0},{64,96},{96,64},{128,160},{160,128},{192,224},{224,1... | collective-permute-start | bytes 1769480 | tf_op jit(solution)/shard_map/ppermute | solution.py:37
  22.7 3.4 %collective-permute-start.4 = (bf16[384,384]{1,0:T(8,128)(2,1)S(1)}, bf16[384,384]{1,0:T(8,128)(2,1)S(1)}, u32[]{:S(2)}, u32[]{:S(2)}) collective-permute-start(bf16[384,384]{1,0:T(8,128)(2,1)S(1)} %pad_maximum_fusion.own_qg.refs_2_.refs_1_), channel_id=1, source_target_pairs={{4,8},{8,4},{12,16},{16,12},{20,24},{24,20},{5,9},{9,5},{13,17},{1... | collective-permute-start | bytes 884744 | tf_op jit(solution)/shard_map/ppermute | solution.py:37
  26.1 1.9 %collective-permute-start.5 = (bf16[384,384]{1,0:T(8,128)(2,1)S(1)}, bf16[384,384]{1,0:T(8,128)(2,1)S(1)}, u32[]{:S(2)}, u32[]{:S(2)}) collective-permute-start(bf16[384,384]{1,0:T(8,128)(2,1)S(1)} %pad_maximum_fusion.own_qg.refs_2_.refs_1_), channel_id=1, source_target_pairs={{0,4},{4,0},{8,12},{12,8},{16,20},{20,16},{24,28},{28,24},{1,5},{5... | collective-permute-start | bytes 884744 | tf_op jit(solution)/shard_map/ppermute | solution.py:37
  28.0 0.0 collective-permute-done.6.corner_fa
  28.0 0.7 collective-permute-done.7.corner_fb
  28.7 0.0 copy-done
  28.7 3.4 %shard_map.85 = (bf16[192,384]{1,0:T(8,128)(2,1)S(1)}, f32[8,192]{1,0:T(8,128)S(1)}, f32[192,128]{1,0:T(8,128)S(1)}, f32[1,1728]{1,0:T(1,128)S(1)}, bf16[1728,38...) custom-call(s32[1,1,1,27]{3,2,1,0:T(1,128)S(1)} %copy-done, s32[1,1,1,27]{3,2,1,0:T(1,128)S(1)} %copy-done, ...), custom_call_target="tpu_custom_call" | custom-call | tf_op jit(solution)/shard_map/pallas_call | solution.py:261
  32.1 2.7 %collective-permute-start.8 = (f32[8,192]{1,0:T(8,128)S(1)}, f32[8,192]{1,0:T(8,128)S(1)}, u32[]{:S(2)}, u32[]{:S(2)}) collective-permute-start(f32[8,192]{1,0:T(8,128)S(1)} %get-tuple-element.32.refs_5_.refs_4_), channel_id=1, source_target_pairs={{0,4},{4,0},{8,12},{12,8},{16,20},{20,16},{24,28},{28,24},{1,5},{5... | collective-permute-start | bytes 18440 | tf_op jit(solution)/shard_map/ppermute | solution.py:37
  34.8 6.2 %collective-permute-start.9 = (f32[8,192]{1,0:T(8,128)S(1)}, f32[8,192]{1,0:T(8,128)S(1)}, u32[]{:S(2)}, u32[]{:S(2)}) collective-permute-start(f32[8,192]{1,0:T(8,128)S(1)} %get-tuple-element.32.refs_5_.refs_4_), channel_id=1, source_target_pairs={{4,8},{8,4},{12,16},{16,12},{20,24},{24,20},{5,9},{9,5},{13,17},{1... | collective-permute-start | bytes 18440 | tf_op jit(solution)/shard_map/ppermute | solution.py:37
  41.0 0.0 collective-permute-done.4.refs_3_.refs_2_
  41.0 0.0 collective-permute-done.5.refs_4_.refs_3_
  41.0 0.0 collective-permute-done.8.refs_6_.refs_5_
  41.0 1.0 %collective-permute-done.9.refs_7_.refs_6_ = f32[8,192]{1,0:T(8,128)S(1)} collective-permute-done((f32[8,192]{1,0:T(8,128)S(1)}, f32[8,192]{1,0:T(8,128)S(1)}, u32[]{:S(2)}, u32[]{:S(2)}) %collective-permute-start.9) | collective-permute-done | bytes 6176 | tf_op jit(solution)/shard_map/ppermute | solution.py:37
  42.0 1.8 %shard_map.86 = (bf16[400,384]{1,0:T(8,128)(2,1)S(1)}, bf16[384,384]{1,0:T(8,128)(2,1)S(1)}) custom-call(bf16[384,384]{1,0:T(8,128)(2,1)S(1)} %collective-permute-done.kv_fb.refs_0_, bf16[384,384]{1,0:T(8,128)(2,1)S(1)} %collective-permute-done.1.kv_fa.refs_1_, bf16[384,384]{1,0:T(8,128)(2,1)S(1)} %pad_maximum_fusion.own_qg.refs_2_.refs_1_, ...), custom_call_target="tpu_custom_call" | custom-call | tf_op jit(solution)/shard_map/pallas_call | solution.py:278
  43.8 4.9 %collective-permute-start.11 = (bf16[400,384]{1,0:T(8,128)(2,1)S(1)}, bf16[400,384]{1,0:T(8,128)(2,1)S(1)}, u32[]{:S(2)}, u32[]{:S(2)}) collective-permute-start(bf16[400,384]{1,0:T(8,128)(2,1)S(1)} %get-tuple-element.35), channel_id=1, source_target_pairs={{32,64},{64,32},{96,128},{128,96},{160,192},{192,160},{224,256},{2... | collective-permute-start | bytes 921608 | tf_op jit(solution)/shard_map/ppermute | solution.py:37
  48.7 1.9 %collective-permute-start.10 = (bf16[384,384]{1,0:T(8,128)(2,1)S(1)}, bf16[384,384]{1,0:T(8,128)(2,1)S(1)}, u32[]{:S(2)}, u32[]{:S(2)}) collective-permute-start(bf16[384,384]{1,0:T(8,128)(2,1)S(1)} %get-tuple-element.33), channel_id=1, source_target_pairs={{0,32},{32,0},{64,96},{96,64},{128,160},{160,128},{192,224},{224,1... | collective-permute-start | bytes 884744 | tf_op jit(solution)/shard_map/ppermute | solution.py:37
  50.7 1.5 %collective-permute-done.10.got_a = bf16[384,384]{1,0:T(8,128)(2,1)S(1)} collective-permute-done((bf16[384,384]{1,0:T(8,128)(2,1)S(1)}, bf16[384,384]{1,0:T(8,128)(2,1)S(1)}, u32[]{:S(2)}, u32[]{:S(2)}) %collective-permute-start.10) | collective-permute-done | bytes 294944 | tf_op jit(solution)/shard_map/ppermute | solution.py:37
  52.2 2.2 %shard_map.88.query_blocks = bf16[4,2,48,384]{3,2,1,0:T(8,128)(2,1)S(1)} custom-call(bf16[384,384]{1,0:T(8,128)(2,1)S(1)} %pad_maximum_fusion.own_qg.refs_2_.refs_1_, bf16[1728,384]{1,0:T(8,128)(2,1)S(1)} %get-tuple-element.37.key_ref, bf16[1728,384]{1,0:T(8,128)(2,1)S(1)} %get-tuple-element.38.value_ref, ...), custom_call_target="tpu_custom_call" | custom-call | tf_op jit(solution)/shard_map/pallas_call | solution.py:289
  54.4 1.1 %shard_map.87.own_ref = f32[384,384]{1,0:T(8,128)S(1)} custom-call(bf16[384,384]{1,0:T(8,128)(2,1)S(1)} %pad_maximum_fusion.1.kv.refs_0_, bf16[384,384]{1,0:T(8,128)(2,1)S(1)} %pad_maximum_fusion.own_qg.refs_2_.refs_1_, bf16[384,384]{1,0:T(8,128)(2,1)S(1)} %collective-permute-done.4.refs_3_.refs_2_, ...), custom_call_target="tpu_custom_call" | custom-call | tf_op jit(solution)/shard_map/pallas_call | solution.py:278
  55.5 0.0 collective-permute-done.11.got_b
  55.5 0.3 shard_map.89
  55.8 7.5 %collective-permute-start.12 = (bf16[4,48,384]{2,1,0:T(8,128)(2,1)S(1)}, bf16[4,48,384]{2,1,0:T(8,128)(2,1)S(1)}, u32[]{:S(2)}, u32[]{:S(2)}) collective-permute-start(bf16[4,48,384]{2,1,0:T(8,128)(2,1)S(1)} %get-tuple-element.42), channel_id=1, source_target_pairs={{0,2},{1,3},{2,0},{3,1},{4,6},{5,7},{6,4},{7,5},{8,10},{9,11},{10,... | collective-permute-start | bytes 442376 | tf_op jit(solution)/shard_map/ppermute | solution.py:233
  63.3 2.0 %collective-permute-start.13 = (bf16[4,48,384]{2,1,0:T(8,128)(2,1)S(1)}, bf16[4,48,384]{2,1,0:T(8,128)(2,1)S(1)}, u32[]{:S(2)}, u32[]{:S(2)}) collective-permute-start(bf16[4,48,384]{2,1,0:T(8,128)(2,1)S(1)} %get-tuple-element.43), channel_id=1, source_target_pairs={{0,3},{1,2},{2,1},{3,0},{4,7},{5,6},{6,5},{7,4},{8,11},{9,10},{10,... | collective-permute-start | bytes 442376 | tf_op jit(solution)/shard_map/ppermute | solution.py:233
  65.2 2.4 %collective-permute-start.14 = (bf16[4,48,384]{2,1,0:T(8,128)(2,1)S(1)}, bf16[4,48,384]{2,1,0:T(8,128)(2,1)S(1)}, u32[]{:S(2)}, u32[]{:S(2)}) collective-permute-start(bf16[4,48,384]{2,1,0:T(8,128)(2,1)S(1)} %get-tuple-element.44), channel_id=1, source_target_pairs={{0,1},{1,0},{2,3},{3,2},{4,5},{5,4},{6,7},{7,6},{8,9},{9,8},{10,11... | collective-permute-start | bytes 442376 | tf_op jit(solution)/shard_map/ppermute | solution.py:233
  67.6 0.0 collective-permute-done.12.refs_0_
  67.6 9.7 %collective-permute-done.13.refs_1_ = bf16[4,48,384]{2,1,0:T(8,128)(2,1)S(1)} collective-permute-done((bf16[4,48,384]{2,1,0:T(8,128)(2,1)S(1)}, bf16[4,48,384]{2,1,0:T(8,128)(2,1)S(1)}, u32[]{:S(2)}, u32[]{:S(2)}) %collective-permute-start.13) | collective-permute-done | bytes 147488 | tf_op jit(solution)/shard_map/ppermute | solution.py:233
  77.3 1.2 %collective-permute-done.14.refs_2_ = bf16[4,48,384]{2,1,0:T(8,128)(2,1)S(1)} collective-permute-done((bf16[4,48,384]{2,1,0:T(8,128)(2,1)S(1)}, bf16[4,48,384]{2,1,0:T(8,128)(2,1)S(1)}, u32[]{:S(2)}, u32[]{:S(2)}) %collective-permute-start.14) | collective-permute-done | bytes 147488 | tf_op jit(solution)/shard_map/ppermute | solution.py:233
  78.6 1.0 %shard_map.90 = (bf16[24,2,1536]{2,1,0:T(2,128)(2,1)}, bf16[24,2,1536]{2,1,0:T(2,128)(2,1)}, bf16[24,2,1536]{2,1,0:T(2,128)(2,1)}, bf16[24,2,1536]{2,1,0:T(2,128)(2,1)}) custom-call(bf16[4,48,384]{2,1,0:T(8,128)(2,1)S(1)} %collective-permute-done.12.refs_0_, bf16[4,48,384]{2,1,0:T(8,128)(2,1)S(1)} %collective-permute-done.13.refs_1_, ...), custom_call_target="tpu_custom_call" | custom-call | tf_op jit(solution)/shard_map/pallas_call | solution.py:304
Async XLA Ops:
  0.6 28.1 %copy-start = (s32[1,1,1,27]{3,2,1,0:T(1,128)S(1)}, s32[1,1,1,27]{3,2,1,0:T(1,128)}, u32[]{:S(2)}) copy-start(s32[1,1,1,27]{3,2,1,0:T(1,128)} %pairs_v.1) | copy-start | bytes 328
  1.7 15.2 %collective-permute-start.2 = (bf16[384,384]{1,0:T(8,128)(2,1)S(1)}, bf16[384,384]{1,0:T(8,128)(2,1)S(1)}, u32[]{:S(2)}, u32[]{:S(2)}) collective-permute-start(bf16[384,384]{1,0:T(8,128)(2,1)S(1)} %pad_maximum_fusion.1.kv.refs_0_), channel_id=1, source_target_pairs={{0,4},{4,0},{8,12},{12,8},{16,20},{20,16},{24,28},{28,24},{1,5},{5... | collective-permute-start | bytes 884744 | tf_op jit(solution)/shard_map/ppermute | solution.py:37
  3.6 13.3 %collective-permute-start.3 = (bf16[384,384]{1,0:T(8,128)(2,1)S(1)}, bf16[384,384]{1,0:T(8,128)(2,1)S(1)}, u32[]{:S(2)}, u32[]{:S(2)}) collective-permute-start(bf16[384,384]{1,0:T(8,128)(2,1)S(1)} %pad_maximum_fusion.1.kv.refs_0_), channel_id=1, source_target_pairs={{4,8},{8,4},{12,16},{16,12},{20,24},{24,20},{5,9},{9,5},{13,17},{1... | collective-permute-start | bytes 884744 | tf_op jit(solution)/shard_map/ppermute | solution.py:37
  9.7 11.1 %collective-permute-start = (bf16[384,384]{1,0:T(8,128)(2,1)S(1)}, bf16[384,384]{1,0:T(8,128)(2,1)S(1)}, u32[]{:S(2)}, u32[]{:S(2)}) collective-permute-start(bf16[384,384]{1,0:T(8,128)(2,1)S(1)} %pad_maximum_fusion.1.kv.refs_0_), channel_id=1, source_target_pairs={{32,64},{64,32},{96,128},{128,96},{160,192},{192,160},{224,256},{2... | collective-permute-start | bytes 884744 | tf_op jit(solution)/shard_map/ppermute | solution.py:37
  13.9 6.8 %collective-permute-start.1 = (bf16[384,384]{1,0:T(8,128)(2,1)S(1)}, bf16[384,384]{1,0:T(8,128)(2,1)S(1)}, u32[]{:S(2)}, u32[]{:S(2)}) collective-permute-start(bf16[384,384]{1,0:T(8,128)(2,1)S(1)} %pad_maximum_fusion.1.kv.refs_0_), channel_id=1, source_target_pairs={{0,32},{32,0},{64,96},{96,64},{128,160},{160,128},{192,224},{224,1... | collective-permute-start | bytes 884744 | tf_op jit(solution)/shard_map/ppermute | solution.py:37
  17.0 11.7 %collective-permute-start.7 = (bf16[784,384]{1,0:T(8,128)(2,1)S(1)}, bf16[784,384]{1,0:T(8,128)(2,1)S(1)}, u32[]{:S(2)}, u32[]{:S(2)}) collective-permute-start(bf16[784,384]{1,0:T(8,128)(2,1)S(1)} %get-tuple-element.31), channel_id=1, source_target_pairs={{32,64},{64,32},{96,128},{128,96},{160,192},{192,160},{224,256},{2... | collective-permute-start | bytes 1806344 | tf_op jit(solution)/shard_map/ppermute | solution.py:37
  20.8 7.2 %collective-permute-start.6 = (bf16[768,384]{1,0:T(8,128)(2,1)S(1)}, bf16[768,384]{1,0:T(8,128)(2,1)S(1)}, u32[]{:S(2)}, u32[]{:S(2)}) collective-permute-start(bf16[768,384]{1,0:T(8,128)(2,1)S(1)} %get-tuple-element.30.kv_rows), channel_id=1, source_target_pairs={{0,32},{32,0},{64,96},{96,64},{128,160},{160,128},{192,224},{224,1... | collective-permute-start | bytes 1769480 | tf_op jit(solution)/shard_map/ppermute | solution.py:37
  22.7 18.3 %collective-permute-start.4 = (bf16[384,384]{1,0:T(8,128)(2,1)S(1)}, bf16[384,384]{1,0:T(8,128)(2,1)S(1)}, u32[]{:S(2)}, u32[]{:S(2)}) collective-permute-start(bf16[384,384]{1,0:T(8,128)(2,1)S(1)} %pad_maximum_fusion.own_qg.refs_2_.refs_1_), channel_id=1, source_target_pairs={{4,8},{8,4},{12,16},{16,12},{20,24},{24,20},{5,9},{9,5},{13,17},{1... | collective-permute-start | bytes 884744 | tf_op jit(solution)/shard_map/ppermute | solution.py:37
  26.1 14.9 %collective-permute-start.5 = (bf16[384,384]{1,0:T(8,128)(2,1)S(1)}, bf16[384,384]{1,0:T(8,128)(2,1)S(1)}, u32[]{:S(2)}, u32[]{:S(2)}) collective-permute-start(bf16[384,384]{1,0:T(8,128)(2,1)S(1)} %pad_maximum_fusion.own_qg.refs_2_.refs_1_), channel_id=1, source_target_pairs={{0,4},{4,0},{8,12},{12,8},{16,20},{20,16},{24,28},{28,24},{1,5},{5... | collective-permute-start | bytes 884744 | tf_op jit(solution)/shard_map/ppermute | solution.py:37
  32.1 8.9 %collective-permute-start.8 = (f32[8,192]{1,0:T(8,128)S(1)}, f32[8,192]{1,0:T(8,128)S(1)}, u32[]{:S(2)}, u32[]{:S(2)}) collective-permute-start(f32[8,192]{1,0:T(8,128)S(1)} %get-tuple-element.32.refs_5_.refs_4_), channel_id=1, source_target_pairs={{0,4},{4,0},{8,12},{12,8},{16,20},{20,16},{24,28},{28,24},{1,5},{5... | collective-permute-start | bytes 18440 | tf_op jit(solution)/shard_map/ppermute | solution.py:37
  34.8 7.2 %collective-permute-start.9 = (f32[8,192]{1,0:T(8,128)S(1)}, f32[8,192]{1,0:T(8,128)S(1)}, u32[]{:S(2)}, u32[]{:S(2)}) collective-permute-start(f32[8,192]{1,0:T(8,128)S(1)} %get-tuple-element.32.refs_5_.refs_4_), channel_id=1, source_target_pairs={{4,8},{8,4},{12,16},{16,12},{20,24},{24,20},{5,9},{9,5},{13,17},{1... | collective-permute-start | bytes 18440 | tf_op jit(solution)/shard_map/ppermute | solution.py:37
  43.8 11.7 %collective-permute-start.11 = (bf16[400,384]{1,0:T(8,128)(2,1)S(1)}, bf16[400,384]{1,0:T(8,128)(2,1)S(1)}, u32[]{:S(2)}, u32[]{:S(2)}) collective-permute-start(bf16[400,384]{1,0:T(8,128)(2,1)S(1)} %get-tuple-element.35), channel_id=1, source_target_pairs={{32,64},{64,32},{96,128},{128,96},{160,192},{192,160},{224,256},{2... | collective-permute-start | bytes 921608 | tf_op jit(solution)/shard_map/ppermute | solution.py:37
  48.7 3.5 %collective-permute-start.10 = (bf16[384,384]{1,0:T(8,128)(2,1)S(1)}, bf16[384,384]{1,0:T(8,128)(2,1)S(1)}, u32[]{:S(2)}, u32[]{:S(2)}) collective-permute-start(bf16[384,384]{1,0:T(8,128)(2,1)S(1)} %get-tuple-element.33), channel_id=1, source_target_pairs={{0,32},{32,0},{64,96},{96,64},{128,160},{160,128},{192,224},{224,1... | collective-permute-start | bytes 884744 | tf_op jit(solution)/shard_map/ppermute | solution.py:37
  55.8 11.8 %collective-permute-start.12 = (bf16[4,48,384]{2,1,0:T(8,128)(2,1)S(1)}, bf16[4,48,384]{2,1,0:T(8,128)(2,1)S(1)}, u32[]{:S(2)}, u32[]{:S(2)}) collective-permute-start(bf16[4,48,384]{2,1,0:T(8,128)(2,1)S(1)} %get-tuple-element.42), channel_id=1, source_target_pairs={{0,2},{1,3},{2,0},{3,1},{4,6},{5,7},{6,4},{7,5},{8,10},{9,11},{10,... | collective-permute-start | bytes 442376 | tf_op jit(solution)/shard_map/ppermute | solution.py:233
  63.3 14.1 %collective-permute-start.13 = (bf16[4,48,384]{2,1,0:T(8,128)(2,1)S(1)}, bf16[4,48,384]{2,1,0:T(8,128)(2,1)S(1)}, u32[]{:S(2)}, u32[]{:S(2)}) collective-permute-start(bf16[4,48,384]{2,1,0:T(8,128)(2,1)S(1)} %get-tuple-element.43), channel_id=1, source_target_pairs={{0,3},{1,2},{2,1},{3,0},{4,7},{5,6},{6,5},{7,4},{8,11},{9,10},{10,... | collective-permute-start | bytes 442376 | tf_op jit(solution)/shard_map/ppermute | solution.py:233
  65.2 13.4 %collective-permute-start.14 = (bf16[4,48,384]{2,1,0:T(8,128)(2,1)S(1)}, bf16[4,48,384]{2,1,0:T(8,128)(2,1)S(1)}, u32[]{:S(2)}, u32[]{:S(2)}) collective-permute-start(bf16[4,48,384]{2,1,0:T(8,128)(2,1)S(1)} %get-tuple-element.44), channel_id=1, source_target_pairs={{0,1},{1,0},{2,3},{3,2},{4,5},{5,4},{6,7},{7,6},{8,9},{9,8},{10,11... | collective-permute-start | bytes 442376 | tf_op jit(solution)/shard_map/ppermute | solution.py:233

commit v10 on v9

--- a/solution.py
+++ b/solution.py
@@ -285,7 +285,7 @@
 
     term_b, term_a = terms((2, 1), ((bf16, 16), (bf16, 0)), kv_fb, kv_fa)
     got_b, got_a = pair_swap(term_b, "frame", 1), pair_swap(term_a, "frame", 0)
-    (own,) = terms((0,), ((f32, 0),), after(own_kv, got_a))
+    (own,) = terms((0,), ((f32, 0),), after(own_kv, term_b))
     sent_q = call(
         query_grad_kernel,
         jax.ShapeDtypeStruct((heads, 2, span, feats), bf16),

time: 80.1 us -> 79 us (0.986)
  waiting for transfers between devices: 14.3 us -> 13.2 us
    ppermute x12, waiting for transfers between devices: 3.29 us -> 2.2 us  [pair_swap(): return lax.ppermute(value, axis, pairs)]
  transfers between devices with their start and end apart: 15 -> 15, of which waited for: 5 -> 5; matrix products, arithmetic and copies ran while one was open for 1% -> 1% of each run, Pallas kernels for 8% -> 9%
where the time goes in v10:
time: 79 us; the launch traced here: 78.5 us
  starting transfers between devices  52.6 us (67%)
  waiting for transfers between devices  13.2 us (17%)
  Pallas kernels  9.8 us (12%)
  other arithmetic  2.03 us (3%)
  between operations  0.88 us (1%)
    ppermute x12, starting transfers between devices, pair_swap(): return lax.ppermute(value, axis, pairs)  40.8 us
    ppermute x3, starting transfers between devices, head_swap(): lax.ppermute(value, 'head', [(i, i ^ k) for i in range(count)])  11.8 us
    ppermute x3, waiting for transfers between devices, head_swap(): lax.ppermute(value, 'head', [(i, i ^ k) for i in range(count)])  11 us
    pallas_call x1, Pallas kernels, body(): call(query_kernel, (jax.ShapeDtypeStruct((TILE, feats), bf16), jax.ShapeD...  3.38 us
    pallas_call x2, Pallas kernels, terms(): call(lambda *refs: key_kernel(sides, *refs), [jax.ShapeDtypeStruct((2 * T...  2.87 us
    ppermute x12, waiting for transfers between devices, pair_swap(): return lax.ppermute(value, axis, pairs)  2.2 us
    pallas_call x1, Pallas kernels, body(): call(query_grad_kernel, jax.ShapeDtypeStruct((heads, 2, span, feats), bf1...  2.16 us
    max x2, other arithmetic, stacked(): jnp.maximum(low, jnp.pad(second, ((rows, 0), (0, 0)), constant_values=-jn...  2.03 us
  transfers between devices with their start and end apart: 15, of which 5 were waited for; matrix products, arithmetic and copies ran while one was open for 1% of the time, Pallas kernels for 9%

profile of v10, /device:TPU:65, one launch (start us, length us, event | category | flops | bytes accessed | tf_op | source)
XLA Modules:
  0.0 78.5 jit_solution(1489812406897717344)
XLA Ops:
  0.6 0.0 copy-start
  0.6 1.0 %pad_maximum_fusion.1.kv.refs_0_ = bf16[384,384]{1,0:T(8,128)(2,1)S(1)} fusion(bf16[192,384]{1,0:T(8,128)(2,1)} %bitcast.8, bf16[192,384]{1,0:T(8,128)(2,1)} %bitcast.9), kind=kLoop, calls=%fused_computation.1 | loop fusion | flops 589824 | bytes 589824 | tf_op jit(solution)/shard_map/max | solution.py:239
  1.7 1.9 %collective-permute-start.2 = (bf16[384,384]{1,0:T(8,128)(2,1)S(1)}, bf16[384,384]{1,0:T(8,128)(2,1)S(1)}, u32[]{:S(2)}, u32[]{:S(2)}) collective-permute-start(bf16[384,384]{1,0:T(8,128)(2,1)S(1)} %pad_maximum_fusion.1.kv.refs_0_), channel_id=1, source_target_pairs={{0,4},{4,0},{8,12},{12,8},{16,20},{20,16},{24,28},{28,24},{1,5},{5... | collective-permute-start | bytes 884744 | tf_op jit(solution)/shard_map/ppermute | solution.py:37
  3.6 6.1 %collective-permute-start.3 = (bf16[384,384]{1,0:T(8,128)(2,1)S(1)}, bf16[384,384]{1,0:T(8,128)(2,1)S(1)}, u32[]{:S(2)}, u32[]{:S(2)}) collective-permute-start(bf16[384,384]{1,0:T(8,128)(2,1)S(1)} %pad_maximum_fusion.1.kv.refs_0_), channel_id=1, source_target_pairs={{4,8},{8,4},{12,16},{16,12},{20,24},{24,20},{5,9},{9,5},{13,17},{1... | collective-permute-start | bytes 884744 | tf_op jit(solution)/shard_map/ppermute | solution.py:37
  9.7 4.2 %collective-permute-start = (bf16[384,384]{1,0:T(8,128)(2,1)S(1)}, bf16[384,384]{1,0:T(8,128)(2,1)S(1)}, u32[]{:S(2)}, u32[]{:S(2)}) collective-permute-start(bf16[384,384]{1,0:T(8,128)(2,1)S(1)} %pad_maximum_fusion.1.kv.refs_0_), channel_id=1, source_target_pairs={{32,64},{64,32},{96,128},{128,96},{160,192},{192,160},{224,256},{2... | collective-permute-start | bytes 884744 | tf_op jit(solution)/shard_map/ppermute | solution.py:37
  13.9 1.9 %collective-permute-start.1 = (bf16[384,384]{1,0:T(8,128)(2,1)S(1)}, bf16[384,384]{1,0:T(8,128)(2,1)S(1)}, u32[]{:S(2)}, u32[]{:S(2)}) collective-permute-start(bf16[384,384]{1,0:T(8,128)(2,1)S(1)} %pad_maximum_fusion.1.kv.refs_0_), channel_id=1, source_target_pairs={{0,32},{32,0},{64,96},{96,64},{128,160},{160,128},{192,224},{224,1... | collective-permute-start | bytes 884744 | tf_op jit(solution)/shard_map/ppermute | solution.py:37
  15.9 1.0 %pad_maximum_fusion.own_qg.refs_2_.refs_1_ = bf16[384,384]{1,0:T(8,128)(2,1)S(1)} fusion(bf16[192,384]{1,0:T(8,128)(2,1)} %bitcast.10, bf16[192,384]{1,0:T(8,128)(2,1)} %bitcast.11), kind=kLoop, calls=%fused_computation | loop fusion | flops 589824 | bytes 589824 | tf_op jit(solution)/shard_map/max | solution.py:239
  16.9 0.0 collective-permute-done.2.a_ref
  16.9 0.0 collective-permute-done.3.b_ref
  16.9 0.1 shard_map.84
  17.0 3.7 %collective-permute-start.7 = (bf16[784,384]{1,0:T(8,128)(2,1)S(1)}, bf16[784,384]{1,0:T(8,128)(2,1)S(1)}, u32[]{:S(2)}, u32[]{:S(2)}) collective-permute-start(bf16[784,384]{1,0:T(8,128)(2,1)S(1)} %get-tuple-element.31), channel_id=1, source_target_pairs={{32,64},{64,32},{96,128},{128,96},{160,192},{192,160},{224,256},{2... | collective-permute-start | bytes 1806344 | tf_op jit(solution)/shard_map/ppermute | solution.py:37
  20.7 0.0 collective-permute-done.kv_fb.refs_0_
  20.8 0.0 collective-permute-done.1.kv_fa.refs_1_
  20.8 1.9 %collective-permute-start.6 = (bf16[768,384]{1,0:T(8,128)(2,1)S(1)}, bf16[768,384]{1,0:T(8,128)(2,1)S(1)}, u32[]{:S(2)}, u32[]{:S(2)}) collective-permute-start(bf16[768,384]{1,0:T(8,128)(2,1)S(1)} %get-tuple-element.30.kv_rows), channel_id=1, source_target_pairs={{0,32},{32,0},{64,96},{96,64},{128,160},{160,128},{192,224},{224,1... | collective-permute-start | bytes 1769480 | tf_op jit(solution)/shard_map/ppermute | solution.py:37
  22.7 3.4 %collective-permute-start.4 = (bf16[384,384]{1,0:T(8,128)(2,1)S(1)}, bf16[384,384]{1,0:T(8,128)(2,1)S(1)}, u32[]{:S(2)}, u32[]{:S(2)}) collective-permute-start(bf16[384,384]{1,0:T(8,128)(2,1)S(1)} %pad_maximum_fusion.own_qg.refs_2_.refs_1_), channel_id=1, source_target_pairs={{4,8},{8,4},{12,16},{16,12},{20,24},{24,20},{5,9},{9,5},{13,17},{1... | collective-permute-start | bytes 884744 | tf_op jit(solution)/shard_map/ppermute | solution.py:37
  26.1 1.9 %collective-permute-start.5 = (bf16[384,384]{1,0:T(8,128)(2,1)S(1)}, bf16[384,384]{1,0:T(8,128)(2,1)S(1)}, u32[]{:S(2)}, u32[]{:S(2)}) collective-permute-start(bf16[384,384]{1,0:T(8,128)(2,1)S(1)} %pad_maximum_fusion.own_qg.refs_2_.refs_1_), channel_id=1, source_target_pairs={{0,4},{4,0},{8,12},{12,8},{16,20},{20,16},{24,28},{28,24},{1,5},{5... | collective-permute-start | bytes 884744 | tf_op jit(solution)/shard_map/ppermute | solution.py:37
  28.0 0.0 collective-permute-done.6.corner_fa
  28.0 0.7 collective-permute-done.7.corner_fb
  28.7 0.0 copy-done
  28.7 3.4 %shard_map.85 = (bf16[192,384]{1,0:T(8,128)(2,1)S(1)}, f32[8,192]{1,0:T(8,128)S(1)}, f32[192,128]{1,0:T(8,128)S(1)}, f32[1,1728]{1,0:T(1,128)S(1)}, bf16[1728,38...) custom-call(s32[1,1,1,27]{3,2,1,0:T(1,128)S(1)} %copy-done, s32[1,1,1,27]{3,2,1,0:T(1,128)S(1)} %copy-done, ...), custom_call_target="tpu_custom_call" | custom-call | tf_op jit(solution)/shard_map/pallas_call | solution.py:261
  32.1 2.7 %collective-permute-start.8 = (f32[8,192]{1,0:T(8,128)S(1)}, f32[8,192]{1,0:T(8,128)S(1)}, u32[]{:S(2)}, u32[]{:S(2)}) collective-permute-start(f32[8,192]{1,0:T(8,128)S(1)} %get-tuple-element.32.refs_5_.refs_4_), channel_id=1, source_target_pairs={{0,4},{4,0},{8,12},{12,8},{16,20},{20,16},{24,28},{28,24},{1,5},{5... | collective-permute-start | bytes 18440 | tf_op jit(solution)/shard_map/ppermute | solution.py:37
  34.8 6.2 %collective-permute-start.9 = (f32[8,192]{1,0:T(8,128)S(1)}, f32[8,192]{1,0:T(8,128)S(1)}, u32[]{:S(2)}, u32[]{:S(2)}) collective-permute-start(f32[8,192]{1,0:T(8,128)S(1)} %get-tuple-element.32.refs_5_.refs_4_), channel_id=1, source_target_pairs={{4,8},{8,4},{12,16},{16,12},{20,24},{24,20},{5,9},{9,5},{13,17},{1... | collective-permute-start | bytes 18440 | tf_op jit(solution)/shard_map/ppermute | solution.py:37
  40.9 0.0 collective-permute-done.4.refs_3_.refs_2_
  41.0 0.0 collective-permute-done.5.refs_4_.refs_3_
  41.0 0.0 collective-permute-done.8.refs_6_.refs_5_
  41.0 1.0 %collective-permute-done.9.refs_7_.refs_6_ = f32[8,192]{1,0:T(8,128)S(1)} collective-permute-done((f32[8,192]{1,0:T(8,128)S(1)}, f32[8,192]{1,0:T(8,128)S(1)}, u32[]{:S(2)}, u32[]{:S(2)}) %collective-permute-start.9) | collective-permute-done | bytes 6176 | tf_op jit(solution)/shard_map/ppermute | solution.py:37
  42.0 1.8 %shard_map.86 = (bf16[400,384]{1,0:T(8,128)(2,1)S(1)}, bf16[384,384]{1,0:T(8,128)(2,1)S(1)}) custom-call(bf16[384,384]{1,0:T(8,128)(2,1)S(1)} %collective-permute-done.kv_fb.refs_0_, bf16[384,384]{1,0:T(8,128)(2,1)S(1)} %collective-permute-done.1.kv_fa.refs_1_, bf16[384,384]{1,0:T(8,128)(2,1)S(1)} %pad_maximum_fusion.own_qg.refs_2_.refs_1_, ...), custom_call_target="tpu_custom_call" | custom-call | tf_op jit(solution)/shard_map/pallas_call | solution.py:278
  43.8 4.9 %collective-permute-start.10 = (bf16[400,384]{1,0:T(8,128)(2,1)S(1)}, bf16[400,384]{1,0:T(8,128)(2,1)S(1)}, u32[]{:S(2)}, u32[]{:S(2)}) collective-permute-start(bf16[400,384]{1,0:T(8,128)(2,1)S(1)} %get-tuple-element.33), channel_id=1, source_target_pairs={{32,64},{64,32},{96,128},{128,96},{160,192},{192,160},{224,256},{2... | collective-permute-start | bytes 921608 | tf_op jit(solution)/shard_map/ppermute | solution.py:37
  48.7 1.9 %collective-permute-start.11 = (bf16[384,384]{1,0:T(8,128)(2,1)S(1)}, bf16[384,384]{1,0:T(8,128)(2,1)S(1)}, u32[]{:S(2)}, u32[]{:S(2)}) collective-permute-start(bf16[384,384]{1,0:T(8,128)(2,1)S(1)} %get-tuple-element.35), channel_id=1, source_target_pairs={{0,32},{32,0},{64,96},{96,64},{128,160},{160,128},{192,224},{224,1... | collective-permute-start | bytes 884744 | tf_op jit(solution)/shard_map/ppermute | solution.py:37
  50.6 1.1 %shard_map.87.own_ref = f32[384,384]{1,0:T(8,128)S(1)} custom-call(bf16[384,384]{1,0:T(8,128)(2,1)S(1)} %pad_maximum_fusion.1.kv.refs_0_, bf16[384,384]{1,0:T(8,128)(2,1)S(1)} %pad_maximum_fusion.own_qg.refs_2_.refs_1_, bf16[384,384]{1,0:T(8,128)(2,1)S(1)} %collective-permute-done.4.refs_3_.refs_2_, ...), custom_call_target="tpu_custom_call" | custom-call | tf_op jit(solution)/shard_map/pallas_call | solution.py:278
  51.7 0.5 collective-permute-done.11.got_a
  52.2 2.2 %shard_map.88.query_blocks = bf16[4,2,48,384]{3,2,1,0:T(8,128)(2,1)S(1)} custom-call(bf16[384,384]{1,0:T(8,128)(2,1)S(1)} %pad_maximum_fusion.own_qg.refs_2_.refs_1_, bf16[1728,384]{1,0:T(8,128)(2,1)S(1)} %get-tuple-element.37.key_ref, bf16[1728,384]{1,0:T(8,128)(2,1)S(1)} %get-tuple-element.38.value_ref, ...), custom_call_target="tpu_custom_call" | custom-call | tf_op jit(solution)/shard_map/pallas_call | solution.py:289
  54.4 0.0 collective-permute-done.10.got_b
  54.4 0.3 shard_map.89
  54.7 7.5 %collective-permute-start.12 = (bf16[4,48,384]{2,1,0:T(8,128)(2,1)S(1)}, bf16[4,48,384]{2,1,0:T(8,128)(2,1)S(1)}, u32[]{:S(2)}, u32[]{:S(2)}) collective-permute-start(bf16[4,48,384]{2,1,0:T(8,128)(2,1)S(1)} %get-tuple-element.42), channel_id=1, source_target_pairs={{0,2},{1,3},{2,0},{3,1},{4,6},{5,7},{6,4},{7,5},{8,10},{9,11},{10,... | collective-permute-start | bytes 442376 | tf_op jit(solution)/shard_map/ppermute | solution.py:233
  62.1 2.0 %collective-permute-start.13 = (bf16[4,48,384]{2,1,0:T(8,128)(2,1)S(1)}, bf16[4,48,384]{2,1,0:T(8,128)(2,1)S(1)}, u32[]{:S(2)}, u32[]{:S(2)}) collective-permute-start(bf16[4,48,384]{2,1,0:T(8,128)(2,1)S(1)} %get-tuple-element.43), channel_id=1, source_target_pairs={{0,3},{1,2},{2,1},{3,0},{4,7},{5,6},{6,5},{7,4},{8,11},{9,10},{10,... | collective-permute-start | bytes 442376 | tf_op jit(solution)/shard_map/ppermute | solution.py:233
  64.1 2.4 %collective-permute-start.14 = (bf16[4,48,384]{2,1,0:T(8,128)(2,1)S(1)}, bf16[4,48,384]{2,1,0:T(8,128)(2,1)S(1)}, u32[]{:S(2)}, u32[]{:S(2)}) collective-permute-start(bf16[4,48,384]{2,1,0:T(8,128)(2,1)S(1)} %get-tuple-element.44), channel_id=1, source_target_pairs={{0,1},{1,0},{2,3},{3,2},{4,5},{5,4},{6,7},{7,6},{8,9},{9,8},{10,11... | collective-permute-start | bytes 442376 | tf_op jit(solution)/shard_map/ppermute | solution.py:233
  66.5 0.0 collective-permute-done.12.refs_0_
  66.5 9.6 %collective-permute-done.13.refs_1_ = bf16[4,48,384]{2,1,0:T(8,128)(2,1)S(1)} collective-permute-done((bf16[4,48,384]{2,1,0:T(8,128)(2,1)S(1)}, bf16[4,48,384]{2,1,0:T(8,128)(2,1)S(1)}, u32[]{:S(2)}, u32[]{:S(2)}) %collective-permute-start.13) | collective-permute-done | bytes 147488 | tf_op jit(solution)/shard_map/ppermute | solution.py:233
  76.1 1.5 %collective-permute-done.14.refs_2_ = bf16[4,48,384]{2,1,0:T(8,128)(2,1)S(1)} collective-permute-done((bf16[4,48,384]{2,1,0:T(8,128)(2,1)S(1)}, bf16[4,48,384]{2,1,0:T(8,128)(2,1)S(1)}, u32[]{:S(2)}, u32[]{:S(2)}) %collective-permute-start.14) | collective-permute-done | bytes 147488 | tf_op jit(solution)/shard_map/ppermute | solution.py:233
  77.5 1.0 %shard_map.90 = (bf16[24,2,1536]{2,1,0:T(2,128)(2,1)}, bf16[24,2,1536]{2,1,0:T(2,128)(2,1)}, bf16[24,2,1536]{2,1,0:T(2,128)(2,1)}, bf16[24,2,1536]{2,1,0:T(2,128)(2,1)}) custom-call(bf16[4,48,384]{2,1,0:T(8,128)(2,1)S(1)} %collective-permute-done.12.refs_0_, bf16[4,48,384]{2,1,0:T(8,128)(2,1)S(1)} %collective-permute-done.13.refs_1_, ...), custom_call_target="tpu_custom_call" | custom-call | tf_op jit(solution)/shard_map/pallas_call | solution.py:304
Async XLA Ops:
  0.6 28.1 %copy-start = (s32[1,1,1,27]{3,2,1,0:T(1,128)S(1)}, s32[1,1,1,27]{3,2,1,0:T(1,128)}, u32[]{:S(2)}) copy-start(s32[1,1,1,27]{3,2,1,0:T(1,128)} %pairs_v.1) | copy-start | bytes 328
  1.7 15.2 %collective-permute-start.2 = (bf16[384,384]{1,0:T(8,128)(2,1)S(1)}, bf16[384,384]{1,0:T(8,128)(2,1)S(1)}, u32[]{:S(2)}, u32[]{:S(2)}) collective-permute-start(bf16[384,384]{1,0:T(8,128)(2,1)S(1)} %pad_maximum_fusion.1.kv.refs_0_), channel_id=1, source_target_pairs={{0,4},{4,0},{8,12},{12,8},{16,20},{20,16},{24,28},{28,24},{1,5},{5... | collective-permute-start | bytes 884744 | tf_op jit(solution)/shard_map/ppermute | solution.py:37
  3.6 13.3 %collective-permute-start.3 = (bf16[384,384]{1,0:T(8,128)(2,1)S(1)}, bf16[384,384]{1,0:T(8,128)(2,1)S(1)}, u32[]{:S(2)}, u32[]{:S(2)}) collective-permute-start(bf16[384,384]{1,0:T(8,128)(2,1)S(1)} %pad_maximum_fusion.1.kv.refs_0_), channel_id=1, source_target_pairs={{4,8},{8,4},{12,16},{16,12},{20,24},{24,20},{5,9},{9,5},{13,17},{1... | collective-permute-start | bytes 884744 | tf_op jit(solution)/shard_map/ppermute | solution.py:37
  9.7 11.1 %collective-permute-start = (bf16[384,384]{1,0:T(8,128)(2,1)S(1)}, bf16[384,384]{1,0:T(8,128)(2,1)S(1)}, u32[]{:S(2)}, u32[]{:S(2)}) collective-permute-start(bf16[384,384]{1,0:T(8,128)(2,1)S(1)} %pad_maximum_fusion.1.kv.refs_0_), channel_id=1, source_target_pairs={{32,64},{64,32},{96,128},{128,96},{160,192},{192,160},{224,256},{2... | collective-permute-start | bytes 884744 | tf_op jit(solution)/shard_map/ppermute | solution.py:37
  13.9 6.8 %collective-permute-start.1 = (bf16[384,384]{1,0:T(8,128)(2,1)S(1)}, bf16[384,384]{1,0:T(8,128)(2,1)S(1)}, u32[]{:S(2)}, u32[]{:S(2)}) collective-permute-start(bf16[384,384]{1,0:T(8,128)(2,1)S(1)} %pad_maximum_fusion.1.kv.refs_0_), channel_id=1, source_target_pairs={{0,32},{32,0},{64,96},{96,64},{128,160},{160,128},{192,224},{224,1... | collective-permute-start | bytes 884744 | tf_op jit(solution)/shard_map/ppermute | solution.py:37
  17.0 11.7 %collective-permute-start.7 = (bf16[784,384]{1,0:T(8,128)(2,1)S(1)}, bf16[784,384]{1,0:T(8,128)(2,1)S(1)}, u32[]{:S(2)}, u32[]{:S(2)}) collective-permute-start(bf16[784,384]{1,0:T(8,128)(2,1)S(1)} %get-tuple-element.31), channel_id=1, source_target_pairs={{32,64},{64,32},{96,128},{128,96},{160,192},{192,160},{224,256},{2... | collective-permute-start | bytes 1806344 | tf_op jit(solution)/shard_map/ppermute | solution.py:37
  20.8 7.2 %collective-permute-start.6 = (bf16[768,384]{1,0:T(8,128)(2,1)S(1)}, bf16[768,384]{1,0:T(8,128)(2,1)S(1)}, u32[]{:S(2)}, u32[]{:S(2)}) collective-permute-start(bf16[768,384]{1,0:T(8,128)(2,1)S(1)} %get-tuple-element.30.kv_rows), channel_id=1, source_target_pairs={{0,32},{32,0},{64,96},{96,64},{128,160},{160,128},{192,224},{224,1... | collective-permute-start | bytes 1769480 | tf_op jit(solution)/shard_map/ppermute | solution.py:37
  22.7 18.3 %collective-permute-start.4 = (bf16[384,384]{1,0:T(8,128)(2,1)S(1)}, bf16[384,384]{1,0:T(8,128)(2,1)S(1)}, u32[]{:S(2)}, u32[]{:S(2)}) collective-permute-start(bf16[384,384]{1,0:T(8,128)(2,1)S(1)} %pad_maximum_fusion.own_qg.refs_2_.refs_1_), channel_id=1, source_target_pairs={{4,8},{8,4},{12,16},{16,12},{20,24},{24,20},{5,9},{9,5},{13,17},{1... | collective-permute-start | bytes 884744 | tf_op jit(solution)/shard_map/ppermute | solution.py:37
  26.1 14.9 %collective-permute-start.5 = (bf16[384,384]{1,0:T(8,128)(2,1)S(1)}, bf16[384,384]{1,0:T(8,128)(2,1)S(1)}, u32[]{:S(2)}, u32[]{:S(2)}) collective-permute-start(bf16[384,384]{1,0:T(8,128)(2,1)S(1)} %pad_maximum_fusion.own_qg.refs_2_.refs_1_), channel_id=1, source_target_pairs={{0,4},{4,0},{8,12},{12,8},{16,20},{20,16},{24,28},{28,24},{1,5},{5... | collective-permute-start | bytes 884744 | tf_op jit(solution)/shard_map/ppermute | solution.py:37
  32.1 8.9 %collective-permute-start.8 = (f32[8,192]{1,0:T(8,128)S(1)}, f32[8,192]{1,0:T(8,128)S(1)}, u32[]{:S(2)}, u32[]{:S(2)}) collective-permute-start(f32[8,192]{1,0:T(8,128)S(1)} %get-tuple-element.32.refs_5_.refs_4_), channel_id=1, source_target_pairs={{0,4},{4,0},{8,12},{12,8},{16,20},{20,16},{24,28},{28,24},{1,5},{5... | collective-permute-start | bytes 18440 | tf_op jit(solution)/shard_map/ppermute | solution.py:37
  34.8 7.2 %collective-permute-start.9 = (f32[8,192]{1,0:T(8,128)S(1)}, f32[8,192]{1,0:T(8,128)S(1)}, u32[]{:S(2)}, u32[]{:S(2)}) collective-permute-start(f32[8,192]{1,0:T(8,128)S(1)} %get-tuple-element.32.refs_5_.refs_4_), channel_id=1, source_target_pairs={{4,8},{8,4},{12,16},{16,12},{20,24},{24,20},{5,9},{9,5},{13,17},{1... | collective-permute-start | bytes 18440 | tf_op jit(solution)/shard_map/ppermute | solution.py:37
  43.8 10.6 %collective-permute-start.10 = (bf16[400,384]{1,0:T(8,128)(2,1)S(1)}, bf16[400,384]{1,0:T(8,128)(2,1)S(1)}, u32[]{:S(2)}, u32[]{:S(2)}) collective-permute-start(bf16[400,384]{1,0:T(8,128)(2,1)S(1)} %get-tuple-element.33), channel_id=1, source_target_pairs={{32,64},{64,32},{96,128},{128,96},{160,192},{192,160},{224,256},{2... | collective-permute-start | bytes 921608 | tf_op jit(solution)/shard_map/ppermute | solution.py:37
  48.7 3.5 %collective-permute-start.11 = (bf16[384,384]{1,0:T(8,128)(2,1)S(1)}, bf16[384,384]{1,0:T(8,128)(2,1)S(1)}, u32[]{:S(2)}, u32[]{:S(2)}) collective-permute-start(bf16[384,384]{1,0:T(8,128)(2,1)S(1)} %get-tuple-element.35), channel_id=1, source_target_pairs={{0,32},{32,0},{64,96},{96,64},{128,160},{160,128},{192,224},{224,1... | collective-permute-start | bytes 884744 | tf_op jit(solution)/shard_map/ppermute | solution.py:37
  54.7 11.8 %collective-permute-start.12 = (bf16[4,48,384]{2,1,0:T(8,128)(2,1)S(1)}, bf16[4,48,384]{2,1,0:T(8,128)(2,1)S(1)}, u32[]{:S(2)}, u32[]{:S(2)}) collective-permute-start(bf16[4,48,384]{2,1,0:T(8,128)(2,1)S(1)} %get-tuple-element.42), channel_id=1, source_target_pairs={{0,2},{1,3},{2,0},{3,1},{4,6},{5,7},{6,4},{7,5},{8,10},{9,11},{10,... | collective-permute-start | bytes 442376 | tf_op jit(solution)/shard_map/ppermute | solution.py:233
  62.1 13.9 %collective-permute-start.13 = (bf16[4,48,384]{2,1,0:T(8,128)(2,1)S(1)}, bf16[4,48,384]{2,1,0:T(8,128)(2,1)S(1)}, u32[]{:S(2)}, u32[]{:S(2)}) collective-permute-start(bf16[4,48,384]{2,1,0:T(8,128)(2,1)S(1)} %get-tuple-element.43), channel_id=1, source_target_pairs={{0,3},{1,2},{2,1},{3,0},{4,7},{5,6},{6,5},{7,4},{8,11},{9,10},{10,... | collective-permute-start | bytes 442376 | tf_op jit(solution)/shard_map/ppermute | solution.py:233
  64.1 13.4 %collective-permute-start.14 = (bf16[4,48,384]{2,1,0:T(8,128)(2,1)S(1)}, bf16[4,48,384]{2,1,0:T(8,128)(2,1)S(1)}, u32[]{:S(2)}, u32[]{:S(2)}) collective-permute-start(bf16[4,48,384]{2,1,0:T(8,128)(2,1)S(1)} %get-tuple-element.44), channel_id=1, source_target_pairs={{0,1},{1,0},{2,3},{3,2},{4,5},{5,4},{6,7},{7,6},{8,9},{9,8},{10,11... | collective-permute-start | bytes 442376 | tf_op jit(solution)/shard_map/ppermute | solution.py:233

commit v11 on v10

--- a/solution.py
+++ b/solution.py
@@ -81,8 +81,8 @@
     ]
 
 
-def far_first(heads):
-    return [heads // 2] + [k for k in reversed(range(heads)) if k != heads // 2]
+def send_order(heads):
+    return list(reversed(range(heads)))
 
 
 def assemble_kernel(*refs):
@@ -90,7 +90,7 @@
     got_refs, out_refs = refs[:heads], refs[heads:]
     feats = got_refs[0].shape[2]
     me = lax.axis_index("head")
-    for k, ref in zip(far_first(heads), got_refs):
+    for k, ref in zip(send_order(heads), got_refs):
         place = pl.ds(pl.multiple_of((me ^ k) * feats, HEAD_DIM), feats)
         for i, out_ref in enumerate(out_refs):
             out_ref[:, :, place] = ref[i].reshape(out_ref.shape[:2] + (feats,))
@@ -298,7 +298,7 @@
         [VMEM] * 4,
         [VMEM] * heads,
     )(own, got_b, got_a, sent_q)
-    got = [head_swap(sent[k], k) for k in far_first(heads)]
+    got = [head_swap(sent[k], k) for k in send_order(heads)]
 
     out = jax.ShapeDtypeStruct((frames_dev * rows_dev, columns // heads, heads * feats), bf16)
     outs = call(assemble_kernel, [out] * 4, [VMEM] * heads, [VMEM] * 4)(*got)

time: 79 us -> 82.3 us (1.042)
  the two profiles are of different devices: /device:TPU:65 before, /device:TPU:193 now
where the time goes in v11:
time: 82.3 us; the launch traced here: 81.7 us
  starting transfers between devices  51.5 us (63%)
  waiting for transfers between devices  17.5 us (21%)
  Pallas kernels  9.8 us (12%)
  other arithmetic  2.03 us (2%)
  between operations  0.89 us (1%)
    ppermute x12, starting transfers between devices, pair_swap(): return lax.ppermute(value, axis, pairs)  39.7 us
    ppermute x3, waiting for transfers between devices, head_swap(): lax.ppermute(value, 'head', [(i, i ^ k) for i in range(count)])  13.8 us
    ppermute x3, starting transfers between devices, head_swap(): lax.ppermute(value, 'head', [(i, i ^ k) for i in range(count)])  11.8 us
    ppermute x12, waiting for transfers between devices, pair_swap(): return lax.ppermute(value, axis, pairs)  3.73 us
    pallas_call x1, Pallas kernels, body(): call(query_kernel, (jax.ShapeDtypeStruct((TILE, feats), bf16), jax.ShapeD...  3.38 us
    pallas_call x2, Pallas kernels, terms(): call(lambda *refs: key_kernel(sides, *refs), [jax.ShapeDtypeStruct((2 * T...  2.86 us
    pallas_call x1, Pallas kernels, body(): call(query_grad_kernel, jax.ShapeDtypeStruct((heads, 2, span, feats), bf1...  2.16 us
    max x2, other arithmetic, stacked(): jnp.maximum(low, jnp.pad(second, ((rows, 0), (0, 0)), constant_values=-jn...  2.03 us
  transfers between devices with their start and end apart: 15, of which 5 were waited for; matrix products, arithmetic and copies ran while one was open for 1% of the time, Pallas kernels for 8%

profile of v11, /device:TPU:193, one launch (start us, length us, event | category | flops | bytes accessed | tf_op | source)
XLA Modules:
  0.0 81.7 jit_solution(1922158092578111855)
XLA Ops:
  0.6 0.0 copy-start
  0.6 1.0 %pad_maximum_fusion.1.kv.refs_0_ = bf16[384,384]{1,0:T(8,128)(2,1)S(1)} fusion(bf16[192,384]{1,0:T(8,128)(2,1)} %bitcast.8, bf16[192,384]{1,0:T(8,128)(2,1)} %bitcast.9), kind=kLoop, calls=%fused_computation.1 | loop fusion | flops 589824 | bytes 589824 | tf_op jit(solution)/shard_map/max | solution.py:239
  1.7 1.9 %collective-permute-start.2 = (bf16[384,384]{1,0:T(8,128)(2,1)S(1)}, bf16[384,384]{1,0:T(8,128)(2,1)S(1)}, u32[]{:S(2)}, u32[]{:S(2)}) collective-permute-start(bf16[384,384]{1,0:T(8,128)(2,1)S(1)} %pad_maximum_fusion.1.kv.refs_0_), channel_id=1, source_target_pairs={{0,4},{4,0},{8,12},{12,8},{16,20},{20,16},{24,28},{28,24},{1,5},{5... | collective-permute-start | bytes 884744 | tf_op jit(solution)/shard_map/ppermute | solution.py:37
  3.6 6.4 %collective-permute-start.3 = (bf16[384,384]{1,0:T(8,128)(2,1)S(1)}, bf16[384,384]{1,0:T(8,128)(2,1)S(1)}, u32[]{:S(2)}, u32[]{:S(2)}) collective-permute-start(bf16[384,384]{1,0:T(8,128)(2,1)S(1)} %pad_maximum_fusion.1.kv.refs_0_), channel_id=1, source_target_pairs={{4,8},{8,4},{12,16},{16,12},{20,24},{24,20},{5,9},{9,5},{13,17},{1... | collective-permute-start | bytes 884744 | tf_op jit(solution)/shard_map/ppermute | solution.py:37
  10.0 4.2 %collective-permute-start = (bf16[384,384]{1,0:T(8,128)(2,1)S(1)}, bf16[384,384]{1,0:T(8,128)(2,1)S(1)}, u32[]{:S(2)}, u32[]{:S(2)}) collective-permute-start(bf16[384,384]{1,0:T(8,128)(2,1)S(1)} %pad_maximum_fusion.1.kv.refs_0_), channel_id=1, source_target_pairs={{32,64},{64,32},{96,128},{128,96},{160,192},{192,160},{224,256},{2... | collective-permute-start | bytes 884744 | tf_op jit(solution)/shard_map/ppermute | solution.py:37
  14.2 1.9 %collective-permute-start.1 = (bf16[384,384]{1,0:T(8,128)(2,1)S(1)}, bf16[384,384]{1,0:T(8,128)(2,1)S(1)}, u32[]{:S(2)}, u32[]{:S(2)}) collective-permute-start(bf16[384,384]{1,0:T(8,128)(2,1)S(1)} %pad_maximum_fusion.1.kv.refs_0_), channel_id=1, source_target_pairs={{0,32},{32,0},{64,96},{96,64},{128,160},{160,128},{192,224},{224,1... | collective-permute-start | bytes 884744 | tf_op jit(solution)/shard_map/ppermute | solution.py:37
  16.2 1.0 %pad_maximum_fusion.own_qg.refs_2_.refs_1_ = bf16[384,384]{1,0:T(8,128)(2,1)S(1)} fusion(bf16[192,384]{1,0:T(8,128)(2,1)} %bitcast.10, bf16[192,384]{1,0:T(8,128)(2,1)} %bitcast.11), kind=kLoop, calls=%fused_computation | loop fusion | flops 589824 | bytes 589824 | tf_op jit(solution)/shard_map/max | solution.py:239
  17.2 0.0 collective-permute-done.2.a_ref
  17.2 0.0 collective-permute-done.3.b_ref
  17.2 0.1 shard_map.84
  17.3 3.7 %collective-permute-start.7 = (bf16[784,384]{1,0:T(8,128)(2,1)S(1)}, bf16[784,384]{1,0:T(8,128)(2,1)S(1)}, u32[]{:S(2)}, u32[]{:S(2)}) collective-permute-start(bf16[784,384]{1,0:T(8,128)(2,1)S(1)} %get-tuple-element.31), channel_id=1, source_target_pairs={{32,64},{64,32},{96,128},{128,96},{160,192},{192,160},{224,256},{2... | collective-permute-start | bytes 1806344 | tf_op jit(solution)/shard_map/ppermute | solution.py:37
  21.1 0.0 collective-permute-done.kv_fb.refs_0_
  21.1 0.0 collective-permute-done.1.kv_fa.refs_1_
  21.1 1.9 %collective-permute-start.6 = (bf16[768,384]{1,0:T(8,128)(2,1)S(1)}, bf16[768,384]{1,0:T(8,128)(2,1)S(1)}, u32[]{:S(2)}, u32[]{:S(2)}) collective-permute-start(bf16[768,384]{1,0:T(8,128)(2,1)S(1)} %get-tuple-element.30.kv_rows), channel_id=1, source_target_pairs={{0,32},{32,0},{64,96},{96,64},{128,160},{160,128},{192,224},{224,1... | collective-permute-start | bytes 1769480 | tf_op jit(solution)/shard_map/ppermute | solution.py:37
  23.0 4.6 %collective-permute-start.4 = (bf16[384,384]{1,0:T(8,128)(2,1)S(1)}, bf16[384,384]{1,0:T(8,128)(2,1)S(1)}, u32[]{:S(2)}, u32[]{:S(2)}) collective-permute-start(bf16[384,384]{1,0:T(8,128)(2,1)S(1)} %pad_maximum_fusion.own_qg.refs_2_.refs_1_), channel_id=1, source_target_pairs={{4,8},{8,4},{12,16},{16,12},{20,24},{24,20},{5,9},{9,5},{13,17},{1... | collective-permute-start | bytes 884744 | tf_op jit(solution)/shard_map/ppermute | solution.py:37
  27.6 1.9 %collective-permute-start.5 = (bf16[384,384]{1,0:T(8,128)(2,1)S(1)}, bf16[384,384]{1,0:T(8,128)(2,1)S(1)}, u32[]{:S(2)}, u32[]{:S(2)}) collective-permute-start(bf16[384,384]{1,0:T(8,128)(2,1)S(1)} %pad_maximum_fusion.own_qg.refs_2_.refs_1_), channel_id=1, source_target_pairs={{0,4},{4,0},{8,12},{12,8},{16,20},{20,16},{24,28},{28,24},{1,5},{5... | collective-permute-start | bytes 884744 | tf_op jit(solution)/shard_map/ppermute | solution.py:37
  29.5 0.0 collective-permute-done.6.corner_fa
  29.5 0.0 collective-permute-done.7.corner_fb
  29.5 0.0 copy-done
  29.5 3.4 %shard_map.85 = (bf16[192,384]{1,0:T(8,128)(2,1)S(1)}, f32[8,192]{1,0:T(8,128)S(1)}, f32[192,128]{1,0:T(8,128)S(1)}, f32[1,1728]{1,0:T(1,128)S(1)}, bf16[1728,38...) custom-call(s32[1,1,1,27]{3,2,1,0:T(1,128)S(1)} %copy-done, s32[1,1,1,27]{3,2,1,0:T(1,128)S(1)} %copy-done, ...), custom_call_target="tpu_custom_call" | custom-call | tf_op jit(solution)/shard_map/pallas_call | solution.py:261
  32.9 3.4 %collective-permute-start.8 = (f32[8,192]{1,0:T(8,128)S(1)}, f32[8,192]{1,0:T(8,128)S(1)}, u32[]{:S(2)}, u32[]{:S(2)}) collective-permute-start(f32[8,192]{1,0:T(8,128)S(1)} %get-tuple-element.32.refs_5_.refs_4_), channel_id=1, source_target_pairs={{0,4},{4,0},{8,12},{12,8},{16,20},{20,16},{24,28},{28,24},{1,5},{5... | collective-permute-start | bytes 18440 | tf_op jit(solution)/shard_map/ppermute | solution.py:37
  36.3 2.3 %collective-permute-start.9 = (f32[8,192]{1,0:T(8,128)S(1)}, f32[8,192]{1,0:T(8,128)S(1)}, u32[]{:S(2)}, u32[]{:S(2)}) collective-permute-start(f32[8,192]{1,0:T(8,128)S(1)} %get-tuple-element.32.refs_5_.refs_4_), channel_id=1, source_target_pairs={{4,8},{8,4},{12,16},{16,12},{20,24},{24,20},{5,9},{9,5},{13,17},{1... | collective-permute-start | bytes 18440 | tf_op jit(solution)/shard_map/ppermute | solution.py:37
  38.6 0.0 collective-permute-done.4.refs_3_.refs_2_
  38.6 0.0 collective-permute-done.5.refs_4_.refs_3_
  38.7 0.0 collective-permute-done.8.refs_6_.refs_5_
  38.7 3.2 %collective-permute-done.9.refs_7_.refs_6_ = f32[8,192]{1,0:T(8,128)S(1)} collective-permute-done((f32[8,192]{1,0:T(8,128)S(1)}, f32[8,192]{1,0:T(8,128)S(1)}, u32[]{:S(2)}, u32[]{:S(2)}) %collective-permute-start.9) | collective-permute-done | bytes 6176 | tf_op jit(solution)/shard_map/ppermute | solution.py:37
  41.9 1.8 %shard_map.86 = (bf16[400,384]{1,0:T(8,128)(2,1)S(1)}, bf16[384,384]{1,0:T(8,128)(2,1)S(1)}) custom-call(bf16[384,384]{1,0:T(8,128)(2,1)S(1)} %collective-permute-done.kv_fb.refs_0_, bf16[384,384]{1,0:T(8,128)(2,1)S(1)} %collective-permute-done.1.kv_fa.refs_1_, bf16[384,384]{1,0:T(8,128)(2,1)S(1)} %pad_maximum_fusion.own_qg.refs_2_.refs_1_, ...), custom_call_target="tpu_custom_call" | custom-call | tf_op jit(solution)/shard_map/pallas_call | solution.py:278
  43.7 5.5 %collective-permute-start.10 = (bf16[400,384]{1,0:T(8,128)(2,1)S(1)}, bf16[400,384]{1,0:T(8,128)(2,1)S(1)}, u32[]{:S(2)}, u32[]{:S(2)}) collective-permute-start(bf16[400,384]{1,0:T(8,128)(2,1)S(1)} %get-tuple-element.33), channel_id=1, source_target_pairs={{32,64},{64,32},{96,128},{128,96},{160,192},{192,160},{224,256},{2... | collective-permute-start | bytes 921608 | tf_op jit(solution)/shard_map/ppermute | solution.py:37
  49.2 1.9 %collective-permute-start.11 = (bf16[384,384]{1,0:T(8,128)(2,1)S(1)}, bf16[384,384]{1,0:T(8,128)(2,1)S(1)}, u32[]{:S(2)}, u32[]{:S(2)}) collective-permute-start(bf16[384,384]{1,0:T(8,128)(2,1)S(1)} %get-tuple-element.35), channel_id=1, source_target_pairs={{0,32},{32,0},{64,96},{96,64},{128,160},{160,128},{192,224},{224,1... | collective-permute-start | bytes 884744 | tf_op jit(solution)/shard_map/ppermute | solution.py:37
  51.1 1.1 %shard_map.87.own_ref = f32[384,384]{1,0:T(8,128)S(1)} custom-call(bf16[384,384]{1,0:T(8,128)(2,1)S(1)} %pad_maximum_fusion.1.kv.refs_0_, bf16[384,384]{1,0:T(8,128)(2,1)S(1)} %pad_maximum_fusion.own_qg.refs_2_.refs_1_, bf16[384,384]{1,0:T(8,128)(2,1)S(1)} %collective-permute-done.4.refs_3_.refs_2_, ...), custom_call_target="tpu_custom_call" | custom-call | tf_op jit(solution)/shard_map/pallas_call | solution.py:278
  52.2 0.5 collective-permute-done.11.got_a
  52.7 2.2 %shard_map.88.query_blocks = bf16[4,2,48,384]{3,2,1,0:T(8,128)(2,1)S(1)} custom-call(bf16[384,384]{1,0:T(8,128)(2,1)S(1)} %pad_maximum_fusion.own_qg.refs_2_.refs_1_, bf16[1728,384]{1,0:T(8,128)(2,1)S(1)} %get-tuple-element.37.key_ref, bf16[1728,384]{1,0:T(8,128)(2,1)S(1)} %get-tuple-element.38.value_ref, ...), custom_call_target="tpu_custom_call" | custom-call | tf_op jit(solution)/shard_map/pallas_call | solution.py:289
  54.9 0.0 collective-permute-done.10.got_b
  54.9 0.3 shard_map.89
  55.2 5.9 %collective-permute-start.12 = (bf16[4,48,384]{2,1,0:T(8,128)(2,1)S(1)}, bf16[4,48,384]{2,1,0:T(8,128)(2,1)S(1)}, u32[]{:S(2)}, u32[]{:S(2)}) collective-permute-start(bf16[4,48,384]{2,1,0:T(8,128)(2,1)S(1)} %get-tuple-element.42), channel_id=1, source_target_pairs={{0,3},{1,2},{2,1},{3,0},{4,7},{5,6},{6,5},{7,4},{8,11},{9,10},{10,... | collective-permute-start | bytes 442376 | tf_op jit(solution)/shard_map/ppermute | solution.py:233
  61.1 3.5 %collective-permute-start.13 = (bf16[4,48,384]{2,1,0:T(8,128)(2,1)S(1)}, bf16[4,48,384]{2,1,0:T(8,128)(2,1)S(1)}, u32[]{:S(2)}, u32[]{:S(2)}) collective-permute-start(bf16[4,48,384]{2,1,0:T(8,128)(2,1)S(1)} %get-tuple-element.43), channel_id=1, source_target_pairs={{0,2},{1,3},{2,0},{3,1},{4,6},{5,7},{6,4},{7,5},{8,10},{9,11},{10,... | collective-permute-start | bytes 442376 | tf_op jit(solution)/shard_map/ppermute | solution.py:233
  64.6 2.4 %collective-permute-start.14 = (bf16[4,48,384]{2,1,0:T(8,128)(2,1)S(1)}, bf16[4,48,384]{2,1,0:T(8,128)(2,1)S(1)}, u32[]{:S(2)}, u32[]{:S(2)}) collective-permute-start(bf16[4,48,384]{2,1,0:T(8,128)(2,1)S(1)} %get-tuple-element.44), channel_id=1, source_target_pairs={{0,1},{1,0},{2,3},{3,2},{4,5},{5,4},{6,7},{7,6},{8,9},{9,8},{10,11... | collective-permute-start | bytes 442376 | tf_op jit(solution)/shard_map/ppermute | solution.py:233
  67.0 6.2 %collective-permute-done.12.refs_0_ = bf16[4,48,384]{2,1,0:T(8,128)(2,1)S(1)} collective-permute-done((bf16[4,48,384]{2,1,0:T(8,128)(2,1)S(1)}, bf16[4,48,384]{2,1,0:T(8,128)(2,1)S(1)}, u32[]{:S(2)}, u32[]{:S(2)}) %collective-permute-start.12) | collective-permute-done | bytes 147488 | tf_op jit(solution)/shard_map/ppermute | solution.py:233
  73.1 2.7 %collective-permute-done.13.refs_1_ = bf16[4,48,384]{2,1,0:T(8,128)(2,1)S(1)} collective-permute-done((bf16[4,48,384]{2,1,0:T(8,128)(2,1)S(1)}, bf16[4,48,384]{2,1,0:T(8,128)(2,1)S(1)}, u32[]{:S(2)}, u32[]{:S(2)}) %collective-permute-start.13) | collective-permute-done | bytes 147488 | tf_op jit(solution)/shard_map/ppermute | solution.py:233
  75.9 4.9 %collective-permute-done.14.refs_2_ = bf16[4,48,384]{2,1,0:T(8,128)(2,1)S(1)} collective-permute-done((bf16[4,48,384]{2,1,0:T(8,128)(2,1)S(1)}, bf16[4,48,384]{2,1,0:T(8,128)(2,1)S(1)}, u32[]{:S(2)}, u32[]{:S(2)}) %collective-permute-start.14) | collective-permute-done | bytes 147488 | tf_op jit(solution)/shard_map/ppermute | solution.py:233
  80.8 1.0 %shard_map.90 = (bf16[24,2,1536]{2,1,0:T(2,128)(2,1)}, bf16[24,2,1536]{2,1,0:T(2,128)(2,1)}, bf16[24,2,1536]{2,1,0:T(2,128)(2,1)}, bf16[24,2,1536]{2,1,0:T(2,128)(2,1)}) custom-call(bf16[4,48,384]{2,1,0:T(8,128)(2,1)S(1)} %collective-permute-done.12.refs_0_, bf16[4,48,384]{2,1,0:T(8,128)(2,1)S(1)} %collective-permute-done.13.refs_1_, ...), custom_call_target="tpu_custom_call" | custom-call | tf_op jit(solution)/shard_map/pallas_call | solution.py:304
Async XLA Ops:
  0.6 28.9 %copy-start = (s32[1,1,1,27]{3,2,1,0:T(1,128)S(1)}, s32[1,1,1,27]{3,2,1,0:T(1,128)}, u32[]{:S(2)}) copy-start(s32[1,1,1,27]{3,2,1,0:T(1,128)} %pairs_v.1) | copy-start | bytes 328
  1.7 15.5 %collective-permute-start.2 = (bf16[384,384]{1,0:T(8,128)(2,1)S(1)}, bf16[384,384]{1,0:T(8,128)(2,1)S(1)}, u32[]{:S(2)}, u32[]{:S(2)}) collective-permute-start(bf16[384,384]{1,0:T(8,128)(2,1)S(1)} %pad_maximum_fusion.1.kv.refs_0_), channel_id=1, source_target_pairs={{0,4},{4,0},{8,12},{12,8},{16,20},{20,16},{24,28},{28,24},{1,5},{5... | collective-permute-start | bytes 884744 | tf_op jit(solution)/shard_map/ppermute | solution.py:37
  3.6 13.6 %collective-permute-start.3 = (bf16[384,384]{1,0:T(8,128)(2,1)S(1)}, bf16[384,384]{1,0:T(8,128)(2,1)S(1)}, u32[]{:S(2)}, u32[]{:S(2)}) collective-permute-start(bf16[384,384]{1,0:T(8,128)(2,1)S(1)} %pad_maximum_fusion.1.kv.refs_0_), channel_id=1, source_target_pairs={{4,8},{8,4},{12,16},{16,12},{20,24},{24,20},{5,9},{9,5},{13,17},{1... | collective-permute-start | bytes 884744 | tf_op jit(solution)/shard_map/ppermute | solution.py:37
  10.0 11.1 %collective-permute-start = (bf16[384,384]{1,0:T(8,128)(2,1)S(1)}, bf16[384,384]{1,0:T(8,128)(2,1)S(1)}, u32[]{:S(2)}, u32[]{:S(2)}) collective-permute-start(bf16[384,384]{1,0:T(8,128)(2,1)S(1)} %pad_maximum_fusion.1.kv.refs_0_), channel_id=1, source_target_pairs={{32,64},{64,32},{96,128},{128,96},{160,192},{192,160},{224,256},{2... | collective-permute-start | bytes 884744 | tf_op jit(solution)/shard_map/ppermute | solution.py:37
  14.2 6.8 %collective-permute-start.1 = (bf16[384,384]{1,0:T(8,128)(2,1)S(1)}, bf16[384,384]{1,0:T(8,128)(2,1)S(1)}, u32[]{:S(2)}, u32[]{:S(2)}) collective-permute-start(bf16[384,384]{1,0:T(8,128)(2,1)S(1)} %pad_maximum_fusion.1.kv.refs_0_), channel_id=1, source_target_pairs={{0,32},{32,0},{64,96},{96,64},{128,160},{160,128},{192,224},{224,1... | collective-permute-start | bytes 884744 | tf_op jit(solution)/shard_map/ppermute | solution.py:37
  17.3 12.2 %collective-permute-start.7 = (bf16[784,384]{1,0:T(8,128)(2,1)S(1)}, bf16[784,384]{1,0:T(8,128)(2,1)S(1)}, u32[]{:S(2)}, u32[]{:S(2)}) collective-permute-start(bf16[784,384]{1,0:T(8,128)(2,1)S(1)} %get-tuple-element.31), channel_id=1, source_target_pairs={{32,64},{64,32},{96,128},{128,96},{160,192},{192,160},{224,256},{2... | collective-permute-start | bytes 1806344 | tf_op jit(solution)/shard_map/ppermute | solution.py:37
  21.1 8.4 %collective-permute-start.6 = (bf16[768,384]{1,0:T(8,128)(2,1)S(1)}, bf16[768,384]{1,0:T(8,128)(2,1)S(1)}, u32[]{:S(2)}, u32[]{:S(2)}) collective-permute-start(bf16[768,384]{1,0:T(8,128)(2,1)S(1)} %get-tuple-element.30.kv_rows), channel_id=1, source_target_pairs={{0,32},{32,0},{64,96},{96,64},{128,160},{160,128},{192,224},{224,1... | collective-permute-start | bytes 1769480 | tf_op jit(solution)/shard_map/ppermute | solution.py:37
  23.0 15.6 %collective-permute-start.4 = (bf16[384,384]{1,0:T(8,128)(2,1)S(1)}, bf16[384,384]{1,0:T(8,128)(2,1)S(1)}, u32[]{:S(2)}, u32[]{:S(2)}) collective-permute-start(bf16[384,384]{1,0:T(8,128)(2,1)S(1)} %pad_maximum_fusion.own_qg.refs_2_.refs_1_), channel_id=1, source_target_pairs={{4,8},{8,4},{12,16},{16,12},{20,24},{24,20},{5,9},{9,5},{13,17},{1... | collective-permute-start | bytes 884744 | tf_op jit(solution)/shard_map/ppermute | solution.py:37
  27.6 11.1 %collective-permute-start.5 = (bf16[384,384]{1,0:T(8,128)(2,1)S(1)}, bf16[384,384]{1,0:T(8,128)(2,1)S(1)}, u32[]{:S(2)}, u32[]{:S(2)}) collective-permute-start(bf16[384,384]{1,0:T(8,128)(2,1)S(1)} %pad_maximum_fusion.own_qg.refs_2_.refs_1_), channel_id=1, source_target_pairs={{0,4},{4,0},{8,12},{12,8},{16,20},{20,16},{24,28},{28,24},{1,5},{5... | collective-permute-start | bytes 884744 | tf_op jit(solution)/shard_map/ppermute | solution.py:37
  32.9 5.7 %collective-permute-start.8 = (f32[8,192]{1,0:T(8,128)S(1)}, f32[8,192]{1,0:T(8,128)S(1)}, u32[]{:S(2)}, u32[]{:S(2)}) collective-permute-start(f32[8,192]{1,0:T(8,128)S(1)} %get-tuple-element.32.refs_5_.refs_4_), channel_id=1, source_target_pairs={{0,4},{4,0},{8,12},{12,8},{16,20},{20,16},{24,28},{28,24},{1,5},{5... | collective-permute-start | bytes 18440 | tf_op jit(solution)/shard_map/ppermute | solution.py:37
  36.3 5.6 %collective-permute-start.9 = (f32[8,192]{1,0:T(8,128)S(1)}, f32[8,192]{1,0:T(8,128)S(1)}, u32[]{:S(2)}, u32[]{:S(2)}) collective-permute-start(f32[8,192]{1,0:T(8,128)S(1)} %get-tuple-element.32.refs_5_.refs_4_), channel_id=1, source_target_pairs={{4,8},{8,4},{12,16},{16,12},{20,24},{24,20},{5,9},{9,5},{13,17},{1... | collective-permute-start | bytes 18440 | tf_op jit(solution)/shard_map/ppermute | solution.py:37
  43.7 11.1 %collective-permute-start.10 = (bf16[400,384]{1,0:T(8,128)(2,1)S(1)}, bf16[400,384]{1,0:T(8,128)(2,1)S(1)}, u32[]{:S(2)}, u32[]{:S(2)}) collective-permute-start(bf16[400,384]{1,0:T(8,128)(2,1)S(1)} %get-tuple-element.33), channel_id=1, source_target_pairs={{32,64},{64,32},{96,128},{128,96},{160,192},{192,160},{224,256},{2... | collective-permute-start | bytes 921608 | tf_op jit(solution)/shard_map/ppermute | solution.py:37
  49.2 3.5 %collective-permute-start.11 = (bf16[384,384]{1,0:T(8,128)(2,1)S(1)}, bf16[384,384]{1,0:T(8,128)(2,1)S(1)}, u32[]{:S(2)}, u32[]{:S(2)}) collective-permute-start(bf16[384,384]{1,0:T(8,128)(2,1)S(1)} %get-tuple-element.35), channel_id=1, source_target_pairs={{0,32},{32,0},{64,96},{96,64},{128,160},{160,128},{192,224},{224,1... | collective-permute-start | bytes 884744 | tf_op jit(solution)/shard_map/ppermute | solution.py:37
  55.2 18.0 %collective-permute-start.12 = (bf16[4,48,384]{2,1,0:T(8,128)(2,1)S(1)}, bf16[4,48,384]{2,1,0:T(8,128)(2,1)S(1)}, u32[]{:S(2)}, u32[]{:S(2)}) collective-permute-start(bf16[4,48,384]{2,1,0:T(8,128)(2,1)S(1)} %get-tuple-element.42), channel_id=1, source_target_pairs={{0,3},{1,2},{2,1},{3,0},{4,7},{5,6},{6,5},{7,4},{8,11},{9,10},{10,... | collective-permute-start | bytes 442376 | tf_op jit(solution)/shard_map/ppermute | solution.py:233
  61.1 14.8 %collective-permute-start.13 = (bf16[4,48,384]{2,1,0:T(8,128)(2,1)S(1)}, bf16[4,48,384]{2,1,0:T(8,128)(2,1)S(1)}, u32[]{:S(2)}, u32[]{:S(2)}) collective-permute-start(bf16[4,48,384]{2,1,0:T(8,128)(2,1)S(1)} %get-tuple-element.43), channel_id=1, source_target_pairs={{0,2},{1,3},{2,0},{3,1},{4,6},{5,7},{6,4},{7,5},{8,10},{9,11},{10,... | collective-permute-start | bytes 442376 | tf_op jit(solution)/shard_map/ppermute | solution.py:233
  64.6 16.1 %collective-permute-start.14 = (bf16[4,48,384]{2,1,0:T(8,128)(2,1)S(1)}, bf16[4,48,384]{2,1,0:T(8,128)(2,1)S(1)}, u32[]{:S(2)}, u32[]{:S(2)}) collective-permute-start(bf16[4,48,384]{2,1,0:T(8,128)(2,1)S(1)} %get-tuple-element.44), channel_id=1, source_target_pairs={{0,1},{1,0},{2,3},{3,2},{4,5},{5,4},{6,7},{7,6},{8,9},{9,8},{10,11... | collective-permute-start | bytes 442376 | tf_op jit(solution)/shard_map/ppermute | solution.py:233

commit v12 on v10

--- a/solution.py
+++ b/solution.py
@@ -291,7 +291,7 @@
         jax.ShapeDtypeStruct((heads, 2, span, feats), bf16),
         [VMEM] * 6,
         VMEM,
-    )(after(qg, got_a), key_near, value_near, attended, column, bias)
+    )(after(qg, term_b), key_near, value_near, attended, column, bias)
     sent = call(
         fold_kernel,
         [jax.ShapeDtypeStruct((4, span, feats), bf16)] * heads,

time: 79 us -> 78.9 us (level)
  transfers between devices with their start and end apart: 15 -> 15, of which waited for: 5 -> 4; matrix products, arithmetic and copies ran while one was open for 1% -> 1% of each run, Pallas kernels for 9% -> 9%
where the time goes in v12:
time: 78.9 us; the launch traced here: 78.4 us
  starting transfers between devices  52.6 us (67%)
  waiting for transfers between devices  13.1 us (17%)
  Pallas kernels  9.84 us (12%)
  other arithmetic  2.03 us (3%)
  between operations  0.89 us (1%)
    ppermute x12, starting transfers between devices, pair_swap(): return lax.ppermute(value, axis, pairs)  40.8 us
    ppermute x3, starting transfers between devices, head_swap(): lax.ppermute(value, 'head', [(i, i ^ k) for i in range(count)])  11.8 us
    ppermute x3, waiting for transfers between devices, head_swap(): lax.ppermute(value, 'head', [(i, i ^ k) for i in range(count)])  11.3 us
    pallas_call x1, Pallas kernels, body(): call(query_kernel, (jax.ShapeDtypeStruct((TILE, feats), bf16), jax.ShapeD...  3.4 us
    pallas_call x2, Pallas kernels, terms(): call(lambda *refs: key_kernel(sides, *refs), [jax.ShapeDtypeStruct((2 * T...  2.87 us
    pallas_call x1, Pallas kernels, body(): call(query_grad_kernel, jax.ShapeDtypeStruct((heads, 2, span, feats), bf1...  2.17 us
    max x2, other arithmetic, stacked(): jnp.maximum(low, jnp.pad(second, ((rows, 0), (0, 0)), constant_values=-jn...  2.03 us
    ppermute x12, waiting for transfers between devices, pair_swap(): return lax.ppermute(value, axis, pairs)  1.74 us
  transfers between devices with their start and end apart: 15, of which 4 were waited for; matrix products, arithmetic and copies ran while one was open for 1% of the time, Pallas kernels for 9%

profile of v12, /device:TPU:65, one launch (start us, length us, event | category | flops | bytes accessed | tf_op | source)
XLA Modules:
  0.0 78.4 jit_solution(2444455659683696964)
XLA Ops:
  0.6 0.0 copy-start
  0.6 1.0 %pad_maximum_fusion.1.kv.refs_0_ = bf16[384,384]{1,0:T(8,128)(2,1)S(1)} fusion(bf16[192,384]{1,0:T(8,128)(2,1)} %bitcast.8, bf16[192,384]{1,0:T(8,128)(2,1)} %bitcast.9), kind=kLoop, calls=%fused_computation.1 | loop fusion | flops 589824 | bytes 589824 | tf_op jit(solution)/shard_map/max | solution.py:239
  1.7 1.9 %collective-permute-start.2 = (bf16[384,384]{1,0:T(8,128)(2,1)S(1)}, bf16[384,384]{1,0:T(8,128)(2,1)S(1)}, u32[]{:S(2)}, u32[]{:S(2)}) collective-permute-start(bf16[384,384]{1,0:T(8,128)(2,1)S(1)} %pad_maximum_fusion.1.kv.refs_0_), channel_id=1, source_target_pairs={{0,4},{4,0},{8,12},{12,8},{16,20},{20,16},{24,28},{28,24},{1,5},{5... | collective-permute-start | bytes 884744 | tf_op jit(solution)/shard_map/ppermute | solution.py:37
  3.6 6.1 %collective-permute-start.3 = (bf16[384,384]{1,0:T(8,128)(2,1)S(1)}, bf16[384,384]{1,0:T(8,128)(2,1)S(1)}, u32[]{:S(2)}, u32[]{:S(2)}) collective-permute-start(bf16[384,384]{1,0:T(8,128)(2,1)S(1)} %pad_maximum_fusion.1.kv.refs_0_), channel_id=1, source_target_pairs={{4,8},{8,4},{12,16},{16,12},{20,24},{24,20},{5,9},{9,5},{13,17},{1... | collective-permute-start | bytes 884744 | tf_op jit(solution)/shard_map/ppermute | solution.py:37
  9.7 4.2 %collective-permute-start = (bf16[384,384]{1,0:T(8,128)(2,1)S(1)}, bf16[384,384]{1,0:T(8,128)(2,1)S(1)}, u32[]{:S(2)}, u32[]{:S(2)}) collective-permute-start(bf16[384,384]{1,0:T(8,128)(2,1)S(1)} %pad_maximum_fusion.1.kv.refs_0_), channel_id=1, source_target_pairs={{32,64},{64,32},{96,128},{128,96},{160,192},{192,160},{224,256},{2... | collective-permute-start | bytes 884744 | tf_op jit(solution)/shard_map/ppermute | solution.py:37
  13.9 1.9 %collective-permute-start.1 = (bf16[384,384]{1,0:T(8,128)(2,1)S(1)}, bf16[384,384]{1,0:T(8,128)(2,1)S(1)}, u32[]{:S(2)}, u32[]{:S(2)}) collective-permute-start(bf16[384,384]{1,0:T(8,128)(2,1)S(1)} %pad_maximum_fusion.1.kv.refs_0_), channel_id=1, source_target_pairs={{0,32},{32,0},{64,96},{96,64},{128,160},{160,128},{192,224},{224,1... | collective-permute-start | bytes 884744 | tf_op jit(solution)/shard_map/ppermute | solution.py:37
  15.9 1.0 %pad_maximum_fusion.own_qg.refs_2_.refs_1_ = bf16[384,384]{1,0:T(8,128)(2,1)S(1)} fusion(bf16[192,384]{1,0:T(8,128)(2,1)} %bitcast.10, bf16[192,384]{1,0:T(8,128)(2,1)} %bitcast.11), kind=kLoop, calls=%fused_computation | loop fusion | flops 589824 | bytes 589824 | tf_op jit(solution)/shard_map/max | solution.py:239
  16.9 0.0 collective-permute-done.2.a_ref
  16.9 0.0 collective-permute-done.3.b_ref
  16.9 0.1 shard_map.84
  17.0 3.7 %collective-permute-start.7 = (bf16[784,384]{1,0:T(8,128)(2,1)S(1)}, bf16[784,384]{1,0:T(8,128)(2,1)S(1)}, u32[]{:S(2)}, u32[]{:S(2)}) collective-permute-start(bf16[784,384]{1,0:T(8,128)(2,1)S(1)} %get-tuple-element.31), channel_id=1, source_target_pairs={{32,64},{64,32},{96,128},{128,96},{160,192},{192,160},{224,256},{2... | collective-permute-start | bytes 1806344 | tf_op jit(solution)/shard_map/ppermute | solution.py:37
  20.7 0.0 collective-permute-done.kv_fb.refs_0_
  20.8 0.0 collective-permute-done.1.kv_fa.refs_1_
  20.8 1.9 %collective-permute-start.6 = (bf16[768,384]{1,0:T(8,128)(2,1)S(1)}, bf16[768,384]{1,0:T(8,128)(2,1)S(1)}, u32[]{:S(2)}, u32[]{:S(2)}) collective-permute-start(bf16[768,384]{1,0:T(8,128)(2,1)S(1)} %get-tuple-element.30.kv_rows), channel_id=1, source_target_pairs={{0,32},{32,0},{64,96},{96,64},{128,160},{160,128},{192,224},{224,1... | collective-permute-start | bytes 1769480 | tf_op jit(solution)/shard_map/ppermute | solution.py:37
  22.7 3.4 %collective-permute-start.4 = (bf16[384,384]{1,0:T(8,128)(2,1)S(1)}, bf16[384,384]{1,0:T(8,128)(2,1)S(1)}, u32[]{:S(2)}, u32[]{:S(2)}) collective-permute-start(bf16[384,384]{1,0:T(8,128)(2,1)S(1)} %pad_maximum_fusion.own_qg.refs_2_.refs_1_), channel_id=1, source_target_pairs={{4,8},{8,4},{12,16},{16,12},{20,24},{24,20},{5,9},{9,5},{13,17},{1... | collective-permute-start | bytes 884744 | tf_op jit(solution)/shard_map/ppermute | solution.py:37
  26.1 1.9 %collective-permute-start.5 = (bf16[384,384]{1,0:T(8,128)(2,1)S(1)}, bf16[384,384]{1,0:T(8,128)(2,1)S(1)}, u32[]{:S(2)}, u32[]{:S(2)}) collective-permute-start(bf16[384,384]{1,0:T(8,128)(2,1)S(1)} %pad_maximum_fusion.own_qg.refs_2_.refs_1_), channel_id=1, source_target_pairs={{0,4},{4,0},{8,12},{12,8},{16,20},{20,16},{24,28},{28,24},{1,5},{5... | collective-permute-start | bytes 884744 | tf_op jit(solution)/shard_map/ppermute | solution.py:37
  28.0 0.0 collective-permute-done.6.corner_fa
  28.0 0.7 collective-permute-done.7.corner_fb
  28.7 0.0 copy-done
  28.7 3.4 %shard_map.85 = (bf16[192,384]{1,0:T(8,128)(2,1)S(1)}, f32[8,192]{1,0:T(8,128)S(1)}, f32[192,128]{1,0:T(8,128)S(1)}, f32[1,1728]{1,0:T(1,128)S(1)}, bf16[1728,38...) custom-call(s32[1,1,1,27]{3,2,1,0:T(1,128)S(1)} %copy-done, s32[1,1,1,27]{3,2,1,0:T(1,128)S(1)} %copy-done, ...), custom_call_target="tpu_custom_call" | custom-call | tf_op jit(solution)/shard_map/pallas_call | solution.py:261
  32.1 2.7 %collective-permute-start.8 = (f32[8,192]{1,0:T(8,128)S(1)}, f32[8,192]{1,0:T(8,128)S(1)}, u32[]{:S(2)}, u32[]{:S(2)}) collective-permute-start(f32[8,192]{1,0:T(8,128)S(1)} %get-tuple-element.32.refs_5_.refs_4_), channel_id=1, source_target_pairs={{0,4},{4,0},{8,12},{12,8},{16,20},{20,16},{24,28},{28,24},{1,5},{5... | collective-permute-start | bytes 18440 | tf_op jit(solution)/shard_map/ppermute | solution.py:37
  34.8 6.2 %collective-permute-start.9 = (f32[8,192]{1,0:T(8,128)S(1)}, f32[8,192]{1,0:T(8,128)S(1)}, u32[]{:S(2)}, u32[]{:S(2)}) collective-permute-start(f32[8,192]{1,0:T(8,128)S(1)} %get-tuple-element.32.refs_5_.refs_4_), channel_id=1, source_target_pairs={{4,8},{8,4},{12,16},{16,12},{20,24},{24,20},{5,9},{9,5},{13,17},{1... | collective-permute-start | bytes 18440 | tf_op jit(solution)/shard_map/ppermute | solution.py:37
  41.0 0.0 collective-permute-done.4.refs_3_.refs_2_
  41.0 0.0 collective-permute-done.5.refs_4_.refs_3_
  41.0 0.0 collective-permute-done.8.refs_6_.refs_5_
  41.0 1.0 %collective-permute-done.9.refs_7_.refs_6_ = f32[8,192]{1,0:T(8,128)S(1)} collective-permute-done((f32[8,192]{1,0:T(8,128)S(1)}, f32[8,192]{1,0:T(8,128)S(1)}, u32[]{:S(2)}, u32[]{:S(2)}) %collective-permute-start.9) | collective-permute-done | bytes 6176 | tf_op jit(solution)/shard_map/ppermute | solution.py:37
  42.0 1.8 %shard_map.86 = (bf16[400,384]{1,0:T(8,128)(2,1)S(1)}, bf16[384,384]{1,0:T(8,128)(2,1)S(1)}) custom-call(bf16[384,384]{1,0:T(8,128)(2,1)S(1)} %collective-permute-done.kv_fb.refs_0_, bf16[384,384]{1,0:T(8,128)(2,1)S(1)} %collective-permute-done.1.kv_fa.refs_1_, bf16[384,384]{1,0:T(8,128)(2,1)S(1)} %pad_maximum_fusion.own_qg.refs_2_.refs_1_, ...), custom_call_target="tpu_custom_call" | custom-call | tf_op jit(solution)/shard_map/pallas_call | solution.py:278
  43.8 4.9 %collective-permute-start.10 = (bf16[400,384]{1,0:T(8,128)(2,1)S(1)}, bf16[400,384]{1,0:T(8,128)(2,1)S(1)}, u32[]{:S(2)}, u32[]{:S(2)}) collective-permute-start(bf16[400,384]{1,0:T(8,128)(2,1)S(1)} %get-tuple-element.33), channel_id=1, source_target_pairs={{32,64},{64,32},{96,128},{128,96},{160,192},{192,160},{224,256},{2... | collective-permute-start | bytes 921608 | tf_op jit(solution)/shard_map/ppermute | solution.py:37
  48.7 1.9 %collective-permute-start.11 = (bf16[384,384]{1,0:T(8,128)(2,1)S(1)}, bf16[384,384]{1,0:T(8,128)(2,1)S(1)}, u32[]{:S(2)}, u32[]{:S(2)}) collective-permute-start(bf16[384,384]{1,0:T(8,128)(2,1)S(1)} %get-tuple-element.35), channel_id=1, source_target_pairs={{0,32},{32,0},{64,96},{96,64},{128,160},{160,128},{192,224},{224,1... | collective-permute-start | bytes 884744 | tf_op jit(solution)/shard_map/ppermute | solution.py:37
  50.7 2.2 %shard_map.88.query_blocks = bf16[4,2,48,384]{3,2,1,0:T(8,128)(2,1)S(1)} custom-call(bf16[384,384]{1,0:T(8,128)(2,1)S(1)} %pad_maximum_fusion.own_qg.refs_2_.refs_1_, bf16[1728,384]{1,0:T(8,128)(2,1)S(1)} %get-tuple-element.37.key_ref, bf16[1728,384]{1,0:T(8,128)(2,1)S(1)} %get-tuple-element.38.value_ref, ...), custom_call_target="tpu_custom_call" | custom-call | tf_op jit(solution)/shard_map/pallas_call | solution.py:289
  52.8 1.1 %shard_map.87.own_ref = f32[384,384]{1,0:T(8,128)S(1)} custom-call(bf16[384,384]{1,0:T(8,128)(2,1)S(1)} %pad_maximum_fusion.1.kv.refs_0_, bf16[384,384]{1,0:T(8,128)(2,1)S(1)} %pad_maximum_fusion.own_qg.refs_2_.refs_1_, bf16[384,384]{1,0:T(8,128)(2,1)S(1)} %collective-permute-done.4.refs_3_.refs_2_, ...), custom_call_target="tpu_custom_call" | custom-call | tf_op jit(solution)/shard_map/pallas_call | solution.py:278
  53.9 0.0 collective-permute-done.11.got_a
  53.9 0.0 collective-permute-done.10.got_b
  53.9 0.3 shard_map.89
  54.3 7.5 %collective-permute-start.12 = (bf16[4,48,384]{2,1,0:T(8,128)(2,1)S(1)}, bf16[4,48,384]{2,1,0:T(8,128)(2,1)S(1)}, u32[]{:S(2)}, u32[]{:S(2)}) collective-permute-start(bf16[4,48,384]{2,1,0:T(8,128)(2,1)S(1)} %get-tuple-element.42), channel_id=1, source_target_pairs={{0,2},{1,3},{2,0},{3,1},{4,6},{5,7},{6,4},{7,5},{8,10},{9,11},{10,... | collective-permute-start | bytes 442376 | tf_op jit(solution)/shard_map/ppermute | solution.py:233
  61.7 2.0 %collective-permute-start.13 = (bf16[4,48,384]{2,1,0:T(8,128)(2,1)S(1)}, bf16[4,48,384]{2,1,0:T(8,128)(2,1)S(1)}, u32[]{:S(2)}, u32[]{:S(2)}) collective-permute-start(bf16[4,48,384]{2,1,0:T(8,128)(2,1)S(1)} %get-tuple-element.43), channel_id=1, source_target_pairs={{0,3},{1,2},{2,1},{3,0},{4,7},{5,6},{6,5},{7,4},{8,11},{9,10},{10,... | collective-permute-start | bytes 442376 | tf_op jit(solution)/shard_map/ppermute | solution.py:233
  63.7 2.4 %collective-permute-start.14 = (bf16[4,48,384]{2,1,0:T(8,128)(2,1)S(1)}, bf16[4,48,384]{2,1,0:T(8,128)(2,1)S(1)}, u32[]{:S(2)}, u32[]{:S(2)}) collective-permute-start(bf16[4,48,384]{2,1,0:T(8,128)(2,1)S(1)} %get-tuple-element.44), channel_id=1, source_target_pairs={{0,1},{1,0},{2,3},{3,2},{4,5},{5,4},{6,7},{7,6},{8,9},{9,8},{10,11... | collective-permute-start | bytes 442376 | tf_op jit(solution)/shard_map/ppermute | solution.py:233
  66.1 0.0 collective-permute-done.12.refs_0_
  66.1 9.9 %collective-permute-done.13.refs_1_ = bf16[4,48,384]{2,1,0:T(8,128)(2,1)S(1)} collective-permute-done((bf16[4,48,384]{2,1,0:T(8,128)(2,1)S(1)}, bf16[4,48,384]{2,1,0:T(8,128)(2,1)S(1)}, u32[]{:S(2)}, u32[]{:S(2)}) %collective-permute-start.13) | collective-permute-done | bytes 147488 | tf_op jit(solution)/shard_map/ppermute | solution.py:233
  76.0 1.4 %collective-permute-done.14.refs_2_ = bf16[4,48,384]{2,1,0:T(8,128)(2,1)S(1)} collective-permute-done((bf16[4,48,384]{2,1,0:T(8,128)(2,1)S(1)}, bf16[4,48,384]{2,1,0:T(8,128)(2,1)S(1)}, u32[]{:S(2)}, u32[]{:S(2)}) %collective-permute-start.14) | collective-permute-done | bytes 147488 | tf_op jit(solution)/shard_map/ppermute | solution.py:233
  77.4 1.0 %shard_map.90 = (bf16[24,2,1536]{2,1,0:T(2,128)(2,1)}, bf16[24,2,1536]{2,1,0:T(2,128)(2,1)}, bf16[24,2,1536]{2,1,0:T(2,128)(2,1)}, bf16[24,2,1536]{2,1,0:T(2,128)(2,1)}) custom-call(bf16[4,48,384]{2,1,0:T(8,128)(2,1)S(1)} %collective-permute-done.12.refs_0_, bf16[4,48,384]{2,1,0:T(8,128)(2,1)S(1)} %collective-permute-done.13.refs_1_, ...), custom_call_target="tpu_custom_call" | custom-call | tf_op jit(solution)/shard_map/pallas_call | solution.py:304
Async XLA Ops:
  0.6 28.1 %copy-start = (s32[1,1,1,27]{3,2,1,0:T(1,128)S(1)}, s32[1,1,1,27]{3,2,1,0:T(1,128)}, u32[]{:S(2)}) copy-start(s32[1,1,1,27]{3,2,1,0:T(1,128)} %pairs_v.1) | copy-start | bytes 328
  1.7 15.2 %collective-permute-start.2 = (bf16[384,384]{1,0:T(8,128)(2,1)S(1)}, bf16[384,384]{1,0:T(8,128)(2,1)S(1)}, u32[]{:S(2)}, u32[]{:S(2)}) collective-permute-start(bf16[384,384]{1,0:T(8,128)(2,1)S(1)} %pad_maximum_fusion.1.kv.refs_0_), channel_id=1, source_target_pairs={{0,4},{4,0},{8,12},{12,8},{16,20},{20,16},{24,28},{28,24},{1,5},{5... | collective-permute-start | bytes 884744 | tf_op jit(solution)/shard_map/ppermute | solution.py:37
  3.6 13.3 %collective-permute-start.3 = (bf16[384,384]{1,0:T(8,128)(2,1)S(1)}, bf16[384,384]{1,0:T(8,128)(2,1)S(1)}, u32[]{:S(2)}, u32[]{:S(2)}) collective-permute-start(bf16[384,384]{1,0:T(8,128)(2,1)S(1)} %pad_maximum_fusion.1.kv.refs_0_), channel_id=1, source_target_pairs={{4,8},{8,4},{12,16},{16,12},{20,24},{24,20},{5,9},{9,5},{13,17},{1... | collective-permute-start | bytes 884744 | tf_op jit(solution)/shard_map/ppermute | solution.py:37
  9.7 11.1 %collective-permute-start = (bf16[384,384]{1,0:T(8,128)(2,1)S(1)}, bf16[384,384]{1,0:T(8,128)(2,1)S(1)}, u32[]{:S(2)}, u32[]{:S(2)}) collective-permute-start(bf16[384,384]{1,0:T(8,128)(2,1)S(1)} %pad_maximum_fusion.1.kv.refs_0_), channel_id=1, source_target_pairs={{32,64},{64,32},{96,128},{128,96},{160,192},{192,160},{224,256},{2... | collective-permute-start | bytes 884744 | tf_op jit(solution)/shard_map/ppermute | solution.py:37
  13.9 6.8 %collective-permute-start.1 = (bf16[384,384]{1,0:T(8,128)(2,1)S(1)}, bf16[384,384]{1,0:T(8,128)(2,1)S(1)}, u32[]{:S(2)}, u32[]{:S(2)}) collective-permute-start(bf16[384,384]{1,0:T(8,128)(2,1)S(1)} %pad_maximum_fusion.1.kv.refs_0_), channel_id=1, source_target_pairs={{0,32},{32,0},{64,96},{96,64},{128,160},{160,128},{192,224},{224,1... | collective-permute-start | bytes 884744 | tf_op jit(solution)/shard_map/ppermute | solution.py:37
  17.0 11.7 %collective-permute-start.7 = (bf16[784,384]{1,0:T(8,128)(2,1)S(1)}, bf16[784,384]{1,0:T(8,128)(2,1)S(1)}, u32[]{:S(2)}, u32[]{:S(2)}) collective-permute-start(bf16[784,384]{1,0:T(8,128)(2,1)S(1)} %get-tuple-element.31), channel_id=1, source_target_pairs={{32,64},{64,32},{96,128},{128,96},{160,192},{192,160},{224,256},{2... | collective-permute-start | bytes 1806344 | tf_op jit(solution)/shard_map/ppermute | solution.py:37
  20.8 7.2 %collective-permute-start.6 = (bf16[768,384]{1,0:T(8,128)(2,1)S(1)}, bf16[768,384]{1,0:T(8,128)(2,1)S(1)}, u32[]{:S(2)}, u32[]{:S(2)}) collective-permute-start(bf16[768,384]{1,0:T(8,128)(2,1)S(1)} %get-tuple-element.30.kv_rows), channel_id=1, source_target_pairs={{0,32},{32,0},{64,96},{96,64},{128,160},{160,128},{192,224},{224,1... | collective-permute-start | bytes 1769480 | tf_op jit(solution)/shard_map/ppermute | solution.py:37
  22.7 18.3 %collective-permute-start.4 = (bf16[384,384]{1,0:T(8,128)(2,1)S(1)}, bf16[384,384]{1,0:T(8,128)(2,1)S(1)}, u32[]{:S(2)}, u32[]{:S(2)}) collective-permute-start(bf16[384,384]{1,0:T(8,128)(2,1)S(1)} %pad_maximum_fusion.own_qg.refs_2_.refs_1_), channel_id=1, source_target_pairs={{4,8},{8,4},{12,16},{16,12},{20,24},{24,20},{5,9},{9,5},{13,17},{1... | collective-permute-start | bytes 884744 | tf_op jit(solution)/shard_map/ppermute | solution.py:37
  26.1 14.9 %collective-permute-start.5 = (bf16[384,384]{1,0:T(8,128)(2,1)S(1)}, bf16[384,384]{1,0:T(8,128)(2,1)S(1)}, u32[]{:S(2)}, u32[]{:S(2)}) collective-permute-start(bf16[384,384]{1,0:T(8,128)(2,1)S(1)} %pad_maximum_fusion.own_qg.refs_2_.refs_1_), channel_id=1, source_target_pairs={{0,4},{4,0},{8,12},{12,8},{16,20},{20,16},{24,28},{28,24},{1,5},{5... | collective-permute-start | bytes 884744 | tf_op jit(solution)/shard_map/ppermute | solution.py:37
  32.1 8.9 %collective-permute-start.8 = (f32[8,192]{1,0:T(8,128)S(1)}, f32[8,192]{1,0:T(8,128)S(1)}, u32[]{:S(2)}, u32[]{:S(2)}) collective-permute-start(f32[8,192]{1,0:T(8,128)S(1)} %get-tuple-element.32.refs_5_.refs_4_), channel_id=1, source_target_pairs={{0,4},{4,0},{8,12},{12,8},{16,20},{20,16},{24,28},{28,24},{1,5},{5... | collective-permute-start | bytes 18440 | tf_op jit(solution)/shard_map/ppermute | solution.py:37
  34.8 7.2 %collective-permute-start.9 = (f32[8,192]{1,0:T(8,128)S(1)}, f32[8,192]{1,0:T(8,128)S(1)}, u32[]{:S(2)}, u32[]{:S(2)}) collective-permute-start(f32[8,192]{1,0:T(8,128)S(1)} %get-tuple-element.32.refs_5_.refs_4_), channel_id=1, source_target_pairs={{4,8},{8,4},{12,16},{16,12},{20,24},{24,20},{5,9},{9,5},{13,17},{1... | collective-permute-start | bytes 18440 | tf_op jit(solution)/shard_map/ppermute | solution.py:37
  43.8 10.1 %collective-permute-start.10 = (bf16[400,384]{1,0:T(8,128)(2,1)S(1)}, bf16[400,384]{1,0:T(8,128)(2,1)S(1)}, u32[]{:S(2)}, u32[]{:S(2)}) collective-permute-start(bf16[400,384]{1,0:T(8,128)(2,1)S(1)} %get-tuple-element.33), channel_id=1, source_target_pairs={{32,64},{64,32},{96,128},{128,96},{160,192},{192,160},{224,256},{2... | collective-permute-start | bytes 921608 | tf_op jit(solution)/shard_map/ppermute | solution.py:37
  48.7 5.2 %collective-permute-start.11 = (bf16[384,384]{1,0:T(8,128)(2,1)S(1)}, bf16[384,384]{1,0:T(8,128)(2,1)S(1)}, u32[]{:S(2)}, u32[]{:S(2)}) collective-permute-start(bf16[384,384]{1,0:T(8,128)(2,1)S(1)} %get-tuple-element.35), channel_id=1, source_target_pairs={{0,32},{32,0},{64,96},{96,64},{128,160},{160,128},{192,224},{224,1... | collective-permute-start | bytes 884744 | tf_op jit(solution)/shard_map/ppermute | solution.py:37
  54.3 11.8 %collective-permute-start.12 = (bf16[4,48,384]{2,1,0:T(8,128)(2,1)S(1)}, bf16[4,48,384]{2,1,0:T(8,128)(2,1)S(1)}, u32[]{:S(2)}, u32[]{:S(2)}) collective-permute-start(bf16[4,48,384]{2,1,0:T(8,128)(2,1)S(1)} %get-tuple-element.42), channel_id=1, source_target_pairs={{0,2},{1,3},{2,0},{3,1},{4,6},{5,7},{6,4},{7,5},{8,10},{9,11},{10,... | collective-permute-start | bytes 442376 | tf_op jit(solution)/shard_map/ppermute | solution.py:233
  61.7 14.3 %collective-permute-start.13 = (bf16[4,48,384]{2,1,0:T(8,128)(2,1)S(1)}, bf16[4,48,384]{2,1,0:T(8,128)(2,1)S(1)}, u32[]{:S(2)}, u32[]{:S(2)}) collective-permute-start(bf16[4,48,384]{2,1,0:T(8,128)(2,1)S(1)} %get-tuple-element.43), channel_id=1, source_target_pairs={{0,3},{1,2},{2,1},{3,0},{4,7},{5,6},{6,5},{7,4},{8,11},{9,10},{10,... | collective-permute-start | bytes 442376 | tf_op jit(solution)/shard_map/ppermute | solution.py:233
  63.7 13.7 %collective-permute-start.14 = (bf16[4,48,384]{2,1,0:T(8,128)(2,1)S(1)}, bf16[4,48,384]{2,1,0:T(8,128)(2,1)S(1)}, u32[]{:S(2)}, u32[]{:S(2)}) collective-permute-start(bf16[4,48,384]{2,1,0:T(8,128)(2,1)S(1)} %get-tuple-element.44), channel_id=1, source_target_pairs={{0,1},{1,0},{2,3},{3,2},{4,5},{5,4},{6,7},{7,6},{8,9},{9,8},{10,11... | collective-permute-start | bytes 442376 | tf_op jit(solution)/shard_map/ppermute | solution.py:233
